TPU v7x, 128 devices: a whole 4x4x4 slice. The times are simulated.
128 devices in a mesh: row: 4 (over y), col: 32 (over z, x, core).
Axes of the slice: x: 4, y: 4, z: 4, core: 2. Of those that a mesh axis runs over, the one named last changes fastest.
Arguments:
- coarse: bfloat16 [64, 256, 256], P('row', 'col'), may hold values from -3.5 to 3.5
- norm1_gain: float32 [256], replicated, may hold values from 0.25 to 1.75
- norm1_bias: float32 [256], replicated, may hold values from -2.5 to 2.5
- w_qkv: bfloat16 [256, 768], replicated, may hold values from -1.25 to 1.25
- w_proj: bfloat16 [256, 256], replicated, may hold values from -0.375 to 0.375
- second_norm2_gain: float32 [256], replicated, may hold values from 0.25 to 1.75
- second_norm2_bias: float32 [256], replicated, may hold values from -2.5 to 2.5
- conv_weight: bfloat16 [3, 3, 256, 256], replicated, may hold values from -0.125 to 0.125
- conv_bias: float32 [256], replicated, may hold values from -2.5 to 2.5
- cotangent: bfloat16 [128, 512, 256], P('row', 'col'), may hold values from -6 to 6
Outputs:
- fine_out: bfloat16 [128, 512, 256], P('row', 'col')
- gradient_upsampled_field: bfloat16 [128, 512, 256], P('row', 'col')
- grad_conv: float32 [3, 3, 256, 256], replicated
- grad_norm: float32 [2, 256], replicated
All inputs are finite; a program needn't handle non-finite values.
Results may differ from a plain program's by a relative error of at most 0.009.
The roundings to bfloat16 on the way count: a program that leaves them out, or rounds other values in their place, can miss the bound.
Values may be sent and summed in bfloat16 or wider, within the bound.
No kernel may reach another device: no remote copies, remote signals or barrier semaphores. Data moves between devices by JAX's collectives and lax.ppermute only.
A program may use at most 128 MiB of HBM per device.

v0:
```python
import jax
import jax.numpy as jnp
from jax import lax
from jax.sharding import PartitionSpec as P

HEADS = 4
GROUPS = 32


EPS = 1e-05


def with_halo(cells, sides, width):
    for axis, dim in sides:
        count = lax.axis_size(axis)
        ends = count - 1
        head = lax.slice_in_dim(cells, 0, width, axis=dim)
        tail = lax.slice_in_dim(cells, cells.shape[dim] - width, cells.shape[dim], axis=dim)
        cells = jnp.concatenate(
            [
                lax.ppermute(tail, axis, [(i, (i + 1) % count) for i in range(ends)]),
                cells,
                lax.ppermute(head, axis, [((i + 1) % count, i) for i in range(ends)]),
            ],
            axis=dim,
        )
    return cells


def group_statistics(values):
    width = values.shape[2]
    share = width // GROUPS
    devices = lax.axis_size("row") * lax.axis_size("col")
    count = values.shape[0] * values.shape[1] * devices * share
    first = lax.psum(jnp.sum(values, axis=(0, 1)), ("row", "col"))
    centre = jnp.sum(first.reshape(GROUPS, share), axis=1) / count
    centre_full = jnp.repeat(centre, share)
    centered = values - centre_full
    second = lax.psum(jnp.sum(centered * centered, axis=(0, 1)), ("row", "col"))
    spread = jnp.sum(second.reshape(GROUPS, share), axis=1) / count
    inverse = jnp.repeat(lax.rsqrt(spread + EPS), share)
    return ((values - centre_full) * inverse, inverse)


def upsample(padded):
    upper_even = 0.25 * padded[:-2] + 0.75 * padded[1:-1]
    upper_odd = 0.75 * padded[1:-1] + 0.25 * padded[2:]
    rows_done = jnp.stack([upper_even, upper_odd], axis=1).reshape((-1,) + padded.shape[1:])
    left_even = 0.25 * rows_done[:, :-2] + 0.75 * rows_done[:, 1:-1]
    right_odd = 0.75 * rows_done[:, 1:-1] + 0.25 * rows_done[:, 2:]
    return jnp.stack([left_even, right_odd], axis=2).reshape(
        rows_done.shape[0], -1, padded.shape[2]
    )


def query_blocks(queries):
    length = queries.shape[0]
    shaped = queries.reshape(length // length, length, queries.shape[1], queries.shape[2])
    start_max = jnp.full(shaped.shape[:3], -1e30, jnp.float32)
    start_total = jnp.zeros(shaped.shape[:3], jnp.float32)
    start_accum = jnp.zeros(shaped.shape, jnp.float32)
    return (shaped, (start_max, start_total, start_accum))


def fold_keys(shaped, carry, piece):
    keys, values = piece
    count = keys.shape[0]
    key_block = 2048
    key_blocks = keys.reshape(count // key_block, key_block, keys.shape[1], keys.shape[2])
    value_blocks = values.reshape(count // key_block, key_block, values.shape[1], values.shape[2])
    scale_value = keys.shape[2] ** (-0.5)

    def per_query(parts):
        query_block, running_max, running_total, running_accum = parts

        def per_key(state, pair):
            best, total, accum = state
            key_part, value_part = pair
            scores = (
                jnp.einsum(
                    "qhd,khd->hqk", query_block, key_part, preferred_element_type=jnp.float32
                )
                * scale_value
            )
            fresh = jnp.maximum(best, jnp.max(scores, axis=2).T)
            shrink = jnp.exp(best - fresh)
            weights = jnp.exp(scores - fresh.T[:, :, None])
            total = total * shrink + jnp.sum(weights, axis=2).T
            accum = accum * shrink[:, :, None] + jnp.einsum(
                "hqk,khd->qhd",
                weights.astype(jnp.bfloat16),
                value_part,
                preferred_element_type=jnp.float32,
            )
            return ((fresh, total, accum), None)

        final, unused = lax.scan(
            per_key, (running_max, running_total, running_accum), (key_blocks, value_blocks)
        )
        return final

    return lax.map(per_query, (shaped,) + tuple(carry))


def finish(carry):
    result = carry[2] / carry[1][:, :, :, None]
    return result.reshape(-1, result.shape[2], result.shape[3]).astype(jnp.bfloat16)


def per_device(
    coarse,
    norm1_gain,
    norm1_bias,
    w_qkv,
    w_proj,
    second_norm2_gain,
    second_norm2_bias,
    conv_weight,
    conv_bias,
    cotangent,
):
    block_rows, block_cols, width = coarse.shape
    tokens = block_rows * block_cols
    base = coarse.astype(jnp.float32)
    normed1, unused = group_statistics(base)
    normed1 = (normed1 * norm1_gain + norm1_bias).astype(jnp.bfloat16).reshape(tokens, width)
    triple = jnp.dot(normed1, w_qkv, preferred_element_type=jnp.float32).astype(jnp.bfloat16)
    triple = triple.reshape(tokens, 3, HEADS, width // HEADS)
    shaped, start = query_blocks(triple[:, 0])
    folded = fold_keys(
        shaped,
        start,
        (
            lax.all_gather(triple[:, 1], ("row", "col"), axis=0, tiled=True),
            lax.all_gather(triple[:, 2], ("row", "col"), axis=0, tiled=True),
        ),
    )
    attended = finish(folded)
    attended = attended.reshape(tokens, width)
    merged = (
        base.reshape(tokens, width) + jnp.dot(attended, w_proj, preferred_element_type=jnp.float32)
    ).astype(jnp.bfloat16)
    merged = merged.reshape(block_rows, block_cols, width)
    coarse_pad = with_halo(merged, (("row", 0), ("col", 1)), 1)
    upsampled_field = upsample(coarse_pad.astype(jnp.float32))
    normalized_input2, inverse_deviation2 = group_statistics(upsampled_field)
    offset_values = normalized_input2 * second_norm2_gain + second_norm2_bias
    hidden = jax.nn.silu(offset_values).astype(jnp.bfloat16)
    fine_rows, fine_cols = (upsampled_field.shape[0], upsampled_field.shape[1])
    hidden_pad = with_halo(hidden, (("row", 0), ("col", 1)), 1)
    flat_grad = cotangent.reshape(-1, width)
    output = jnp.zeros((fine_rows * fine_cols, width), jnp.float32) + conv_bias
    weight_rows = []
    for tap_row in range(3):
        weight_cols = []
        for tap_col in range(3):
            window = hidden_pad[
                tap_row : tap_row + fine_rows, tap_col : tap_col + fine_cols
            ].reshape(-1, width)
            output = output + jnp.dot(
                window, conv_weight[tap_row, tap_col], preferred_element_type=jnp.float32
            )
            weight_cols.append(
                lax.dot_general(
                    window, flat_grad, (((0,), (0,)), ((), ())), preferred_element_type=jnp.float32
                )
            )
        weight_rows.append(jnp.stack(weight_cols))
    weight_terms = jnp.stack(weight_rows)
    fine_out = output.astype(jnp.bfloat16).reshape(fine_rows, fine_cols, width)
    weight_total = lax.psum(weight_terms, ("row", "col"))
    grad_pad = with_halo(cotangent, (("row", 0), ("col", 1)), 1)
    grad_hidden = jnp.zeros((fine_rows * fine_cols, width), jnp.float32)
    for tap_row in range(3):
        for tap_col in range(3):
            back_window = grad_pad[
                2 - tap_row : 2 - tap_row + fine_rows, 2 - tap_col : 2 - tap_col + fine_cols
            ].reshape(-1, width)
            grad_hidden = grad_hidden + lax.dot_general(
                back_window,
                conv_weight[tap_row, tap_col],
                (((1,), (1,)), ((), ())),
                preferred_element_type=jnp.float32,
            )
    grad_hidden = grad_hidden.reshape(fine_rows, fine_cols, width)
    sigmoid_value = jax.nn.sigmoid(offset_values)
    gradient_of_offset = grad_hidden * sigmoid_value * (1.0 + offset_values * (1.0 - sigmoid_value))
    channel_sums = jnp.stack(
        [
            jnp.sum(gradient_of_offset * normalized_input2, axis=(0, 1)),
            jnp.sum(gradient_of_offset, axis=(0, 1)),
        ]
    )
    channel_total = lax.psum(channel_sums, ("row", "col"))
    devices = lax.axis_size("row") * lax.axis_size("col")
    root = jnp.sqrt(jnp.float32(fine_rows * fine_cols * devices))
    grad_conv = weight_total / root
    grad_norm = channel_total / root
    share = width // GROUPS
    count = jnp.float32(fine_rows * fine_cols * devices * share)
    mean_over_bias = jnp.repeat(
        jnp.sum((second_norm2_gain * channel_total[1]).reshape(GROUPS, share), axis=1) / count,
        share,
    )
    mean_over_weight = jnp.repeat(
        jnp.sum((second_norm2_gain * channel_total[0]).reshape(GROUPS, share), axis=1) / count,
        share,
    )
    gradient_upsampled_field = (
        inverse_deviation2
        * (
            gradient_of_offset * second_norm2_gain
            - mean_over_bias
            - normalized_input2 * mean_over_weight
        )
    ).astype(jnp.bfloat16)
    return (fine_out, gradient_upsampled_field, grad_conv, grad_norm)


def solution(mesh):
    return jax.shard_map(
        per_device,
        mesh=mesh,
        in_specs=(
            P("row", "col", None),
            P(),
            P(),
            P(),
            P(),
            P(),
            P(),
            P(),
            P(),
            P("row", "col", None),
        ),
        out_specs=(P("row", "col", None), P("row", "col", None), P(), P()),
        check_vma=False,
    )
```

profile of v0, /device:TPU:1, one launch (start us, length us, event | category | flops | bytes accessed | tf_op | source)
XLA Modules:
  0.0 811.7 jit_solution(10426550589056723127)
XLA Ops:
  8.3 68.8 %psum.42 = f32[32,8]{1,0:T(8,128)S(1)} all-reduce(f32[32,8]{1,0:T(8,128)S(1)} %reshape.220), channel_id=1, replica_groups=mesh['row'=4,'col'=32] {'row','col'}, use_global_device_ids=true, to_apply=%region_1.0 | all-reduce | flops 256 | bytes 2048 | tf_op jit(solution)/shard_map/psum | solution.py:35
  78.3 62.6 %psum.43 = f32[32,8]{1,0:T(8,128)S(1)} all-reduce(f32[32,8]{1,0:T(8,128)S(1)} %reshape.221), channel_id=1, replica_groups=mesh['row'=4,'col'=32] {'row','col'}, use_global_device_ids=true, to_apply=%region_4.0 | all-reduce | flops 256 | bytes 2048 | tf_op jit(solution)/shard_map/psum | solution.py:39
  144.7 2.6 collective-permute-start.8
  148.7 3.0 collective-permute-done.9
  151.9 4.3 collective-permute-start.10
  156.3 2.1 collective-permute-start.11
  161.3 58.7 %all-gather.5.cloned.1.call-done = bf16[16384,1,4,64]{0,3,2,1:T(8,128)(2,1)} async-done(((bf16[128,1,4,64]{0,3,2,1:T(8,128)(2,1)}), bf16[16384,1,4,64]{0,3,2,1:T(8,128)(2,1)}) %all-gather.5.cloned.1.call-update) | async-done | bytes 8388624 | tf_op jit(solution)/shard_map/all_gather | solution.py:134
  220.1 16.2 %copy.89 = bf16[32,8,8,2048]{3,2,1,0:T(8,128)(2,1)} copy(bf16[32,8,8,2048]{3,1,2,0:T(8,128)(2,1)} %bitcast.231) | data formatting | bytes 16777216
  236.2 11.5 %copy.60 = bf16[8,2048,4,64]{1,3,2,0:T(8,128)(2,1)} copy(bf16[8,2048,4,64]{1,0,3,2:T(8,128)(2,1)} %bitcast.229) | data formatting | bytes 16777216
  247.7 54.7 %all-gather.7.cloned.1.call-done = bf16[16384,1,4,64]{0,3,2,1:T(8,128)(2,1)} async-done(((bf16[128,1,4,64]{0,3,2,1:T(8,128)(2,1)}), bf16[16384,1,4,64]{0,3,2,1:T(8,128)(2,1)}) %all-gather.7.cloned.1.call-update) | async-done | bytes 8388624 | tf_op jit(solution)/shard_map/all_gather | solution.py:135
  302.4 16.6 %copy.90 = bf16[32,8,8,2048]{3,2,1,0:T(8,128)(2,1)} copy(bf16[32,8,8,2048]{3,1,2,0:T(8,128)(2,1)} %bitcast.232) | data formatting | bytes 16777216
  318.9 11.2 %copy.61 = bf16[8,2048,4,64]{1,3,2,0:T(8,128)(2,1)} copy(bf16[8,2048,4,64]{1,0,3,2:T(8,128)(2,1)} %bitcast.230) | data formatting | bytes 16777216
  330.1 77.8 %while.24 = (s32[]{:T(128)}, f32[128,4]{0,1:T(4,128)S(1)}, f32[128,4]{0,1:T(4,128)S(1)}, f32[128,4,64]{0,2,1:T(8,128)S(1)}, bf16[8,2048,4,64]{1,3,2,0:T(8,128)(2...) while((s32[]{:T(128)}, f32[128,4]{0,1:T(4,128)S(1)}, ...), condition=%wide.region_9.10_spmd.clone, body=%wide.region_6.9_spmd.clone.sunk | while | flops 276924928 | bytes 31818884 | solution.py:97
  330.1 4.1 bitcast_reduce_fusion.2
  334.2 3.0 fusion.152
  337.7 2.2 fusion.153
  339.9 4.0 bitcast_reduce_fusion.2
  344.0 3.0 fusion.152
  347.4 2.2 fusion.153
  349.6 4.0 bitcast_reduce_fusion.2
  353.7 3.0 fusion.152
  357.1 2.2 fusion.153
  359.3 4.0 bitcast_reduce_fusion.2
  363.4 3.0 fusion.152
  366.8 2.2 fusion.153
  369.0 4.0 bitcast_reduce_fusion.2
  373.1 3.0 fusion.152
  376.6 2.2 fusion.153
  378.8 4.0 bitcast_reduce_fusion.2
  382.8 3.0 fusion.152
  386.3 2.2 fusion.153
  388.5 4.0 bitcast_reduce_fusion.2
  392.5 3.0 fusion.152
  396.0 2.2 fusion.153
  398.2 4.0 bitcast_reduce_fusion.2
  402.3 3.0 fusion.152
  405.7 2.2 fusion.153
  408.2 3.1 collective-permute-start
  413.7 1.9 collective-permute-done.1
  415.7 4.4 collective-permute-start.2
  423.0 2.0 collective-permute-done.3
  426.2 66.2 %psum.44 = f32[32,8]{1,0:T(8,128)S(1)} all-reduce(f32[32,8]{1,0:T(8,128)S(1)} %reshape.229), channel_id=1, replica_groups=mesh['row'=4,'col'=32] {'row','col'}, use_global_device_ids=true, to_apply=%region_12.13 | all-reduce | flops 256 | bytes 2048 | tf_op jit(solution)/shard_map/psum | solution.py:35
  492.9 63.3 %psum.45 = f32[32,8]{1,0:T(8,128)S(1)} all-reduce(f32[32,8]{1,0:T(8,128)S(1)} %reshape.230), channel_id=1, replica_groups=mesh['row'=4,'col'=32] {'row','col'}, use_global_device_ids=true, to_apply=%region_15.16 | all-reduce | flops 256 | bytes 2048 | tf_op jit(solution)/shard_map/psum | solution.py:39
  558.3 2.8 multiply_reduce_fusion
  561.0 63.4 %psum.46 = f32[2,256]{1,0:T(2,128)S(1)} all-reduce(f32[2,256]{1,0:T(2,128)S(1)} %pad_maximum_fusion.16), channel_id=1, replica_groups=mesh['row'=4,'col'=32] {'row','col'}, use_global_device_ids=true, to_apply=%region_19.20 | all-reduce | flops 512 | bytes 4096 | tf_op jit(solution)/shard_map/psum | solution.py:194
  634.5 4.3 collective-permute-start.6
  652.4 149.2 %all-reduce.2.cloned.1.call-done = f32[3,3,256,256]{3,2,1,0:T(8,128)} async-done(((f32[3,3,256,256]{3,2,1,0:T(8,128)}), f32[3,3,256,256]{3,2,1,0:T(8,128)}) %all-reduce.2.cloned.1.call-update) | async-done | bytes 2359312 | tf_op jit(solution)/shard_map/psum | solution.py:171
  801.7 3.3 broadcast_multiply_fusion
  (197 shorter events, 46.5 us)
Async XLA Ops:
  7.2 134.1 %copy-start = (bf16[256,768]{1,0:T(8,128)(2,1)S(1)}, bf16[256,768]{1,0:T(8,128)(2,1)}, u32[]{:S(2)}) copy-start(bf16[256,768]{1,0:T(8,128)(2,1)} %param.15) | copy-start | bytes 1179652
  7.2 144.6 %copy-start.4 = (bf16[32,16,256]{2,1,0:T(8,128)(2,1)S(1)}, bf16[32,16,256]{2,1,0:T(8,128)(2,1)}, u32[]{:S(2)}) copy-start(bf16[32,16,256]{2,1,0:T(8,128)(2,1)} %param.21) | copy-start | bytes 786436
  7.2 151.2 %copy-start.3 = (bf16[3,3,256,256]{3,2,1,0:T(8,128)(2,1)S(1)}, bf16[3,3,256,256]{3,2,1,0:T(8,128)(2,1)}, u32[]{:S(2)}) copy-start(bf16[3,3,256,256]{3,2,1,0:T(8,128)(2,1)} %param.19) | copy-start | bytes 3538948
  7.2 212.9 %all-gather.5.cloned.1.call-start = ((), (), s32[]{:S(2)}) async-start(), calls=%async_computation.1 | async-start | bytes 8454144 | tf_op jit(solution)/shard_map/all_gather | solution.py:134
  143.2 159.1 %all-gather.7.cloned.1.call-start = ((), (), s32[]{:S(2)}) async-start(), calls=%async_computation.2 | async-start | bytes 8454144 | tf_op jit(solution)/shard_map/all_gather | solution.py:135
  144.0 657.7 %all-reduce.2.cloned.1.call-start = ((), (), s32[]{:S(2)}) async-start(), calls=%async_computation | async-start | bytes 4718592 | tf_op jit(solution)/shard_map/psum | solution.py:171
  144.7 4.0 collective-permute-start.8
  147.4 4.4 collective-permute-start.9
  151.9 7.8 collective-permute-start.10
  156.3 3.5 collective-permute-start.11
  330.1 77.8 %copy-start.5 = (bf16[16,8,256]{2,1,0:T(8,128)(2,1)S(1)}, bf16[16,8,256]{2,1,0:T(8,128)(2,1)}, u32[]{:S(2)}) copy-start(bf16[16,8,256]{2,1,0:T(8,128)(2,1)} %param.12) | copy-start | bytes 196612
  330.1 77.8 %copy-start.8 = (bf16[256,256]{1,0:T(8,128)(2,1)S(1)}, bf16[256,256]{1,0:T(8,128)(2,1)}, u32[]{:S(2)}) copy-start(bf16[256,256]{1,0:T(8,128)(2,1)} %param.16) | copy-start | bytes 393220
  334.2 3.4 copy-start.2
  343.9 3.4 copy-start.2
  353.7 3.4 copy-start.2
  363.4 3.4 copy-start.2
  373.1 3.4 copy-start.2
  382.8 3.4 copy-start.2
  392.5 3.4 copy-start.2
  402.3 3.4 copy-start.2
  408.2 5.5 collective-permute-start
  411.3 4.4 collective-permute-start.1
  415.7 7.4 collective-permute-start.2
  420.1 5.0 collective-permute-start.3
  425.2 131.3 %copy-start.9 = (f32[256]{0:T(256)S(1)}, f32[256]{0:T(256)}, u32[]{:S(2)}) copy-start(f32[256]{0:T(256)} %param.17) | copy-start | bytes 3076
  425.2 131.3 %copy-start.10 = (f32[256]{0:T(256)S(1)}, f32[256]{0:T(256)}, u32[]{:S(2)}) copy-start(f32[256]{0:T(256)} %param.18) | copy-start | bytes 3076
  627.8 4.9 collective-permute-start.4
  629.5 4.5 collective-permute-start.5
  634.5 7.5 collective-permute-start.6
  638.8 5.1 collective-permute-start.7
  646.0 1.0 copy-start.7
  648.7 1.0 copy-start.11
  648.7 1.2 copy-start.6
  651.5 153.4 %copy-start.1 = (bf16[256,768]{1,0:T(8,128)(2,1)S(1)}, bf16[256,768]{1,0:T(8,128)(2,1)}, u32[]{:S(2)}) copy-start(bf16[256,768]{1,0:T(8,128)(2,1)} %param.15) | copy-start | bytes 1179652
Sparse Core Ops, SparseCore 0:
  143.3 76.6 all-gather.4
  223.5 78.8 all-gather.6
  648.8 152.8 all-reduce.1
where the time goes:
time: 817 us; the launch traced here: 812 us
  blocking collectives  324 us (40%)
  waiting for transfers between devices  274 us (34%)
  local copies, waits for them, and re-layouts  68 us (8%)
  matrix products  64.6 us (8%)
  other arithmetic  36 us (4%)
  starting transfers between devices  30.4 us (4%)
  between operations  14.7 us (2%)
    psum x1, waiting for transfers between devices, per_device(): weight_total = lax.psum(weight_terms, ('row', 'col'))  149 us
    psum x2, blocking collectives, group_statistics(): first = lax.psum(jnp.sum(values, axis=(0, 1)), ('row', 'col'))  135 us
    psum x2, blocking collectives, group_statistics(): second = lax.psum(jnp.sum(centered * centered, axis=(0, 1)), ('row', 'col'))  126 us
    psum x1, blocking collectives, per_device(): channel_total = lax.psum(channel_sums, ('row', 'col'))  63.4 us
    all_gather x1, waiting for transfers between devices, per_device(): lax.all_gather(triple[:, 1], ('row', 'col'), axis=0, tiled=True)  58.7 us
    unnamed x28, local copies, waits for them, and re-layouts  56.8 us
    all_gather x1, waiting for transfers between devices, per_device(): lax.all_gather(triple[:, 2], ('row', 'col'), axis=0, tiled=True)  54.7 us
    dot_general x8, matrix products, per_key(): jnp.einsum('qhd,khd->hqk', query_block, key_part, preferred_element_type=...  32.4 us
  transfers between devices with their start and end apart: 15, of which 8 were waited for; matrix products, arithmetic and copies ran while one was open for 5% of the time, Pallas kernels for 0%

commit v1 on v0

v1 whole, which is shorter than its diff:
```python
import functools

import jax
import jax.numpy as jnp
import numpy as np
from jax import lax
from jax.experimental import pallas as pl
from jax.experimental.pallas import tpu as pltpu
from jax.sharding import Mesh, PartitionSpec as P

HEADS = 4
HD = 64
C = 256
SHARE = 8
EPS = 1e-05
F32 = jnp.float32
BF16 = jnp.bfloat16
VMEM_LIMIT = 50 * 2**20
ZXC = ("z", "x", "c")
ALL = ("y", "z", "x", "c")

CELLS_IN = 192
FINE_ROWS = 34
WIN = FINE_ROWS * 16


def upsample_matrix():
    def line(f):
        i = f // 2
        return {i: 0.75, (i - 1 if f % 2 == 0 else i + 1): 0.25}

    table = np.zeros((3, FINE_ROWS, 16, CELLS_IN), np.float32)
    for b in range(3):
        for fr in range(FINE_ROWS):
            for j in range(16):
                for r, wr in line(fr - 1).items():
                    for c, wc in line(j + b - 1).items():
                        table[b, fr, j, (r + 1) * 10 + c + 1] += wr * wc
    return table.reshape(3 * WIN, CELLS_IN)


UPSAMPLE = upsample_matrix()


def params(grid=None):
    return pltpu.CompilerParams(
        vmem_limit_bytes=VMEM_LIMIT,
        dimension_semantics=None if grid is None else ("arbitrary",) * grid,
    )


def dot(a, b, contract=((1,), (0,))):
    return lax.dot_general(a, b, (contract, ((), ())), preferred_element_type=F32)


def dot_exact(a, b, contract=((1,), (0,))):
    return lax.dot_general(
        a, b, (contract, ((), ())), preferred_element_type=F32, precision=lax.Precision.HIGHEST
    )


def iota(shape, dim):
    return lax.broadcasted_iota(jnp.int32, shape, dim)


def group_row(mean_c, var_c):
    same = jnp.where((iota((C, C), 0) >> 3) == (iota((C, C), 1) >> 3), 1.0 / SHARE, 0.0)
    mean8 = jnp.broadcast_to(mean_c, (8, C))
    spread = mean8 - dot_exact(mean8, same)
    var8 = jnp.broadcast_to(var_c, (8, C)) + spread * spread
    lane = iota((C, 128), 1)
    group = iota((C, 128), 0) >> 3
    to_mean = jnp.where(lane == group, 1.0 / SHARE, 0.0)
    to_var = jnp.where(lane == group + 32, 1.0 / SHARE, 0.0)
    return dot_exact(mean8, to_mean) + dot_exact(var8, to_var)


def combine_groups(rows):
    count = rows.shape[0]
    mean = jnp.sum(rows, axis=0, keepdims=True) / count
    off = rows - mean
    scatter = jnp.sum(off * off, axis=0, keepdims=True) / count
    group = iota((128, C), 1) >> 3
    lane = iota((128, C), 0)
    from_mean = jnp.where(lane == group, 1.0, 0.0)
    from_var = jnp.where(lane == group + 32, 1.0, 0.0)
    mean8 = jnp.broadcast_to(mean, (8, 128))
    scatter8 = jnp.broadcast_to(scatter, (8, 128))
    mean_c = dot_exact(mean8, from_mean)
    var_c = dot_exact(mean8, from_var) + dot_exact(scatter8, from_mean)
    return mean_c[:1], lax.rsqrt(var_c + EPS)[:1]


def split3(value):
    high = value.astype(BF16)
    rest = value - high.astype(F32)
    middle = rest.astype(BF16)
    low = (rest - middle.astype(F32)).astype(BF16)
    return high, middle, low


def channel_stats(value):
    count = value.shape[0]
    mean = jnp.sum(value, axis=0, keepdims=True) / count
    off = value - mean
    return mean, jnp.sum(off * off, axis=0, keepdims=True) / count


def stats_kernel(a, b, c, d, out):
    parts = [r[...].astype(F32) for r in (a, b, c, d)]
    count = 4 * parts[0].shape[0]
    mean = sum(jnp.sum(p, axis=0, keepdims=True) for p in parts) / count
    var = 0.0
    for p in parts:
        off = p - mean
        var = var + jnp.sum(off * off, axis=0, keepdims=True)
    out[...] = group_row(mean, var / count)


def local_stats(pieces):
    return pl.pallas_call(
        stats_kernel,
        out_shape=jax.ShapeDtypeStruct((8, 128), F32),
        compiler_params=params(),
    )(*pieces)


def attention_kernel(
    order, q_ref, k0, k1, k2, k3, s0, s1, s2, s3, gain, bias, w_qkv, out, keys, values, norm
):
    step = pl.program_id(0)

    @pl.when(step == 0)
    def _():
        rows = jnp.concatenate([s0[...], s1[...], s2[...], s3[...]], axis=0)
        mean, inverse = combine_groups(rows)
        norm[0:1, :] = mean
        norm[1:2, :] = inverse
        for i, piece in enumerate((k0, k1, k2, k3)):
            normed = (piece[...].astype(F32) - mean) * inverse
            normed = (normed * gain[...] + bias[...]).astype(BF16)
            both = dot(normed, w_qkv[:, C:])
            size = piece.shape[0]
            keys[pl.ds(i * size, size), :] = both[:, :C].astype(BF16)
            values[pl.ds(i * size, size), :] = both[:, C:].astype(BF16)

    normed = (q_ref[0].astype(F32) - norm[0:1, :]) * norm[1:2, :]
    normed = (normed * gain[...] + bias[...]).astype(BF16)
    queries = dot(normed, w_qkv[:, :C]).astype(BF16) * jnp.asarray(HD**-0.5, BF16)
    head_of = iota((CELLS_IN, C), 1) >> 6
    lane = iota((CELLS_IN, 128), 1)
    result = jnp.zeros((CELLS_IN, C), F32)
    logs = jnp.zeros((CELLS_IN, 128), F32)
    for head in range(HEADS):
        mine = head_of == head
        masked = jnp.where(mine, queries, jnp.zeros_like(queries))
        scores = dot(masked, keys[...], ((1,), (1,)))
        top = jnp.max(scores, axis=1, keepdims=True)
        weights = jnp.exp(scores - top)
        total = jnp.sum(weights, axis=1, keepdims=True)
        mixed = dot(weights.astype(BF16), values[...])
        result = jnp.where(mine, mixed / total, result)
        logs = jnp.where(lane == head, top + jnp.log(total), logs)
    out[0, :CELLS_IN, :] = result.astype(BF16)
    turned = jnp.concatenate([logs.T[:8], jnp.zeros((8, 64), F32)], axis=1)
    high, middle, low = split3(turned)
    line = iota((16, C), 0)
    packed = jnp.zeros((16, C), F32)
    for i, part in enumerate((high, middle, low)):
        wide = part.astype(F32)
        wide = jnp.concatenate([wide, wide], axis=0)
        if i:
            wide = pltpu.roll(wide, 4 * i, 0)
        packed = jnp.where((line >= 4 * i) & (line < 4 * i + 4), wide, packed)
    out[0, CELLS_IN:, :] = packed.astype(BF16)


def partial_attention(order, queries, pieces, stats, gain, bias, w_qkv):
    whole = lambda shape: pl.BlockSpec(shape, lambda i, o: (0,) * len(shape))
    key_count = sum(p.shape[0] for p in pieces)
    return pl.pallas_call(
        attention_kernel,
        out_shape=jax.ShapeDtypeStruct((8, CELLS_IN + 16, C), BF16),
        grid_spec=pltpu.PrefetchScalarGridSpec(
            num_scalar_prefetch=1,
            grid=(8,),
            in_specs=[pl.BlockSpec((1, CELLS_IN, C), lambda i, o: (i, 0, 0))]
            + [whole(p.shape) for p in pieces]
            + [whole(s.shape) for s in stats]
            + [whole((1, C)), whole((1, C)), whole(w_qkv.shape)],
            out_specs=pl.BlockSpec((1, CELLS_IN + 16, C), lambda i, o: (o[i], 0, 0)),
            scratch_shapes=[
                pltpu.VMEM((key_count, C), BF16),
                pltpu.VMEM((key_count, C), BF16),
                pltpu.VMEM((8, C), F32),
            ],
        ),
        compiler_params=params(1),
    )(order, queries, *pieces, *stats, gain, bias, w_qkv)


def merge_kernel(flags, parts, coarse, w_proj, up, merged_out, stats_out):
    count = parts.shape[0]
    logs = []
    for i in range(count):
        tail = parts[i, CELLS_IN:, :].astype(F32)
        logs.append(tail[0:4] + tail[4:8] + tail[8:12])
    top = functools.reduce(jnp.maximum, logs)
    shares = [jnp.exp(v - top) for v in logs]
    total = sum(shares)
    spread = jnp.where((iota((8, C), 1) >> 6) == iota((8, C), 0), 1.0, 0.0)
    attended = jnp.zeros((CELLS_IN, C), F32)
    for i in range(count):
        share = shares[i] / total
        share = jnp.concatenate([share, jnp.zeros_like(share)], axis=0)[:, :CELLS_IN]
        wide = dot_exact(share, spread, ((0,), (0,)))
        attended = attended + wide * parts[i, :CELLS_IN, :].astype(F32)
    merged = coarse[...].astype(F32) + dot(attended.astype(BF16), w_proj[...])
    cell = iota((CELLS_IN, C), 0)
    col = lax.rem(cell, 10)
    outside = (
        ((cell < 10) & (flags[0] == 1))
        | ((cell >= 170) & (flags[1] == 1))
        | ((col == 0) & (flags[2] == 1))
        | ((col == 9) & (flags[3] == 1))
        | (cell >= 180)
    )
    merged = jnp.where(outside, 0.0, merged).astype(BF16)
    merged_out[...] = merged
    field = dot(up[WIN + 16 : WIN + 528, :], merged)
    mean, var = channel_stats(field)
    stats_out[...] = jnp.broadcast_to(group_row(mean, var)[:1], stats_out.shape)


def merge(flags, parts, coarse, w_proj, up):
    vmem = pl.BlockSpec(memory_space=pltpu.VMEM)
    return pl.pallas_call(
        merge_kernel,
        out_shape=(
            jax.ShapeDtypeStruct((CELLS_IN, C), BF16),
            jax.ShapeDtypeStruct((128, 128), F32),
        ),
        in_specs=[pl.BlockSpec(memory_space=pltpu.SMEM)] + [vmem] * 4,
        out_specs=(vmem, vmem),
        compiler_params=params(),
    )(flags, parts, coarse, w_proj, up)


def back_kernel(c0, c1, c2, weight, out):
    windows = (c0, c1, c2)
    total = jnp.zeros((512, C), F32)
    for a in range(3):
        for b in range(3):
            window = windows[2 - b][16 * (2 - a) : 16 * (2 - a) + 512, :]
            total = total + dot(window, weight[3 * a + b], ((1,), (1,)))
    out[...] = total


def back_conv(windows, weight):
    return pl.pallas_call(
        back_kernel,
        out_shape=jax.ShapeDtypeStruct((512, C), F32),
        compiler_params=params(),
        cost_estimate=pl.CostEstimate(
            flops=9 * 2 * 512 * C * C, bytes_accessed=3 * 10**6, transcendentals=0
        ),
    )(*windows, weight)


def conv_kernel(
    flags,
    merged,
    up,
    stats,
    gain,
    bias,
    weight,
    conv_bias,
    cot,
    grad_hidden,
    fine_out,
    halves,
    shift_out,
    xhat_out,
    inverse_out,
    hid0,
    hid1,
    hid2,
):
    mean, inverse = combine_groups(stats[...])
    inverse_out[...] = jnp.broadcast_to(inverse, (8, C))
    hidden = (hid0, hid1, hid2)
    row = iota((WIN, C), 0)
    col = row & 15
    for b in range(3):
        field = dot(up[b * WIN : (b + 1) * WIN, :], merged[...])
        xhat = (field - mean) * inverse
        shifted = xhat * gain[...] + bias[...]
        sig = 1.0 / (1.0 + jnp.exp(-shifted))
        outside = ((row < 16) & (flags[0] == 1)) | ((row >= 528) & (flags[1] == 1))
        if b == 0:
            outside = outside | ((col == 0) & (flags[2] == 1))
        if b == 2:
            outside = outside | ((col == 15) & (flags[3] == 1))
        hidden[b][...] = jnp.where(outside, 0.0, shifted * sig).astype(BF16)
        if b == 1:
            inner = slice(16, 528)
            s, t = sig[inner], shifted[inner]
            grad_shift = grad_hidden[...] * s * (1.0 + t * (1.0 - s))
            shift_out[...] = grad_shift
            xhat_out[...] = xhat[inner]
            sum_w = jnp.sum(grad_shift * xhat[inner], axis=0, keepdims=True)
            sum_b = jnp.sum(grad_shift, axis=0, keepdims=True)
            rows = []
            for part in range(3):
                for value in (sum_w, sum_b):
                    piece = split3(value)[part].astype(F32)
                    rows += [piece[:, :128], piece[:, 128:]]
            tail = jnp.concatenate(rows + [jnp.zeros((4, 128), F32)], axis=0).astype(BF16)
            halves[0, 2304:, :] = tail
            halves[1, 2304:, :] = tail
    total = jnp.zeros((512, C), F32) + conv_bias[...]
    for a in range(3):
        for b in range(3):
            tap = 3 * a + b
            window = hidden[b][16 * a : 16 * a + 512, :]
            total = total + dot(window, weight[tap])
            product = dot(window, cot[...], ((0,), (0,)))
            halves[0, tap * C : (tap + 1) * C, :] = product[:, :128].astype(BF16)
            halves[1, tap * C : (tap + 1) * C, :] = product[:, 128:].astype(BF16)
    fine_out[...] = total.astype(BF16)


def conv(flags, merged, up, stats, gain, bias, weight, conv_bias, cot, grad_hidden):
    vmem = pl.BlockSpec(memory_space=pltpu.VMEM)
    return pl.pallas_call(
        conv_kernel,
        out_shape=(
            jax.ShapeDtypeStruct((512, C), BF16),
            jax.ShapeDtypeStruct((2, 2320, 128), BF16),
            jax.ShapeDtypeStruct((512, C), F32),
            jax.ShapeDtypeStruct((512, C), F32),
            jax.ShapeDtypeStruct((8, C), F32),
        ),
        in_specs=[pl.BlockSpec(memory_space=pltpu.SMEM)] + [vmem] * 9,
        out_specs=(vmem,) * 5,
        scratch_shapes=[pltpu.VMEM((WIN, C), BF16)] * 3,
        compiler_params=params(),
    )(flags, merged, up, stats, gain, bias, weight, conv_bias, cot, grad_hidden)


def pair_kernel(kept, got, out, total):
    total[...] = kept[...].astype(F32) + got[...].astype(F32)
    tails = [r[2304:, :].astype(F32) for r in (kept, got)]
    sums = sum(t[0:4] + t[4:8] + t[8:12] for t in tails)
    parts = [p.astype(F32) for p in split3(sums)]
    tail = jnp.concatenate([jnp.zeros((36, 128), F32)] + parts, axis=0)
    own = iota((48, 128), 0) < 36
    for i in range(64):
        out[i] = jnp.where(own, total[36 * i : 36 * i + 48, :], tail).astype(BF16)


def pair_sum(kept, got):
    return pl.pallas_call(
        pair_kernel,
        out_shape=jax.ShapeDtypeStruct((64, 48, 128), BF16),
        scratch_shapes=[pltpu.VMEM((2320, 128), F32)],
        compiler_params=params(),
    )(kept, got)


def shift(value, axis, count, step):
    return lax.ppermute(value, axis, [((i + step) % count, i) for i in range(count)])


def line_halo(value, axis, count, dim):
    size = value.shape[dim]
    tail = lax.slice_in_dim(value, size - 1, size, axis=dim)
    head = lax.slice_in_dim(value, 0, 1, axis=dim)
    before = lax.ppermute(tail, axis, [(i, i + 1) for i in range(count - 1)])
    after = lax.ppermute(head, axis, [(i + 1, i) for i in range(count - 1)])
    return jnp.concatenate([before, value, after], axis=dim)


def per_device(
    coarse,
    norm1_gain,
    norm1_bias,
    w_qkv,
    w_proj,
    second_norm2_gain,
    second_norm2_bias,
    conv_weight,
    conv_bias,
    cotangent,
):
    y, c = lax.axis_index("y"), lax.axis_index("c")
    block = lax.axis_index(ZXC)
    flags = jnp.stack([y == 0, y == 3, block == 0, block == 31]).astype(jnp.int32)
    up = jnp.asarray(UPSAMPLE, BF16)
    taps = conv_weight.reshape(9, C, C)

    own = coarse.reshape(128, C)
    line = jnp.concatenate([own] + [shift(own, "x", 4, k) for k in (1, 3, 2)], axis=0)
    pieces = [line] + [shift(line, "z", 4, k) for k in (1, 3, 2)]

    wide = line_halo(coarse, ZXC, 32, 1)
    blocks = [wide] + [shift(wide, "y", 4, k) for k in (1, 2, 3)]
    around = []
    for k in range(4):
        cells = jnp.concatenate([blocks[k - 1][-1:], blocks[k], blocks[(k + 1) % 4][:1]], axis=0)
        around.append(jnp.pad(cells.reshape(180, C), ((0, CELLS_IN - 180), (0, 0))))
    mine = jnp.stack(around)
    queries = jnp.concatenate([mine, shift(mine, "c", 2, 1)], axis=0)
    order = jnp.stack(
        [((y + k) % 4) * 2 + (c + j) % 2 for j in range(2) for k in range(4)]
    ).astype(jnp.int32)

    grad = line_halo(line_halo(cotangent, "y", 4, 0), ZXC, 32, 1)
    windows = [grad[:, b : b + 16].reshape(WIN, C) for b in range(3)]
    grad_hidden = back_conv(windows, taps)

    stats = local_stats(pieces)
    stats = jnp.concatenate([stats, shift(stats, "c", 2, 1)], axis=0)
    stats = [stats] + [shift(stats, "y", 4, k) for k in (1, 2, 3)]
    partial = partial_attention(
        order, queries, pieces, stats, norm1_gain[None], norm1_bias[None], w_qkv
    )
    partial = lax.all_to_all(partial, ("y", "c"), 0, 0, tiled=True)
    merged, stats2 = merge(flags, partial, mine[0], w_proj, up)
    stats2 = lax.all_to_all(stats2.reshape(128, 1, 128), ALL, 0, 0, tiled=True)
    fine, halves, grad_shift, xhat, inverse = conv(
        flags,
        merged,
        up,
        stats2.reshape(128, 128),
        second_norm2_gain[None],
        second_norm2_bias[None],
        taps,
        conv_bias[None],
        cotangent.reshape(512, C),
        grad_hidden,
    )

    kept = lax.dynamic_index_in_dim(halves, c, 0, keepdims=False)
    given = lax.dynamic_index_in_dim(halves, 1 - c, 0, keepdims=False)
    sent = pair_sum(kept, shift(given, "c", 2, 1))
    got = lax.all_to_all(sent, ("y", "z", "x"), 0, 0, tiled=True)
    total = jnp.sum(got.astype(F32), axis=0)
    root = jnp.sqrt(jnp.float32(65536))
    sums = jnp.sum(total[36:].reshape(3, 2, C), axis=0)
    chunk = (total[:36] / root).astype(BF16)
    spread = lax.all_to_all(
        jnp.broadcast_to(chunk[None], (64, 36, 128)), ("y", "z", "x"), 0, 0, tiled=True
    ).reshape(2304, 128)
    other = shift(spread, "c", 2, 1)
    left = jnp.where(c == 0, spread, other)
    right = jnp.where(c == 0, other, spread)
    grad_conv = jnp.concatenate([left, right], axis=1).astype(F32).reshape(3, 3, C, C)
    grad_norm = sums / root

    count = jnp.float32(65536 * SHARE)
    per_group = (second_norm2_gain * sums).reshape(2, 32, SHARE).sum(axis=2) / count
    mean_w, mean_b = jnp.repeat(per_group, SHARE, axis=1)
    field = inverse[0] * (grad_shift * second_norm2_gain - mean_b - xhat * mean_w)
    return (
        fine.reshape(32, 16, C),
        field.astype(BF16).reshape(32, 16, C),
        grad_conv,
        grad_norm,
    )


def solution(mesh):
    split = Mesh(mesh.devices.reshape(4, 4, 4, 2), ALL)
    cells = P("y", ZXC, None)
    return jax.shard_map(
        per_device,
        mesh=split,
        in_specs=(cells,) + (P(),) * 8 + (cells,),
        out_specs=(cells, cells, P(), P()),
        check_vma=False,
    )
```

time: 817 us -> 179 us (0.22)
  blocking collectives: 324 us -> 19.9 us
  waiting for transfers between devices: 274 us -> 35.8 us
  matrix products: 64.6 us -> 0 us
  local copies, waits for them, and re-layouts: 68 us -> 8.4 us
  Pallas kernels: 0 us -> 40.8 us
  starting transfers between devices: 30.4 us -> 65.3 us
  other arithmetic: 36 us -> 6.38 us
  between operations: 14.7 us -> 1.16 us
    psum x5 -> x0, blocking collectives: 324 us -> none  [the longest x2 135 us: group_statistics(): first = lax.psum(jnp.sum(values, axis=(0, 1)), ('row', 'col'))]
    psum x1 -> x0, waiting for transfers between devices: 149 us -> none  [per_device(): weight_total = lax.psum(weight_terms, ('row', 'col'))]
    all_gather x2 -> x0, waiting for transfers between devices: 113 us -> none  [the longest x1 58.7 us: per_device(): lax.all_gather(triple[:, 1], ('row', 'col'), axis=0, tiled=True)]
    dot_general x45 -> x0, matrix products: 64.6 us -> none  [the longest x8 32.4 us: per_key(): jnp.einsum('qhd,khd->hqk', query_block, key_part, preferred_element_type=...]
    unnamed x28 -> x42, local copies, waits for them, and re-layouts: 56.8 us -> 3.19 us
    pallas_call x0 -> x6, Pallas kernels: none -> 40.8 us  [the longest x1 31.8 us: partial_attention(): pl.pallas_call(attention_kernel, out_shape=jax.ShapeDtypeStruct((8, CELLS...]
    reduce_sum x19 -> x3, other arithmetic: 27 us -> 0.25 us  [the longest x1 0.14 us: per_device(): total = jnp.sum(got.astype(F32), axis=0)]
    all_to_all x0 -> x3, waiting for transfers between devices: none -> 20.1 us  [the longest x1 12.5 us: per_device(): lax.all_to_all(jnp.broadcast_to(chunk[None], (64, 36, 128)), ('y', 'z', '...]
  transfers between devices with their start and end apart: 15 -> 25, of which waited for: 8 -> 10; matrix products, arithmetic and copies ran while one was open for 5% -> 3% of each run, Pallas kernels for 0% -> 3%
where the time goes in v1:
time: 179 us; the launch traced here: 178 us
  starting transfers between devices  65.3 us (36%)
  Pallas kernels  40.8 us (23%)
  waiting for transfers between devices  35.8 us (20%)
  blocking collectives  19.9 us (11%)
  local copies, waits for them, and re-layouts  8.4 us (5%)
  other arithmetic  6.38 us (4%)
    pallas_call x1, Pallas kernels, partial_attention(): pl.pallas_call(attention_kernel, out_shape=jax.ShapeDtypeStruct((8, CELLS...  31.8 us
    ppermute x16, starting transfers between devices, shift(): lax.ppermute(value, axis, [((i + step) % count, i) for i in range(count)])  29.5 us
    all_to_all x1, blocking collectives, per_device(): got = lax.all_to_all(sent, ('y', 'z', 'x'), 0, 0, tiled=True)  19.9 us
    all_to_all x1, waiting for transfers between devices, per_device(): lax.all_to_all(jnp.broadcast_to(chunk[None], (64, 36, 128)), ('y', 'z', '...  12.5 us
    ppermute x3, starting transfers between devices, line_halo(): before = lax.ppermute(tail, axis, [(i, i + 1) for i in range(count - 1)])  10.5 us
    ppermute x16, waiting for transfers between devices, shift(): lax.ppermute(value, axis, [((i + step) % count, i) for i in range(count)])  9 us
    all_to_all x1, starting transfers between devices, per_device(): stats2 = lax.all_to_all(stats2.reshape(128, 1, 128), ALL, 0, 0, tiled=True)  8.88 us
    all_to_all x1, waiting for transfers between devices, per_device(): stats2 = lax.all_to_all(stats2.reshape(128, 1, 128), ALL, 0, 0, tiled=True)  7.51 us
  transfers between devices with their start and end apart: 25, of which 10 were waited for; matrix products, arithmetic and copies ran while one was open for 3% of the time, Pallas kernels for 3%

profile of v1, /device:TPU:1, one launch (start us, length us, event | category | flops | bytes accessed | tf_op | source)
XLA Modules:
  0.0 177.8 jit_solution(15307605948189167190)
XLA Ops:
  0.6 1.0 fusion.8
  1.6 4.5 %collective-permute-start = (bf16[16,1,256]{2,1,0:T(2,128)(2,1)S(1)}, bf16[16,1,256]{2,1,0:T(2,128)(2,1)S(1)}, u32[]{:S(2)}, u32[]{:S(2)}) collective-permute-start(bf16[16,1,256]{2,1,0:T(2,128)(2,1)S(1)} %get-tuple-element.38), channel_id=1, source_target_pairs={{0,1},{1,2},{2,3},{3,4},{4,5},{5,6},{6,7},{7,8},{8,9},{9,10},{10,1... | collective-permute-start | bytes 24584 | tf_op jit(solution)/shard_map/ppermute | solution.py:380
  6.1 1.9 %collective-permute-start.1 = (bf16[16,1,256]{2,1,0:T(2,128)(2,1)S(1)}, bf16[16,1,256]{2,1,0:T(2,128)(2,1)S(1)}, u32[]{:S(2)}, u32[]{:S(2)}) collective-permute-start(bf16[16,1,256]{2,1,0:T(2,128)(2,1)S(1)} %get-tuple-element.39), channel_id=1, source_target_pairs={{1,0},{2,1},{3,2},{4,3},{5,4},{6,5},{7,6},{8,7},{9,8},{10,9},{11,1... | collective-permute-start | bytes 24584 | tf_op jit(solution)/shard_map/ppermute | solution.py:381
  8.1 2.5 %collective-permute-start.8 = (bf16[128,256]{1,0:T(8,128)(2,1)}, bf16[128,256]{1,0:T(8,128)(2,1)S(1)}, u32[]{:S(2)}, u32[]{:S(2)}) collective-permute-start(bf16[128,256]{1,0:T(8,128)(2,1)} %bitcast.70), channel_id=1, source_target_pairs={{4,0},{6,2},{0,4},{2,6},{5,1},{7,3},{1,5},{3,7},{12,8},{14,10},{8,... | collective-permute-start | bytes 196616 | tf_op jit(solution)/shard_map/ppermute | solution.py:373
  10.6 0.9 collective-permute-start.7
  11.5 1.7 collective-permute-start.6
  13.4 0.9 pad_maximum_fusion.8
  14.3 3.0 %collective-permute-start.4 = (bf16[16,10,256]{2,1,0:T(8,128)(2,1)S(1)}, bf16[16,10,256]{2,1,0:T(8,128)(2,1)S(1)}, u32[]{:S(2)}, u32[]{:S(2)}) collective-permute-start(bf16[16,10,256]{2,1,0:T(8,128)(2,1)S(1)} %pad_maximum_fusion.8), channel_id=1, source_target_pairs={{64,0},{96,32},{0,64},{32,96},{65,1},{97,33},{1,65},{33,97},{66,2}... | collective-permute-start | bytes 245768 | tf_op jit(solution)/shard_map/ppermute | solution.py:373
  17.3 0.8 collective-permute-start.3
  18.1 0.7 collective-permute-start.2
  18.8 0.9 pad_maximum_fusion.3.a.k0
  19.6 3.7 %collective-permute-start.11 = (bf16[512,256]{1,0:T(8,128)(2,1)S(1)}, bf16[512,256]{1,0:T(8,128)(2,1)S(1)}, u32[]{:S(2)}, u32[]{:S(2)}) collective-permute-start(bf16[512,256]{1,0:T(8,128)(2,1)S(1)} %pad_maximum_fusion.3.a.k0), channel_id=1, source_target_pairs={{16,0},{24,8},{0,16},{8,24},{17,1},{25,9},{1,17},{9,25},{18,2},{26... | collective-permute-start | bytes 786440 | tf_op jit(solution)/shard_map/ppermute | solution.py:373
  23.3 0.7 collective-permute-start.10
  24.0 1.9 %collective-permute-start.9 = (bf16[512,256]{1,0:T(8,128)(2,1)S(1)}, bf16[512,256]{1,0:T(8,128)(2,1)S(1)}, u32[]{:S(2)}, u32[]{:S(2)}) collective-permute-start(bf16[512,256]{1,0:T(8,128)(2,1)S(1)} %pad_maximum_fusion.3.a.k0), channel_id=1, source_target_pairs={{8,0},{16,8},{24,16},{0,24},{9,1},{17,9},{25,17},{1,25},{10,2},{18... | collective-permute-start | bytes 786440 | tf_op jit(solution)/shard_map/ppermute | solution.py:373
  26.6 3.5 %collective-permute-start.5 = (bf16[4,192,256]{2,1,0:T(8,128)(2,1)S(1)}, bf16[4,192,256]{2,1,0:T(8,128)(2,1)S(1)}, u32[]{:S(2)}, u32[]{:S(2)}) collective-permute-start(bf16[4,192,256]{2,1,0:T(8,128)(2,1)S(1)} %pad_maximum_fusion), channel_id=1, source_target_pairs={{1,0},{0,1},{3,2},{2,3},{5,4},{4,5},{7,6},{6,7},{9,8},{8,9},{11,10... | collective-permute-start | bytes 1179656 | tf_op jit(solution)/shard_map/ppermute | solution.py:373
  30.1 4.0 %collective-permute-done.10.c.k2 = bf16[512,256]{1,0:T(8,128)(2,1)S(1)} collective-permute-done((bf16[512,256]{1,0:T(8,128)(2,1)S(1)}, bf16[512,256]{1,0:T(8,128)(2,1)S(1)}, u32[]{:S(2)}, u32[]{:S(2)}) %collective-permute-start.10) | collective-permute-done | bytes 262176 | tf_op jit(solution)/shard_map/ppermute | solution.py:373
  34.1 1.1 shard_map.138
  35.1 2.9 %collective-permute-start.12 = (f32[8,128]{1,0:T(8,128)S(1)}, f32[8,128]{1,0:T(8,128)S(1)}, u32[]{:S(2)}, u32[]{:S(2)}) collective-permute-start(f32[8,128]{1,0:T(8,128)S(1)} %shard_map.138), channel_id=1, source_target_pairs={{1,0},{0,1},{3,2},{2,3},{5,4},{4,5},{7,6},{6,7},{9,8},{8,9},{11,10... | collective-permute-start | bytes 12296 | tf_op jit(solution)/shard_map/ppermute | solution.py:373
  38.0 0.8 collective-permute-done.12
  39.2 2.8 %collective-permute-start.14 = (f32[16,128]{1,0:T(8,128)S(1)}, f32[16,128]{1,0:T(8,128)S(1)}, u32[]{:S(2)}, u32[]{:S(2)}) collective-permute-start(f32[16,128]{1,0:T(8,128)S(1)} %pad_maximum_fusion.9.s0), channel_id=1, source_target_pairs={{64,0},{96,32},{0,64},{32,96},{65,1},{97,33},{1,65},{33,97},{66,2}... | collective-permute-start | bytes 24584 | tf_op jit(solution)/shard_map/ppermute | solution.py:373
  42.5 0.7 collective-permute-done.14.s2
  43.2 1.4 collective-permute-done.13.s1
  44.6 31.8 %shard_map.139 = bf16[8,208,256]{2,1,0:T(8,128)(2,1)} custom-call(s32[8]{0:T(128)S(1)} %stack.70.order, bf16[8,192,256]{2,1,0:T(8,128)(2,1)S(1)} %constant_dynamic-update-slice_fusion.q_ref, bf16[512,256]{1,0:T(8,128)(2,1)S(1)} %pad_maximum_fusion.3.a.k0, bf16[512,256]{1,0:T(8,128)(2,1)S(1)} %collective-permute-done.9.b.k1, ...), custom_call_target="tpu_custom_call" | custom-call | tf_op jit(solution)/shard_map/pallas_call | solution.py:181
  76.4 5.5 %all-to-all-start = ((bf16[8,208,256]{2,1,0:T(8,128)(2,1)}), bf16[8,208,256]{2,1,0:T(8,128)(2,1)S(1)}, u32[]{:S(2)}, u32[]{:S(2)}) async-start(bf16[8,208,256]{2,1,0:T(8,128)(2,1)} %shard_map.139), calls=%async_computation | async-start | bytes 1703936 | tf_op jit(solution)/shard_map/all_to_all | solution.py:429
  82.0 3.3 %collective-permute-start.16 = (bf16[1,16,256]{2,1,0:T(8,128)(2,1)S(1)}, bf16[1,16,256]{2,1,0:T(8,128)(2,1)S(1)}, u32[]{:S(2)}, u32[]{:S(2)}) collective-permute-start(bf16[1,16,256]{2,1,0:T(8,128)(2,1)S(1)} %get-tuple-element.27), channel_id=1, source_target_pairs={{0,32},{32,64},{64,96},{1,33},{33,65},{65,97},{2,34},{34,66},{66,9... | collective-permute-start | bytes 24584 | tf_op jit(solution)/shard_map/ppermute | solution.py:380
  85.3 1.3 collective-permute-start.17
  86.6 5.2 %collective-permute-done.16 = bf16[1,16,256]{2,1,0:T(8,128)(2,1)S(1)} collective-permute-done((bf16[1,16,256]{2,1,0:T(8,128)(2,1)S(1)}, bf16[1,16,256]{2,1,0:T(8,128)(2,1)S(1)}, u32[]{:S(2)}, u32[]{:S(2)}) %collective-permute-start.16) | collective-permute-done | bytes 8224 | tf_op jit(solution)/shard_map/ppermute | solution.py:380
  91.8 1.5 collective-permute-done.17
  94.0 3.1 %collective-permute-start.19 = (bf16[34,1,256]{2,1,0:T(2,128)(2,1)}, bf16[34,1,256]{2,1,0:T(2,128)(2,1)S(1)}, u32[]{:S(2)}, u32[]{:S(2)}) collective-permute-start(bf16[34,1,256]{2,1,0:T(2,128)(2,1)} %get-tuple-element.24), channel_id=1, source_target_pairs={{1,0},{2,1},{3,2},{4,3},{5,4},{6,5},{7,6},{8,7},{9,8},{10,9},{11,1... | collective-permute-start | bytes 52232 | tf_op jit(solution)/shard_map/ppermute | solution.py:381
  97.1 2.7 %collective-permute-start.18 = (bf16[34,1,256]{2,1,0:T(2,128)(2,1)}, bf16[34,1,256]{2,1,0:T(2,128)(2,1)}, u32[]{:S(2)}, u32[]{:S(2)}) collective-permute-start(bf16[34,1,256]{2,1,0:T(2,128)(2,1)} %get-tuple-element.25), channel_id=1, source_target_pairs={{0,1},{1,2},{2,3},{3,4},{4,5},{5,6},{6,7},{7,8},{8,9},{9,10},{10,1... | collective-permute-start | bytes 52232 | tf_op jit(solution)/shard_map/ppermute | solution.py:380
  99.9 0.9 copy-done.8
  100.8 3.0 %shard_map.140 = (bf16[192,256]{1,0:T(8,128)(2,1)S(1)}, f32[128,128]{1,0:T(8,128)S(1)}) custom-call(s32[4]{0:T(128)S(1)} %add_convert_fusion.flags, bf16[8,208,256]{2,1,0:T(8,128)(2,1)S(1)} %all-to-all-done.parts, bf16[192,256]{1,0:T(8,128)(2,1)S(1)} %get-tuple-element.36.coarse, bf16[256,256]{1,0:T(8,128)(2,1)S(1)} %copy-done.8, bf16[1632,192]{1,0:T(8,128)(2,1)S(1)} %copy-done.1), custom_call_target="tpu_custom_call" | custom-call | tf_op jit(solution)/shard_map/pallas_call | solution.py:237
  105.0 8.9 %all-to-all-start.1 = ((f32[128,1,128]{2,1,0:T(1,128)}), f32[128,1,128]{2,1,0:T(1,128)S(1)}, u32[]{:S(2)}, u32[]{:S(2)}) async-start(f32[128,1,128]{2,1,0:T(1,128)} %bitcast.62), calls=%async_computation.1 | async-start | bytes 131072 | tf_op jit(solution)/shard_map/all_to_all | solution.py:431
  114.0 1.0 pad_maximum_fusion.1
  115.0 0.8 shard_map.141.grad_hidden
  115.8 7.5 %all-to-all-done.1 = f32[128,1,128]{2,1,0:T(1,128)S(1)} async-done(((f32[128,1,128]{2,1,0:T(1,128)}), f32[128,1,128]{2,1,0:T(1,128)S(1)}, u32[]{:S(2)}, u32[]{:S(2)}) %all-to-all-start.1) | async-done | bytes 65568 | tf_op jit(solution)/shard_map/all_to_all | solution.py:431
  123.4 0.9 copy-done.10
  124.3 3.9 %shard_map.142 = (bf16[512,256]{1,0:T(8,128)(2,1)}, bf16[2,2320,128]{2,1,0:T(8,128)(2,1)}, f32[512,256]{1,0:T(8,128)S(1)}, f32[512,256]{1,0:T(8,128)S(1)}, f32[8,256]{1,0:T(8,128)S(1)}) custom-call(s32[4]{0:T(128)S(1)} %add_convert_fusion.flags, bf16[192,256]{1,0:T(8,128)(2,1)S(1)} %copy-done.10, bf16[1632,192]{1,0:T(8,128)(2,1)S(1)} %copy-done.1, ...), custom_call_target="tpu_custom_call" | custom-call | tf_op jit(solution)/shard_map/pallas_call | solution.py:336
  128.2 1.7 dynamic-slice_bitcast_fusion
  129.9 0.9 collective-permute-start.20
  130.8 1.6 collective-permute-done.20.got
  132.7 19.9 %all_to_all.20 = bf16[64,48,128]{2,1,0:T(8,128)(2,1)S(1)} all-to-all(bf16[64,48,128]{2,1,0:T(8,128)(2,1)S(1)} %shard_map.143), channel_id=1, replica_groups=mesh['y'=4,'z'=4,'x'=4,'c'=2] {'y','z','x'}, dimensions={0} | all-to-all | bytes 1572864 | tf_op jit(solution)/shard_map/all_to_all | solution.py:448
  152.8 0.9 broadcast_in_dim.41
  153.7 4.6 %all-to-all-start.3 = ((bf16[64,36,128]{2,1,0:T(8,128)(2,1)}), bf16[64,36,128]{2,1,0:T(8,128)(2,1)S(1)}, u32[]{:S(2)}, u32[]{:S(2)}) async-start(bf16[64,36,128]{2,1,0:T(8,128)(2,1)} %broadcast_in_dim.41), calls=%async_computation.3 | async-start | bytes 1310720 | tf_op jit(solution)/shard_map/all_to_all | solution.py:453
  158.7 12.5 %all-to-all-done.3 = bf16[64,36,128]{2,1,0:T(8,128)(2,1)S(1)} async-done(((bf16[64,36,128]{2,1,0:T(8,128)(2,1)}), bf16[64,36,128]{2,1,0:T(8,128)(2,1)S(1)}, u32[]{:S(2)}, u32[]{:S(2)}) %all-to-all-start.3) | async-done | bytes 589856 | tf_op jit(solution)/shard_map/all_to_all | solution.py:453
  171.4 3.0 %collective-permute-start.21 = (bf16[2304,128]{1,0:T(8,128)(2,1)S(1)}, bf16[2304,128]{1,0:T(8,128)(2,1)S(1)}, u32[]{:S(2)}, u32[]{:S(2)}) collective-permute-start(bf16[2304,128]{1,0:T(8,128)(2,1)S(1)} %reshape.91), channel_id=1, source_target_pairs={{1,0},{0,1},{3,2},{2,3},{5,4},{4,5},{7,6},{6,7},{9,8},{8,9},{11,10... | collective-permute-start | bytes 1769480 | tf_op jit(solution)/shard_map/ppermute | solution.py:373
  175.3 0.8 multiply_convert_fusion
  176.2 1.6 maximum_convert_fusion
  (100 shorter events, 5.4 us)
Async XLA Ops:
  0.6 25.6 %copy-start.17 = (bf16[16,8,256]{2,1,0:T(8,128)(2,1)S(1)}, bf16[16,8,256]{2,1,0:T(8,128)(2,1)}, u32[]{:S(2)}) copy-start(bf16[16,8,256]{2,1,0:T(8,128)(2,1)} %param.11) | copy-start | bytes 196612
  1.6 11.7 %collective-permute-start = (bf16[16,1,256]{2,1,0:T(2,128)(2,1)S(1)}, bf16[16,1,256]{2,1,0:T(2,128)(2,1)S(1)}, u32[]{:S(2)}, u32[]{:S(2)}) collective-permute-start(bf16[16,1,256]{2,1,0:T(2,128)(2,1)S(1)} %get-tuple-element.38), channel_id=1, source_target_pairs={{0,1},{1,2},{2,3},{3,4},{4,5},{5,6},{6,7},{7,8},{8,9},{9,10},{10,1... | collective-permute-start | bytes 24584 | tf_op jit(solution)/shard_map/ppermute | solution.py:380
  6.1 7.2 %collective-permute-start.1 = (bf16[16,1,256]{2,1,0:T(2,128)(2,1)S(1)}, bf16[16,1,256]{2,1,0:T(2,128)(2,1)S(1)}, u32[]{:S(2)}, u32[]{:S(2)}) collective-permute-start(bf16[16,1,256]{2,1,0:T(2,128)(2,1)S(1)} %get-tuple-element.39), channel_id=1, source_target_pairs={{1,0},{2,1},{3,2},{4,3},{5,4},{6,5},{7,6},{8,7},{9,8},{10,9},{11,1... | collective-permute-start | bytes 24584 | tf_op jit(solution)/shard_map/ppermute | solution.py:381
  8.1 10.0 %collective-permute-start.8 = (bf16[128,256]{1,0:T(8,128)(2,1)}, bf16[128,256]{1,0:T(8,128)(2,1)S(1)}, u32[]{:S(2)}, u32[]{:S(2)}) collective-permute-start(bf16[128,256]{1,0:T(8,128)(2,1)} %bitcast.70), channel_id=1, source_target_pairs={{4,0},{6,2},{0,4},{2,6},{5,1},{7,3},{1,5},{3,7},{12,8},{14,10},{8,... | collective-permute-start | bytes 196616 | tf_op jit(solution)/shard_map/ppermute | solution.py:373
  10.6 8.2 %collective-permute-start.7 = (bf16[128,256]{1,0:T(8,128)(2,1)}, bf16[128,256]{1,0:T(8,128)(2,1)S(1)}, u32[]{:S(2)}, u32[]{:S(2)}) collective-permute-start(bf16[128,256]{1,0:T(8,128)(2,1)} %bitcast.71), channel_id=1, source_target_pairs={{6,0},{0,2},{2,4},{4,6},{7,1},{1,3},{3,5},{5,7},{14,8},{8,10},{10,... | collective-permute-start | bytes 196616 | tf_op jit(solution)/shard_map/ppermute | solution.py:373
  11.5 7.2 %collective-permute-start.6 = (bf16[128,256]{1,0:T(8,128)(2,1)}, bf16[128,256]{1,0:T(8,128)(2,1)S(1)}, u32[]{:S(2)}, u32[]{:S(2)}) collective-permute-start(bf16[128,256]{1,0:T(8,128)(2,1)} %bitcast.72), channel_id=1, source_target_pairs={{2,0},{4,2},{6,4},{0,6},{3,1},{5,3},{7,5},{1,7},{10,8},{12,10},{14... | collective-permute-start | bytes 196616 | tf_op jit(solution)/shard_map/ppermute | solution.py:373
  14.3 9.8 %collective-permute-start.4 = (bf16[16,10,256]{2,1,0:T(8,128)(2,1)S(1)}, bf16[16,10,256]{2,1,0:T(8,128)(2,1)S(1)}, u32[]{:S(2)}, u32[]{:S(2)}) collective-permute-start(bf16[16,10,256]{2,1,0:T(8,128)(2,1)S(1)} %pad_maximum_fusion.8), channel_id=1, source_target_pairs={{64,0},{96,32},{0,64},{32,96},{65,1},{97,33},{1,65},{33,97},{66,2}... | collective-permute-start | bytes 245768 | tf_op jit(solution)/shard_map/ppermute | solution.py:373
  17.3 8.7 %collective-permute-start.3 = (bf16[16,10,256]{2,1,0:T(8,128)(2,1)S(1)}, bf16[16,10,256]{2,1,0:T(8,128)(2,1)S(1)}, u32[]{:S(2)}, u32[]{:S(2)}) collective-permute-start(bf16[16,10,256]{2,1,0:T(8,128)(2,1)S(1)} %pad_maximum_fusion.8), channel_id=1, source_target_pairs={{32,0},{64,32},{96,64},{0,96},{33,1},{65,33},{97,65},{1,97},{34,2}... | collective-permute-start | bytes 245768 | tf_op jit(solution)/shard_map/ppermute | solution.py:373
  18.1 8.0 %collective-permute-start.2 = (bf16[16,10,256]{2,1,0:T(8,128)(2,1)S(1)}, bf16[16,10,256]{2,1,0:T(8,128)(2,1)S(1)}, u32[]{:S(2)}, u32[]{:S(2)}) collective-permute-start(bf16[16,10,256]{2,1,0:T(8,128)(2,1)S(1)} %pad_maximum_fusion.8), channel_id=1, source_target_pairs={{96,0},{0,32},{32,64},{64,96},{97,1},{1,33},{33,65},{65,97},{98,2}... | collective-permute-start | bytes 245768 | tf_op jit(solution)/shard_map/ppermute | solution.py:373
  19.6 10.5 %collective-permute-start.11 = (bf16[512,256]{1,0:T(8,128)(2,1)S(1)}, bf16[512,256]{1,0:T(8,128)(2,1)S(1)}, u32[]{:S(2)}, u32[]{:S(2)}) collective-permute-start(bf16[512,256]{1,0:T(8,128)(2,1)S(1)} %pad_maximum_fusion.3.a.k0), channel_id=1, source_target_pairs={{16,0},{24,8},{0,16},{8,24},{17,1},{25,9},{1,17},{9,25},{18,2},{26... | collective-permute-start | bytes 786440 | tf_op jit(solution)/shard_map/ppermute | solution.py:373
  23.3 10.8 %collective-permute-start.10 = (bf16[512,256]{1,0:T(8,128)(2,1)S(1)}, bf16[512,256]{1,0:T(8,128)(2,1)S(1)}, u32[]{:S(2)}, u32[]{:S(2)}) collective-permute-start(bf16[512,256]{1,0:T(8,128)(2,1)S(1)} %pad_maximum_fusion.3.a.k0), channel_id=1, source_target_pairs={{24,0},{0,8},{8,16},{16,24},{25,1},{1,9},{9,17},{17,25},{26,2},{2,... | collective-permute-start | bytes 786440 | tf_op jit(solution)/shard_map/ppermute | solution.py:373
  24.0 10.1 %collective-permute-start.9 = (bf16[512,256]{1,0:T(8,128)(2,1)S(1)}, bf16[512,256]{1,0:T(8,128)(2,1)S(1)}, u32[]{:S(2)}, u32[]{:S(2)}) collective-permute-start(bf16[512,256]{1,0:T(8,128)(2,1)S(1)} %pad_maximum_fusion.3.a.k0), channel_id=1, source_target_pairs={{8,0},{16,8},{24,16},{0,24},{9,1},{17,9},{25,17},{1,25},{10,2},{18... | collective-permute-start | bytes 786440 | tf_op jit(solution)/shard_map/ppermute | solution.py:373
  26.5 18.2 %copy-start.7 = (bf16[256,768]{1,0:T(8,128)(2,1)S(1)}, bf16[256,768]{1,0:T(8,128)(2,1)}, u32[]{:S(2)}) copy-start(bf16[256,768]{1,0:T(8,128)(2,1)} %w_qkv.1) | copy-start | bytes 1179652
  26.5 18.2 %copy-start.13 = (f32[256]{0:T(256)S(1)}, f32[256]{0:T(256)}, u32[]{:S(2)}) copy-start(f32[256]{0:T(256)} %param.12) | copy-start | bytes 3076
  26.5 18.1 %copy-start.14 = (f32[256]{0:T(256)S(1)}, f32[256]{0:T(256)}, u32[]{:S(2)}) copy-start(f32[256]{0:T(256)} %param.13) | copy-start | bytes 3076
  26.6 15.4 %collective-permute-start.5 = (bf16[4,192,256]{2,1,0:T(8,128)(2,1)S(1)}, bf16[4,192,256]{2,1,0:T(8,128)(2,1)S(1)}, u32[]{:S(2)}, u32[]{:S(2)}) collective-permute-start(bf16[4,192,256]{2,1,0:T(8,128)(2,1)S(1)} %pad_maximum_fusion), channel_id=1, source_target_pairs={{1,0},{0,1},{3,2},{2,3},{5,4},{4,5},{7,6},{6,7},{9,8},{8,9},{11,10... | collective-permute-start | bytes 1179656 | tf_op jit(solution)/shard_map/ppermute | solution.py:373
  35.1 3.7 %collective-permute-start.12 = (f32[8,128]{1,0:T(8,128)S(1)}, f32[8,128]{1,0:T(8,128)S(1)}, u32[]{:S(2)}, u32[]{:S(2)}) collective-permute-start(f32[8,128]{1,0:T(8,128)S(1)} %shard_map.138), channel_id=1, source_target_pairs={{1,0},{0,1},{3,2},{2,3},{5,4},{4,5},{7,6},{6,7},{9,8},{8,9},{11,10... | collective-permute-start | bytes 12296 | tf_op jit(solution)/shard_map/ppermute | solution.py:373
  38.8 3.7 %collective-permute-start.15 = (f32[16,128]{1,0:T(8,128)S(1)}, f32[16,128]{1,0:T(8,128)S(1)}, u32[]{:S(2)}, u32[]{:S(2)}) collective-permute-start(f32[16,128]{1,0:T(8,128)S(1)} %pad_maximum_fusion.9.s0), channel_id=1, source_target_pairs={{96,0},{0,32},{32,64},{64,96},{97,1},{1,33},{33,65},{65,97},{98,2}... | collective-permute-start | bytes 24584 | tf_op jit(solution)/shard_map/ppermute | solution.py:373
  39.2 4.0 %collective-permute-start.14 = (f32[16,128]{1,0:T(8,128)S(1)}, f32[16,128]{1,0:T(8,128)S(1)}, u32[]{:S(2)}, u32[]{:S(2)}) collective-permute-start(f32[16,128]{1,0:T(8,128)S(1)} %pad_maximum_fusion.9.s0), channel_id=1, source_target_pairs={{64,0},{96,32},{0,64},{32,96},{65,1},{97,33},{1,65},{33,97},{66,2}... | collective-permute-start | bytes 24584 | tf_op jit(solution)/shard_map/ppermute | solution.py:373
  42.0 2.6 %collective-permute-start.13 = (f32[16,128]{1,0:T(8,128)S(1)}, f32[16,128]{1,0:T(8,128)S(1)}, u32[]{:S(2)}, u32[]{:S(2)}) collective-permute-start(f32[16,128]{1,0:T(8,128)S(1)} %pad_maximum_fusion.9.s0), channel_id=1, source_target_pairs={{32,0},{64,32},{96,64},{0,96},{33,1},{65,33},{97,65},{1,97},{34,2}... | collective-permute-start | bytes 24584 | tf_op jit(solution)/shard_map/ppermute | solution.py:373
  76.4 5.5 %copy-start.2 = (bf16[32,16,256]{2,1,0:T(8,128)(2,1)S(1)}, bf16[32,16,256]{2,1,0:T(8,128)(2,1)}, u32[]{:S(2)}) copy-start(bf16[32,16,256]{2,1,0:T(8,128)(2,1)} %param.20) | copy-start | bytes 786436
  76.4 23.4 %copy-start.1 = (bf16[1632,192]{1,0:T(8,128)(2,1)S(1)}, bf16[1632,192]{1,0:T(8,128)(2,1)}, u32[]{:S(2)}) copy-start(bf16[1632,192]{1,0:T(8,128)(2,1)} %constant.102.clone.up) | copy-start | bytes 1880068
  76.4 23.4 %all-to-all-start = ((bf16[8,208,256]{2,1,0:T(8,128)(2,1)}), bf16[8,208,256]{2,1,0:T(8,128)(2,1)S(1)}, u32[]{:S(2)}, u32[]{:S(2)}) async-start(bf16[8,208,256]{2,1,0:T(8,128)(2,1)} %shard_map.139), calls=%async_computation | async-start | bytes 1703936 | tf_op jit(solution)/shard_map/all_to_all | solution.py:429
  82.0 9.8 %collective-permute-start.16 = (bf16[1,16,256]{2,1,0:T(8,128)(2,1)S(1)}, bf16[1,16,256]{2,1,0:T(8,128)(2,1)S(1)}, u32[]{:S(2)}, u32[]{:S(2)}) collective-permute-start(bf16[1,16,256]{2,1,0:T(8,128)(2,1)S(1)} %get-tuple-element.27), channel_id=1, source_target_pairs={{0,32},{32,64},{64,96},{1,33},{33,65},{65,97},{2,34},{34,66},{66,9... | collective-permute-start | bytes 24584 | tf_op jit(solution)/shard_map/ppermute | solution.py:380
  85.3 8.1 %collective-permute-start.17 = (bf16[1,16,256]{2,1,0:T(8,128)(2,1)S(1)}, bf16[1,16,256]{2,1,0:T(8,128)(2,1)S(1)}, u32[]{:S(2)}, u32[]{:S(2)}) collective-permute-start(bf16[1,16,256]{2,1,0:T(8,128)(2,1)S(1)} %get-tuple-element.26), channel_id=1, source_target_pairs={{32,0},{64,32},{96,64},{33,1},{65,33},{97,65},{34,2},{66,34},{98,6... | collective-permute-start | bytes 24584 | tf_op jit(solution)/shard_map/ppermute | solution.py:381
  91.8 23.2 %copy-start = (bf16[3,3,256,256]{3,2,1,0:T(8,128)(2,1)S(1)}, bf16[3,3,256,256]{3,2,1,0:T(8,128)(2,1)}, u32[]{:S(2)}) copy-start(bf16[3,3,256,256]{3,2,1,0:T(8,128)(2,1)} %param.18) | copy-start | bytes 3538948
  94.0 19.9 %collective-permute-start.19 = (bf16[34,1,256]{2,1,0:T(2,128)(2,1)}, bf16[34,1,256]{2,1,0:T(2,128)(2,1)S(1)}, u32[]{:S(2)}, u32[]{:S(2)}) collective-permute-start(bf16[34,1,256]{2,1,0:T(2,128)(2,1)} %get-tuple-element.24), channel_id=1, source_target_pairs={{1,0},{2,1},{3,2},{4,3},{5,4},{6,5},{7,6},{8,7},{9,8},{10,9},{11,1... | collective-permute-start | bytes 52232 | tf_op jit(solution)/shard_map/ppermute | solution.py:381
  97.1 16.9 %collective-permute-start.18 = (bf16[34,1,256]{2,1,0:T(2,128)(2,1)}, bf16[34,1,256]{2,1,0:T(2,128)(2,1)}, u32[]{:S(2)}, u32[]{:S(2)}) collective-permute-start(bf16[34,1,256]{2,1,0:T(2,128)(2,1)} %get-tuple-element.25), channel_id=1, source_target_pairs={{0,1},{1,2},{2,3},{3,4},{4,5},{5,6},{6,7},{7,8},{8,9},{9,10},{10,1... | collective-permute-start | bytes 52232 | tf_op jit(solution)/shard_map/ppermute | solution.py:380
  99.9 0.9 copy-start.8
  103.8 0.7 copy-start.9
  104.4 0.6 copy-start.11
  105.0 18.3 %all-to-all-start.1 = ((f32[128,1,128]{2,1,0:T(1,128)}), f32[128,1,128]{2,1,0:T(1,128)S(1)}, u32[]{:S(2)}, u32[]{:S(2)}) async-start(f32[128,1,128]{2,1,0:T(1,128)} %bitcast.62), calls=%async_computation.1 | async-start | bytes 131072 | tf_op jit(solution)/shard_map/all_to_all | solution.py:431
  113.9 9.4 %copy-start.12 = (f32[256]{0:T(256)S(1)}, f32[256]{0:T(256)}, u32[]{:S(2)}) copy-start(f32[256]{0:T(256)} %param.16) | copy-start | bytes 3076
  113.9 9.4 %copy-start.15 = (f32[256]{0:T(256)S(1)}, f32[256]{0:T(256)}, u32[]{:S(2)}) copy-start(f32[256]{0:T(256)} %param.17) | copy-start | bytes 3076
  114.0 9.4 %copy-start.16 = (f32[256]{0:T(256)S(1)}, f32[256]{0:T(256)}, u32[]{:S(2)}) copy-start(f32[256]{0:T(256)} %param.19) | copy-start | bytes 3076
  123.4 0.9 copy-start.10
  128.2 4.5 %copy-start.3 = (f32[512,256]{1,0:T(8,128)}, f32[512,256]{1,0:T(8,128)S(1)}, u32[]{:S(2)}) copy-start(f32[512,256]{1,0:T(8,128)S(1)} %get-tuple-element.15) | copy-start | bytes 1572868
  128.2 4.6 %copy-start.5 = (f32[512,256]{1,0:T(8,128)}, f32[512,256]{1,0:T(8,128)S(1)}, u32[]{:S(2)}) copy-start(f32[512,256]{1,0:T(8,128)S(1)} %get-tuple-element.17) | copy-start | bytes 1572868
  129.9 2.6 %collective-permute-start.20 = (bf16[2320,128]{1,0:T(8,128)(2,1)S(1)}, bf16[2320,128]{1,0:T(8,128)(2,1)S(1)}, u32[]{:S(2)}, u32[]{:S(2)}) collective-permute-start(bf16[2320,128]{1,0:T(8,128)(2,1)S(1)} %get-tuple-element.18), channel_id=1, source_target_pairs={{1,0},{0,1},{3,2},{2,3},{5,4},{4,5},{7,6},{6,7},{9,8},{8,9},{11,10... | collective-permute-start | bytes 1781768 | tf_op jit(solution)/shard_map/ppermute | solution.py:373
  152.8 22.5 %copy-start.4 = (f32[512,256]{1,0:T(8,128)S(1)}, f32[512,256]{1,0:T(8,128)}, u32[]{:S(2)}) copy-start(f32[512,256]{1,0:T(8,128)} %copy-done.3) | copy-start | bytes 1572868
  152.8 22.5 %copy-start.6 = (f32[512,256]{1,0:T(8,128)S(1)}, f32[512,256]{1,0:T(8,128)}, u32[]{:S(2)}) copy-start(f32[512,256]{1,0:T(8,128)} %copy-done.5) | copy-start | bytes 1572868
  153.7 17.5 %all-to-all-start.3 = ((bf16[64,36,128]{2,1,0:T(8,128)(2,1)}), bf16[64,36,128]{2,1,0:T(8,128)(2,1)S(1)}, u32[]{:S(2)}, u32[]{:S(2)}) async-start(bf16[64,36,128]{2,1,0:T(8,128)(2,1)} %broadcast_in_dim.41), calls=%async_computation.3 | async-start | bytes 1310720 | tf_op jit(solution)/shard_map/all_to_all | solution.py:453
  171.4 4.7 %collective-permute-start.21 = (bf16[2304,128]{1,0:T(8,128)(2,1)S(1)}, bf16[2304,128]{1,0:T(8,128)(2,1)S(1)}, u32[]{:S(2)}, u32[]{:S(2)}) collective-permute-start(bf16[2304,128]{1,0:T(8,128)(2,1)S(1)} %reshape.91), channel_id=1, source_target_pairs={{1,0},{0,1},{3,2},{2,3},{5,4},{4,5},{7,6},{6,7},{9,8},{8,9},{11,10... | collective-permute-start | bytes 1769480 | tf_op jit(solution)/shard_map/ppermute | solution.py:373

commit v2 on v1

--- a/solution.py
+++ b/solution.py
@@ -20,6 +20,7 @@
 ALL = ("y", "z", "x", "c")
 
 CELLS_IN = 192
+STRIP = 1200
 FINE_ROWS = 34
 WIN = FINE_ROWS * 16
 
@@ -106,97 +107,100 @@
     return mean, jnp.sum(off * off, axis=0, keepdims=True) / count
 
 
-def stats_kernel(a, b, c, d, out):
-    parts = [r[...].astype(F32) for r in (a, b, c, d)]
-    count = 4 * parts[0].shape[0]
-    mean = sum(jnp.sum(p, axis=0, keepdims=True) for p in parts) / count
-    var = 0.0
-    for p in parts:
-        off = p - mean
-        var = var + jnp.sum(off * off, axis=0, keepdims=True)
-    out[...] = group_row(mean, var / count)
-
-
-def local_stats(pieces):
+def stats_kernel(cells, out):
+    mean, var = channel_stats(cells[...].astype(F32))
+    out[...] = jnp.broadcast_to(group_row(mean, var)[:1], out.shape)
+
+
+def local_stats(cells):
     return pl.pallas_call(
         stats_kernel,
-        out_shape=jax.ShapeDtypeStruct((8, 128), F32),
-        compiler_params=params(),
-    )(*pieces)
+        out_shape=jax.ShapeDtypeStruct((128, 128), F32),
+        compiler_params=params(),
+    )(cells)
 
 
 def attention_kernel(
-    order, q_ref, k0, k1, k2, k3, s0, s1, s2, s3, gain, bias, w_qkv, out, keys, values, norm
+    order, q_ref, k0, k1, k2, k3, stats, gain, bias, w_qkv, pick, out, keys, values, found, logs
 ):
-    step = pl.program_id(0)
-
-    @pl.when(step == 0)
-    def _():
-        rows = jnp.concatenate([s0[...], s1[...], s2[...], s3[...]], axis=0)
-        mean, inverse = combine_groups(rows)
-        norm[0:1, :] = mean
-        norm[1:2, :] = inverse
-        for i, piece in enumerate((k0, k1, k2, k3)):
-            normed = (piece[...].astype(F32) - mean) * inverse
-            normed = (normed * gain[...] + bias[...]).astype(BF16)
-            both = dot(normed, w_qkv[:, C:])
-            size = piece.shape[0]
-            keys[pl.ds(i * size, size), :] = both[:, :C].astype(BF16)
-            values[pl.ds(i * size, size), :] = both[:, C:].astype(BF16)
-
-    normed = (q_ref[0].astype(F32) - norm[0:1, :]) * norm[1:2, :]
-    normed = (normed * gain[...] + bias[...]).astype(BF16)
-    queries = dot(normed, w_qkv[:, :C]).astype(BF16) * jnp.asarray(HD**-0.5, BF16)
-    head_of = iota((CELLS_IN, C), 1) >> 6
-    lane = iota((CELLS_IN, 128), 1)
-    result = jnp.zeros((CELLS_IN, C), F32)
-    logs = jnp.zeros((CELLS_IN, 128), F32)
+    mean, inverse = combine_groups(stats[...])
+
+    def norm(cells):
+        normed = (cells.astype(F32) - mean) * inverse
+        return (normed * gain[...] + bias[...]).astype(BF16)
+
+    head_of = iota((512, C), 1) >> 6
+    for i, piece in enumerate((k0, k1, k2, k3)):
+        both = dot(norm(piece[...]), w_qkv[:, C:])
+        rows = slice(512 * i, 512 * i + 512)
+        keys[rows, :] = both[:, :C].astype(BF16)
+        for head in range(HEADS):
+            values[head, rows, :] = jnp.where(head_of == head, both[:, C:], 1.0).astype(BF16)
+
+    scale = HD**-0.5 * float(np.log2(np.e))
+    queries = (dot(norm(q_ref[...]), w_qkv[:, :C]) * scale).astype(BF16)
+    head_of = iota((STRIP, C), 1) >> 6
+    lane = iota((STRIP, 128), 1)
+    result = jnp.zeros((STRIP, C), F32)
+    packed = jnp.zeros((STRIP, 128), F32)
     for head in range(HEADS):
         mine = head_of == head
         masked = jnp.where(mine, queries, jnp.zeros_like(queries))
-        scores = dot(masked, keys[...], ((1,), (1,)))
-        top = jnp.max(scores, axis=1, keepdims=True)
-        weights = jnp.exp(scores - top)
-        total = jnp.sum(weights, axis=1, keepdims=True)
-        mixed = dot(weights.astype(BF16), values[...])
+        best, mixed = None, None
+        for i in range(4):
+            rows = slice(512 * i, 512 * i + 512)
+            scores = dot(masked, keys[rows, :], ((1,), (1,)))
+            top = jnp.max(scores, axis=1, keepdims=True)
+            fresh = top if i == 0 else jnp.maximum(best, top)
+            product = dot(jnp.exp2(scores - fresh).astype(BF16), values[head, rows, :])
+            mixed = product if i == 0 else mixed * jnp.exp2(best - fresh) + product
+            best = fresh
+        total = pltpu.roll(mixed, HD, 1)
         result = jnp.where(mine, mixed / total, result)
-        logs = jnp.where(lane == head, top + jnp.log(total), logs)
-    out[0, :CELLS_IN, :] = result.astype(BF16)
-    turned = jnp.concatenate([logs.T[:8], jnp.zeros((8, 64), F32)], axis=1)
-    high, middle, low = split3(turned)
-    line = iota((16, C), 0)
-    packed = jnp.zeros((16, C), F32)
-    for i, part in enumerate((high, middle, low)):
-        wide = part.astype(F32)
-        wide = jnp.concatenate([wide, wide], axis=0)
-        if i:
-            wide = pltpu.roll(wide, 4 * i, 0)
-        packed = jnp.where((line >= 4 * i) & (line < 4 * i + 4), wide, packed)
-    out[0, CELLS_IN:, :] = packed.astype(BF16)
+        spot = 0 if head else 128
+        log = best + jnp.log2(mixed[:, spot : spot + 128])
+        for part, value in enumerate(split3(log)):
+            packed = jnp.where(lane == 4 * part + head, value.astype(F32), packed)
+    found[...] = result.astype(BF16)
+    logs[...] = packed.astype(BF16)
+    for step in range(4):
+        rows = slice(288 * step, 288 * step + 336)
+        for side in range(2):
+            chosen = pick[side]
+            place = order[2 * step + side]
+            out[place, :CELLS_IN, :] = dot(chosen, found[rows, :]).astype(BF16)
+            turned = dot(logs[rows, :], chosen, ((0,), (1,)))[:16]
+            turned = jnp.concatenate([turned, jnp.zeros((16, 64), F32)], axis=1)
+            out[place, CELLS_IN:, :] = turned.astype(BF16)
+
+
+def pick_matrix():
+    table = np.zeros((2, CELLS_IN, 336), np.float32)
+    for side in range(2):
+        for r in range(18):
+            for q in range(10):
+                table[side, r * 10 + q, r * 18 + 8 * side + q] = 1.0
+    return table
+
+
+PICK = pick_matrix()
 
 
 def partial_attention(order, queries, pieces, stats, gain, bias, w_qkv):
-    whole = lambda shape: pl.BlockSpec(shape, lambda i, o: (0,) * len(shape))
-    key_count = sum(p.shape[0] for p in pieces)
+    vmem = pl.BlockSpec(memory_space=pltpu.VMEM)
     return pl.pallas_call(
         attention_kernel,
         out_shape=jax.ShapeDtypeStruct((8, CELLS_IN + 16, C), BF16),
-        grid_spec=pltpu.PrefetchScalarGridSpec(
-            num_scalar_prefetch=1,
-            grid=(8,),
-            in_specs=[pl.BlockSpec((1, CELLS_IN, C), lambda i, o: (i, 0, 0))]
-            + [whole(p.shape) for p in pieces]
-            + [whole(s.shape) for s in stats]
-            + [whole((1, C)), whole((1, C)), whole(w_qkv.shape)],
-            out_specs=pl.BlockSpec((1, CELLS_IN + 16, C), lambda i, o: (o[i], 0, 0)),
-            scratch_shapes=[
-                pltpu.VMEM((key_count, C), BF16),
-                pltpu.VMEM((key_count, C), BF16),
-                pltpu.VMEM((8, C), F32),
-            ],
-        ),
-        compiler_params=params(1),
-    )(order, queries, *pieces, *stats, gain, bias, w_qkv)
+        in_specs=[pl.BlockSpec(memory_space=pltpu.SMEM)] + [vmem] * 10,
+        out_specs=vmem,
+        scratch_shapes=[
+            pltpu.VMEM((2048, C), BF16),
+            pltpu.VMEM((HEADS, 2048, C), BF16),
+            pltpu.VMEM((STRIP, C), BF16),
+            pltpu.VMEM((STRIP, 128), BF16),
+        ],
+        compiler_params=params(),
+    )(order, queries, *pieces, stats, gain, bias, w_qkv, jnp.asarray(PICK, BF16))
 
 
 def merge_kernel(flags, parts, coarse, w_proj, up, merged_out, stats_out):
@@ -206,7 +210,7 @@
         tail = parts[i, CELLS_IN:, :].astype(F32)
         logs.append(tail[0:4] + tail[4:8] + tail[8:12])
     top = functools.reduce(jnp.maximum, logs)
-    shares = [jnp.exp(v - top) for v in logs]
+    shares = [jnp.exp2(v - top) for v in logs]
     total = sum(shares)
     spread = jnp.where((iota((8, C), 1) >> 6) == iota((8, C), 0), 1.0, 0.0)
     attended = jnp.zeros((CELLS_IN, C), F32)
@@ -401,33 +405,33 @@
     taps = conv_weight.reshape(9, C, C)
 
     own = coarse.reshape(128, C)
+    stats = local_stats(own)
+    stats = lax.all_to_all(stats.reshape(128, 1, 128), ALL, 0, 0, tiled=True).reshape(128, 128)
+
     line = jnp.concatenate([own] + [shift(own, "x", 4, k) for k in (1, 3, 2)], axis=0)
     pieces = [line] + [shift(line, "z", 4, k) for k in (1, 3, 2)]
 
     wide = line_halo(coarse, ZXC, 32, 1)
     blocks = [wide] + [shift(wide, "y", 4, k) for k in (1, 2, 3)]
-    around = []
-    for k in range(4):
-        cells = jnp.concatenate([blocks[k - 1][-1:], blocks[k], blocks[(k + 1) % 4][:1]], axis=0)
-        around.append(jnp.pad(cells.reshape(180, C), ((0, CELLS_IN - 180), (0, 0))))
-    mine = jnp.stack(around)
-    queries = jnp.concatenate([mine, shift(mine, "c", 2, 1)], axis=0)
-    order = jnp.stack(
-        [((y + k) % 4) * 2 + (c + j) % 2 for j in range(2) for k in range(4)]
-    ).astype(jnp.int32)
+    rows = jnp.concatenate([blocks[3][-1:]] + blocks + [blocks[0][:1]], axis=0)
+    other = shift(rows, "c", 2, 1)
+    left = jnp.where(c == 0, rows, other)[:, :9]
+    right = jnp.where(c == 0, other, rows)[:, 1:]
+    queries = jnp.concatenate([left, right], axis=1).reshape(66 * 18, C)
+    queries = jnp.pad(queries, ((0, STRIP - 66 * 18), (0, 0)))
+    mine = jnp.pad(rows[:18].reshape(180, C), ((0, CELLS_IN - 180), (0, 0)))
+    order = jnp.stack([((y + k) % 4) * 2 + j for k in range(4) for j in range(2)])
+    order = order.astype(jnp.int32)
 
     grad = line_halo(line_halo(cotangent, "y", 4, 0), ZXC, 32, 1)
     windows = [grad[:, b : b + 16].reshape(WIN, C) for b in range(3)]
     grad_hidden = back_conv(windows, taps)
 
-    stats = local_stats(pieces)
-    stats = jnp.concatenate([stats, shift(stats, "c", 2, 1)], axis=0)
-    stats = [stats] + [shift(stats, "y", 4, k) for k in (1, 2, 3)]
     partial = partial_attention(
         order, queries, pieces, stats, norm1_gain[None], norm1_bias[None], w_qkv
     )
     partial = lax.all_to_all(partial, ("y", "c"), 0, 0, tiled=True)
-    merged, stats2 = merge(flags, partial, mine[0], w_proj, up)
+    merged, stats2 = merge(flags, partial, mine, w_proj, up)
     stats2 = lax.all_to_all(stats2.reshape(128, 1, 128), ALL, 0, 0, tiled=True)
     fine, halves, grad_shift, xhat, inverse = conv(
         flags,

time: 179 us -> 170 us (0.950)
  Pallas kernels: 40.8 us -> 26.1 us
  local copies, waits for them, and re-layouts: 8.4 us -> 14.8 us
  waiting for transfers between devices: 35.8 us -> 38 us
  starting transfers between devices: 65.3 us -> 63.5 us
    pallas_call x1, Pallas kernels: 31.8 us -> 16.7 us  [partial_attention(): pl.pallas_call(attention_kernel, out_shape=jax.ShapeDtypeStruct((8, CELLS...]
    all_to_all x0 -> x1, starting transfers between devices: none -> 8.73 us  [per_device(): lax.all_to_all(stats.reshape(128, 1, 128), ALL, 0, 0, tiled=True)]
    ppermute x16 -> x12, starting transfers between devices: 29.5 us -> 21 us  [shift(): lax.ppermute(value, axis, [((i + step) % count, i) for i in range(count)])]
    ppermute x3, waiting for transfers between devices: 5.19 us -> 0.01 us  [line_halo(): before = lax.ppermute(tail, axis, [(i, i + 1) for i in range(count - 1)])]
    all_to_all x1, waiting for transfers between devices: 0.01 us -> 4.84 us  [per_device(): partial = lax.all_to_all(partial, ('y', 'c'), 0, 0, tiled=True)]
    unnamed x42 -> x44, local copies, waits for them, and re-layouts: 3.19 us -> 6.49 us
    ppermute x16 -> x12, waiting for transfers between devices: 9 us -> 10.9 us  [shift(): lax.ppermute(value, axis, [((i + step) % count, i) for i in range(count)])]
  transfers between devices with their start and end apart: 25 -> 22, of which waited for: 10 -> 7; matrix products, arithmetic and copies ran while one was open for 3% -> 6% of each run, Pallas kernels for 3% -> 13%
where the time goes in v2:
time: 170 us; the launch traced here: 169 us
  starting transfers between devices  63.5 us (37%)
  waiting for transfers between devices  38 us (22%)
  Pallas kernels  26.1 us (15%)
  blocking collectives  19.9 us (12%)
  local copies, waits for them, and re-layouts  14.8 us (9%)
  other arithmetic  5.55 us (3%)
    ppermute x12, starting transfers between devices, shift(): lax.ppermute(value, axis, [((i + step) % count, i) for i in range(count)])  21 us
    all_to_all x1, blocking collectives, per_device(): got = lax.all_to_all(sent, ('y', 'z', 'x'), 0, 0, tiled=True)  19.9 us
    pallas_call x1, Pallas kernels, partial_attention(): pl.pallas_call(attention_kernel, out_shape=jax.ShapeDtypeStruct((8, CELLS...  16.7 us
    all_to_all x1, waiting for transfers between devices, per_device(): lax.all_to_all(jnp.broadcast_to(chunk[None], (64, 36, 128)), ('y', 'z', '...  12.5 us
    ppermute x3, starting transfers between devices, line_halo(): before = lax.ppermute(tail, axis, [(i, i + 1) for i in range(count - 1)])  11.4 us
    ppermute x12, waiting for transfers between devices, shift(): lax.ppermute(value, axis, [((i + step) % count, i) for i in range(count)])  10.9 us
    all_to_all x1, starting transfers between devices, per_device(): lax.all_to_all(stats.reshape(128, 1, 128), ALL, 0, 0, tiled=True)  8.73 us
    all_to_all x1, waiting for transfers between devices, per_device(): stats2 = lax.all_to_all(stats2.reshape(128, 1, 128), ALL, 0, 0, tiled=True)  7.51 us
  transfers between devices with their start and end apart: 22, of which 7 were waited for; matrix products, arithmetic and copies ran while one was open for 6% of the time, Pallas kernels for 13%

profile of v2, /device:TPU:1, one launch (start us, length us, event | category | flops | bytes accessed | tf_op | source)
XLA Modules:
  0.0 168.9 jit_solution(2187479530781967793)
XLA Ops:
  0.6 0.9 fusion.3
  1.6 4.5 %collective-permute-start = (bf16[16,1,256]{2,0,1:T(8,128)(2,1)S(1)}, bf16[16,1,256]{2,0,1:T(8,128)(2,1)S(1)}, u32[]{:S(2)}, u32[]{:S(2)}) collective-permute-start(bf16[16,1,256]{2,0,1:T(8,128)(2,1)S(1)} %copy.24), channel_id=1, source_target_pairs={{0,1},{1,2},{2,3},{3,4},{4,5},{5,6},{6,7},{7,8},{8,9},{9,10},{10,1... | collective-permute-start | bytes 24584 | tf_op jit(solution)/shard_map/ppermute | solution.py:384
  6.1 1.9 %collective-permute-start.1 = (bf16[16,1,256]{2,0,1:T(8,128)(2,1)S(1)}, bf16[16,1,256]{2,0,1:T(8,128)(2,1)S(1)}, u32[]{:S(2)}, u32[]{:S(2)}) collective-permute-start(bf16[16,1,256]{2,0,1:T(8,128)(2,1)S(1)} %copy.25), channel_id=1, source_target_pairs={{1,0},{2,1},{3,2},{4,3},{5,4},{6,5},{7,6},{8,7},{9,8},{10,9},{11,1... | collective-permute-start | bytes 24584 | tf_op jit(solution)/shard_map/ppermute | solution.py:385
  8.1 0.9 constant_dynamic-update-slice_fusion.1
  8.9 2.2 %collective-permute-done.1 = bf16[16,1,256]{2,0,1:T(8,128)(2,1)S(1)} collective-permute-done((bf16[16,1,256]{2,0,1:T(8,128)(2,1)S(1)}, bf16[16,1,256]{2,0,1:T(8,128)(2,1)S(1)}, u32[]{:S(2)}, u32[]{:S(2)}) %collective-permute-start.1) | collective-permute-done | bytes 8224 | tf_op jit(solution)/shard_map/ppermute | solution.py:385
  11.1 1.3 collective-permute-start.2
  12.4 2.6 %collective-permute-start.4 = (bf16[16,10,256]{2,0,1:T(8,128)(2,1)S(1)}, bf16[16,10,256]{2,0,1:T(8,128)(2,1)S(1)}, u32[]{:S(2)}, u32[]{:S(2)}) collective-permute-start(bf16[16,10,256]{2,0,1:T(8,128)(2,1)S(1)} %constant_dynamic-update-slice_fusion), channel_id=1, source_target_pairs={{64,0},{96,32},{0,64},{32,96},{65,1},{97,33},{1,65},{33,97},{66,2}... | collective-permute-start | bytes 245768 | tf_op jit(solution)/shard_map/ppermute | solution.py:377
  15.0 1.1 collective-permute-start.3
  16.1 2.5 %collective-permute-start.8 = (bf16[128,256]{1,0:T(8,128)(2,1)}, bf16[128,256]{1,0:T(8,128)(2,1)S(1)}, u32[]{:S(2)}, u32[]{:S(2)}) collective-permute-start(bf16[128,256]{1,0:T(8,128)(2,1)} %bitcast.50), channel_id=1, source_target_pairs={{4,0},{6,2},{0,4},{2,6},{5,1},{7,3},{1,5},{3,7},{12,8},{14,10},{8,... | collective-permute-start | bytes 196616 | tf_op jit(solution)/shard_map/ppermute | solution.py:377
  18.5 3.1 %collective-permute-start.7 = (bf16[128,256]{1,0:T(8,128)(2,1)}, bf16[128,256]{1,0:T(8,128)(2,1)S(1)}, u32[]{:S(2)}, u32[]{:S(2)}) collective-permute-start(bf16[128,256]{1,0:T(8,128)(2,1)} %bitcast.51), channel_id=1, source_target_pairs={{6,0},{0,2},{2,4},{4,6},{7,1},{1,3},{3,5},{5,7},{14,8},{8,10},{10,... | collective-permute-start | bytes 196616 | tf_op jit(solution)/shard_map/ppermute | solution.py:377
  21.7 0.9 concatenate.34
  23.2 0.7 fusion.2
  23.9 1.3 collective-permute-start.13
  25.2 0.8 copy-done.3
  26.1 1.3 shard_map.147
  27.4 8.7 %all-to-all-start = ((f32[128,1,128]{2,1,0:T(1,128)}), f32[128,1,128]{2,1,0:T(1,128)S(1)}, u32[]{:S(2)}, u32[]{:S(2)}) async-start(f32[128,1,128]{2,1,0:T(1,128)} %bitcast.14), calls=%async_computation | async-start | bytes 131072 | tf_op jit(solution)/shard_map/all_to_all | solution.py:409
  36.2 3.3 %collective-permute-start.12 = (bf16[1,16,256]{2,1,0:T(8,128)(2,1)S(1)}, bf16[1,16,256]{2,1,0:T(8,128)(2,1)S(1)}, u32[]{:S(2)}, u32[]{:S(2)}) collective-permute-start(bf16[1,16,256]{2,1,0:T(8,128)(2,1)S(1)} %get-tuple-element.29), channel_id=1, source_target_pairs={{0,32},{32,64},{64,96},{1,33},{33,65},{65,97},{2,34},{34,66},{66,9... | collective-permute-start | bytes 24584 | tf_op jit(solution)/shard_map/ppermute | solution.py:384
  39.6 0.9 pad_maximum_fusion.3.k0
  40.4 3.2 %collective-permute-start.11 = (bf16[512,256]{1,0:T(8,128)(2,1)S(1)}, bf16[512,256]{1,0:T(8,128)(2,1)S(1)}, u32[]{:S(2)}, u32[]{:S(2)}) collective-permute-start(bf16[512,256]{1,0:T(8,128)(2,1)S(1)} %pad_maximum_fusion.3.k0), channel_id=1, source_target_pairs={{16,0},{24,8},{0,16},{8,24},{17,1},{25,9},{1,17},{9,25},{18,2},{26... | collective-permute-start | bytes 786440 | tf_op jit(solution)/shard_map/ppermute | solution.py:377
  44.2 2.1 %collective-permute-start.9 = (bf16[512,256]{1,0:T(8,128)(2,1)S(1)}, bf16[512,256]{1,0:T(8,128)(2,1)S(1)}, u32[]{:S(2)}, u32[]{:S(2)}) collective-permute-start(bf16[512,256]{1,0:T(8,128)(2,1)S(1)} %pad_maximum_fusion.3.k0), channel_id=1, source_target_pairs={{8,0},{16,8},{24,16},{0,24},{9,1},{17,9},{25,17},{1,25},{10,2},{18... | collective-permute-start | bytes 786440 | tf_op jit(solution)/shard_map/ppermute | solution.py:377
  46.9 3.0 %collective-permute-done.11.k3 = bf16[512,256]{1,0:T(8,128)(2,1)S(1)} collective-permute-done((bf16[512,256]{1,0:T(8,128)(2,1)S(1)}, bf16[512,256]{1,0:T(8,128)(2,1)S(1)}, u32[]{:S(2)}, u32[]{:S(2)}) %collective-permute-start.11) | collective-permute-done | bytes 262176 | tf_op jit(solution)/shard_map/ppermute | solution.py:377
  49.9 6.3 %collective-permute-done.10.k2 = bf16[512,256]{1,0:T(8,128)(2,1)S(1)} collective-permute-done((bf16[512,256]{1,0:T(8,128)(2,1)S(1)}, bf16[512,256]{1,0:T(8,128)(2,1)S(1)}, u32[]{:S(2)}, u32[]{:S(2)}) %collective-permute-start.10) | collective-permute-done | bytes 262176 | tf_op jit(solution)/shard_map/ppermute | solution.py:377
  56.2 16.7 %shard_map.148 = bf16[8,208,256]{2,1,0:T(8,128)(2,1)} custom-call(s32[8]{0:T(128)S(1)} %stack.55.order, bf16[1200,256]{1,0:T(8,128)(2,1)S(1)} %pad.8.q_ref, bf16[512,256]{1,0:T(8,128)(2,1)S(1)} %pad_maximum_fusion.3.k0, bf16[512,256]{1,0:T(8,128)(2,1)S(1)} %collective-permute-done.9.k1, bf16[512,256]{1,0:T(8,128)(2,1)S(1)} %collective-permute-done.10.k2, ...), custom_call_target="tpu_custom_call" | custom-call | tf_op jit(solution)/shard_map/pallas_call | solution.py:191
  72.9 5.1 %all-to-all-start.1 = ((bf16[8,208,256]{2,1,0:T(8,128)(2,1)}), bf16[8,208,256]{2,1,0:T(8,128)(2,1)S(1)}, u32[]{:S(2)}, u32[]{:S(2)}) async-start(bf16[8,208,256]{2,1,0:T(8,128)(2,1)} %shard_map.148), calls=%async_computation.1 | async-start | bytes 1703936 | tf_op jit(solution)/shard_map/all_to_all | solution.py:433
  78.9 1.9 %collective-permute-start.15 = (bf16[34,1,256]{2,1,0:T(2,128)(2,1)}, bf16[34,1,256]{2,1,0:T(2,128)(2,1)S(1)}, u32[]{:S(2)}, u32[]{:S(2)}) collective-permute-start(bf16[34,1,256]{2,1,0:T(2,128)(2,1)} %get-tuple-element.26), channel_id=1, source_target_pairs={{1,0},{2,1},{3,2},{4,3},{5,4},{6,5},{7,6},{8,7},{9,8},{10,9},{11,1... | collective-permute-start | bytes 52232 | tf_op jit(solution)/shard_map/ppermute | solution.py:385
  80.8 3.6 %collective-permute-start.14 = (bf16[34,1,256]{2,1,0:T(2,128)(2,1)}, bf16[34,1,256]{2,1,0:T(2,128)(2,1)}, u32[]{:S(2)}, u32[]{:S(2)}) collective-permute-start(bf16[34,1,256]{2,1,0:T(2,128)(2,1)} %get-tuple-element.27), channel_id=1, source_target_pairs={{0,1},{1,2},{2,3},{3,4},{4,5},{5,6},{6,7},{7,8},{8,9},{9,10},{10,1... | collective-permute-start | bytes 52232 | tf_op jit(solution)/shard_map/ppermute | solution.py:384
  85.2 1.0 pad.9.coarse
  86.2 4.8 %all-to-all-done.1.parts = bf16[8,208,256]{2,1,0:T(8,128)(2,1)S(1)} async-done(((bf16[8,208,256]{2,1,0:T(8,128)(2,1)}), bf16[8,208,256]{2,1,0:T(8,128)(2,1)S(1)}, u32[]{:S(2)}, u32[]{:S(2)}) %all-to-all-start.1) | async-done | bytes 852000 | tf_op jit(solution)/shard_map/all_to_all | solution.py:433
  91.1 0.9 copy-done.10
  92.0 3.0 %shard_map.149 = (bf16[192,256]{1,0:T(8,128)(2,1)S(1)}, f32[128,128]{1,0:T(8,128)S(1)}) custom-call(s32[4]{0:T(128)S(1)} %add_convert_fusion.flags, bf16[8,208,256]{2,1,0:T(8,128)(2,1)S(1)} %all-to-all-done.1.parts, bf16[192,256]{1,0:T(8,128)(2,1)S(1)} %pad.9.coarse, bf16[256,256]{1,0:T(8,128)(2,1)S(1)} %copy-done.10, bf16[1632,192]{1,0:T(8,128)(2,1)S(1)} %copy-done.1), custom_call_target="tpu_custom_call" | custom-call | tf_op jit(solution)/shard_map/pallas_call | solution.py:241
  96.3 7.4 %all-to-all-start.2 = ((f32[128,1,128]{2,1,0:T(1,128)}), f32[128,1,128]{2,1,0:T(1,128)S(1)}, u32[]{:S(2)}, u32[]{:S(2)}) async-start(f32[128,1,128]{2,1,0:T(1,128)} %bitcast.57), calls=%async_computation.2 | async-start | bytes 131072 | tf_op jit(solution)/shard_map/all_to_all | solution.py:435
  103.7 1.0 pad_maximum_fusion.1
  104.8 0.8 shard_map.150.grad_hidden
  105.6 7.5 %all-to-all-done.2 = f32[128,1,128]{2,1,0:T(1,128)S(1)} async-done(((f32[128,1,128]{2,1,0:T(1,128)}), f32[128,1,128]{2,1,0:T(1,128)S(1)}, u32[]{:S(2)}, u32[]{:S(2)}) %all-to-all-start.2) | async-done | bytes 65568 | tf_op jit(solution)/shard_map/all_to_all | solution.py:435
  113.1 0.9 copy-done.12
  114.0 4.0 %shard_map.151 = (bf16[512,256]{1,0:T(8,128)(2,1)}, bf16[2,2320,128]{2,1,0:T(8,128)(2,1)}, f32[512,256]{1,0:T(8,128)S(1)}, f32[512,256]{1,0:T(8,128)S(1)}, f32[8,256]{1,0:T(8,128)S(1)}) custom-call(s32[4]{0:T(128)S(1)} %add_convert_fusion.flags, bf16[192,256]{1,0:T(8,128)(2,1)S(1)} %copy-done.12, bf16[1632,192]{1,0:T(8,128)(2,1)S(1)} %copy-done.1, ...), custom_call_target="tpu_custom_call" | custom-call | tf_op jit(solution)/shard_map/pallas_call | solution.py:340
  118.0 0.8 copy-done.4
  118.8 0.8 copy-done.6
  119.6 1.3 dynamic-slice_bitcast_fusion
  121.0 0.9 collective-permute-start.16
  121.9 1.6 collective-permute-done.16.got
  123.8 19.9 %all_to_all.25 = bf16[64,48,128]{2,1,0:T(8,128)(2,1)S(1)} all-to-all(bf16[64,48,128]{2,1,0:T(8,128)(2,1)S(1)} %shard_map.152), channel_id=1, replica_groups=mesh['y'=4,'z'=4,'x'=4,'c'=2] {'y','z','x'}, dimensions={0} | all-to-all | bytes 1572864 | tf_op jit(solution)/shard_map/all_to_all | solution.py:452
  143.9 0.9 broadcast_in_dim.41
  144.8 4.6 %all-to-all-start.4 = ((bf16[64,36,128]{2,1,0:T(8,128)(2,1)}), bf16[64,36,128]{2,1,0:T(8,128)(2,1)S(1)}, u32[]{:S(2)}, u32[]{:S(2)}) async-start(bf16[64,36,128]{2,1,0:T(8,128)(2,1)} %broadcast_in_dim.41), calls=%async_computation.4 | async-start | bytes 1310720 | tf_op jit(solution)/shard_map/all_to_all | solution.py:457
  149.8 12.5 %all-to-all-done.4 = bf16[64,36,128]{2,1,0:T(8,128)(2,1)S(1)} async-done(((bf16[64,36,128]{2,1,0:T(8,128)(2,1)}), bf16[64,36,128]{2,1,0:T(8,128)(2,1)S(1)}, u32[]{:S(2)}, u32[]{:S(2)}) %all-to-all-start.4) | async-done | bytes 589856 | tf_op jit(solution)/shard_map/all_to_all | solution.py:457
  162.4 3.0 %collective-permute-start.17 = (bf16[2304,128]{1,0:T(8,128)(2,1)S(1)}, bf16[2304,128]{1,0:T(8,128)(2,1)S(1)}, u32[]{:S(2)}, u32[]{:S(2)}) collective-permute-start(bf16[2304,128]{1,0:T(8,128)(2,1)S(1)} %reshape.91), channel_id=1, source_target_pairs={{1,0},{0,1},{3,2},{2,3},{5,4},{4,5},{7,6},{6,7},{9,8},{8,9},{11,10... | collective-permute-start | bytes 1769480 | tf_op jit(solution)/shard_map/ppermute | solution.py:377
  166.4 0.8 multiply_convert_fusion
  167.3 1.6 maximum_convert_fusion
  (90 shorter events, 6.7 us)
Async XLA Ops:
  1.6 6.5 %collective-permute-start = (bf16[16,1,256]{2,0,1:T(8,128)(2,1)S(1)}, bf16[16,1,256]{2,0,1:T(8,128)(2,1)S(1)}, u32[]{:S(2)}, u32[]{:S(2)}) collective-permute-start(bf16[16,1,256]{2,0,1:T(8,128)(2,1)S(1)} %copy.24), channel_id=1, source_target_pairs={{0,1},{1,2},{2,3},{3,4},{4,5},{5,6},{6,7},{7,8},{8,9},{9,10},{10,1... | collective-permute-start | bytes 24584 | tf_op jit(solution)/shard_map/ppermute | solution.py:384
  6.1 5.0 %collective-permute-start.1 = (bf16[16,1,256]{2,0,1:T(8,128)(2,1)S(1)}, bf16[16,1,256]{2,0,1:T(8,128)(2,1)S(1)}, u32[]{:S(2)}, u32[]{:S(2)}) collective-permute-start(bf16[16,1,256]{2,0,1:T(8,128)(2,1)S(1)} %copy.25), channel_id=1, source_target_pairs={{1,0},{2,1},{3,2},{4,3},{5,4},{6,5},{7,6},{8,7},{9,8},{10,9},{11,1... | collective-permute-start | bytes 24584 | tf_op jit(solution)/shard_map/ppermute | solution.py:385
  11.1 10.5 %collective-permute-start.2 = (bf16[16,10,256]{2,0,1:T(8,128)(2,1)S(1)}, bf16[16,10,256]{2,0,1:T(8,128)(2,1)S(1)}, u32[]{:S(2)}, u32[]{:S(2)}) collective-permute-start(bf16[16,10,256]{2,0,1:T(8,128)(2,1)S(1)} %constant_dynamic-update-slice_fusion), channel_id=1, source_target_pairs={{96,0},{0,32},{32,64},{64,96},{97,1},{1,33},{33,65},{65,97},{98,2}... | collective-permute-start | bytes 245768 | tf_op jit(solution)/shard_map/ppermute | solution.py:377
  12.4 9.3 %collective-permute-start.4 = (bf16[16,10,256]{2,0,1:T(8,128)(2,1)S(1)}, bf16[16,10,256]{2,0,1:T(8,128)(2,1)S(1)}, u32[]{:S(2)}, u32[]{:S(2)}) collective-permute-start(bf16[16,10,256]{2,0,1:T(8,128)(2,1)S(1)} %constant_dynamic-update-slice_fusion), channel_id=1, source_target_pairs={{64,0},{96,32},{0,64},{32,96},{65,1},{97,33},{1,65},{33,97},{66,2}... | collective-permute-start | bytes 245768 | tf_op jit(solution)/shard_map/ppermute | solution.py:377
  15.0 6.7 %collective-permute-start.3 = (bf16[16,10,256]{2,0,1:T(8,128)(2,1)S(1)}, bf16[16,10,256]{2,0,1:T(8,128)(2,1)S(1)}, u32[]{:S(2)}, u32[]{:S(2)}) collective-permute-start(bf16[16,10,256]{2,0,1:T(8,128)(2,1)S(1)} %constant_dynamic-update-slice_fusion), channel_id=1, source_target_pairs={{32,0},{64,32},{96,64},{0,96},{33,1},{65,33},{97,65},{1,97},{34,2}... | collective-permute-start | bytes 245768 | tf_op jit(solution)/shard_map/ppermute | solution.py:377
  16.1 20.2 %collective-permute-start.8 = (bf16[128,256]{1,0:T(8,128)(2,1)}, bf16[128,256]{1,0:T(8,128)(2,1)S(1)}, u32[]{:S(2)}, u32[]{:S(2)}) collective-permute-start(bf16[128,256]{1,0:T(8,128)(2,1)} %bitcast.50), channel_id=1, source_target_pairs={{4,0},{6,2},{0,4},{2,6},{5,1},{7,3},{1,5},{3,7},{12,8},{14,10},{8,... | collective-permute-start | bytes 196616 | tf_op jit(solution)/shard_map/ppermute | solution.py:377
  18.5 21.0 %collective-permute-start.7 = (bf16[128,256]{1,0:T(8,128)(2,1)}, bf16[128,256]{1,0:T(8,128)(2,1)S(1)}, u32[]{:S(2)}, u32[]{:S(2)}) collective-permute-start(bf16[128,256]{1,0:T(8,128)(2,1)} %bitcast.51), channel_id=1, source_target_pairs={{6,0},{0,2},{2,4},{4,6},{7,1},{1,3},{3,5},{5,7},{14,8},{8,10},{10,... | collective-permute-start | bytes 196616 | tf_op jit(solution)/shard_map/ppermute | solution.py:377
  21.6 17.9 %collective-permute-start.6 = (bf16[128,256]{1,0:T(8,128)(2,1)}, bf16[128,256]{1,0:T(8,128)(2,1)S(1)}, u32[]{:S(2)}, u32[]{:S(2)}) collective-permute-start(bf16[128,256]{1,0:T(8,128)(2,1)} %bitcast.52), channel_id=1, source_target_pairs={{2,0},{4,2},{6,4},{0,6},{3,1},{5,3},{7,5},{1,7},{10,8},{12,10},{14... | collective-permute-start | bytes 196616 | tf_op jit(solution)/shard_map/ppermute | solution.py:377
  22.6 21.6 %collective-permute-start.5 = (bf16[66,10,256]{2,0,1:T(8,128)(2,1)S(1)}, bf16[66,10,256]{2,0,1:T(8,128)(2,1)S(1)}, u32[]{:S(2)}, u32[]{:S(2)}) collective-permute-start(bf16[66,10,256]{2,0,1:T(8,128)(2,1)S(1)} %concatenate.34), channel_id=1, source_target_pairs={{1,0},{0,1},{3,2},{2,3},{5,4},{4,5},{7,6},{6,7},{9,8},{8,9},{11,10... | collective-permute-start | bytes 1013768 | tf_op jit(solution)/shard_map/ppermute | solution.py:377
  23.9 54.3 %collective-permute-start.13 = (bf16[1,16,256]{2,1,0:T(8,128)(2,1)S(1)}, bf16[1,16,256]{2,1,0:T(8,128)(2,1)S(1)}, u32[]{:S(2)}, u32[]{:S(2)}) collective-permute-start(bf16[1,16,256]{2,1,0:T(8,128)(2,1)S(1)} %get-tuple-element.28), channel_id=1, source_target_pairs={{32,0},{64,32},{96,64},{33,1},{65,33},{97,65},{34,2},{66,34},{98,6... | collective-permute-start | bytes 24584 | tf_op jit(solution)/shard_map/ppermute | solution.py:385
  25.2 0.8 copy-start.3
  27.4 19.6 %all-to-all-start = ((f32[128,1,128]{2,1,0:T(1,128)}), f32[128,1,128]{2,1,0:T(1,128)S(1)}, u32[]{:S(2)}, u32[]{:S(2)}) async-start(f32[128,1,128]{2,1,0:T(1,128)} %bitcast.14), calls=%async_computation | async-start | bytes 131072 | tf_op jit(solution)/shard_map/all_to_all | solution.py:409
  36.2 41.9 %collective-permute-start.12 = (bf16[1,16,256]{2,1,0:T(8,128)(2,1)S(1)}, bf16[1,16,256]{2,1,0:T(8,128)(2,1)S(1)}, u32[]{:S(2)}, u32[]{:S(2)}) collective-permute-start(bf16[1,16,256]{2,1,0:T(8,128)(2,1)S(1)} %get-tuple-element.29), channel_id=1, source_target_pairs={{0,32},{32,64},{64,96},{1,33},{33,65},{65,97},{2,34},{34,66},{66,9... | collective-permute-start | bytes 24584 | tf_op jit(solution)/shard_map/ppermute | solution.py:384
  40.4 9.5 %collective-permute-start.11 = (bf16[512,256]{1,0:T(8,128)(2,1)S(1)}, bf16[512,256]{1,0:T(8,128)(2,1)S(1)}, u32[]{:S(2)}, u32[]{:S(2)}) collective-permute-start(bf16[512,256]{1,0:T(8,128)(2,1)S(1)} %pad_maximum_fusion.3.k0), channel_id=1, source_target_pairs={{16,0},{24,8},{0,16},{8,24},{17,1},{25,9},{1,17},{9,25},{18,2},{26... | collective-permute-start | bytes 786440 | tf_op jit(solution)/shard_map/ppermute | solution.py:377
  43.6 12.5 %collective-permute-start.10 = (bf16[512,256]{1,0:T(8,128)(2,1)S(1)}, bf16[512,256]{1,0:T(8,128)(2,1)S(1)}, u32[]{:S(2)}, u32[]{:S(2)}) collective-permute-start(bf16[512,256]{1,0:T(8,128)(2,1)S(1)} %pad_maximum_fusion.3.k0), channel_id=1, source_target_pairs={{24,0},{0,8},{8,16},{16,24},{25,1},{1,9},{9,17},{17,25},{26,2},{2,... | collective-permute-start | bytes 786440 | tf_op jit(solution)/shard_map/ppermute | solution.py:377
  44.2 12.0 %collective-permute-start.9 = (bf16[512,256]{1,0:T(8,128)(2,1)S(1)}, bf16[512,256]{1,0:T(8,128)(2,1)S(1)}, u32[]{:S(2)}, u32[]{:S(2)}) collective-permute-start(bf16[512,256]{1,0:T(8,128)(2,1)S(1)} %pad_maximum_fusion.3.k0), channel_id=1, source_target_pairs={{8,0},{16,8},{24,16},{0,24},{9,1},{17,9},{25,17},{1,25},{10,2},{18... | collective-permute-start | bytes 786440 | tf_op jit(solution)/shard_map/ppermute | solution.py:377
  46.6 9.5 %copy-start.8 = (bf16[256,768]{1,0:T(8,128)(2,1)S(1)}, bf16[256,768]{1,0:T(8,128)(2,1)}, u32[]{:S(2)}) copy-start(bf16[256,768]{1,0:T(8,128)(2,1)} %w_qkv.1) | copy-start | bytes 1179652
  46.7 9.5 %copy-start.9 = (bf16[2,192,336]{2,1,0:T(8,128)(2,1)S(1)}, bf16[2,192,336]{2,1,0:T(8,128)(2,1)}, u32[]{:S(2)}) copy-start(bf16[2,192,336]{2,1,0:T(8,128)(2,1)} %constant.82.clone.pick) | copy-start | bytes 774148
  46.7 9.5 %copy-start.15 = (f32[256]{0:T(256)S(1)}, f32[256]{0:T(256)}, u32[]{:S(2)}) copy-start(f32[256]{0:T(256)} %param.13) | copy-start | bytes 3076
  46.7 9.5 %copy-start.16 = (f32[256]{0:T(256)S(1)}, f32[256]{0:T(256)}, u32[]{:S(2)}) copy-start(f32[256]{0:T(256)} %param.14) | copy-start | bytes 3076
  72.9 5.2 %copy-start.2 = (bf16[32,16,256]{2,1,0:T(8,128)(2,1)S(1)}, bf16[32,16,256]{2,1,0:T(8,128)(2,1)}, u32[]{:S(2)}) copy-start(bf16[32,16,256]{2,1,0:T(8,128)(2,1)} %param.21) | copy-start | bytes 786436
  72.9 18.1 %copy-start.1 = (bf16[1632,192]{1,0:T(8,128)(2,1)S(1)}, bf16[1632,192]{1,0:T(8,128)(2,1)}, u32[]{:S(2)}) copy-start(bf16[1632,192]{1,0:T(8,128)(2,1)} %constant.81.clone.up) | copy-start | bytes 1880068
  72.9 18.1 %all-to-all-start.1 = ((bf16[8,208,256]{2,1,0:T(8,128)(2,1)}), bf16[8,208,256]{2,1,0:T(8,128)(2,1)S(1)}, u32[]{:S(2)}, u32[]{:S(2)}) async-start(bf16[8,208,256]{2,1,0:T(8,128)(2,1)} %shard_map.148), calls=%async_computation.1 | async-start | bytes 1703936 | tf_op jit(solution)/shard_map/all_to_all | solution.py:433
  78.9 24.8 %collective-permute-start.15 = (bf16[34,1,256]{2,1,0:T(2,128)(2,1)}, bf16[34,1,256]{2,1,0:T(2,128)(2,1)S(1)}, u32[]{:S(2)}, u32[]{:S(2)}) collective-permute-start(bf16[34,1,256]{2,1,0:T(2,128)(2,1)} %get-tuple-element.26), channel_id=1, source_target_pairs={{1,0},{2,1},{3,2},{4,3},{5,4},{6,5},{7,6},{8,7},{9,8},{10,9},{11,1... | collective-permute-start | bytes 52232 | tf_op jit(solution)/shard_map/ppermute | solution.py:385
  80.8 22.9 %collective-permute-start.14 = (bf16[34,1,256]{2,1,0:T(2,128)(2,1)}, bf16[34,1,256]{2,1,0:T(2,128)(2,1)}, u32[]{:S(2)}, u32[]{:S(2)}) collective-permute-start(bf16[34,1,256]{2,1,0:T(2,128)(2,1)} %get-tuple-element.27), channel_id=1, source_target_pairs={{0,1},{1,2},{2,3},{3,4},{4,5},{5,6},{6,7},{7,8},{8,9},{9,10},{10,1... | collective-permute-start | bytes 52232 | tf_op jit(solution)/shard_map/ppermute | solution.py:384
  85.2 19.5 %copy-start = (bf16[3,3,256,256]{3,2,1,0:T(8,128)(2,1)S(1)}, bf16[3,3,256,256]{3,2,1,0:T(8,128)(2,1)}, u32[]{:S(2)}) copy-start(bf16[3,3,256,256]{3,2,1,0:T(8,128)(2,1)} %param.19) | copy-start | bytes 3538948
  91.1 0.9 copy-start.10
  95.0 0.7 copy-start.11
  95.6 0.6 copy-start.13
  96.3 16.8 %all-to-all-start.2 = ((f32[128,1,128]{2,1,0:T(1,128)}), f32[128,1,128]{2,1,0:T(1,128)S(1)}, u32[]{:S(2)}, u32[]{:S(2)}) async-start(f32[128,1,128]{2,1,0:T(1,128)} %bitcast.57), calls=%async_computation.2 | async-start | bytes 131072 | tf_op jit(solution)/shard_map/all_to_all | solution.py:435
  103.7 9.4 %copy-start.14 = (f32[256]{0:T(256)S(1)}, f32[256]{0:T(256)}, u32[]{:S(2)}) copy-start(f32[256]{0:T(256)} %param.17) | copy-start | bytes 3076
  103.7 9.4 %copy-start.17 = (f32[256]{0:T(256)S(1)}, f32[256]{0:T(256)}, u32[]{:S(2)}) copy-start(f32[256]{0:T(256)} %param.18) | copy-start | bytes 3076
  103.7 9.4 %copy-start.18 = (f32[256]{0:T(256)S(1)}, f32[256]{0:T(256)}, u32[]{:S(2)}) copy-start(f32[256]{0:T(256)} %param.20) | copy-start | bytes 3076
  113.1 0.9 copy-start.12
  118.0 0.8 copy-start.4
  118.8 0.8 copy-start.6
  121.0 2.6 %collective-permute-start.16 = (bf16[2320,128]{1,0:T(8,128)(2,1)S(1)}, bf16[2320,128]{1,0:T(8,128)(2,1)S(1)}, u32[]{:S(2)}, u32[]{:S(2)}) collective-permute-start(bf16[2320,128]{1,0:T(8,128)(2,1)S(1)} %get-tuple-element.18), channel_id=1, source_target_pairs={{1,0},{0,1},{3,2},{2,3},{5,4},{4,5},{7,6},{6,7},{9,8},{8,9},{11,10... | collective-permute-start | bytes 1781768 | tf_op jit(solution)/shard_map/ppermute | solution.py:377
  143.9 22.5 %copy-start.5 = (f32[512,256]{1,0:T(8,128)S(1)}, f32[512,256]{1,0:T(8,128)}, u32[]{:S(2)}) copy-start(f32[512,256]{1,0:T(8,128)} %copy-done.4) | copy-start | bytes 1572868
  143.9 22.5 %copy-start.7 = (f32[512,256]{1,0:T(8,128)S(1)}, f32[512,256]{1,0:T(8,128)}, u32[]{:S(2)}) copy-start(f32[512,256]{1,0:T(8,128)} %copy-done.6) | copy-start | bytes 1572868
  144.8 17.5 %all-to-all-start.4 = ((bf16[64,36,128]{2,1,0:T(8,128)(2,1)}), bf16[64,36,128]{2,1,0:T(8,128)(2,1)S(1)}, u32[]{:S(2)}, u32[]{:S(2)}) async-start(bf16[64,36,128]{2,1,0:T(8,128)(2,1)} %broadcast_in_dim.41), calls=%async_computation.4 | async-start | bytes 1310720 | tf_op jit(solution)/shard_map/all_to_all | solution.py:457
  162.4 4.7 %collective-permute-start.17 = (bf16[2304,128]{1,0:T(8,128)(2,1)S(1)}, bf16[2304,128]{1,0:T(8,128)(2,1)S(1)}, u32[]{:S(2)}, u32[]{:S(2)}) collective-permute-start(bf16[2304,128]{1,0:T(8,128)(2,1)S(1)} %reshape.91), channel_id=1, source_target_pairs={{1,0},{0,1},{3,2},{2,3},{5,4},{4,5},{7,6},{6,7},{9,8},{8,9},{11,10... | collective-permute-start | bytes 1769480 | tf_op jit(solution)/shard_map/ppermute | solution.py:377

commit v3 on v2

--- a/solution.py
+++ b/solution.py
@@ -20,7 +20,8 @@
 ALL = ("y", "z", "x", "c")
 
 CELLS_IN = 192
-STRIP = 1200
+STRIP = 672
+KEY_BLOCK = 512
 FINE_ROWS = 34
 WIN = FINE_ROWS * 16
 
@@ -107,32 +108,40 @@
     return mean, jnp.sum(off * off, axis=0, keepdims=True) / count
 
 
-def stats_kernel(cells, out):
-    mean, var = channel_stats(cells[...].astype(F32))
-    out[...] = jnp.broadcast_to(group_row(mean, var)[:1], out.shape)
-
-
-def local_stats(cells):
+def stats_kernel(mine, other, out):
+    parts = [r[...].astype(F32) for r in (mine, other)]
+    count = 2 * parts[0].shape[0]
+    mean = sum(jnp.sum(p, axis=0, keepdims=True) for p in parts) / count
+    var = 0.0
+    for part in parts:
+        off = part - mean
+        var = var + jnp.sum(off * off, axis=0, keepdims=True)
+    out[...] = group_row(mean, var / count)
+
+
+def local_stats(mine, other):
     return pl.pallas_call(
         stats_kernel,
-        out_shape=jax.ShapeDtypeStruct((128, 128), F32),
-        compiler_params=params(),
-    )(cells)
+        out_shape=jax.ShapeDtypeStruct((8, 128), F32),
+        compiler_params=params(),
+    )(mine, other)
 
 
 def attention_kernel(
-    order, q_ref, k0, k1, k2, k3, stats, gain, bias, w_qkv, pick, out, keys, values, found, logs
+    order, q_ref, mine, other, s0, s1, s2, s3, gain, bias, w_qkv, out, keys, values
 ):
-    mean, inverse = combine_groups(stats[...])
+    stats = jnp.concatenate([s0[...], s1[...], s2[...], s3[...]], axis=0)
+    mean, inverse = combine_groups(stats)
 
     def norm(cells):
         normed = (cells.astype(F32) - mean) * inverse
         return (normed * gain[...] + bias[...]).astype(BF16)
 
     head_of = iota((512, C), 1) >> 6
-    for i, piece in enumerate((k0, k1, k2, k3)):
-        both = dot(norm(piece[...]), w_qkv[:, C:])
+    for i in range(8):
         rows = slice(512 * i, 512 * i + 512)
+        cells = (mine, other)[i // 4][512 * (i % 4) : 512 * (i % 4) + 512, :]
+        both = dot(norm(cells), w_qkv[:, C:])
         keys[rows, :] = both[:, :C].astype(BF16)
         for head in range(HEADS):
             values[head, rows, :] = jnp.where(head_of == head, both[:, C:], 1.0).astype(BF16)
@@ -144,63 +153,41 @@
     result = jnp.zeros((STRIP, C), F32)
     packed = jnp.zeros((STRIP, 128), F32)
     for head in range(HEADS):
-        mine = head_of == head
-        masked = jnp.where(mine, queries, jnp.zeros_like(queries))
+        own = head_of == head
+        masked = jnp.where(own, queries, jnp.zeros_like(queries))
         best, mixed = None, None
-        for i in range(4):
-            rows = slice(512 * i, 512 * i + 512)
+        for i in range(4096 // KEY_BLOCK):
+            rows = slice(KEY_BLOCK * i, KEY_BLOCK * (i + 1))
             scores = dot(masked, keys[rows, :], ((1,), (1,)))
             top = jnp.max(scores, axis=1, keepdims=True)
             fresh = top if i == 0 else jnp.maximum(best, top)
             product = dot(jnp.exp2(scores - fresh).astype(BF16), values[head, rows, :])
             mixed = product if i == 0 else mixed * jnp.exp2(best - fresh) + product
             best = fresh
-        total = pltpu.roll(mixed, HD, 1)
-        result = jnp.where(mine, mixed / total, result)
+        result = jnp.where(own, mixed / pltpu.roll(mixed, HD, 1), result)
         spot = 0 if head else 128
         log = best + jnp.log2(mixed[:, spot : spot + 128])
         for part, value in enumerate(split3(log)):
             packed = jnp.where(lane == 4 * part + head, value.astype(F32), packed)
-    found[...] = result.astype(BF16)
-    logs[...] = packed.astype(BF16)
+    result = result.astype(BF16)
     for step in range(4):
-        rows = slice(288 * step, 288 * step + 336)
-        for side in range(2):
-            chosen = pick[side]
-            place = order[2 * step + side]
-            out[place, :CELLS_IN, :] = dot(chosen, found[rows, :]).astype(BF16)
-            turned = dot(logs[rows, :], chosen, ((0,), (1,)))[:16]
-            turned = jnp.concatenate([turned, jnp.zeros((16, 64), F32)], axis=1)
-            out[place, CELLS_IN:, :] = turned.astype(BF16)
-
-
-def pick_matrix():
-    table = np.zeros((2, CELLS_IN, 336), np.float32)
-    for side in range(2):
-        for r in range(18):
-            for q in range(10):
-                table[side, r * 10 + q, r * 18 + 8 * side + q] = 1.0
-    return table
-
-
-PICK = pick_matrix()
-
-
-def partial_attention(order, queries, pieces, stats, gain, bias, w_qkv):
+        rows = slice(160 * step, 160 * step + CELLS_IN)
+        place = order[step]
+        out[place, :CELLS_IN, :] = result[rows]
+        turned = jnp.concatenate([packed[rows], jnp.zeros((64, 128), F32)], axis=0).T[:16]
+        out[place, CELLS_IN:, :] = turned.astype(BF16)
+
+
+def partial_attention(order, queries, mine, other, stats, gain, bias, w_qkv):
     vmem = pl.BlockSpec(memory_space=pltpu.VMEM)
     return pl.pallas_call(
         attention_kernel,
-        out_shape=jax.ShapeDtypeStruct((8, CELLS_IN + 16, C), BF16),
+        out_shape=jax.ShapeDtypeStruct((4, CELLS_IN + 16, C), BF16),
         in_specs=[pl.BlockSpec(memory_space=pltpu.SMEM)] + [vmem] * 10,
         out_specs=vmem,
-        scratch_shapes=[
-            pltpu.VMEM((2048, C), BF16),
-            pltpu.VMEM((HEADS, 2048, C), BF16),
-            pltpu.VMEM((STRIP, C), BF16),
-            pltpu.VMEM((STRIP, 128), BF16),
-        ],
-        compiler_params=params(),
-    )(order, queries, *pieces, stats, gain, bias, w_qkv, jnp.asarray(PICK, BF16))
+        scratch_shapes=[pltpu.VMEM((4096, C), BF16), pltpu.VMEM((HEADS, 4096, C), BF16)],
+        compiler_params=params(),
+    )(order, queries, mine, other, *stats, gain, bias, w_qkv)
 
 
 def merge_kernel(flags, parts, coarse, w_proj, up, merged_out, stats_out):
@@ -271,29 +258,24 @@
     )(*windows, weight)
 
 
-def conv_kernel(
+def hidden_kernel(
     flags,
     merged,
     up,
     stats,
     gain,
     bias,
-    weight,
-    conv_bias,
     cot,
     grad_hidden,
-    fine_out,
-    halves,
+    kept,
+    given,
+    hidden,
     shift_out,
     xhat_out,
     inverse_out,
-    hid0,
-    hid1,
-    hid2,
 ):
     mean, inverse = combine_groups(stats[...])
     inverse_out[...] = jnp.broadcast_to(inverse, (8, C))
-    hidden = (hid0, hid1, hid2)
     row = iota((WIN, C), 0)
     col = row & 15
     for b in range(3):
@@ -306,7 +288,7 @@
             outside = outside | ((col == 0) & (flags[2] == 1))
         if b == 2:
             outside = outside | ((col == 15) & (flags[3] == 1))
-        hidden[b][...] = jnp.where(outside, 0.0, shifted * sig).astype(BF16)
+        hidden[b] = jnp.where(outside, 0.0, shifted * sig).astype(BF16)
         if b == 1:
             inner = slice(16, 528)
             s, t = sig[inner], shifted[inner]
@@ -321,36 +303,53 @@
                     piece = split3(value)[part].astype(F32)
                     rows += [piece[:, :128], piece[:, 128:]]
             tail = jnp.concatenate(rows + [jnp.zeros((4, 128), F32)], axis=0).astype(BF16)
-            halves[0, 2304:, :] = tail
-            halves[1, 2304:, :] = tail
-    total = jnp.zeros((512, C), F32) + conv_bias[...]
+            kept[2304:, :] = tail
+            given[2304:, :] = tail
+    first = flags[4] == 0
     for a in range(3):
         for b in range(3):
-            tap = 3 * a + b
-            window = hidden[b][16 * a : 16 * a + 512, :]
-            total = total + dot(window, weight[tap])
-            product = dot(window, cot[...], ((0,), (0,)))
-            halves[0, tap * C : (tap + 1) * C, :] = product[:, :128].astype(BF16)
-            halves[1, tap * C : (tap + 1) * C, :] = product[:, 128:].astype(BF16)
-    fine_out[...] = total.astype(BF16)
-
-
-def conv(flags, merged, up, stats, gain, bias, weight, conv_bias, cot, grad_hidden):
+            rows = slice((3 * a + b) * C, (3 * a + b + 1) * C)
+            product = dot(hidden[b, 16 * a : 16 * a + 512, :], cot[...], ((0,), (0,)))
+            left, right = product[:, :128].astype(BF16), product[:, 128:].astype(BF16)
+            kept[rows, :] = jnp.where(first, left, right)
+            given[rows, :] = jnp.where(first, right, left)
+
+
+def hidden_and_kernel_gradient(flags, merged, up, stats, gain, bias, cot, grad_hidden):
     vmem = pl.BlockSpec(memory_space=pltpu.VMEM)
     return pl.pallas_call(
-        conv_kernel,
+        hidden_kernel,
         out_shape=(
-            jax.ShapeDtypeStruct((512, C), BF16),
-            jax.ShapeDtypeStruct((2, 2320, 128), BF16),
+            jax.ShapeDtypeStruct((2320, 128), BF16),
+            jax.ShapeDtypeStruct((2320, 128), BF16),
+            jax.ShapeDtypeStruct((3, WIN, C), BF16),
             jax.ShapeDtypeStruct((512, C), F32),
             jax.ShapeDtypeStruct((512, C), F32),
             jax.ShapeDtypeStruct((8, C), F32),
         ),
-        in_specs=[pl.BlockSpec(memory_space=pltpu.SMEM)] + [vmem] * 9,
-        out_specs=(vmem,) * 5,
-        scratch_shapes=[pltpu.VMEM((WIN, C), BF16)] * 3,
-        compiler_params=params(),
-    )(flags, merged, up, stats, gain, bias, weight, conv_bias, cot, grad_hidden)
+        in_specs=[pl.BlockSpec(memory_space=pltpu.SMEM)] + [vmem] * 7,
+        out_specs=(vmem,) * 6,
+        compiler_params=params(),
+    )(flags, merged, up, stats, gain, bias, cot, grad_hidden)
+
+
+def conv_kernel(hidden, weight, conv_bias, fine_out):
+    total = jnp.zeros((512, C), F32) + conv_bias[...]
+    for a in range(3):
+        for b in range(3):
+            total = total + dot(hidden[b, 16 * a : 16 * a + 512, :], weight[3 * a + b])
+    fine_out[...] = total.astype(BF16)
+
+
+def conv(hidden, weight, conv_bias):
+    return pl.pallas_call(
+        conv_kernel,
+        out_shape=jax.ShapeDtypeStruct((512, C), BF16),
+        compiler_params=params(),
+        cost_estimate=pl.CostEstimate(
+            flops=9 * 2 * 512 * C * C, bytes_accessed=3 * 10**6, transcendentals=0
+        ),
+    )(hidden, weight, conv_bias)
 
 
 def pair_kernel(kept, got, out, total):
@@ -375,15 +374,6 @@
 
 def shift(value, axis, count, step):
     return lax.ppermute(value, axis, [((i + step) % count, i) for i in range(count)])
-
-
-def line_halo(value, axis, count, dim):
-    size = value.shape[dim]
-    tail = lax.slice_in_dim(value, size - 1, size, axis=dim)
-    head = lax.slice_in_dim(value, 0, 1, axis=dim)
-    before = lax.ppermute(tail, axis, [(i, i + 1) for i in range(count - 1)])
-    after = lax.ppermute(head, axis, [(i + 1, i) for i in range(count - 1)])
-    return jnp.concatenate([before, value, after], axis=dim)
 
 
 def per_device(
@@ -400,59 +390,61 @@
 ):
     y, c = lax.axis_index("y"), lax.axis_index("c")
     block = lax.axis_index(ZXC)
-    flags = jnp.stack([y == 0, y == 3, block == 0, block == 31]).astype(jnp.int32)
+    flags = jnp.stack([y == 0, y == 3, block == 0, block == 31, c == 1]).astype(jnp.int32)
     up = jnp.asarray(UPSAMPLE, BF16)
     taps = conv_weight.reshape(9, C, C)
 
     own = coarse.reshape(128, C)
-    stats = local_stats(own)
-    stats = lax.all_to_all(stats.reshape(128, 1, 128), ALL, 0, 0, tiled=True).reshape(128, 128)
-
-    line = jnp.concatenate([own] + [shift(own, "x", 4, k) for k in (1, 3, 2)], axis=0)
-    pieces = [line] + [shift(line, "z", 4, k) for k in (1, 3, 2)]
-
-    wide = line_halo(coarse, ZXC, 32, 1)
-    blocks = [wide] + [shift(wide, "y", 4, k) for k in (1, 2, 3)]
-    rows = jnp.concatenate([blocks[3][-1:]] + blocks + [blocks[0][:1]], axis=0)
-    other = shift(rows, "c", 2, 1)
-    left = jnp.where(c == 0, rows, other)[:, :9]
-    right = jnp.where(c == 0, other, rows)[:, 1:]
-    queries = jnp.concatenate([left, right], axis=1).reshape(66 * 18, C)
-    queries = jnp.pad(queries, ((0, STRIP - 66 * 18), (0, 0)))
-    mine = jnp.pad(rows[:18].reshape(180, C), ((0, CELLS_IN - 180), (0, 0)))
-    order = jnp.stack([((y + k) % 4) * 2 + j for k in range(4) for j in range(2)])
-    order = order.astype(jnp.int32)
-
-    grad = line_halo(line_halo(cotangent, "y", 4, 0), ZXC, 32, 1)
+    cells = lax.all_to_all(
+        jnp.broadcast_to(own[None], (16, 128, C)), ("z", "x"), 0, 0, tiled=True
+    ).reshape(2048, C)
+
+    first = jnp.concatenate([coarse[:, 0], cotangent[:, 0]], axis=0)
+    last = jnp.concatenate([coarse[:, -1], cotangent[:, -1]], axis=0)
+    before = lax.ppermute(last, ZXC, [(i, i + 1) for i in range(31)])[:, None]
+    after = lax.ppermute(first, ZXC, [(i + 1, i) for i in range(31)])[:, None]
+    wide = jnp.concatenate([before[:16], coarse, after[:16]], axis=1).reshape(160, C)
+    grad = jnp.concatenate([before[16:], cotangent, after[16:]], axis=1)
+    below = shift(jnp.concatenate([wide, grad[0]], axis=0), "y", 4, 1)
+    above = shift(jnp.concatenate([wide, grad[-1]], axis=0), "y", 4, 3)
+    blocks = [above[150:160], wide, below[:160], shift(wide, "y", 4, 2), above[:160], wide[:10]]
+    queries = jnp.pad(jnp.concatenate(blocks, axis=0), ((0, STRIP - 660), (0, 0)))
+    top = jnp.where(y == 0, 0, above[160:])[None].astype(BF16)
+    bottom = jnp.where(y == 3, 0, below[160:])[None].astype(BF16)
+    grad = jnp.concatenate([top, grad, bottom], axis=0)
     windows = [grad[:, b : b + 16].reshape(WIN, C) for b in range(3)]
+    cells, queries = lax.optimization_barrier((cells, queries))
+    other = shift(cells, "c", 2, 1)
+
+    stats = local_stats(cells, other)
+    stats = [stats] + [shift(stats, "y", 4, k) for k in (1, 2, 3)]
+    order = jnp.stack([(y + k) % 4 for k in range(4)]).astype(jnp.int32)
+
+    partial = partial_attention(
+        order, queries, cells, other, stats, norm1_gain[None], norm1_bias[None], w_qkv
+    )
+    partial = lax.all_to_all(partial, "y", 0, 0, tiled=True)
+    merged, stats2 = merge(flags, partial, queries[:CELLS_IN], w_proj, up)
+    stats2 = lax.all_to_all(stats2.reshape(128, 1, 128), ALL, 0, 0, tiled=True)
     grad_hidden = back_conv(windows, taps)
-
-    partial = partial_attention(
-        order, queries, pieces, stats, norm1_gain[None], norm1_bias[None], w_qkv
-    )
-    partial = lax.all_to_all(partial, ("y", "c"), 0, 0, tiled=True)
-    merged, stats2 = merge(flags, partial, mine, w_proj, up)
-    stats2 = lax.all_to_all(stats2.reshape(128, 1, 128), ALL, 0, 0, tiled=True)
-    fine, halves, grad_shift, xhat, inverse = conv(
+    kept, given, hidden, grad_shift, xhat, inverse = hidden_and_kernel_gradient(
         flags,
         merged,
         up,
         stats2.reshape(128, 128),
         second_norm2_gain[None],
         second_norm2_bias[None],
-        taps,
-        conv_bias[None],
         cotangent.reshape(512, C),
         grad_hidden,
     )
 
-    kept = lax.dynamic_index_in_dim(halves, c, 0, keepdims=False)
-    given = lax.dynamic_index_in_dim(halves, 1 - c, 0, keepdims=False)
     sent = pair_sum(kept, shift(given, "c", 2, 1))
+    sent, hidden = lax.optimization_barrier((sent, hidden))
     got = lax.all_to_all(sent, ("y", "z", "x"), 0, 0, tiled=True)
+    fine = conv(hidden, taps, conv_bias[None])
+
     total = jnp.sum(got.astype(F32), axis=0)
     root = jnp.sqrt(jnp.float32(65536))
-    sums = jnp.sum(total[36:].reshape(3, 2, C), axis=0)
     chunk = (total[:36] / root).astype(BF16)
     spread = lax.all_to_all(
         jnp.broadcast_to(chunk[None], (64, 36, 128)), ("y", "z", "x"), 0, 0, tiled=True
@@ -461,6 +453,7 @@
     left = jnp.where(c == 0, spread, other)
     right = jnp.where(c == 0, other, spread)
     grad_conv = jnp.concatenate([left, right], axis=1).astype(F32).reshape(3, 3, C, C)
+    sums = jnp.sum(total[36:].reshape(3, 2, C), axis=0)
     grad_norm = sums / root
 
     count = jnp.float32(65536 * SHARE)

time: 170 us -> 151 us (0.89)
  starting transfers between devices: 63.5 us -> 45 us
    ppermute x6 -> x2, starting transfers between devices: 16.6 us -> 6.43 us  [the longest x1 3.33 us: per_device(): after = lax.ppermute(first, ZXC, [(i + 1, i) for i in range(31)])[:, None]]
    ppermute x12 -> x9, starting transfers between devices: 21 us -> 13.4 us  [shift(): lax.ppermute(value, axis, [((i + step) % count, i) for i in range(count)])]
    all_to_all x2, waiting for transfers between devices: 4.85 us -> 9.13 us  [the longest x1 5.33 us: per_device(): lax.all_to_all(jnp.broadcast_to(own[None], (16, 128, C)), ('z', 'x'), 0,...]
    ppermute x6 -> x2, waiting for transfers between devices: 2.17 us -> 0.01 us  [the longest x1 0.01 us: per_device(): before = lax.ppermute(last, ZXC, [(i, i + 1) for i in range(31)])[:, None]]
    broadcast_in_dim x0 -> x1, local copies, waits for them, and re-layouts: none -> 1.91 us  [per_device(): jnp.broadcast_to(own[None], (16, 128, C))]
    ppermute x12 -> x9, waiting for transfers between devices: 10.9 us -> 9.25 us  [shift(): lax.ppermute(value, axis, [((i + step) % count, i) for i in range(count)])]
    unnamed x44 -> x42, local copies, waits for them, and re-layouts: 6.49 us -> 4.94 us
    slice x6 -> x16, local copies, waits for them, and re-layouts: 2.39 us -> 3.7 us  [the longest x2 2.02 us: per_device(): last = jnp.concatenate([coarse[:, -1], cotangent[:, -1]], axis=0)]
  transfers between devices with their start and end apart: 22 -> 15, of which waited for: 7 -> 8; matrix products, arithmetic and copies ran while one was open for 6% -> 7% of each run, Pallas kernels for 13% -> 2%
where the time goes in v3:
time: 151 us
  starting transfers between devices  45 us (30%)
  waiting for transfers between devices  36.5 us (24%)
  Pallas kernels  27 us (18%)
  blocking collectives  19.9 us (13%)
  local copies, waits for them, and re-layouts  14.5 us (10%)
  other arithmetic  6.68 us (4%)
    all_to_all x1, blocking collectives, per_device(): got = lax.all_to_all(sent, ('y', 'z', 'x'), 0, 0, tiled=True)  19.9 us
    pallas_call x1, Pallas kernels, partial_attention(): pl.pallas_call(attention_kernel, out_shape=jax.ShapeDtypeStruct((4, CELLS...  17 us
    ppermute x9, starting transfers between devices, shift(): lax.ppermute(value, axis, [((i + step) % count, i) for i in range(count)])  13.4 us
    all_to_all x1, waiting for transfers between devices, per_device(): lax.all_to_all(jnp.broadcast_to(chunk[None], (64, 36, 128)), ('y', 'z', '...  10.9 us
    ppermute x9, waiting for transfers between devices, shift(): lax.ppermute(value, axis, [((i + step) % count, i) for i in range(count)])  9.25 us
    all_to_all x1, starting transfers between devices, per_device(): lax.all_to_all(jnp.broadcast_to(own[None], (16, 128, C)), ('z', 'x'), 0,...  9.24 us
    all_to_all x1, waiting for transfers between devices, per_device(): stats2 = lax.all_to_all(stats2.reshape(128, 1, 128), ALL, 0, 0, tiled=True)  7.18 us
    all_to_all x1, starting transfers between devices, per_device(): stats2 = lax.all_to_all(stats2.reshape(128, 1, 128), ALL, 0, 0, tiled=True)  6.8 us
  transfers between devices with their start and end apart: 15, of which 8 were waited for; matrix products, arithmetic and copies ran while one was open for 7% of the time, Pallas kernels for 2%

profile of v3, /device:TPU:1, one launch (start us, length us, event | category | flops | bytes accessed | tf_op | source)
XLA Modules:
  0.0 150.7 jit_solution(16558692192172936255)
XLA Ops:
  0.7 1.0 fusion.6
  1.7 1.0 fusion.5
  2.7 3.3 %collective-permute-start.1 = (bf16[48,256]{1,0:T(8,128)(2,1)S(1)}, bf16[48,256]{1,0:T(8,128)(2,1)S(1)}, u32[]{:S(2)}, u32[]{:S(2)}) collective-permute-start(bf16[48,256]{1,0:T(8,128)(2,1)S(1)} %pad_maximum_fusion.5), channel_id=1, source_target_pairs={{1,0},{2,1},{3,2},{4,3},{5,4},{6,5},{7,6},{8,7},{9,8},{10,9},{11,1... | collective-permute-start | bytes 73736 | tf_op jit(solution)/shard_map/ppermute | solution.py:405
  6.1 3.1 %collective-permute-start = (bf16[48,256]{1,0:T(8,128)(2,1)S(1)}, bf16[48,256]{1,0:T(8,128)(2,1)S(1)}, u32[]{:S(2)}, u32[]{:S(2)}) collective-permute-start(bf16[48,256]{1,0:T(8,128)(2,1)S(1)} %pad_maximum_fusion.4), channel_id=1, source_target_pairs={{0,1},{1,2},{2,3},{3,4},{4,5},{5,6},{6,7},{7,8},{8,9},{9,10},{10,1... | collective-permute-start | bytes 73736 | tf_op jit(solution)/shard_map/ppermute | solution.py:404
  9.2 1.9 %broadcast_in_dim.53 = bf16[16,128,256]{2,1,0:T(8,128)(2,1)} broadcast(bf16[128,256]{1,0:T(8,128)(2,1)} %bitcast.81), dimensions={1,2} | broadcast | bytes 1114112 | tf_op jit(solution)/shard_map/broadcast_in_dim | solution.py:399
  11.1 9.2 %all-to-all-start = ((bf16[16,128,256]{2,1,0:T(8,128)(2,1)}), bf16[16,128,256]{2,1,0:T(8,128)(2,1)S(1)}, u32[]{:S(2)}, u32[]{:S(2)}) async-start(bf16[16,128,256]{2,1,0:T(8,128)(2,1)} %broadcast_in_dim.53), calls=%async_computation | async-start | bytes 2097152 | tf_op jit(solution)/shard_map/all_to_all | solution.py:398
  20.7 3.0 %collective-permute-start.4 = (bf16[160,256]{1,0:T(8,128)(2,1)S(1)}, bf16[160,256]{1,0:T(8,128)(2,1)S(1)}, u32[]{:S(2)}, u32[]{:S(2)}) collective-permute-start(bf16[160,256]{1,0:T(8,128)(2,1)S(1)} %reshape.74), channel_id=1, source_target_pairs={{64,0},{96,32},{0,64},{32,96},{65,1},{97,33},{1,65},{33,97},{66,2}... | collective-permute-start | bytes 245768 | tf_op jit(solution)/shard_map/ppermute | solution.py:376
  23.8 0.8 collective-permute-start.3
  24.6 0.7 collective-permute-start.2
  25.3 4.3 %collective-permute-done.2 = bf16[178,256]{1,0:T(8,128)(2,1)S(1)} collective-permute-done((bf16[178,256]{1,0:T(8,128)(2,1)S(1)}, bf16[178,256]{1,0:T(8,128)(2,1)S(1)}, u32[]{:S(2)}, u32[]{:S(2)}) %collective-permute-start.2) | collective-permute-done | bytes 91168 | tf_op jit(solution)/shard_map/ppermute | solution.py:376
  29.7 0.6 copy-done.18
  30.2 1.2 concatenate.38
  31.4 5.3 %all-to-all-done = bf16[16,128,256]{2,1,0:T(8,128)(2,1)S(1)} async-done(((bf16[16,128,256]{2,1,0:T(8,128)(2,1)}), bf16[16,128,256]{2,1,0:T(8,128)(2,1)S(1)}, u32[]{:S(2)}, u32[]{:S(2)}) %all-to-all-start) | async-done | bytes 1048608 | tf_op jit(solution)/shard_map/all_to_all | solution.py:398
  37.0 2.4 %collective-permute-done.5.other = bf16[2048,256]{1,0:T(8,128)(2,1)S(1)} collective-permute-done((bf16[2048,256]{1,0:T(8,128)(2,1)S(1)}, bf16[2048,256]{1,0:T(8,128)(2,1)S(1)}, u32[]{:S(2)}, u32[]{:S(2)}) %collective-permute-start.5) | collective-permute-done | bytes 1048608 | tf_op jit(solution)/shard_map/ppermute | solution.py:376
  39.4 1.4 shard_map.138.s0
  40.9 1.3 collective-permute-start.8
  42.2 2.6 %collective-permute-start.7 = (f32[8,128]{1,0:T(8,128)S(1)}, f32[8,128]{1,0:T(8,128)S(1)}, u32[]{:S(2)}, u32[]{:S(2)}) collective-permute-start(f32[8,128]{1,0:T(8,128)S(1)} %shard_map.138.s0), channel_id=1, source_target_pairs={{64,0},{96,32},{0,64},{32,96},{65,1},{97,33},{1,65},{33,97},{66,2}... | collective-permute-start | bytes 12296 | tf_op jit(solution)/shard_map/ppermute | solution.py:376
  44.8 1.1 collective-permute-start.6
  45.9 0.6 fusion.1
  46.5 0.8 collective-permute-done.6.s1
  47.3 1.0 copy-done.8
  48.3 17.0 %shard_map.139 = bf16[4,208,256]{2,1,0:T(8,128)(2,1)S(1)} custom-call(s32[4]{0:T(128)S(1)} %pad_add_fusion.order, bf16[672,256]{1,0:T(8,128)(2,1)S(1)} %pad.4.q_ref, bf16[2048,256]{1,0:T(8,128)(2,1)S(1)} %bitcast.66, bf16[2048,256]{1,0:T(8,128)(2,1)S(1)} %collective-permute-done.5.other, f32[8,128]{1,0:T(8,128)S(1)} %shard_map.138.s0, ...), custom_call_target="tpu_custom_call" | custom-call | tf_op jit(solution)/shard_map/pallas_call | solution.py:183
  65.3 0.7 copy-done.3
  66.1 3.5 %all-to-all-start.1 = ((bf16[4,208,256]{2,1,0:T(8,128)(2,1)}), bf16[4,208,256]{2,1,0:T(8,128)(2,1)S(1)}, u32[]{:S(2)}, u32[]{:S(2)}) async-start(bf16[4,208,256]{2,1,0:T(8,128)(2,1)} %copy-done.3), calls=%async_computation.1 | async-start | bytes 851968 | tf_op jit(solution)/shard_map/all_to_all | solution.py:426
  69.5 0.8 fusion.2
  70.4 1.8 %pad_maximum_fusion = bf16[34,18,256]{2,1,0:T(8,128)(2,1)} fusion(bf16[1,18,256]{2,1,0:T(8,128)(2,1)} %fusion.1, bf16[32,1,256]{2,1,0:T(2,128)(2,1)} %copy-done.16, bf16[32,16,256]{2,1,0:T(8,128)(2,1)S(1)} %copy-done.2, bf16[32,1,256]{2,1,0:T(2,128)(2,1)} %copy-done.17, bf16[1,18,256]{2,1,0:T(8,128)(2,1)S(1)} %fusion.2), kind=kLoop, calls=%fused_computation.5 | loop fusion | flops 1566720 | bytes 626688 | tf_op jit(solution)/shard_map/concatenate | solution.py:414
  72.1 3.8 %all-to-all-done.1.parts = bf16[4,208,256]{2,1,0:T(8,128)(2,1)S(1)} async-done(((bf16[4,208,256]{2,1,0:T(8,128)(2,1)}), bf16[4,208,256]{2,1,0:T(8,128)(2,1)S(1)}, u32[]{:S(2)}, u32[]{:S(2)}) %all-to-all-start.1) | async-done | bytes 426016 | tf_op jit(solution)/shard_map/all_to_all | solution.py:426
  75.9 0.9 copy-done.9
  76.9 3.0 %shard_map.140 = (bf16[192,256]{1,0:T(8,128)(2,1)S(1)}, f32[128,128]{1,0:T(8,128)}) custom-call(s32[5]{0:T(128)S(1)} %convert_element_type.21.flags, bf16[4,208,256]{2,1,0:T(8,128)(2,1)S(1)} %all-to-all-done.1.parts, bf16[192,256]{1,0:T(8,128)(2,1)S(1)} %slice.107.coarse, bf16[256,256]{1,0:T(8,128)(2,1)S(1)} %copy-done.9, bf16[1632,192]{1,0:T(8,128)(2,1)S(1)} %copy-done.1), custom_call_target="tpu_custom_call" | custom-call | tf_op jit(solution)/shard_map/pallas_call | solution.py:228
  79.9 6.8 %all-to-all-start.2 = ((f32[128,1,128]{2,1,0:T(1,128)}), f32[128,1,128]{2,1,0:T(1,128)S(1)}, u32[]{:S(2)}, u32[]{:S(2)}) async-start(f32[128,1,128]{2,1,0:T(1,128)} %bitcast.25), calls=%async_computation.2 | async-start | bytes 131072 | tf_op jit(solution)/shard_map/all_to_all | solution.py:428
  86.7 1.6 %fusion.4 = (bf16[34,16,256]{2,1,0:T(8,128)(2,1)S(1)}, bf16[34,16,256]{2,1,0:T(8,128)(2,1)S(1)}, bf16[34,16,256]{2,1,0:T(8,128)(2,1)S(1)}) fusion(bf16[34,18,256]{2,1,0:T(8,128)(2,1)} %pad_maximum_fusion), kind=kLoop, calls=%fused_computation.36 | loop fusion | bytes 1671168 | tf_op jit(solution)/shard_map/slice | solution.py:415
  88.3 0.8 shard_map.141.grad_hidden
  89.1 7.2 %all-to-all-done.2 = f32[128,1,128]{2,1,0:T(1,128)S(1)} async-done(((f32[128,1,128]{2,1,0:T(1,128)}), f32[128,1,128]{2,1,0:T(1,128)S(1)}, u32[]{:S(2)}, u32[]{:S(2)}) %all-to-all-start.2) | async-done | bytes 65568 | tf_op jit(solution)/shard_map/all_to_all | solution.py:428
  96.2 3.1 %shard_map.142 = (bf16[2320,128]{1,0:T(8,128)(2,1)S(1)}, bf16[2320,128]{1,0:T(8,128)(2,1)S(1)}, bf16[3,544,256]{2,1,0:T(8,128)(2,1)S(1)}, f32[512,256]{1,0:T(8,1...) custom-call(s32[5]{0:T(128)S(1)} %convert_element_type.21.flags, bf16[192,256]{1,0:T(8,128)(2,1)S(1)} %get-tuple-element.18.merged, ...), custom_call_target="tpu_custom_call" | custom-call | tf_op jit(solution)/shard_map/pallas_call | solution.py:320
  99.3 0.8 copy-done.4
  100.1 0.8 copy-done.6
  101.0 0.9 collective-permute-start.9
  101.8 1.6 %collective-permute-done.9.got = bf16[2320,128]{1,0:T(8,128)(2,1)S(1)} collective-permute-done((bf16[2320,128]{1,0:T(8,128)(2,1)S(1)}, bf16[2320,128]{1,0:T(8,128)(2,1)S(1)}, u32[]{:S(2)}, u32[]{:S(2)}) %collective-permute-start.9) | collective-permute-done | bytes 593952 | tf_op jit(solution)/shard_map/ppermute | solution.py:376
  103.7 19.9 %all_to_all.25 = bf16[64,48,128]{2,1,0:T(8,128)(2,1)S(1)} all-to-all(bf16[64,48,128]{2,1,0:T(8,128)(2,1)S(1)} %shard_map.143), channel_id=1, replica_groups=mesh['y'=4,'z'=4,'x'=4,'c'=2] {'y','z','x'}, dimensions={0} | all-to-all | bytes 1572864 | tf_op jit(solution)/shard_map/all_to_all | solution.py:443
  123.8 0.9 broadcast_in_dim.66
  124.7 5.6 %all-to-all-start.4 = ((bf16[64,36,128]{2,1,0:T(8,128)(2,1)}), bf16[64,36,128]{2,1,0:T(8,128)(2,1)}, u32[]{:S(2)}, u32[]{:S(2)}) async-start(bf16[64,36,128]{2,1,0:T(8,128)(2,1)} %broadcast_in_dim.66), calls=%async_computation.4 | async-start | bytes 1310720 | tf_op jit(solution)/shard_map/all_to_all | solution.py:449
  130.4 1.5 shard_map.144
  132.1 10.9 %all-to-all-done.4 = bf16[64,36,128]{2,1,0:T(8,128)(2,1)} async-done(((bf16[64,36,128]{2,1,0:T(8,128)(2,1)}), bf16[64,36,128]{2,1,0:T(8,128)(2,1)}, u32[]{:S(2)}, u32[]{:S(2)}) %all-to-all-start.4) | async-done | bytes 589856 | tf_op jit(solution)/shard_map/all_to_all | solution.py:449
  143.1 1.2 reshape.85
  144.3 3.0 %collective-permute-start.10 = (bf16[2304,128]{1,0:T(8,128)(2,1)S(1)}, bf16[2304,128]{1,0:T(8,128)(2,1)S(1)}, u32[]{:S(2)}, u32[]{:S(2)}) collective-permute-start(bf16[2304,128]{1,0:T(8,128)(2,1)S(1)} %reshape.85), channel_id=1, source_target_pairs={{1,0},{0,1},{3,2},{2,3},{5,4},{4,5},{7,6},{6,7},{9,8},{8,9},{11,10... | collective-permute-start | bytes 1769480 | tf_op jit(solution)/shard_map/ppermute | solution.py:376
  147.6 0.6 broadcast_multiply_fusion
  148.2 0.8 multiply_convert_fusion
  149.1 1.6 %maximum_convert_fusion = f32[3,3,256,256]{3,2,1,0:T(8,128)} fusion(bf16[3,3,256,128]{3,2,1,0:T(8,128)(2,1)S(1)} %bitcast.80, bf16[3,3,256,128]{3,2,1,0:T(8,128)(2,1)S(1)} %bitcast.79), kind=kLoop, calls=%fused_computation.1 | loop fusion | flops 2359296 | bytes 3538944 | tf_op jit(solution)/shard_map/convert_element_type | solution.py:455
  (84 shorter events, 1.7 us)
Async XLA Ops:
  0.6 19.9 %copy-start.15 = (bf16[16,8,256]{2,1,0:T(8,128)(2,1)S(1)}, bf16[16,8,256]{2,1,0:T(8,128)(2,1)}, u32[]{:S(2)}) copy-start(bf16[16,8,256]{2,1,0:T(8,128)(2,1)} %param.11) | copy-start | bytes 196612
  0.6 23.1 %copy-start.2 = (bf16[32,16,256]{2,1,0:T(8,128)(2,1)S(1)}, bf16[32,16,256]{2,1,0:T(8,128)(2,1)}, u32[]{:S(2)}) copy-start(bf16[32,16,256]{2,1,0:T(8,128)(2,1)} %param.20) | copy-start | bytes 786436
  2.7 17.7 %collective-permute-start.1 = (bf16[48,256]{1,0:T(8,128)(2,1)S(1)}, bf16[48,256]{1,0:T(8,128)(2,1)S(1)}, u32[]{:S(2)}, u32[]{:S(2)}) collective-permute-start(bf16[48,256]{1,0:T(8,128)(2,1)S(1)} %pad_maximum_fusion.5), channel_id=1, source_target_pairs={{1,0},{2,1},{3,2},{4,3},{5,4},{6,5},{7,6},{8,7},{9,8},{10,9},{11,1... | collective-permute-start | bytes 73736 | tf_op jit(solution)/shard_map/ppermute | solution.py:405
  6.1 14.4 %collective-permute-start = (bf16[48,256]{1,0:T(8,128)(2,1)S(1)}, bf16[48,256]{1,0:T(8,128)(2,1)S(1)}, u32[]{:S(2)}, u32[]{:S(2)}) collective-permute-start(bf16[48,256]{1,0:T(8,128)(2,1)S(1)} %pad_maximum_fusion.4), channel_id=1, source_target_pairs={{0,1},{1,2},{2,3},{3,4},{4,5},{5,6},{6,7},{7,8},{8,9},{9,10},{10,1... | collective-permute-start | bytes 73736 | tf_op jit(solution)/shard_map/ppermute | solution.py:404
  11.1 25.7 %all-to-all-start = ((bf16[16,128,256]{2,1,0:T(8,128)(2,1)}), bf16[16,128,256]{2,1,0:T(8,128)(2,1)S(1)}, u32[]{:S(2)}, u32[]{:S(2)}) async-start(bf16[16,128,256]{2,1,0:T(8,128)(2,1)} %broadcast_in_dim.53), calls=%async_computation | async-start | bytes 2097152 | tf_op jit(solution)/shard_map/all_to_all | solution.py:398
  20.5 9.2 %copy-start.16 = (bf16[32,1,256]{2,1,0:T(2,128)(2,1)}, bf16[32,1,256]{2,1,0:T(2,128)(2,1)S(1)}, u32[]{:S(2)}) copy-start(bf16[32,1,256]{2,1,0:T(2,128)(2,1)S(1)} %copy.42) | copy-start | bytes 49156
  20.6 9.7 %copy-start.17 = (bf16[32,1,256]{2,1,0:T(2,128)(2,1)}, bf16[32,1,256]{2,1,0:T(2,128)(2,1)S(1)}, u32[]{:S(2)}) copy-start(bf16[32,1,256]{2,1,0:T(2,128)(2,1)S(1)} %copy.41) | copy-start | bytes 49156
  20.7 26.6 %copy-start.11 = (f32[256]{0:T(256)S(1)}, f32[256]{0:T(256)}, u32[]{:S(2)}) copy-start(f32[256]{0:T(256)} %param.12) | copy-start | bytes 3076
  20.7 26.6 %copy-start.12 = (f32[256]{0:T(256)S(1)}, f32[256]{0:T(256)}, u32[]{:S(2)}) copy-start(f32[256]{0:T(256)} %param.13) | copy-start | bytes 3076
  20.7 9.5 %collective-permute-start.4 = (bf16[160,256]{1,0:T(8,128)(2,1)S(1)}, bf16[160,256]{1,0:T(8,128)(2,1)S(1)}, u32[]{:S(2)}, u32[]{:S(2)}) collective-permute-start(bf16[160,256]{1,0:T(8,128)(2,1)S(1)} %reshape.74), channel_id=1, source_target_pairs={{64,0},{96,32},{0,64},{32,96},{65,1},{97,33},{1,65},{33,97},{66,2}... | collective-permute-start | bytes 245768 | tf_op jit(solution)/shard_map/ppermute | solution.py:376
  23.8 5.9 %collective-permute-start.3 = (bf16[178,256]{1,0:T(8,128)(2,1)S(1)}, bf16[178,256]{1,0:T(8,128)(2,1)S(1)}, u32[]{:S(2)}, u32[]{:S(2)}) collective-permute-start(bf16[178,256]{1,0:T(8,128)(2,1)S(1)} %get-tuple-element.37), channel_id=1, source_target_pairs={{32,0},{64,32},{96,64},{0,96},{33,1},{65,33},{97,65},{1,97},{34,2}... | collective-permute-start | bytes 273416 | tf_op jit(solution)/shard_map/ppermute | solution.py:376
  24.6 5.0 %collective-permute-start.2 = (bf16[178,256]{1,0:T(8,128)(2,1)S(1)}, bf16[178,256]{1,0:T(8,128)(2,1)S(1)}, u32[]{:S(2)}, u32[]{:S(2)}) collective-permute-start(bf16[178,256]{1,0:T(8,128)(2,1)S(1)} %get-tuple-element.38), channel_id=1, source_target_pairs={{96,0},{0,32},{32,64},{64,96},{97,1},{1,33},{33,65},{65,97},{98,2}... | collective-permute-start | bytes 273416 | tf_op jit(solution)/shard_map/ppermute | solution.py:376
  29.6 0.6 copy-start.18
  36.8 2.7 %collective-permute-start.5 = (bf16[2048,256]{1,0:T(8,128)(2,1)S(1)}, bf16[2048,256]{1,0:T(8,128)(2,1)S(1)}, u32[]{:S(2)}, u32[]{:S(2)}) collective-permute-start(bf16[2048,256]{1,0:T(8,128)(2,1)S(1)} %bitcast.64), channel_id=1, source_target_pairs={{1,0},{0,1},{3,2},{2,3},{5,4},{4,5},{7,6},{6,7},{9,8},{8,9},{11,10... | collective-permute-start | bytes 3145736 | tf_op jit(solution)/shard_map/ppermute | solution.py:376
  40.9 5.6 %collective-permute-start.8 = (f32[8,128]{1,0:T(8,128)S(1)}, f32[8,128]{1,0:T(8,128)S(1)}, u32[]{:S(2)}, u32[]{:S(2)}) collective-permute-start(f32[8,128]{1,0:T(8,128)S(1)} %shard_map.138.s0), channel_id=1, source_target_pairs={{96,0},{0,32},{32,64},{64,96},{97,1},{1,33},{33,65},{65,97},{98,2}... | collective-permute-start | bytes 12296 | tf_op jit(solution)/shard_map/ppermute | solution.py:376
  42.2 4.3 %collective-permute-start.7 = (f32[8,128]{1,0:T(8,128)S(1)}, f32[8,128]{1,0:T(8,128)S(1)}, u32[]{:S(2)}, u32[]{:S(2)}) collective-permute-start(f32[8,128]{1,0:T(8,128)S(1)} %shard_map.138.s0), channel_id=1, source_target_pairs={{64,0},{96,32},{0,64},{32,96},{65,1},{97,33},{1,65},{33,97},{66,2}... | collective-permute-start | bytes 12296 | tf_op jit(solution)/shard_map/ppermute | solution.py:376
  44.8 2.5 %collective-permute-start.6 = (f32[8,128]{1,0:T(8,128)S(1)}, f32[8,128]{1,0:T(8,128)S(1)}, u32[]{:S(2)}, u32[]{:S(2)}) collective-permute-start(f32[8,128]{1,0:T(8,128)S(1)} %shard_map.138.s0), channel_id=1, source_target_pairs={{32,0},{64,32},{96,64},{0,96},{33,1},{65,33},{97,65},{1,97},{34,2}... | collective-permute-start | bytes 12296 | tf_op jit(solution)/shard_map/ppermute | solution.py:376
  47.3 1.0 copy-start.8
  48.3 27.6 %copy-start.1 = (bf16[1632,192]{1,0:T(8,128)(2,1)S(1)}, bf16[1632,192]{1,0:T(8,128)(2,1)}, u32[]{:S(2)}) copy-start(bf16[1632,192]{1,0:T(8,128)(2,1)} %constant.64.clone.up) | copy-start | bytes 1880068
  65.3 0.8 copy-start.3
  66.1 9.9 %all-to-all-start.1 = ((bf16[4,208,256]{2,1,0:T(8,128)(2,1)}), bf16[4,208,256]{2,1,0:T(8,128)(2,1)S(1)}, u32[]{:S(2)}, u32[]{:S(2)}) async-start(bf16[4,208,256]{2,1,0:T(8,128)(2,1)} %copy-done.3), calls=%async_computation.1 | async-start | bytes 851968 | tf_op jit(solution)/shard_map/all_to_all | solution.py:426
  69.5 18.7 %copy-start = (bf16[3,3,256,256]{3,2,1,0:T(8,128)(2,1)S(1)}, bf16[3,3,256,256]{3,2,1,0:T(8,128)(2,1)}, u32[]{:S(2)}) copy-start(bf16[3,3,256,256]{3,2,1,0:T(8,128)(2,1)} %param.18) | copy-start | bytes 3538948
  75.9 0.9 copy-start.9
  79.9 16.4 %copy-start.10 = (f32[256]{0:T(256)S(1)}, f32[256]{0:T(256)}, u32[]{:S(2)}) copy-start(f32[256]{0:T(256)} %param.16) | copy-start | bytes 3076
  79.9 16.4 %copy-start.13 = (f32[256]{0:T(256)S(1)}, f32[256]{0:T(256)}, u32[]{:S(2)}) copy-start(f32[256]{0:T(256)} %param.17) | copy-start | bytes 3076
  79.9 16.4 %all-to-all-start.2 = ((f32[128,1,128]{2,1,0:T(1,128)}), f32[128,1,128]{2,1,0:T(1,128)S(1)}, u32[]{:S(2)}, u32[]{:S(2)}) async-start(f32[128,1,128]{2,1,0:T(1,128)} %bitcast.25), calls=%async_computation.2 | async-start | bytes 131072 | tf_op jit(solution)/shard_map/all_to_all | solution.py:428
  99.3 0.8 copy-start.4
  100.1 0.8 copy-start.6
  101.0 2.5 %collective-permute-start.9 = (bf16[2320,128]{1,0:T(8,128)(2,1)S(1)}, bf16[2320,128]{1,0:T(8,128)(2,1)S(1)}, u32[]{:S(2)}, u32[]{:S(2)}) collective-permute-start(bf16[2320,128]{1,0:T(8,128)(2,1)S(1)} %get-tuple-element.21), channel_id=1, source_target_pairs={{1,0},{0,1},{3,2},{2,3},{5,4},{4,5},{7,6},{6,7},{9,8},{8,9},{11,10... | collective-permute-start | bytes 1781768 | tf_op jit(solution)/shard_map/ppermute | solution.py:376
  103.7 26.7 %copy-start.14 = (f32[256]{0:T(256)S(1)}, f32[256]{0:T(256)}, u32[]{:S(2)}) copy-start(f32[256]{0:T(256)} %param.19) | copy-start | bytes 3076
  124.7 23.5 %copy-start.5 = (f32[512,256]{1,0:T(8,128)S(1)}, f32[512,256]{1,0:T(8,128)}, u32[]{:S(2)}) copy-start(f32[512,256]{1,0:T(8,128)} %copy-done.4) | copy-start | bytes 1572868
  124.7 23.5 %copy-start.7 = (f32[512,256]{1,0:T(8,128)S(1)}, f32[512,256]{1,0:T(8,128)}, u32[]{:S(2)}) copy-start(f32[512,256]{1,0:T(8,128)} %copy-done.6) | copy-start | bytes 1572868
  124.7 18.3 %all-to-all-start.4 = ((bf16[64,36,128]{2,1,0:T(8,128)(2,1)}), bf16[64,36,128]{2,1,0:T(8,128)(2,1)}, u32[]{:S(2)}, u32[]{:S(2)}) async-start(bf16[64,36,128]{2,1,0:T(8,128)(2,1)} %broadcast_in_dim.66), calls=%async_computation.4 | async-start | bytes 1310720 | tf_op jit(solution)/shard_map/all_to_all | solution.py:449
  144.3 4.7 %collective-permute-start.10 = (bf16[2304,128]{1,0:T(8,128)(2,1)S(1)}, bf16[2304,128]{1,0:T(8,128)(2,1)S(1)}, u32[]{:S(2)}, u32[]{:S(2)}) collective-permute-start(bf16[2304,128]{1,0:T(8,128)(2,1)S(1)} %reshape.85), channel_id=1, source_target_pairs={{1,0},{0,1},{3,2},{2,3},{5,4},{4,5},{7,6},{6,7},{9,8},{8,9},{11,10... | collective-permute-start | bytes 1769480 | tf_op jit(solution)/shard_map/ppermute | solution.py:376

commit v4 on v3

v4 whole, which is shorter than its diff:
```python
import functools

import jax
import jax.numpy as jnp
import numpy as np
from jax import lax
from jax.experimental import pallas as pl
from jax.experimental.pallas import tpu as pltpu
from jax.sharding import Mesh, PartitionSpec as P

HEADS = 4
HD = 64
C = 256
SHARE = 8
EPS = 1e-05
F32 = jnp.float32
BF16 = jnp.bfloat16
VMEM_LIMIT = 50 * 2**20
HBM = pl.BlockSpec(memory_space=pltpu.HBM)
ZXC = ("z", "x", "c")
ALL = ("y", "z", "x", "c")

CELLS_IN = 192
STRIP = 672
KEY_BLOCK = 512
FINE_ROWS = 34
WIN = FINE_ROWS * 16


def upsample_matrix():
    def line(f):
        i = f // 2
        return {i: 0.75, (i - 1 if f % 2 == 0 else i + 1): 0.25}

    table = np.zeros((3, FINE_ROWS, 16, CELLS_IN), np.float32)
    for b in range(3):
        for fr in range(FINE_ROWS):
            for j in range(16):
                for r, wr in line(fr - 1).items():
                    for c, wc in line(j + b - 1).items():
                        table[b, fr, j, (r + 1) * 10 + c + 1] += wr * wc
    return table.reshape(3 * WIN, CELLS_IN)


UPSAMPLE = upsample_matrix()


def params(grid=None):
    return pltpu.CompilerParams(
        vmem_limit_bytes=VMEM_LIMIT,
        dimension_semantics=None if grid is None else ("arbitrary",) * grid,
    )


def in_hbm(value):
    return pltpu.with_memory_space_constraint(value, pltpu.HBM)


def dot(a, b, contract=((1,), (0,))):
    return lax.dot_general(a, b, (contract, ((), ())), preferred_element_type=F32)


def dot_exact(a, b):
    size = a.shape[0]
    parts = jnp.concatenate([p.astype(F32) for p in split3(a)], axis=0).astype(BF16)
    result = dot(parts, b.astype(BF16))
    return result[:size] + result[size : 2 * size] + result[2 * size :]


def iota(shape, dim):
    return lax.broadcasted_iota(jnp.int32, shape, dim)


def split3(value):
    high = value.astype(BF16)
    rest = value - high.astype(F32)
    middle = rest.astype(BF16)
    low = (rest - middle.astype(F32)).astype(BF16)
    return high, middle, low


def group_row(mean_c, var_c):
    same = jnp.where((iota((C, C), 0) >> 3) == (iota((C, C), 1) >> 3), 1.0 / SHARE, 0.0)
    mean8 = jnp.broadcast_to(mean_c, (8, C))
    spread = mean8 - dot_exact(mean8, same)
    var8 = jnp.broadcast_to(var_c, (8, C)) + spread * spread
    to_group = jnp.where(iota((C, 128), 1) == (iota((C, 128), 0) >> 3), 1.0 / SHARE, 0.0)
    both = dot_exact(jnp.concatenate([mean8, var8], axis=0), to_group)
    return both[:8] + pltpu.roll(both[8:], 32, 1)


def combine_groups(rows):
    count = rows.shape[0]
    mean = jnp.sum(rows, axis=0, keepdims=True) / count
    off = rows - mean
    scatter = jnp.sum(off * off, axis=0, keepdims=True) / count
    mean8 = jnp.broadcast_to(mean, (8, 128))
    var8 = pltpu.roll(mean8, 96, 1) + scatter
    from_group = jnp.where(iota((128, C), 0) == (iota((128, C), 1) >> 3), 1.0, 0.0)
    both = dot_exact(jnp.concatenate([mean8, var8], axis=0), from_group)
    return both[:1], lax.rsqrt(both[8:9] + EPS)


def channel_stats(value):
    count = value.shape[0]
    mean = jnp.sum(value, axis=0, keepdims=True) / count
    off = value - mean
    return mean, jnp.sum(off * off, axis=0, keepdims=True) / count


def stats_kernel(mine, other, wide, edges, next_out, last_out, far_out):
    parts = [r[...].astype(F32) for r in (mine, other)]
    count = 2 * parts[0].shape[0]
    mean = sum(jnp.sum(p, axis=0, keepdims=True) for p in parts) / count
    var = 0.0
    for part in parts:
        off = part - mean
        var = var + jnp.sum(off * off, axis=0, keepdims=True)
    high, middle, low = [p.astype(F32) for p in split3(group_row(mean, var / count))]
    packed = jnp.concatenate(
        [
            jnp.concatenate([high, middle], axis=1),
            jnp.concatenate([low, jnp.zeros_like(low)], axis=1),
        ],
        axis=0,
    ).astype(BF16)
    for out in (next_out, last_out, far_out):
        out[:16, :] = packed
        out[16:176, :] = wide[...]
    next_out[176:, :] = edges[0]
    last_out[176:, :] = edges[1]


def stats_and_rows(mine, other, wide, edges):
    return pl.pallas_call(
        stats_kernel,
        out_shape=(
            jax.ShapeDtypeStruct((208, C), BF16),
            jax.ShapeDtypeStruct((208, C), BF16),
            jax.ShapeDtypeStruct((176, C), BF16),
        ),
        compiler_params=params(),
    )(mine, other, wide, edges)


def attention_kernel(
    order,
    mine,
    other,
    near,
    far,
    down,
    up,
    gain,
    bias,
    w_far,
    out_far,
    block_far,
    keys,
    values,
    strip,
    w_qkv,
    out,
    block,
    w_sem,
    block_sem,
    out_sems,
):
    load = pltpu.make_async_copy(w_far, w_qkv, w_sem)
    load.start()
    rows = []
    for ref in (near, down, far, up):
        packed = ref[:16, :].astype(F32)
        rows.append(packed[:8, :128] + packed[:8, 128:] + packed[8:, :128])
    mean, inverse = combine_groups(jnp.concatenate(rows, axis=0))

    def norm(cells):
        normed = (cells.astype(F32) - mean) * inverse
        return (normed * gain[...] + bias[...]).astype(BF16)

    for i, ref in enumerate((near, down, far, up)):
        cells = ref[16:176, :].astype(F32)
        strip[10 + 160 * i : 170 + 160 * i, :] = cells
        if i == 0:
            strip[650:660, :] = cells[:10]
        if i == 3:
            strip[:10, :] = cells[150:]
    strip[660:, :] = jnp.zeros((STRIP - 660, C), F32)
    block[...] = strip[:CELLS_IN, :].astype(BF16)
    keep = pltpu.make_async_copy(block, block_far, block_sem)
    keep.start()
    load.wait()

    head_of = iota((512, C), 1) >> 6
    for i in range(8):
        rows = slice(512 * i, 512 * i + 512)
        cells = (mine, other)[i // 4][512 * (i % 4) : 512 * (i % 4) + 512, :]
        both = dot(norm(cells), w_qkv[:, C:])
        keys[rows, :] = both[:, :C].astype(BF16)
        for head in range(HEADS):
            values[head, rows, :] = jnp.where(head_of == head, both[:, C:], 1.0).astype(BF16)

    scale = HD**-0.5 * float(np.log2(np.e))
    queries = (dot(norm(strip[...]), w_qkv[:, :C]) * scale).astype(BF16)
    head_of = iota((STRIP, C), 1) >> 6
    lane = iota((STRIP, 128), 1)
    result = jnp.zeros((STRIP, C), F32)
    packed = jnp.zeros((STRIP, 128), F32)
    for head in range(HEADS):
        own = head_of == head
        masked = jnp.where(own, queries, jnp.zeros_like(queries))
        best, mixed = None, None
        for i in range(4096 // KEY_BLOCK):
            rows = slice(KEY_BLOCK * i, KEY_BLOCK * (i + 1))
            scores = dot(masked, keys[rows, :], ((1,), (1,)))
            top = jnp.max(scores, axis=1, keepdims=True)
            fresh = top if i == 0 else jnp.maximum(best, top)
            product = dot(jnp.exp2(scores - fresh).astype(BF16), values[head, rows, :])
            mixed = product if i == 0 else mixed * jnp.exp2(best - fresh) + product
            best = fresh
        result = jnp.where(own, mixed / pltpu.roll(mixed, HD, 1), result)
        spot = 0 if head else 128
        log = best + jnp.log2(mixed[:, spot : spot + 128])
        for part, value in enumerate(split3(log)):
            packed = jnp.where(lane == 4 * part + head, value.astype(F32), packed)
    result = result.astype(BF16)
    copies = []
    for step in range(4):
        rows = slice(160 * step, 160 * step + CELLS_IN)
        out[step, :CELLS_IN, :] = result[rows]
        turned = jnp.concatenate([packed[rows], jnp.zeros((64, 128), F32)], axis=0).T[:16]
        out[step, CELLS_IN:, :] = turned.astype(BF16)
        copy = pltpu.make_async_copy(out.at[step], out_far.at[order[step]], out_sems.at[step])
        copy.start()
        copies.append(copy)
    keep.wait()
    for copy in copies:
        copy.wait()


def partial_attention(order, mine, other, near, far, down, up, gain, bias, w_qkv):
    vmem = pl.BlockSpec(memory_space=pltpu.VMEM)
    return pl.pallas_call(
        attention_kernel,
        out_shape=(
            pltpu.HBM((4, CELLS_IN + 16, C), BF16),
            pltpu.HBM((CELLS_IN, C), BF16),
        ),
        in_specs=[pl.BlockSpec(memory_space=pltpu.SMEM)] + [vmem] * 8 + [HBM],
        out_specs=(HBM, HBM),
        scratch_shapes=[
            pltpu.VMEM((4096, C), BF16),
            pltpu.VMEM((HEADS, 4096, C), BF16),
            pltpu.VMEM((STRIP, C), F32),
            pltpu.VMEM((C, 3 * C), BF16),
            pltpu.VMEM((4, CELLS_IN + 16, C), BF16),
            pltpu.VMEM((CELLS_IN, C), BF16),
            pltpu.SemaphoreType.DMA,
            pltpu.SemaphoreType.DMA,
            pltpu.SemaphoreType.DMA((4,)),
        ],
        compiler_params=params(),
    )(order, mine, other, near, far, down, up, gain, bias, in_hbm(w_qkv))


def merge_kernel(
    flags, parts, coarse_far, w_far, up, merged_out, stats_out, coarse, w_proj, coarse_sem, w_sem
):
    loads = [
        pltpu.make_async_copy(coarse_far, coarse, coarse_sem),
        pltpu.make_async_copy(w_far, w_proj, w_sem),
    ]
    for load in loads:
        load.start()
    count = parts.shape[0]
    logs = []
    for i in range(count):
        tail = parts[i, CELLS_IN:, :].astype(F32)
        logs.append(tail[0:4] + tail[4:8] + tail[8:12])
    top = functools.reduce(jnp.maximum, logs)
    shares = [jnp.exp2(v - top) for v in logs]
    total = sum(shares)
    spread = jnp.where((iota((16, C), 1) >> 6) == (iota((16, C), 0) & 3), 1.0, 0.0).astype(BF16)
    attended = jnp.zeros((CELLS_IN, C), F32)
    for i in range(count):
        pieces = [p.astype(F32) for p in split3((shares[i] / total)[:, :CELLS_IN])]
        pieces.append(jnp.zeros_like(pieces[0]))
        wide = dot(jnp.concatenate(pieces, axis=0).astype(BF16), spread, ((0,), (0,)))
        attended = attended + wide * parts[i, :CELLS_IN, :].astype(F32)
    for load in loads:
        load.wait()
    merged = coarse[...].astype(F32) + dot(attended.astype(BF16), w_proj[...])
    cell = iota((CELLS_IN, C), 0)
    col = lax.rem(cell, 10)
    outside = (
        ((cell < 10) & (flags[0] == 1))
        | ((cell >= 170) & (flags[1] == 1))
        | ((col == 0) & (flags[2] == 1))
        | ((col == 9) & (flags[3] == 1))
        | (cell >= 180)
    )
    merged = jnp.where(outside, 0.0, merged).astype(BF16)
    merged_out[...] = merged
    field = dot(up[WIN + 16 : WIN + 528, :], merged)
    mean, var = channel_stats(field)
    stats_out[...] = jnp.broadcast_to(group_row(mean, var)[:1], stats_out.shape)


def merge(flags, parts, coarse, w_proj, up):
    vmem = pl.BlockSpec(memory_space=pltpu.VMEM)
    return pl.pallas_call(
        merge_kernel,
        out_shape=(
            jax.ShapeDtypeStruct((CELLS_IN, C), BF16),
            jax.ShapeDtypeStruct((128, 128), F32),
        ),
        in_specs=[pl.BlockSpec(memory_space=pltpu.SMEM), vmem, HBM, HBM, vmem],
        out_specs=(vmem, vmem),
        scratch_shapes=[
            pltpu.VMEM((CELLS_IN, C), BF16),
            pltpu.VMEM((C, C), BF16),
            pltpu.SemaphoreType.DMA,
            pltpu.SemaphoreType.DMA,
        ],
        compiler_params=params(),
    )(flags, parts, in_hbm(coarse), in_hbm(w_proj), up)


def back_kernel(c0, c1, c2, weight, out):
    windows = (c0, c1, c2)
    total = jnp.zeros((512, C), F32)
    for a in range(3):
        for b in range(3):
            window = windows[2 - b][16 * (2 - a) : 16 * (2 - a) + 512, :]
            total = total + dot(window, weight[3 * a + b], ((1,), (1,)))
    out[...] = total


def back_conv(windows, weight):
    return pl.pallas_call(
        back_kernel,
        out_shape=jax.ShapeDtypeStruct((512, C), F32),
        compiler_params=params(),
        cost_estimate=pl.CostEstimate(
            flops=9 * 2 * 512 * C * C, bytes_accessed=3 * 10**6, transcendentals=0
        ),
    )(*windows, weight)


def hidden_kernel(
    flags,
    merged,
    up,
    stats,
    gain,
    bias,
    cot,
    grad_hidden,
    kept,
    given,
    hidden_far,
    hidden,
    sem,
):
    mean, inverse = combine_groups(stats[...])
    row = iota((WIN, C), 0)
    col = row & 15
    for b in range(3):
        field = dot(up[b * WIN : (b + 1) * WIN, :], merged[...])
        xhat = (field - mean) * inverse
        shifted = xhat * gain[...] + bias[...]
        sig = 0.5 * jnp.tanh(0.5 * shifted) + 0.5
        outside = ((row < 16) & (flags[0] == 1)) | ((row >= 528) & (flags[1] == 1))
        if b == 0:
            outside = outside | ((col == 0) & (flags[2] == 1))
        if b == 2:
            outside = outside | ((col == 15) & (flags[3] == 1))
        hidden[b] = jnp.where(outside, 0.0, shifted * sig).astype(BF16)
        if b == 1:
            inner = slice(16, 528)
            s, t = sig[inner], shifted[inner]
            grad_shift = grad_hidden[...] * s * (1.0 + t * (1.0 - s))
            sum_w = jnp.sum(grad_shift * xhat[inner], axis=0, keepdims=True)
            sum_b = jnp.sum(grad_shift, axis=0, keepdims=True)
            rows = []
            for part in range(3):
                for value in (sum_w, sum_b):
                    piece = split3(value)[part].astype(F32)
                    rows += [piece[:, :128], piece[:, 128:]]
            tail = jnp.concatenate(rows + [jnp.zeros((4, 128), F32)], axis=0).astype(BF16)
            kept[2304:, :] = tail
            given[2304:, :] = tail
    keep = pltpu.make_async_copy(hidden, hidden_far, sem)
    keep.start()
    first = flags[4] == 0
    for a in range(3):
        for b in range(3):
            rows = slice((3 * a + b) * C, (3 * a + b + 1) * C)
            product = dot(hidden[b, 16 * a : 16 * a + 512, :], cot[...], ((0,), (0,)))
            left, right = product[:, :128].astype(BF16), product[:, 128:].astype(BF16)
            kept[rows, :] = jnp.where(first, left, right)
            given[rows, :] = jnp.where(first, right, left)
    keep.wait()


def hidden_and_kernel_gradient(flags, merged, up, stats, gain, bias, cot, grad_hidden):
    vmem = pl.BlockSpec(memory_space=pltpu.VMEM)
    return pl.pallas_call(
        hidden_kernel,
        out_shape=(
            jax.ShapeDtypeStruct((2320, 128), BF16),
            jax.ShapeDtypeStruct((2320, 128), BF16),
            pltpu.HBM((3, WIN, C), BF16),
        ),
        in_specs=[pl.BlockSpec(memory_space=pltpu.SMEM)] + [vmem] * 7,
        out_specs=(vmem, vmem, HBM),
        scratch_shapes=[pltpu.VMEM((3, WIN, C), BF16), pltpu.SemaphoreType.DMA],
        compiler_params=params(),
    )(flags, merged, up, stats, gain, bias, cot, grad_hidden)


def conv_kernel(hidden, weight, conv_bias, fine_out):
    total = jnp.zeros((512, C), F32) + conv_bias[...]
    for a in range(3):
        for b in range(3):
            total = total + dot(hidden[b, 16 * a : 16 * a + 512, :], weight[3 * a + b])
    fine_out[...] = total.astype(BF16)


def conv(hidden, weight, conv_bias):
    return pl.pallas_call(
        conv_kernel,
        out_shape=jax.ShapeDtypeStruct((512, C), BF16),
        compiler_params=params(),
        cost_estimate=pl.CostEstimate(
            flops=9 * 2 * 512 * C * C, bytes_accessed=3 * 10**6, transcendentals=0
        ),
    )(hidden, weight, conv_bias)


def pair_kernel(kept, got, out_far, total, out, sems):
    total[...] = kept[...].astype(F32) + got[...].astype(F32)
    tails = [r[2304:, :].astype(F32) for r in (kept, got)]
    sums = sum(t[0:4] + t[4:8] + t[8:12] for t in tails)
    parts = [p.astype(F32) for p in split3(sums)]
    tail = jnp.concatenate([jnp.zeros((36, 128), F32)] + parts, axis=0)
    own = iota((48, 128), 0) < 36
    copies = []
    for i in range(64):
        out[i] = jnp.where(own, total[36 * i : 36 * i + 48, :], tail).astype(BF16)
        if i % 16 == 15:
            part = pl.ds(i - 15, 16)
            copies.append(pltpu.make_async_copy(out.at[part], out_far.at[part], sems.at[i // 16]))
            copies[-1].start()
    for copy in copies:
        copy.wait()


def pair_sum(kept, got):
    return pl.pallas_call(
        pair_kernel,
        out_shape=pltpu.HBM((64, 48, 128), BF16),
        out_specs=HBM,
        scratch_shapes=[
            pltpu.VMEM((2320, 128), F32),
            pltpu.VMEM((64, 48, 128), BF16),
            pltpu.SemaphoreType.DMA((4,)),
        ],
        compiler_params=params(),
    )(kept, got)


def share_kernel(got, out_far, sums, chunk, sems):
    total = jnp.sum(got[...].astype(F32), axis=0)
    chunk[...] = jnp.broadcast_to((total[:40] * (1.0 / 256.0)).astype(BF16)[None], chunk.shape)
    size = chunk.shape[0]
    copies = [
        pltpu.make_async_copy(chunk, out_far.at[pl.ds(size * i, size)], sems.at[i])
        for i in range(out_far.shape[0] // size)
    ]
    for copy in copies:
        copy.start()
    quarters = total[36:40] + total[40:44] + total[44:48]
    weight = jnp.concatenate([quarters[0:1], quarters[1:2]], axis=1)
    shift_sum = jnp.concatenate([quarters[2:3], quarters[3:4]], axis=1)
    sums[...] = jnp.concatenate([weight, shift_sum, jnp.zeros((6, C), F32)], axis=0)
    for copy in copies:
        copy.wait()


def share_sum(got):
    vmem = pl.BlockSpec(memory_space=pltpu.VMEM)
    return pl.pallas_call(
        share_kernel,
        out_shape=(pltpu.HBM((64, 40, 128), BF16), jax.ShapeDtypeStruct((8, C), F32)),
        in_specs=[vmem],
        out_specs=(HBM, vmem),
        scratch_shapes=[pltpu.VMEM((16, 40, 128), BF16), pltpu.SemaphoreType.DMA((4,))],
        compiler_params=params(),
    )(got)


def field_kernel(merged, up, stats, gain, bias, grad_hidden, sums, field_out, norm_out):
    mean, inverse = combine_groups(stats[...])
    value = dot(up[WIN + 16 : WIN + 528, :], merged[...])
    xhat = (value - mean) * inverse
    shifted = xhat * gain[...] + bias[...]
    sig = 0.5 * jnp.tanh(0.5 * shifted) + 0.5
    grad_shift = grad_hidden[...] * sig * (1.0 + shifted * (1.0 - sig))
    same = jnp.where((iota((C, C), 0) >> 3) == (iota((C, C), 1) >> 3), 1.0, 0.0)
    means = dot_exact(sums[...] * gain[...], same) * (1.0 / (65536 * SHARE))
    field = inverse * (grad_shift * gain[...] - means[1:2] - xhat * means[0:1])
    field_out[...] = field.astype(BF16)
    norm_out[...] = sums[:2] * (1.0 / 256.0)


def field_gradient(merged, up, stats, gain, bias, grad_hidden, sums):
    return pl.pallas_call(
        field_kernel,
        out_shape=(
            jax.ShapeDtypeStruct((512, C), BF16),
            jax.ShapeDtypeStruct((2, C), F32),
        ),
        compiler_params=params(),
        cost_estimate=pl.CostEstimate(
            flops=10**9, bytes_accessed=2 * 10**6, transcendentals=2 * 10**5
        ),
    )(merged, up, stats, gain, bias, grad_hidden, sums)


def layout_kernel(flags, mine, other, out_far, out, sems):
    first = flags[4] == 0
    copies = []
    for i in range(0, 64, 2):
        halves = []
        for ref in (mine, other):
            pair = [ref[i + k].astype(F32)[:36] for k in range(2)]
            halves.append(jnp.concatenate(pair, axis=0))
        rows = slice(36 * i, 36 * i + 72)
        out[rows, :128] = jnp.where(first, halves[0], halves[1])
        out[rows, 128:] = jnp.where(first, halves[1], halves[0])
        if i % 8 == 6:
            part = pl.ds(36 * (i - 6), 288)
            copies.append(pltpu.make_async_copy(out.at[part], out_far.at[part], sems.at[i // 8]))
            copies[-1].start()
    for copy in copies:
        copy.wait()


def lay_out(flags, mine, other):
    vmem = pl.BlockSpec(memory_space=pltpu.VMEM)
    return pl.pallas_call(
        layout_kernel,
        out_shape=pltpu.HBM((2304, C), F32),
        in_specs=[pl.BlockSpec(memory_space=pltpu.SMEM), vmem, vmem],
        out_specs=HBM,
        scratch_shapes=[pltpu.VMEM((2304, C), F32), pltpu.SemaphoreType.DMA((8,))],
        compiler_params=params(),
    )(flags, mine, other)


def copies_kernel(cells, out_far, sems):
    copies = [
        pltpu.make_async_copy(cells, out_far.at[i], sems.at[i]) for i in range(out_far.shape[0])
    ]
    for copy in copies:
        copy.start()
    for copy in copies:
        copy.wait()


def copies_of(cells):
    return pl.pallas_call(
        copies_kernel,
        out_shape=pltpu.HBM((16, 128, C), BF16),
        in_specs=[pl.BlockSpec(memory_space=pltpu.VMEM)],
        out_specs=HBM,
        scratch_shapes=[pltpu.SemaphoreType.DMA((16,))],
        compiler_params=params(),
    )(cells)


def shift(value, axis, count, step):
    return lax.ppermute(value, axis, [((i + step) % count, i) for i in range(count)])


def per_device(
    coarse,
    norm1_gain,
    norm1_bias,
    w_qkv,
    w_proj,
    second_norm2_gain,
    second_norm2_bias,
    conv_weight,
    conv_bias,
    cotangent,
):
    y, c = lax.axis_index("y"), lax.axis_index("c")
    block = lax.axis_index(ZXC)
    flags = jnp.stack([y == 0, y == 3, block == 0, block == 31, c == 1]).astype(jnp.int32)
    up = jnp.asarray(UPSAMPLE, BF16)
    taps = conv_weight.reshape(9, C, C)

    own = coarse.reshape(128, C)
    cells = lax.all_to_all(copies_of(own), ("z", "x"), 0, 0, tiled=True).reshape(2048, C)


    first = jnp.concatenate([coarse[:, 0], cotangent[:, 0]], axis=0)
    last = jnp.concatenate([coarse[:, -1], cotangent[:, -1]], axis=0)
    before = lax.ppermute(last, ZXC, [(i, i + 1) for i in range(31)])[:, None]
    after = lax.ppermute(first, ZXC, [(i + 1, i) for i in range(31)])[:, None]
    wide = jnp.concatenate([before[:16], coarse, after[:16]], axis=1).reshape(160, C)
    grad = jnp.concatenate([before[16:], cotangent, after[16:]], axis=1)
    edges = jnp.pad(jnp.stack([grad[0], grad[-1]]), ((0, 0), (0, 14), (0, 0)))
    other = shift(cells, "c", 2, 1)

    near, last, far = stats_and_rows(cells, other, wide, edges)
    below, above, far = (
        shift(near, "y", 4, 1),
        shift(last, "y", 4, 3),
        shift(far, "y", 4, 2),
    )
    top = jnp.where(y == 0, 0, above[176:194])[None].astype(BF16)
    bottom = jnp.where(y == 3, 0, below[176:194])[None].astype(BF16)
    grad = jnp.concatenate([top, grad, bottom], axis=0)
    windows = [grad[:, b : b + 16].reshape(WIN, C) for b in range(3)]
    order = jnp.stack([(y + k) % 4 for k in range(4)]).astype(jnp.int32)

    partial, block = partial_attention(
        order, cells, other, near, far, below, above, norm1_gain[None], norm1_bias[None], w_qkv
    )
    partial = lax.all_to_all(partial, "y", 0, 0, tiled=True)
    merged, stats2 = merge(flags, partial, block, w_proj, up)
    stats2 = lax.all_to_all(stats2.reshape(128, 1, 128), ALL, 0, 0, tiled=True)
    stats2 = stats2.reshape(128, 128)
    grad_hidden = back_conv(windows, taps)
    gain2, bias2 = second_norm2_gain[None], second_norm2_bias[None]
    kept, given, hidden = hidden_and_kernel_gradient(
        flags, merged, up, stats2, gain2, bias2, cotangent.reshape(512, C), grad_hidden
    )

    sent = pair_sum(kept, shift(given, "c", 2, 1))
    got = lax.all_to_all(sent, ("y", "z", "x"), 0, 0, tiled=True)
    fine = conv(hidden, taps, conv_bias[None])
    got, fine = lax.optimization_barrier((got, fine))

    chunk, sums = share_sum(got)
    spread = lax.all_to_all(chunk, ("y", "z", "x"), 0, 0, tiled=True)
    field, grad_norm = field_gradient(merged, up, stats2, gain2, bias2, grad_hidden, sums)
    spread, field = lax.optimization_barrier((spread, field))
    grad_conv = lay_out(flags, spread, shift(spread, "c", 2, 1)).reshape(3, 3, C, C)
    return (
        fine.reshape(32, 16, C),
        field.reshape(32, 16, C),
        grad_conv,
        grad_norm,
    )


def solution(mesh):
    split = Mesh(mesh.devices.reshape(4, 4, 4, 2), ALL)
    cells = P("y", ZXC, None)
    return jax.shard_map(
        per_device,
        mesh=split,
        in_specs=(cells,) + (P(),) * 8 + (cells,),
        out_specs=(cells, cells, P(), P()),
        check_vma=False,
    )
```

time: 151 us -> 141 us (0.934)
  blocking collectives: 19.9 us -> 0 us
  waiting for transfers between devices: 36.5 us -> 53.4 us
  local copies, waits for them, and re-layouts: 14.5 us -> 4.14 us
  Pallas kernels: 27 us -> 33.7 us
  other arithmetic: 6.68 us -> 1.17 us
  starting transfers between devices: 45 us -> 47.1 us
    all_to_all x1 -> x0, blocking collectives: 19.9 us -> none  [per_device(): got = lax.all_to_all(sent, ('y', 'z', 'x'), 0, 0, tiled=True)]
    all_to_all x2 -> x3, waiting for transfers between devices: 16.3 us -> 33.2 us  [the longest x1 12.5 us: per_device(): got = lax.all_to_all(sent, ('y', 'z', 'x'), 0, 0, tiled=True)]
    pallas_call x3 -> x7, Pallas kernels: 18.6 us -> 25.9 us  [the longest x1 18.1 us: partial_attention(): pl.pallas_call(attention_kernel, out_shape=(pltpu.HBM((4, CELLS_IN + 16,...]
    broadcast_in_dim x6 -> x0, local copies, waits for them, and re-layouts: 3.16 us -> none  [the longest x1 1.91 us: per_device(): jnp.broadcast_to(own[None], (16, 128, C))]
    all_to_all x2 -> x3, starting transfers between devices: 14.8 us -> 18 us  [the longest x1 8.44 us: per_device(): lax.all_to_all(copies_of(own), ('z', 'x'), 0, 0, tiled=True)]
    unnamed x42 -> x34, local copies, waits for them, and re-layouts: 4.94 us -> 2.16 us
    convert_element_type x3 -> x0, other arithmetic: 2.38 us -> none  [the longest x1 1.57 us: per_device(): jnp.concatenate([left, right], axis=1).astype(F32).reshape(3, 3, C, C)]
    slice x2, local copies, waits for them, and re-layouts: 2.02 us -> 0.08 us  [per_device(): last = jnp.concatenate([coarse[:, -1], cotangent[:, -1]], axis=0)]
  transfers between devices with their start and end apart: 15 -> 13, of which waited for: 8 -> 9; matrix products, arithmetic and copies ran while one was open for 7% -> 2% of each run, Pallas kernels for 2% -> 3%
where the time goes in v4:
time: 141 us
  waiting for transfers between devices  53.4 us (38%)
  starting transfers between devices  47.1 us (33%)
  Pallas kernels  33.7 us (24%)
  local copies, waits for them, and re-layouts  4.14 us (3%)
    pallas_call x1, Pallas kernels, partial_attention(): pl.pallas_call(attention_kernel, out_shape=(pltpu.HBM((4, CELLS_IN + 16,...  18.1 us
    all_to_all x1, waiting for transfers between devices, per_device(): got = lax.all_to_all(sent, ('y', 'z', 'x'), 0, 0, tiled=True)  12.5 us
    ppermute x6, starting transfers between devices, shift(): lax.ppermute(value, axis, [((i + step) % count, i) for i in range(count)])  12.1 us
    all_to_all x1, waiting for transfers between devices, per_device(): spread = lax.all_to_all(chunk, ('y', 'z', 'x'), 0, 0, tiled=True)  11.5 us
    all_to_all x1, waiting for transfers between devices, per_device(): lax.all_to_all(copies_of(own), ('z', 'x'), 0, 0, tiled=True)  9.25 us
    all_to_all x1, starting transfers between devices, per_device(): lax.all_to_all(copies_of(own), ('z', 'x'), 0, 0, tiled=True)  8.44 us
    ppermute x6, waiting for transfers between devices, shift(): lax.ppermute(value, axis, [((i + step) % count, i) for i in range(count)])  7.66 us
    all_to_all x1, waiting for transfers between devices, per_device(): stats2 = lax.all_to_all(stats2.reshape(128, 1, 128), ALL, 0, 0, tiled=True)  7.07 us
  transfers between devices with their start and end apart: 13, of which 9 were waited for; matrix products, arithmetic and copies ran while one was open for 2% of the time, Pallas kernels for 3%

profile of v4, /device:TPU:1, one launch (start us, length us, event | category | flops | bytes accessed | tf_op | source)
XLA Modules:
  0.0 140.8 jit_solution(15198926361011524443)
XLA Ops:
  0.7 0.9 copy-done.6
  1.5 1.1 shard_map.138
  2.6 8.4 %all-to-all-start = ((bf16[16,128,256]{2,1,0:T(8,128)(2,1)}), bf16[16,128,256]{2,1,0:T(8,128)(2,1)S(1)}, u32[]{:S(2)}, u32[]{:S(2)}) async-start(bf16[16,128,256]{2,1,0:T(8,128)(2,1)} %shard_map.138), calls=%async_computation | async-start | bytes 2097152 | tf_op jit(solution)/shard_map/all_to_all | solution.py:606
  11.1 0.0 copy-start.10
  11.1 0.0 copy-start.11
  11.2 0.1 fusion.14
  11.2 2.9 %collective-permute-start.2 = (bf16[48,256]{1,0:T(8,128)(2,1)S(1)}, bf16[48,256]{1,0:T(8,128)(2,1)S(1)}, u32[]{:S(2)}, u32[]{:S(2)}) collective-permute-start(bf16[48,256]{1,0:T(8,128)(2,1)S(1)} %pad_maximum_fusion.3), channel_id=1, source_target_pairs={{1,0},{2,1},{3,2},{4,3},{5,4},{6,5},{7,6},{8,7},{9,8},{10,9},{11,1... | collective-permute-start | bytes 73736 | tf_op jit(solution)/shard_map/ppermute | solution.py:612
  14.2 3.4 %collective-permute-start.1 = (bf16[48,256]{1,0:T(8,128)(2,1)S(1)}, bf16[48,256]{1,0:T(8,128)(2,1)S(1)}, u32[]{:S(2)}, u32[]{:S(2)}) collective-permute-start(bf16[48,256]{1,0:T(8,128)(2,1)S(1)} %pad_maximum_fusion.2), channel_id=1, source_target_pairs={{0,1},{1,2},{2,3},{3,4},{4,5},{5,6},{6,7},{7,8},{8,9},{9,10},{10,1... | collective-permute-start | bytes 73736 | tf_op jit(solution)/shard_map/ppermute | solution.py:611
  17.7 0.1 stack.41
  17.8 9.3 %all-to-all-done = bf16[16,128,256]{2,1,0:T(8,128)(2,1)S(1)} async-done(((bf16[16,128,256]{2,1,0:T(8,128)(2,1)}), bf16[16,128,256]{2,1,0:T(8,128)(2,1)S(1)}, u32[]{:S(2)}, u32[]{:S(2)}) %all-to-all-start) | async-done | bytes 1048608 | tf_op jit(solution)/shard_map/all_to_all | solution.py:606
  27.1 2.6 %collective-permute-start = (bf16[2048,256]{1,0:T(8,128)(2,1)S(1)}, bf16[2048,256]{1,0:T(8,128)(2,1)S(1)}, u32[]{:S(2)}, u32[]{:S(2)}) collective-permute-start(bf16[2048,256]{1,0:T(8,128)(2,1)S(1)} %bitcast.52), channel_id=1, source_target_pairs={{1,0},{0,1},{3,2},{2,3},{5,4},{4,5},{7,6},{6,7},{9,8},{8,9},{11,10... | collective-permute-start | bytes 3145736 | tf_op jit(solution)/shard_map/ppermute | solution.py:584
  29.8 0.1 pad_maximum_fusion.1
  30.0 2.0 %collective-permute-done.other = bf16[2048,256]{1,0:T(8,128)(2,1)S(1)} collective-permute-done((bf16[2048,256]{1,0:T(8,128)(2,1)S(1)}, bf16[2048,256]{1,0:T(8,128)(2,1)S(1)}, u32[]{:S(2)}, u32[]{:S(2)}) %collective-permute-start) | collective-permute-done | bytes 1048608 | tf_op jit(solution)/shard_map/ppermute | solution.py:584
  32.0 1.3 shard_map.139
  33.2 3.0 %collective-permute-start.3 = (bf16[176,256]{1,0:T(8,128)(2,1)S(1)}, bf16[176,256]{1,0:T(8,128)(2,1)S(1)}, u32[]{:S(2)}, u32[]{:S(2)}) collective-permute-start(bf16[176,256]{1,0:T(8,128)(2,1)S(1)} %get-tuple-element.23), channel_id=1, source_target_pairs={{64,0},{96,32},{0,64},{32,96},{65,1},{97,33},{1,65},{33,97},{66,2}... | collective-permute-start | bytes 270344 | tf_op jit(solution)/shard_map/ppermute | solution.py:584
  36.2 0.4 collective-permute-start.5
  36.6 2.3 %collective-permute-start.4 = (bf16[208,256]{1,0:T(8,128)(2,1)S(1)}, bf16[208,256]{1,0:T(8,128)(2,1)S(1)}, u32[]{:S(2)}, u32[]{:S(2)}) collective-permute-start(bf16[208,256]{1,0:T(8,128)(2,1)S(1)} %get-tuple-element.22.near), channel_id=1, source_target_pairs={{32,0},{64,32},{96,64},{0,96},{33,1},{65,33},{97,65},{1,97},{34,2}... | collective-permute-start | bytes 319496 | tf_op jit(solution)/shard_map/ppermute | solution.py:584
  38.9 0.1 pad_add_fusion.order
  38.9 2.3 %collective-permute-done.5.up = bf16[208,256]{1,0:T(8,128)(2,1)S(1)} collective-permute-done((bf16[208,256]{1,0:T(8,128)(2,1)S(1)}, bf16[208,256]{1,0:T(8,128)(2,1)S(1)}, u32[]{:S(2)}, u32[]{:S(2)}) %collective-permute-start.5) | collective-permute-done | bytes 106528 | tf_op jit(solution)/shard_map/ppermute | solution.py:584
  41.3 18.1 %shard_map.140 = (bf16[4,208,256]{2,1,0:T(8,128)(2,1)}, bf16[192,256]{1,0:T(8,128)(2,1)}) custom-call(s32[4]{0:T(128)S(1)} %pad_add_fusion.order, bf16[2048,256]{1,0:T(8,128)(2,1)S(1)} %bitcast.54, bf16[2048,256]{1,0:T(8,128)(2,1)S(1)} %collective-permute-done.other, bf16[208,256]{1,0:T(8,128)(2,1)S(1)} %get-tuple-element.22.near, ...), custom_call_target="tpu_custom_call" | custom-call | tf_op jit(solution)/shard_map/pallas_call | solution.py:243
  59.3 0.0 copy-start
  59.3 3.8 %all-to-all-start.1 = ((bf16[4,208,256]{2,1,0:T(8,128)(2,1)}), bf16[4,208,256]{2,1,0:T(8,128)(2,1)S(1)}, u32[]{:S(2)}, u32[]{:S(2)}) async-start(bf16[4,208,256]{2,1,0:T(8,128)(2,1)} %get-tuple-element.25), calls=%async_computation.1 | async-start | bytes 851968 | tf_op jit(solution)/shard_map/all_to_all | solution.py:633
  63.1 1.0 pad_maximum_fusion
  64.1 5.4 %all-to-all-done.1.parts = bf16[4,208,256]{2,1,0:T(8,128)(2,1)S(1)} async-done(((bf16[4,208,256]{2,1,0:T(8,128)(2,1)}), bf16[4,208,256]{2,1,0:T(8,128)(2,1)S(1)}, u32[]{:S(2)}, u32[]{:S(2)}) %all-to-all-start.1) | async-done | bytes 426016 | tf_op jit(solution)/shard_map/all_to_all | solution.py:633
  69.5 2.9 %shard_map.141 = (bf16[192,256]{1,0:T(8,128)(2,1)S(1)}, f32[128,128]{1,0:T(8,128)}) custom-call(s32[5]{0:T(128)S(1)} %convert_element_type.8.flags, bf16[4,208,256]{2,1,0:T(8,128)(2,1)S(1)} %all-to-all-done.1.parts, bf16[192,256]{1,0:T(8,128)(2,1)} %get-tuple-element.26.coarse_far, bf16[256,256]{1,0:T(8,128)(2,1)} %w_far.3, bf16[1632,192]{1,0:T(8,128)(2,1)S(1)} %copy-done.1), custom_call_target="tpu_custom_call" | custom-call | tf_op jit(solution)/shard_map/pallas_call | solution.py:311
  72.5 0.0 copy-start.13
  72.5 0.0 copy-start.14
  72.5 6.9 %all-to-all-start.2 = ((f32[128,1,128]{2,1,0:T(1,128)}), f32[128,1,128]{2,1,0:T(1,128)S(1)}, u32[]{:S(2)}, u32[]{:S(2)}) async-start(f32[128,1,128]{2,1,0:T(1,128)} %bitcast.22), calls=%async_computation.2 | async-start | bytes 131072 | tf_op jit(solution)/shard_map/all_to_all | solution.py:635
  79.4 1.7 %fusion.13 = (bf16[34,16,256]{2,1,0:T(8,128)(2,1)S(1)}, bf16[34,16,256]{2,1,0:T(8,128)(2,1)S(1)}, bf16[34,16,256]{2,1,0:T(8,128)(2,1)S(1)}) fusion(bf16[34,18,256]{2,1,0:T(8,128)(2,1)} %pad_maximum_fusion), kind=kLoop, calls=%fused_computation.30 | loop fusion | bytes 1671168 | tf_op jit(solution)/shard_map/slice | solution.py:627
  81.1 0.8 shard_map.142.grad_hidden
  81.9 7.1 %all-to-all-done.2 = f32[128,1,128]{2,1,0:T(1,128)S(1)} async-done(((f32[128,1,128]{2,1,0:T(1,128)}), f32[128,1,128]{2,1,0:T(1,128)S(1)}, u32[]{:S(2)}, u32[]{:S(2)}) %all-to-all-start.2) | async-done | bytes 65568 | tf_op jit(solution)/shard_map/all_to_all | solution.py:635
  89.0 0.0 copy-start.12
  89.0 2.5 %shard_map.143 = (bf16[2320,128]{1,0:T(8,128)(2,1)S(1)}, bf16[2320,128]{1,0:T(8,128)(2,1)S(1)}, bf16[3,544,256]{2,1,0:T(8,128)(2,1)}) custom-call(s32[5]{0:T(128)S(1)} %convert_element_type.8.flags, bf16[192,256]{1,0:T(8,128)(2,1)S(1)} %get-tuple-element.27.merged, bf16[1632,192]{1,0:T(8,128)(2,1)S(1)} %copy-done.1, f32[128,128]{1,0:T(8,128)S(1)} %bitcast.62, ...), custom_call_target="tpu_custom_call" | custom-call | tf_op jit(solution)/shard_map/pallas_call | solution.py:408
  91.5 0.9 collective-permute-start.6
  92.5 1.6 %collective-permute-done.6.got = bf16[2320,128]{1,0:T(8,128)(2,1)S(1)} collective-permute-done((bf16[2320,128]{1,0:T(8,128)(2,1)S(1)}, bf16[2320,128]{1,0:T(8,128)(2,1)S(1)}, u32[]{:S(2)}, u32[]{:S(2)}) %collective-permute-start.6) | collective-permute-done | bytes 593952 | tf_op jit(solution)/shard_map/ppermute | solution.py:584
  94.1 1.1 shard_map.144
  95.2 4.9 %all-to-all-start.3 = ((bf16[64,48,128]{2,1,0:T(8,128)(2,1)}), bf16[64,48,128]{2,1,0:T(8,128)(2,1)S(1)}, u32[]{:S(2)}, u32[]{:S(2)}) async-start(bf16[64,48,128]{2,1,0:T(8,128)(2,1)} %shard_map.144), calls=%async_computation.3 | async-start | bytes 1572864 | tf_op jit(solution)/shard_map/all_to_all | solution.py:644
  100.2 0.0 copy-start.5
  100.2 1.2 copy-done.5
  101.4 1.5 %shard_map.145 = bf16[512,256]{1,0:T(8,128)(2,1)} custom-call(bf16[3,544,256]{2,1,0:T(8,128)(2,1)S(1)} %copy-done.5, bf16[9,256,256]{2,1,0:T(8,128)(2,1)S(1)} %bitcast.56, f32[1,256]{1,0:T(1,128)S(1)} %bitcast.66), custom_call_target="tpu_custom_call" | custom-call | flops 603979776 | bytes 3000000 | tf_op jit(solution)/shard_map/pallas_call | solution.py:431
  102.9 12.5 %all-to-all-done.3.got = bf16[64,48,128]{2,1,0:T(8,128)(2,1)S(1)} async-done(((bf16[64,48,128]{2,1,0:T(8,128)(2,1)}), bf16[64,48,128]{2,1,0:T(8,128)(2,1)S(1)}, u32[]{:S(2)}, u32[]{:S(2)}) %all-to-all-start.3) | async-done | bytes 786464 | tf_op jit(solution)/shard_map/all_to_all | solution.py:644
  115.4 1.0 shard_map.146
  116.4 4.7 %all-to-all-start.4 = ((bf16[64,40,128]{2,1,0:T(8,128)(2,1)}), bf16[64,40,128]{2,1,0:T(8,128)(2,1)S(1)}, u32[]{:S(2)}, u32[]{:S(2)}) async-start(bf16[64,40,128]{2,1,0:T(8,128)(2,1)} %get-tuple-element.34), calls=%async_computation.4 | async-start | bytes 1310720 | tf_op jit(solution)/shard_map/all_to_all | solution.py:649
  121.1 1.4 shard_map.147
  122.4 11.5 %all-to-all-done.4.mine = bf16[64,40,128]{2,1,0:T(8,128)(2,1)S(1)} async-done(((bf16[64,40,128]{2,1,0:T(8,128)(2,1)}), bf16[64,40,128]{2,1,0:T(8,128)(2,1)S(1)}, u32[]{:S(2)}, u32[]{:S(2)}) %all-to-all-start.4) | async-done | bytes 655392 | tf_op jit(solution)/shard_map/all_to_all | solution.py:649
  133.9 2.9 %collective-permute-start.7 = (bf16[64,40,128]{2,1,0:T(8,128)(2,1)S(1)}, bf16[64,40,128]{2,1,0:T(8,128)(2,1)S(1)}, u32[]{:S(2)}, u32[]{:S(2)}) collective-permute-start(bf16[64,40,128]{2,1,0:T(8,128)(2,1)S(1)} %all-to-all-done.4.mine), channel_id=1, source_target_pairs={{1,0},{0,1},{3,2},{2,3},{5,4},{4,5},{7,6},{6,7},{9,8},{8,9},{11,10... | collective-permute-start | bytes 1966088 | tf_op jit(solution)/shard_map/ppermute | solution.py:584
  136.8 1.7 %collective-permute-done.7.other = bf16[64,40,128]{2,1,0:T(8,128)(2,1)S(1)} collective-permute-done((bf16[64,40,128]{2,1,0:T(8,128)(2,1)S(1)}, bf16[64,40,128]{2,1,0:T(8,128)(2,1)S(1)}, u32[]{:S(2)}, u32[]{:S(2)}) %collective-permute-start.7) | collective-permute-done | bytes 655392 | tf_op jit(solution)/shard_map/ppermute | solution.py:584
  138.6 2.0 %shard_map.148 = f32[2304,256]{1,0:T(8,128)} custom-call(s32[5]{0:T(128)S(1)} %copy-done.9, bf16[64,40,128]{2,1,0:T(8,128)(2,1)S(1)} %all-to-all-done.4.mine, bf16[64,40,128]{2,1,0:T(8,128)(2,1)S(1)} %collective-permute-done.7.other), custom_call_target="tpu_custom_call" | custom-call | tf_op jit(solution)/shard_map/pallas_call | solution.py:552
  (46 shorter events, 0.3 us)
Async XLA Ops:
  0.6 10.5 %copy-start.2 = (bf16[32,16,256]{2,1,0:T(8,128)(2,1)S(1)}, bf16[32,16,256]{2,1,0:T(8,128)(2,1)}, u32[]{:S(2)}) copy-start(bf16[32,16,256]{2,1,0:T(8,128)(2,1)} %param.20) | copy-start | bytes 786436
  0.6 0.9 copy-start.6
  1.5 9.5 %copy-start.7 = (bf16[16,8,256]{2,1,0:T(8,128)(2,1)S(1)}, bf16[16,8,256]{2,1,0:T(8,128)(2,1)}, u32[]{:S(2)}) copy-start(bf16[16,8,256]{2,1,0:T(8,128)(2,1)} %param.11) | copy-start | bytes 196612
  2.6 24.4 %all-to-all-start = ((bf16[16,128,256]{2,1,0:T(8,128)(2,1)}), bf16[16,128,256]{2,1,0:T(8,128)(2,1)S(1)}, u32[]{:S(2)}, u32[]{:S(2)}) async-start(bf16[16,128,256]{2,1,0:T(8,128)(2,1)} %shard_map.138), calls=%async_computation | async-start | bytes 2097152 | tf_op jit(solution)/shard_map/all_to_all | solution.py:606
  11.1 30.2 %copy-start.10 = (f32[256]{0:T(256)S(1)}, f32[256]{0:T(256)}, u32[]{:S(2)}) copy-start(f32[256]{0:T(256)} %param.12) | copy-start | bytes 3076
  11.1 30.2 %copy-start.11 = (f32[256]{0:T(256)S(1)}, f32[256]{0:T(256)}, u32[]{:S(2)}) copy-start(f32[256]{0:T(256)} %param.13) | copy-start | bytes 3076
  11.2 18.4 %collective-permute-start.2 = (bf16[48,256]{1,0:T(8,128)(2,1)S(1)}, bf16[48,256]{1,0:T(8,128)(2,1)S(1)}, u32[]{:S(2)}, u32[]{:S(2)}) collective-permute-start(bf16[48,256]{1,0:T(8,128)(2,1)S(1)} %pad_maximum_fusion.3), channel_id=1, source_target_pairs={{1,0},{2,1},{3,2},{4,3},{5,4},{6,5},{7,6},{8,7},{9,8},{10,9},{11,1... | collective-permute-start | bytes 73736 | tf_op jit(solution)/shard_map/ppermute | solution.py:612
  14.2 15.6 %collective-permute-start.1 = (bf16[48,256]{1,0:T(8,128)(2,1)S(1)}, bf16[48,256]{1,0:T(8,128)(2,1)S(1)}, u32[]{:S(2)}, u32[]{:S(2)}) collective-permute-start(bf16[48,256]{1,0:T(8,128)(2,1)S(1)} %pad_maximum_fusion.2), channel_id=1, source_target_pairs={{0,1},{1,2},{2,3},{3,4},{4,5},{5,6},{6,7},{7,8},{8,9},{9,10},{10,1... | collective-permute-start | bytes 73736 | tf_op jit(solution)/shard_map/ppermute | solution.py:611
  17.8 71.2 %copy-start.8 = (s32[5]{0:T(128)}, s32[5]{0:T(128)S(1)}, u32[]{:S(2)}) copy-start(s32[5]{0:T(128)S(1)} %convert_element_type.8.flags) | copy-start | bytes 64
  27.1 4.9 %collective-permute-start = (bf16[2048,256]{1,0:T(8,128)(2,1)S(1)}, bf16[2048,256]{1,0:T(8,128)(2,1)S(1)}, u32[]{:S(2)}, u32[]{:S(2)}) collective-permute-start(bf16[2048,256]{1,0:T(8,128)(2,1)S(1)} %bitcast.52), channel_id=1, source_target_pairs={{1,0},{0,1},{3,2},{2,3},{5,4},{4,5},{7,6},{6,7},{9,8},{8,9},{11,10... | collective-permute-start | bytes 3145736 | tf_op jit(solution)/shard_map/ppermute | solution.py:584
  33.2 36.3 %copy-start.1 = (bf16[1632,192]{1,0:T(8,128)(2,1)S(1)}, bf16[1632,192]{1,0:T(8,128)(2,1)}, u32[]{:S(2)}) copy-start(bf16[1632,192]{1,0:T(8,128)(2,1)} %constant.54.clone.up) | copy-start | bytes 1880068
  33.2 5.7 %collective-permute-start.3 = (bf16[176,256]{1,0:T(8,128)(2,1)S(1)}, bf16[176,256]{1,0:T(8,128)(2,1)S(1)}, u32[]{:S(2)}, u32[]{:S(2)}) collective-permute-start(bf16[176,256]{1,0:T(8,128)(2,1)S(1)} %get-tuple-element.23), channel_id=1, source_target_pairs={{64,0},{96,32},{0,64},{32,96},{65,1},{97,33},{1,65},{33,97},{66,2}... | collective-permute-start | bytes 270344 | tf_op jit(solution)/shard_map/ppermute | solution.py:584
  36.2 5.1 %collective-permute-start.5 = (bf16[208,256]{1,0:T(8,128)(2,1)S(1)}, bf16[208,256]{1,0:T(8,128)(2,1)S(1)}, u32[]{:S(2)}, u32[]{:S(2)}) collective-permute-start(bf16[208,256]{1,0:T(8,128)(2,1)S(1)} %get-tuple-element.24), channel_id=1, source_target_pairs={{96,0},{0,32},{32,64},{64,96},{97,1},{1,33},{33,65},{65,97},{98,2}... | collective-permute-start | bytes 319496 | tf_op jit(solution)/shard_map/ppermute | solution.py:584
  36.6 4.7 %collective-permute-start.4 = (bf16[208,256]{1,0:T(8,128)(2,1)S(1)}, bf16[208,256]{1,0:T(8,128)(2,1)S(1)}, u32[]{:S(2)}, u32[]{:S(2)}) collective-permute-start(bf16[208,256]{1,0:T(8,128)(2,1)S(1)} %get-tuple-element.22.near), channel_id=1, source_target_pairs={{32,0},{64,32},{96,64},{0,96},{33,1},{65,33},{97,65},{1,97},{34,2}... | collective-permute-start | bytes 319496 | tf_op jit(solution)/shard_map/ppermute | solution.py:584
  59.3 21.8 %copy-start = (bf16[3,3,256,256]{3,2,1,0:T(8,128)(2,1)S(1)}, bf16[3,3,256,256]{3,2,1,0:T(8,128)(2,1)}, u32[]{:S(2)}) copy-start(bf16[3,3,256,256]{3,2,1,0:T(8,128)(2,1)} %param.18) | copy-start | bytes 3538948
  59.3 10.2 %all-to-all-start.1 = ((bf16[4,208,256]{2,1,0:T(8,128)(2,1)}), bf16[4,208,256]{2,1,0:T(8,128)(2,1)S(1)}, u32[]{:S(2)}, u32[]{:S(2)}) async-start(bf16[4,208,256]{2,1,0:T(8,128)(2,1)} %get-tuple-element.25), calls=%async_computation.1 | async-start | bytes 851968 | tf_op jit(solution)/shard_map/all_to_all | solution.py:633
  72.5 16.5 %copy-start.13 = (f32[256]{0:T(256)S(1)}, f32[256]{0:T(256)}, u32[]{:S(2)}) copy-start(f32[256]{0:T(256)} %param.16) | copy-start | bytes 3076
  72.5 16.5 %copy-start.14 = (f32[256]{0:T(256)S(1)}, f32[256]{0:T(256)}, u32[]{:S(2)}) copy-start(f32[256]{0:T(256)} %param.17) | copy-start | bytes 3076
  72.5 16.5 %all-to-all-start.2 = ((f32[128,1,128]{2,1,0:T(1,128)}), f32[128,1,128]{2,1,0:T(1,128)S(1)}, u32[]{:S(2)}, u32[]{:S(2)}) async-start(f32[128,1,128]{2,1,0:T(1,128)} %bitcast.22), calls=%async_computation.2 | async-start | bytes 131072 | tf_op jit(solution)/shard_map/all_to_all | solution.py:635
  81.9 13.3 %copy-start.3 = (f32[512,256]{1,0:T(8,128)}, f32[512,256]{1,0:T(8,128)S(1)}, u32[]{:S(2)}) copy-start(f32[512,256]{1,0:T(8,128)S(1)} %shard_map.142.grad_hidden) | copy-start | bytes 1572868
  89.0 11.2 %copy-start.12 = (f32[256]{0:T(256)S(1)}, f32[256]{0:T(256)}, u32[]{:S(2)}) copy-start(f32[256]{0:T(256)} %param.19) | copy-start | bytes 3076
  91.5 2.6 %collective-permute-start.6 = (bf16[2320,128]{1,0:T(8,128)(2,1)S(1)}, bf16[2320,128]{1,0:T(8,128)(2,1)S(1)}, u32[]{:S(2)}, u32[]{:S(2)}) collective-permute-start(bf16[2320,128]{1,0:T(8,128)(2,1)S(1)} %get-tuple-element.30), channel_id=1, source_target_pairs={{1,0},{0,1},{3,2},{2,3},{5,4},{4,5},{7,6},{6,7},{9,8},{8,9},{11,10... | collective-permute-start | bytes 1781768 | tf_op jit(solution)/shard_map/ppermute | solution.py:584
  95.2 20.1 %all-to-all-start.3 = ((bf16[64,48,128]{2,1,0:T(8,128)(2,1)}), bf16[64,48,128]{2,1,0:T(8,128)(2,1)S(1)}, u32[]{:S(2)}, u32[]{:S(2)}) async-start(bf16[64,48,128]{2,1,0:T(8,128)(2,1)} %shard_map.144), calls=%async_computation.3 | async-start | bytes 1572864 | tf_op jit(solution)/shard_map/all_to_all | solution.py:644
  100.2 20.9 %copy-start.4 = (f32[512,256]{1,0:T(8,128)S(1)}, f32[512,256]{1,0:T(8,128)}, u32[]{:S(2)}) copy-start(f32[512,256]{1,0:T(8,128)} %copy-done.3) | copy-start | bytes 1572868
  100.2 1.2 copy-start.5
  116.4 22.2 %copy-start.9 = (s32[5]{0:T(128)S(1)}, s32[5]{0:T(128)}, u32[]{:S(2)}) copy-start(s32[5]{0:T(128)} %copy-done.8) | copy-start | bytes 64
  116.4 17.5 %all-to-all-start.4 = ((bf16[64,40,128]{2,1,0:T(8,128)(2,1)}), bf16[64,40,128]{2,1,0:T(8,128)(2,1)S(1)}, u32[]{:S(2)}, u32[]{:S(2)}) async-start(bf16[64,40,128]{2,1,0:T(8,128)(2,1)} %get-tuple-element.34), calls=%async_computation.4 | async-start | bytes 1310720 | tf_op jit(solution)/shard_map/all_to_all | solution.py:649
  133.9 4.6 %collective-permute-start.7 = (bf16[64,40,128]{2,1,0:T(8,128)(2,1)S(1)}, bf16[64,40,128]{2,1,0:T(8,128)(2,1)S(1)}, u32[]{:S(2)}, u32[]{:S(2)}) collective-permute-start(bf16[64,40,128]{2,1,0:T(8,128)(2,1)S(1)} %all-to-all-done.4.mine), channel_id=1, source_target_pairs={{1,0},{0,1},{3,2},{2,3},{5,4},{4,5},{7,6},{6,7},{9,8},{8,9},{11,10... | collective-permute-start | bytes 1966088 | tf_op jit(solution)/shard_map/ppermute | solution.py:584

commit v5 on v4

--- a/solution.py
+++ b/solution.py
@@ -21,6 +21,7 @@
 ALL = ("y", "z", "x", "c")
 
 CELLS_IN = 192
+PART = CELLS_IN + 16
 STRIP = 672
 KEY_BLOCK = 512
 FINE_ROWS = 34
@@ -50,6 +51,10 @@
         vmem_limit_bytes=VMEM_LIMIT,
         dimension_semantics=None if grid is None else ("arbitrary",) * grid,
     )
+
+
+def in_vmem(value):
+    return pltpu.with_memory_space_constraint(value, pltpu.VMEM)
 
 
 def in_hbm(value):
@@ -108,22 +113,31 @@
     return mean, jnp.sum(off * off, axis=0, keepdims=True) / count
 
 
-def stats_kernel(mine, other, wide, edges, next_out, last_out, far_out):
-    parts = [r[...].astype(F32) for r in (mine, other)]
-    count = 2 * parts[0].shape[0]
-    mean = sum(jnp.sum(p, axis=0, keepdims=True) for p in parts) / count
-    var = 0.0
-    for part in parts:
-        off = part - mean
-        var = var + jnp.sum(off * off, axis=0, keepdims=True)
-    high, middle, low = [p.astype(F32) for p in split3(group_row(mean, var / count))]
-    packed = jnp.concatenate(
-        [
-            jnp.concatenate([high, middle], axis=1),
-            jnp.concatenate([low, jnp.zeros_like(low)], axis=1),
-        ],
-        axis=0,
-    ).astype(BF16)
+def stats_rows(cells):
+    mean, var = channel_stats(cells[...].astype(F32))
+    high, middle, low = [p.astype(F32)[:1] for p in split3(group_row(mean, var))]
+    upper = jnp.concatenate([high, middle], axis=1)
+    return [upper, jnp.concatenate([low, jnp.zeros_like(low)], axis=1)]
+
+
+def stats_kernel(cells, out):
+    out[...] = jnp.concatenate(stats_rows(cells) + [jnp.zeros((6, C), F32)], axis=0)
+
+
+def local_stats(cells):
+    return pl.pallas_call(
+        stats_kernel,
+        out_shape=jax.ShapeDtypeStruct((8, C), F32),
+        compiler_params=params(),
+        cost_estimate=pl.CostEstimate(
+            flops=3 * cells.size, bytes_accessed=2 * cells.size, transcendentals=0
+        ),
+    )(cells)
+
+
+def rows_kernel(first, other, wide, edges, next_out, last_out, far_out):
+    rows = [first[0:2, :]] + stats_rows(other) + [jnp.zeros((12, C), F32)]
+    packed = jnp.concatenate(rows, axis=0).astype(BF16)
     for out in (next_out, last_out, far_out):
         out[:16, :] = packed
         out[16:176, :] = wide[...]
@@ -131,20 +145,19 @@
     last_out[176:, :] = edges[1]
 
 
-def stats_and_rows(mine, other, wide, edges):
-    return pl.pallas_call(
-        stats_kernel,
+def stats_and_rows(first, other, wide, edges):
+    return pl.pallas_call(
+        rows_kernel,
         out_shape=(
-            jax.ShapeDtypeStruct((208, C), BF16),
-            jax.ShapeDtypeStruct((208, C), BF16),
-            jax.ShapeDtypeStruct((176, C), BF16),
-        ),
-        compiler_params=params(),
-    )(mine, other, wide, edges)
+            pltpu.VMEM((208, C), BF16),
+            pltpu.VMEM((208, C), BF16),
+            pltpu.VMEM((176, C), BF16),
+        ),
+        compiler_params=params(),
+    )(first, other, wide, edges)
 
 
 def attention_kernel(
-    order,
     mine,
     other,
     near,
@@ -154,24 +167,27 @@
     gain,
     bias,
     w_far,
-    out_far,
-    block_far,
+    out1,
+    out2,
+    out3,
+    kept_far,
     keys,
     values,
     strip,
     w_qkv,
-    out,
-    block,
+    kept,
     w_sem,
     block_sem,
-    out_sems,
+    kept_sem,
 ):
     load = pltpu.make_async_copy(w_far, w_qkv, w_sem)
     load.start()
     rows = []
     for ref in (near, down, far, up):
         packed = ref[:16, :].astype(F32)
-        rows.append(packed[:8, :128] + packed[:8, 128:] + packed[8:, :128])
+        for i in (0, 2):
+            upper, lower = packed[i : i + 1], packed[i + 1 : i + 2]
+            rows.append(upper[:, :128] + upper[:, 128:] + lower[:, :128])
     mean, inverse = combine_groups(jnp.concatenate(rows, axis=0))
 
     def norm(cells):
@@ -186,26 +202,31 @@
         if i == 3:
             strip[:10, :] = cells[150:]
     strip[660:, :] = jnp.zeros((STRIP - 660, C), F32)
-    block[...] = strip[:CELLS_IN, :].astype(BF16)
-    keep = pltpu.make_async_copy(block, block_far, block_sem)
+    kept[PART:, :] = strip[:CELLS_IN, :].astype(BF16)
+    tail = pl.ds(PART, CELLS_IN)
+    keep = pltpu.make_async_copy(kept.at[tail], kept_far.at[tail], block_sem)
     keep.start()
     load.wait()
 
     head_of = iota((512, C), 1) >> 6
+    ones = jnp.ones((512, C), BF16)
     for i in range(8):
         rows = slice(512 * i, 512 * i + 512)
         cells = (mine, other)[i // 4][512 * (i % 4) : 512 * (i % 4) + 512, :]
         both = dot(norm(cells), w_qkv[:, C:])
-        keys[rows, :] = both[:, :C].astype(BF16)
+        both = both.astype(BF16)
+        keys[rows, :] = both[:, :C]
         for head in range(HEADS):
-            values[head, rows, :] = jnp.where(head_of == head, both[:, C:], 1.0).astype(BF16)
+            values[head, rows, :] = jnp.where(head_of == head, both[:, C:], ones)
 
     scale = HD**-0.5 * float(np.log2(np.e))
     queries = (dot(norm(strip[...]), w_qkv[:, :C]) * scale).astype(BF16)
     head_of = iota((STRIP, C), 1) >> 6
     lane = iota((STRIP, 128), 1)
     result = jnp.zeros((STRIP, C), F32)
-    packed = jnp.zeros((STRIP, 128), F32)
+    totals = jnp.ones((STRIP, C), F32)
+    logs = jnp.zeros((STRIP, 128), F32)
+    tops = jnp.zeros((STRIP, 128), F32)
     for head in range(HEADS):
         own = head_of == head
         masked = jnp.where(own, queries, jnp.zeros_like(queries))
@@ -218,78 +239,78 @@
             product = dot(jnp.exp2(scores - fresh).astype(BF16), values[head, rows, :])
             mixed = product if i == 0 else mixed * jnp.exp2(best - fresh) + product
             best = fresh
-        result = jnp.where(own, mixed / pltpu.roll(mixed, HD, 1), result)
+        result = jnp.where(own, mixed, result)
+        totals = jnp.where(own, pltpu.roll(mixed, HD, 1), totals)
         spot = 0 if head else 128
-        log = best + jnp.log2(mixed[:, spot : spot + 128])
-        for part, value in enumerate(split3(log)):
-            packed = jnp.where(lane == 4 * part + head, value.astype(F32), packed)
-    result = result.astype(BF16)
-    copies = []
-    for step in range(4):
+        logs = jnp.where(lane == head, mixed[:, spot : spot + 128], logs)
+        tops = jnp.where(lane == head, best, tops)
+    result = (result / totals).astype(BF16)
+    logs = tops + jnp.log2(jnp.where(lane < HEADS, logs, 1.0))
+    high, middle, low = [p.astype(F32) for p in split3(logs)]
+    packed = high + pltpu.roll(middle, 4, 1) + pltpu.roll(low, 8, 1)
+    head = pl.ds(0, PART)
+    copy = pltpu.make_async_copy(kept.at[head], kept_far.at[head], kept_sem)
+    for step, out in enumerate((kept, out1, out2, out3)):
         rows = slice(160 * step, 160 * step + CELLS_IN)
-        out[step, :CELLS_IN, :] = result[rows]
+        out[:CELLS_IN, :] = result[rows]
         turned = jnp.concatenate([packed[rows], jnp.zeros((64, 128), F32)], axis=0).T[:16]
-        out[step, CELLS_IN:, :] = turned.astype(BF16)
-        copy = pltpu.make_async_copy(out.at[step], out_far.at[order[step]], out_sems.at[step])
-        copy.start()
-        copies.append(copy)
+        out[CELLS_IN:PART, :] = turned.astype(BF16)
+        if step == 0:
+            copy.start()
     keep.wait()
-    for copy in copies:
-        copy.wait()
-
-
-def partial_attention(order, mine, other, near, far, down, up, gain, bias, w_qkv):
+    copy.wait()
+
+
+def partial_attention(mine, other, near, far, down, up, gain, bias, w_qkv):
     vmem = pl.BlockSpec(memory_space=pltpu.VMEM)
     return pl.pallas_call(
         attention_kernel,
-        out_shape=(
-            pltpu.HBM((4, CELLS_IN + 16, C), BF16),
-            pltpu.HBM((CELLS_IN, C), BF16),
-        ),
-        in_specs=[pl.BlockSpec(memory_space=pltpu.SMEM)] + [vmem] * 8 + [HBM],
-        out_specs=(HBM, HBM),
+        out_shape=(jax.ShapeDtypeStruct((PART, C), BF16),) * 3
+        + (pltpu.HBM((PART + CELLS_IN, C), BF16),),
+        in_specs=[vmem] * 8 + [HBM],
+        out_specs=(vmem, vmem, vmem, HBM),
         scratch_shapes=[
             pltpu.VMEM((4096, C), BF16),
             pltpu.VMEM((HEADS, 4096, C), BF16),
             pltpu.VMEM((STRIP, C), F32),
             pltpu.VMEM((C, 3 * C), BF16),
-            pltpu.VMEM((4, CELLS_IN + 16, C), BF16),
-            pltpu.VMEM((CELLS_IN, C), BF16),
+            pltpu.VMEM((PART + CELLS_IN, C), BF16),
             pltpu.SemaphoreType.DMA,
             pltpu.SemaphoreType.DMA,
-            pltpu.SemaphoreType.DMA((4,)),
+            pltpu.SemaphoreType.DMA,
         ],
         compiler_params=params(),
-    )(order, mine, other, near, far, down, up, gain, bias, in_hbm(w_qkv))
+    )(mine, other, near, in_vmem(far), in_vmem(down), in_vmem(up), gain, bias, in_hbm(w_qkv))
 
 
 def merge_kernel(
-    flags, parts, coarse_far, w_far, up, merged_out, stats_out, coarse, w_proj, coarse_sem, w_sem
+    flags, p1, p2, p3, kept_far, w_far, up, merged_out, stats_out, kept, w_proj, kept_sem, w_sem
 ):
     loads = [
-        pltpu.make_async_copy(coarse_far, coarse, coarse_sem),
+        pltpu.make_async_copy(kept_far, kept, kept_sem),
         pltpu.make_async_copy(w_far, w_proj, w_sem),
     ]
     for load in loads:
         load.start()
-    count = parts.shape[0]
+    parts = (p1, p2, p3, kept)
     logs = []
-    for i in range(count):
-        tail = parts[i, CELLS_IN:, :].astype(F32)
+    for part in parts:
+        if part is kept:
+            loads[0].wait()
+        tail = part[CELLS_IN:PART, :].astype(F32)
         logs.append(tail[0:4] + tail[4:8] + tail[8:12])
     top = functools.reduce(jnp.maximum, logs)
     shares = [jnp.exp2(v - top) for v in logs]
     total = sum(shares)
     spread = jnp.where((iota((16, C), 1) >> 6) == (iota((16, C), 0) & 3), 1.0, 0.0).astype(BF16)
     attended = jnp.zeros((CELLS_IN, C), F32)
-    for i in range(count):
+    for i, part in enumerate(parts):
         pieces = [p.astype(F32) for p in split3((shares[i] / total)[:, :CELLS_IN])]
         pieces.append(jnp.zeros_like(pieces[0]))
         wide = dot(jnp.concatenate(pieces, axis=0).astype(BF16), spread, ((0,), (0,)))
-        attended = attended + wide * parts[i, :CELLS_IN, :].astype(F32)
-    for load in loads:
-        load.wait()
-    merged = coarse[...].astype(F32) + dot(attended.astype(BF16), w_proj[...])
+        attended = attended + wide * part[:CELLS_IN, :].astype(F32)
+    loads[1].wait()
+    merged = kept[PART:, :].astype(F32) + dot(attended.astype(BF16), w_proj[...])
     cell = iota((CELLS_IN, C), 0)
     col = lax.rem(cell, 10)
     outside = (
@@ -306,7 +327,7 @@
     stats_out[...] = jnp.broadcast_to(group_row(mean, var)[:1], stats_out.shape)
 
 
-def merge(flags, parts, coarse, w_proj, up):
+def merge(flags, parts, kept, w_proj, up):
     vmem = pl.BlockSpec(memory_space=pltpu.VMEM)
     return pl.pallas_call(
         merge_kernel,
@@ -314,16 +335,16 @@
             jax.ShapeDtypeStruct((CELLS_IN, C), BF16),
             jax.ShapeDtypeStruct((128, 128), F32),
         ),
-        in_specs=[pl.BlockSpec(memory_space=pltpu.SMEM), vmem, HBM, HBM, vmem],
+        in_specs=[pl.BlockSpec(memory_space=pltpu.SMEM), vmem, vmem, vmem, HBM, HBM, vmem],
         out_specs=(vmem, vmem),
         scratch_shapes=[
-            pltpu.VMEM((CELLS_IN, C), BF16),
+            pltpu.VMEM((PART + CELLS_IN, C), BF16),
             pltpu.VMEM((C, C), BF16),
             pltpu.SemaphoreType.DMA,
             pltpu.SemaphoreType.DMA,
         ],
         compiler_params=params(),
-    )(flags, parts, in_hbm(coarse), in_hbm(w_proj), up)
+    )(flags, *parts, in_hbm(kept), in_hbm(w_proj), up)
 
 
 def back_kernel(c0, c1, c2, weight, out):
@@ -615,7 +636,7 @@
     edges = jnp.pad(jnp.stack([grad[0], grad[-1]]), ((0, 0), (0, 14), (0, 0)))
     other = shift(cells, "c", 2, 1)
 
-    near, last, far = stats_and_rows(cells, other, wide, edges)
+    near, last, far = stats_and_rows(local_stats(cells), other, wide, edges)
     below, above, far = (
         shift(near, "y", 4, 1),
         shift(last, "y", 4, 3),
@@ -625,13 +646,11 @@
     bottom = jnp.where(y == 3, 0, below[176:194])[None].astype(BF16)
     grad = jnp.concatenate([top, grad, bottom], axis=0)
     windows = [grad[:, b : b + 16].reshape(WIN, C) for b in range(3)]
-    order = jnp.stack([(y + k) % 4 for k in range(4)]).astype(jnp.int32)
-
-    partial, block = partial_attention(
-        order, cells, other, near, far, below, above, norm1_gain[None], norm1_bias[None], w_qkv
+    *sent, kept = partial_attention(
+        cells, other, near, far, below, above, norm1_gain[None], norm1_bias[None], w_qkv
     )
-    partial = lax.all_to_all(partial, "y", 0, 0, tiled=True)
-    merged, stats2 = merge(flags, partial, block, w_proj, up)
+    parts = [shift(part, "y", 4, 4 - k) for k, part in zip((1, 2, 3), sent)]
+    merged, stats2 = merge(flags, parts, kept, w_proj, up)
     stats2 = lax.all_to_all(stats2.reshape(128, 1, 128), ALL, 0, 0, tiled=True)
     stats2 = stats2.reshape(128, 128)
     grad_hidden = back_conv(windows, taps)

time: 141 us -> 139 us (0.986)
  starting transfers between devices: 47.1 us -> 45 us
    all_to_all x1 -> x0, waiting for transfers between devices: 5.41 us -> none  [per_device(): partial = lax.all_to_all(partial, 'y', 0, 0, tiled=True)]
    all_to_all x1 -> x0, starting transfers between devices: 3.78 us -> none  [per_device(): partial = lax.all_to_all(partial, 'y', 0, 0, tiled=True)]
    ppermute x6 -> x9, waiting for transfers between devices: 7.66 us -> 11.4 us  [shift(): lax.ppermute(value, axis, [((i + step) % count, i) for i in range(count)])]
    ppermute x6 -> x9, starting transfers between devices: 12.1 us -> 13.8 us  [shift(): lax.ppermute(value, axis, [((i + step) % count, i) for i in range(count)])]
    slice x1, local copies, waits for them, and re-layouts: 1.65 us -> 0.16 us  [per_device(): windows = [grad[:, b:b + 16].reshape(WIN, C) for b in range(3)]]
    pallas_call x2 -> x3, Pallas kernels: 19.3 us -> 20.1 us  [the longest x1 17.6 us: partial_attention(): pl.pallas_call(attention_kernel, out_shape=(jax.ShapeDtypeStruct((PART, C...]
  transfers between devices with their start and end apart: 13 -> 15, of which waited for: 9 -> 10; matrix products, arithmetic and copies ran while one was open for 2% -> 2% of each run, Pallas kernels for 3% -> 3%
where the time goes in v5:
time: 139 us
  waiting for transfers between devices  53.3 us (38%)
  starting transfers between devices  45 us (32%)
  Pallas kernels  34.8 us (25%)
  local copies, waits for them, and re-layouts  3.23 us (2%)
    pallas_call x1, Pallas kernels, partial_attention(): pl.pallas_call(attention_kernel, out_shape=(jax.ShapeDtypeStruct((PART, C...  17.6 us
    ppermute x9, starting transfers between devices, shift(): lax.ppermute(value, axis, [((i + step) % count, i) for i in range(count)])  13.8 us
    all_to_all x1, waiting for transfers between devices, per_device(): got = lax.all_to_all(sent, ('y', 'z', 'x'), 0, 0, tiled=True)  12.5 us
    all_to_all x1, waiting for transfers between devices, per_device(): spread = lax.all_to_all(chunk, ('y', 'z', 'x'), 0, 0, tiled=True)  11.5 us
    ppermute x9, waiting for transfers between devices, shift(): lax.ppermute(value, axis, [((i + step) % count, i) for i in range(count)])  11.4 us
    all_to_all x1, waiting for transfers between devices, per_device(): lax.all_to_all(copies_of(own), ('z', 'x'), 0, 0, tiled=True)  9.44 us
    all_to_all x1, starting transfers between devices, per_device(): lax.all_to_all(copies_of(own), ('z', 'x'), 0, 0, tiled=True)  8.44 us
    all_to_all x1, waiting for transfers between devices, per_device(): stats2 = lax.all_to_all(stats2.reshape(128, 1, 128), ALL, 0, 0, tiled=True)  8.42 us
  transfers between devices with their start and end apart: 15, of which 10 were waited for; matrix products, arithmetic and copies ran while one was open for 2% of the time, Pallas kernels for 3%

profile of v5, /device:TPU:1, one launch (start us, length us, event | category | flops | bytes accessed | tf_op | source)
XLA Modules:
  0.0 138.6 jit_solution(10331494832923923494)
XLA Ops:
  0.7 0.9 copy-done.6
  1.5 1.1 shard_map.138
  2.6 8.4 %all-to-all-start = ((bf16[16,128,256]{2,1,0:T(8,128)(2,1)}), bf16[16,128,256]{2,1,0:T(8,128)(2,1)S(1)}, u32[]{:S(2)}, u32[]{:S(2)}) async-start(bf16[16,128,256]{2,1,0:T(8,128)(2,1)} %shard_map.138), calls=%async_computation | async-start | bytes 2097152 | tf_op jit(solution)/shard_map/all_to_all | solution.py:627
  11.1 0.0 copy-start.11
  11.2 0.1 fusion.14
  11.2 2.9 %collective-permute-start.2 = (bf16[48,256]{1,0:T(8,128)(2,1)S(1)}, bf16[48,256]{1,0:T(8,128)(2,1)S(1)}, u32[]{:S(2)}, u32[]{:S(2)}) collective-permute-start(bf16[48,256]{1,0:T(8,128)(2,1)S(1)} %pad_maximum_fusion.3), channel_id=1, source_target_pairs={{1,0},{2,1},{3,2},{4,3},{5,4},{6,5},{7,6},{8,7},{9,8},{10,9},{11,1... | collective-permute-start | bytes 73736 | tf_op jit(solution)/shard_map/ppermute | solution.py:633
  14.2 3.4 %collective-permute-start.1 = (bf16[48,256]{1,0:T(8,128)(2,1)S(1)}, bf16[48,256]{1,0:T(8,128)(2,1)S(1)}, u32[]{:S(2)}, u32[]{:S(2)}) collective-permute-start(bf16[48,256]{1,0:T(8,128)(2,1)S(1)} %pad_maximum_fusion.2), channel_id=1, source_target_pairs={{0,1},{1,2},{2,3},{3,4},{4,5},{5,6},{6,7},{7,8},{8,9},{9,10},{10,1... | collective-permute-start | bytes 73736 | tf_op jit(solution)/shard_map/ppermute | solution.py:632
  17.6 9.4 %all-to-all-done = bf16[16,128,256]{2,1,0:T(8,128)(2,1)S(1)} async-done(((bf16[16,128,256]{2,1,0:T(8,128)(2,1)}), bf16[16,128,256]{2,1,0:T(8,128)(2,1)S(1)}, u32[]{:S(2)}, u32[]{:S(2)}) %all-to-all-start) | async-done | bytes 1048608 | tf_op jit(solution)/shard_map/all_to_all | solution.py:627
  27.1 2.6 %collective-permute-start = (bf16[2048,256]{1,0:T(8,128)(2,1)S(1)}, bf16[2048,256]{1,0:T(8,128)(2,1)S(1)}, u32[]{:S(2)}, u32[]{:S(2)}) collective-permute-start(bf16[2048,256]{1,0:T(8,128)(2,1)S(1)} %bitcast.48), channel_id=1, source_target_pairs={{1,0},{0,1},{3,2},{2,3},{5,4},{4,5},{7,6},{6,7},{9,8},{8,9},{11,10... | collective-permute-start | bytes 3145736 | tf_op jit(solution)/shard_map/ppermute | solution.py:605
  29.8 0.0 copy-start.15
  29.8 0.1 pad_maximum_fusion.1
  30.0 0.9 shard_map.139.first
  30.9 0.0 copy-start.1
  30.9 1.1 collective-permute-done.other
  32.0 1.6 %shard_map.140 = (bf16[208,256]{1,0:T(8,128)(2,1)S(1)}, bf16[208,256]{1,0:T(8,128)(2,1)}, bf16[176,256]{1,0:T(8,128)(2,1)}) custom-call(f32[8,256]{1,0:T(8,128)S(1)} %shard_map.139.first, bf16[2048,256]{1,0:T(8,128)(2,1)S(1)} %collective-permute-done.other, bf16[160,256]{1,0:T(8,128)(2,1)S(1)} %reshape.53.wide, bf16[2,32,256]{2,1,0:T(8,128)(2,1)S(1)} %pad.4.edges), custom_call_target="tpu_custom_call" | custom-call | tf_op jit(solution)/shard_map/pallas_call | solution.py:149
  33.5 1.3 collective-permute-start.5
  34.8 1.4 %collective-permute-start.4 = (bf16[208,256]{1,0:T(8,128)(2,1)S(1)}, bf16[208,256]{1,0:T(8,128)(2,1)S(1)}, u32[]{:S(2)}, u32[]{:S(2)}) collective-permute-start(bf16[208,256]{1,0:T(8,128)(2,1)S(1)} %get-tuple-element.24.near), channel_id=1, source_target_pairs={{32,0},{64,32},{96,64},{0,96},{33,1},{65,33},{97,65},{1,97},{34,2}... | collective-permute-start | bytes 319496 | tf_op jit(solution)/shard_map/ppermute | solution.py:605
  36.3 1.6 %collective-permute-start.3 = (bf16[176,256]{1,0:T(8,128)(2,1)}, bf16[176,256]{1,0:T(8,128)(2,1)}, u32[]{:S(2)}, u32[]{:S(2)}) collective-permute-start(bf16[176,256]{1,0:T(8,128)(2,1)} %get-tuple-element.25), channel_id=1, source_target_pairs={{64,0},{96,32},{0,64},{32,96},{65,1},{97,33},{1,65},{33,97},{66,2}... | collective-permute-start | bytes 270344 | tf_op jit(solution)/shard_map/ppermute | solution.py:605
  37.9 0.7 stack.26
  38.6 0.7 convert_element_type.8.flags
  39.3 3.1 %collective-permute-done.3.far = bf16[176,256]{1,0:T(8,128)(2,1)} collective-permute-done((bf16[176,256]{1,0:T(8,128)(2,1)}, bf16[176,256]{1,0:T(8,128)(2,1)}, u32[]{:S(2)}, u32[]{:S(2)}) %collective-permute-start.3) | collective-permute-done | bytes 90144 | tf_op jit(solution)/shard_map/ppermute | solution.py:605
  42.3 17.6 %shard_map.141 = (bf16[208,256]{1,0:T(8,128)(2,1)S(1)}, bf16[208,256]{1,0:T(8,128)(2,1)S(1)}, bf16[208,256]{1,0:T(8,128)(2,1)S(1)}, bf16[400,256]{1,0:T(8,128)(2,1)}) custom-call(bf16[2048,256]{1,0:T(8,128)(2,1)S(1)} %bitcast.50, bf16[2048,256]{1,0:T(8,128)(2,1)S(1)} %collective-permute-done.other, bf16[208,256]{1,0:T(8,128)(2,1)S(1)} %get-tuple-element.24.near, ...), custom_call_target="tpu_custom_call" | custom-call | tf_op jit(solution)/shard_map/pallas_call | solution.py:266
  60.0 0.2 collective-permute-start.6
  60.2 1.8 %collective-permute-start.7 = (bf16[208,256]{1,0:T(8,128)(2,1)S(1)}, bf16[208,256]{1,0:T(8,128)(2,1)S(1)}, u32[]{:S(2)}, u32[]{:S(2)}) collective-permute-start(bf16[208,256]{1,0:T(8,128)(2,1)S(1)} %get-tuple-element.28), channel_id=1, source_target_pairs={{64,0},{96,32},{0,64},{32,96},{65,1},{97,33},{1,65},{33,97},{66,2}... | collective-permute-start | bytes 319496 | tf_op jit(solution)/shard_map/ppermute | solution.py:605
  62.0 0.9 collective-permute-start.8
  63.0 0.2 pad_maximum_fusion
  63.2 3.5 %collective-permute-done.6.p1 = bf16[208,256]{1,0:T(8,128)(2,1)S(1)} collective-permute-done((bf16[208,256]{1,0:T(8,128)(2,1)S(1)}, bf16[208,256]{1,0:T(8,128)(2,1)S(1)}, u32[]{:S(2)}, u32[]{:S(2)}) %collective-permute-start.6) | collective-permute-done | bytes 106528 | tf_op jit(solution)/shard_map/ppermute | solution.py:605
  66.8 0.4 collective-permute-done.8.p3
  67.1 3.3 %shard_map.142 = (bf16[192,256]{1,0:T(8,128)(2,1)S(1)}, f32[128,128]{1,0:T(8,128)}) custom-call(s32[5]{0:T(128)S(1)} %convert_element_type.8.flags, bf16[208,256]{1,0:T(8,128)(2,1)S(1)} %collective-permute-done.6.p1, bf16[208,256]{1,0:T(8,128)(2,1)S(1)} %collective-permute-done.7.p2, bf16[208,256]{1,0:T(8,128)(2,1)S(1)} %collective-permute-done.8.p3, ...), custom_call_target="tpu_custom_call" | custom-call | tf_op jit(solution)/shard_map/pallas_call | solution.py:332
  70.5 6.9 %all-to-all-start.1 = ((f32[128,1,128]{2,1,0:T(1,128)}), f32[128,1,128]{2,1,0:T(1,128)S(1)}, u32[]{:S(2)}, u32[]{:S(2)}) async-start(f32[128,1,128]{2,1,0:T(1,128)} %bitcast.18), calls=%async_computation.1 | async-start | bytes 131072 | tf_op jit(solution)/shard_map/all_to_all | solution.py:654
  77.4 0.2 fusion.13
  77.5 0.8 shard_map.143.grad_hidden
  78.4 8.4 %all-to-all-done.1 = f32[128,1,128]{2,1,0:T(1,128)S(1)} async-done(((f32[128,1,128]{2,1,0:T(1,128)}), f32[128,1,128]{2,1,0:T(1,128)S(1)}, u32[]{:S(2)}, u32[]{:S(2)}) %all-to-all-start.1) | async-done | bytes 65568 | tf_op jit(solution)/shard_map/all_to_all | solution.py:654
  86.8 2.5 %shard_map.144 = (bf16[2320,128]{1,0:T(8,128)(2,1)S(1)}, bf16[2320,128]{1,0:T(8,128)(2,1)S(1)}, bf16[3,544,256]{2,1,0:T(8,128)(2,1)}) custom-call(s32[5]{0:T(128)S(1)} %copy-done.9, bf16[192,256]{1,0:T(8,128)(2,1)S(1)} %get-tuple-element.31.merged, bf16[1632,192]{1,0:T(8,128)(2,1)S(1)} %copy-done.1, f32[128,128]{1,0:T(8,128)S(1)} %bitcast.58, ...), custom_call_target="tpu_custom_call" | custom-call | tf_op jit(solution)/shard_map/pallas_call | solution.py:429
  89.3 0.9 collective-permute-start.9
  90.3 1.6 %collective-permute-done.9.got = bf16[2320,128]{1,0:T(8,128)(2,1)S(1)} collective-permute-done((bf16[2320,128]{1,0:T(8,128)(2,1)S(1)}, bf16[2320,128]{1,0:T(8,128)(2,1)S(1)}, u32[]{:S(2)}, u32[]{:S(2)}) %collective-permute-start.9) | collective-permute-done | bytes 593952 | tf_op jit(solution)/shard_map/ppermute | solution.py:605
  91.9 1.1 shard_map.145
  93.1 4.9 %all-to-all-start.2 = ((bf16[64,48,128]{2,1,0:T(8,128)(2,1)}), bf16[64,48,128]{2,1,0:T(8,128)(2,1)S(1)}, u32[]{:S(2)}, u32[]{:S(2)}) async-start(bf16[64,48,128]{2,1,0:T(8,128)(2,1)} %shard_map.145), calls=%async_computation.2 | async-start | bytes 1572864 | tf_op jit(solution)/shard_map/all_to_all | solution.py:663
  98.0 1.2 copy-done.5
  99.2 1.5 %shard_map.146 = bf16[512,256]{1,0:T(8,128)(2,1)} custom-call(bf16[3,544,256]{2,1,0:T(8,128)(2,1)S(1)} %copy-done.5, bf16[9,256,256]{2,1,0:T(8,128)(2,1)S(1)} %bitcast.52, f32[1,256]{1,0:T(1,128)S(1)} %bitcast.62), custom_call_target="tpu_custom_call" | custom-call | flops 603979776 | bytes 3000000 | tf_op jit(solution)/shard_map/pallas_call | solution.py:452
  100.7 12.5 %all-to-all-done.2.got = bf16[64,48,128]{2,1,0:T(8,128)(2,1)S(1)} async-done(((bf16[64,48,128]{2,1,0:T(8,128)(2,1)}), bf16[64,48,128]{2,1,0:T(8,128)(2,1)S(1)}, u32[]{:S(2)}, u32[]{:S(2)}) %all-to-all-start.2) | async-done | bytes 786464 | tf_op jit(solution)/shard_map/all_to_all | solution.py:663
  113.2 1.0 shard_map.147
  114.2 4.7 %all-to-all-start.3 = ((bf16[64,40,128]{2,1,0:T(8,128)(2,1)}), bf16[64,40,128]{2,1,0:T(8,128)(2,1)S(1)}, u32[]{:S(2)}, u32[]{:S(2)}) async-start(bf16[64,40,128]{2,1,0:T(8,128)(2,1)} %get-tuple-element.38), calls=%async_computation.3 | async-start | bytes 1310720 | tf_op jit(solution)/shard_map/all_to_all | solution.py:668
  118.9 1.4 shard_map.148
  120.2 11.5 %all-to-all-done.3.mine = bf16[64,40,128]{2,1,0:T(8,128)(2,1)S(1)} async-done(((bf16[64,40,128]{2,1,0:T(8,128)(2,1)}), bf16[64,40,128]{2,1,0:T(8,128)(2,1)S(1)}, u32[]{:S(2)}, u32[]{:S(2)}) %all-to-all-start.3) | async-done | bytes 655392 | tf_op jit(solution)/shard_map/all_to_all | solution.py:668
  131.7 2.9 %collective-permute-start.10 = (bf16[64,40,128]{2,1,0:T(8,128)(2,1)S(1)}, bf16[64,40,128]{2,1,0:T(8,128)(2,1)S(1)}, u32[]{:S(2)}, u32[]{:S(2)}) collective-permute-start(bf16[64,40,128]{2,1,0:T(8,128)(2,1)S(1)} %all-to-all-done.3.mine), channel_id=1, source_target_pairs={{1,0},{0,1},{3,2},{2,3},{5,4},{4,5},{7,6},{6,7},{9,8},{8,9},{11,10... | collective-permute-start | bytes 1966088 | tf_op jit(solution)/shard_map/ppermute | solution.py:605
  134.6 1.7 %collective-permute-done.10.other = bf16[64,40,128]{2,1,0:T(8,128)(2,1)S(1)} collective-permute-done((bf16[64,40,128]{2,1,0:T(8,128)(2,1)S(1)}, bf16[64,40,128]{2,1,0:T(8,128)(2,1)S(1)}, u32[]{:S(2)}, u32[]{:S(2)}) %collective-permute-start.10) | collective-permute-done | bytes 655392 | tf_op jit(solution)/shard_map/ppermute | solution.py:605
  136.4 2.0 %shard_map.149 = f32[2304,256]{1,0:T(8,128)} custom-call(s32[5]{0:T(128)S(1)} %copy-done.9, bf16[64,40,128]{2,1,0:T(8,128)(2,1)S(1)} %all-to-all-done.3.mine, bf16[64,40,128]{2,1,0:T(8,128)(2,1)S(1)} %collective-permute-done.10.other), custom_call_target="tpu_custom_call" | custom-call | tf_op jit(solution)/shard_map/pallas_call | solution.py:573
  (54 shorter events, 0.3 us)
Async XLA Ops:
  0.6 10.5 %copy-start.2 = (bf16[32,16,256]{2,1,0:T(8,128)(2,1)S(1)}, bf16[32,16,256]{2,1,0:T(8,128)(2,1)}, u32[]{:S(2)}) copy-start(bf16[32,16,256]{2,1,0:T(8,128)(2,1)} %param.20) | copy-start | bytes 786436
  0.6 0.9 copy-start.6
  1.5 9.5 %copy-start.7 = (bf16[16,8,256]{2,1,0:T(8,128)(2,1)S(1)}, bf16[16,8,256]{2,1,0:T(8,128)(2,1)}, u32[]{:S(2)}) copy-start(bf16[16,8,256]{2,1,0:T(8,128)(2,1)} %param.11) | copy-start | bytes 196612
  2.6 24.4 %all-to-all-start = ((bf16[16,128,256]{2,1,0:T(8,128)(2,1)}), bf16[16,128,256]{2,1,0:T(8,128)(2,1)S(1)}, u32[]{:S(2)}, u32[]{:S(2)}) async-start(bf16[16,128,256]{2,1,0:T(8,128)(2,1)} %shard_map.138), calls=%async_computation | async-start | bytes 2097152 | tf_op jit(solution)/shard_map/all_to_all | solution.py:627
  11.1 31.3 %copy-start.10 = (f32[256]{0:T(256)S(1)}, f32[256]{0:T(256)}, u32[]{:S(2)}) copy-start(f32[256]{0:T(256)} %param.12) | copy-start | bytes 3076
  11.1 31.3 %copy-start.11 = (f32[256]{0:T(256)S(1)}, f32[256]{0:T(256)}, u32[]{:S(2)}) copy-start(f32[256]{0:T(256)} %param.13) | copy-start | bytes 3076
  11.2 18.4 %collective-permute-start.2 = (bf16[48,256]{1,0:T(8,128)(2,1)S(1)}, bf16[48,256]{1,0:T(8,128)(2,1)S(1)}, u32[]{:S(2)}, u32[]{:S(2)}) collective-permute-start(bf16[48,256]{1,0:T(8,128)(2,1)S(1)} %pad_maximum_fusion.3), channel_id=1, source_target_pairs={{1,0},{2,1},{3,2},{4,3},{5,4},{6,5},{7,6},{8,7},{9,8},{10,9},{11,1... | collective-permute-start | bytes 73736 | tf_op jit(solution)/shard_map/ppermute | solution.py:633
  14.2 15.6 %collective-permute-start.1 = (bf16[48,256]{1,0:T(8,128)(2,1)S(1)}, bf16[48,256]{1,0:T(8,128)(2,1)S(1)}, u32[]{:S(2)}, u32[]{:S(2)}) collective-permute-start(bf16[48,256]{1,0:T(8,128)(2,1)S(1)} %pad_maximum_fusion.2), channel_id=1, source_target_pairs={{0,1},{1,2},{2,3},{3,4},{4,5},{5,6},{6,7},{7,8},{8,9},{9,10},{10,1... | collective-permute-start | bytes 73736 | tf_op jit(solution)/shard_map/ppermute | solution.py:632
  27.1 4.9 %collective-permute-start = (bf16[2048,256]{1,0:T(8,128)(2,1)S(1)}, bf16[2048,256]{1,0:T(8,128)(2,1)S(1)}, u32[]{:S(2)}, u32[]{:S(2)}) collective-permute-start(bf16[2048,256]{1,0:T(8,128)(2,1)S(1)} %bitcast.48), channel_id=1, source_target_pairs={{1,0},{0,1},{3,2},{2,3},{5,4},{4,5},{7,6},{6,7},{9,8},{8,9},{11,10... | collective-permute-start | bytes 3145736 | tf_op jit(solution)/shard_map/ppermute | solution.py:605
  29.8 1.1 copy-start.15
  30.9 36.3 %copy-start.1 = (bf16[1632,192]{1,0:T(8,128)(2,1)S(1)}, bf16[1632,192]{1,0:T(8,128)(2,1)}, u32[]{:S(2)}) copy-start(bf16[1632,192]{1,0:T(8,128)(2,1)} %constant.31.clone.up) | copy-start | bytes 1880068
  33.5 8.8 %collective-permute-start.5 = (bf16[208,256]{1,0:T(8,128)(2,1)}, bf16[208,256]{1,0:T(8,128)(2,1)S(1)}, u32[]{:S(2)}, u32[]{:S(2)}) collective-permute-start(bf16[208,256]{1,0:T(8,128)(2,1)} %get-tuple-element.26), channel_id=1, source_target_pairs={{96,0},{0,32},{32,64},{64,96},{97,1},{1,33},{33,65},{65,97},{98,2}... | collective-permute-start | bytes 319496 | tf_op jit(solution)/shard_map/ppermute | solution.py:605
  34.8 7.5 %collective-permute-start.4 = (bf16[208,256]{1,0:T(8,128)(2,1)S(1)}, bf16[208,256]{1,0:T(8,128)(2,1)S(1)}, u32[]{:S(2)}, u32[]{:S(2)}) collective-permute-start(bf16[208,256]{1,0:T(8,128)(2,1)S(1)} %get-tuple-element.24.near), channel_id=1, source_target_pairs={{32,0},{64,32},{96,64},{0,96},{33,1},{65,33},{97,65},{1,97},{34,2}... | collective-permute-start | bytes 319496 | tf_op jit(solution)/shard_map/ppermute | solution.py:605
  36.3 6.1 %collective-permute-start.3 = (bf16[176,256]{1,0:T(8,128)(2,1)}, bf16[176,256]{1,0:T(8,128)(2,1)}, u32[]{:S(2)}, u32[]{:S(2)}) collective-permute-start(bf16[176,256]{1,0:T(8,128)(2,1)} %get-tuple-element.25), channel_id=1, source_target_pairs={{64,0},{96,32},{0,64},{32,96},{65,1},{97,33},{1,65},{33,97},{66,2}... | collective-permute-start | bytes 270344 | tf_op jit(solution)/shard_map/ppermute | solution.py:605
  38.6 24.4 %copy-start.16 = (bf16[32,1,256]{2,1,0:T(2,128)(2,1)S(1)}, bf16[32,1,256]{2,1,0:T(2,128)(2,1)}, u32[]{:S(2)}) copy-start(bf16[32,1,256]{2,1,0:T(2,128)(2,1)} %copy-done.15) | copy-start | bytes 49156
  39.3 31.2 %copy-start.8 = (s32[5]{0:T(128)}, s32[5]{0:T(128)S(1)}, u32[]{:S(2)}) copy-start(s32[5]{0:T(128)S(1)} %convert_element_type.8.flags) | copy-start | bytes 64
  60.0 17.5 %copy-start = (bf16[3,3,256,256]{3,2,1,0:T(8,128)(2,1)S(1)}, bf16[3,3,256,256]{3,2,1,0:T(8,128)(2,1)}, u32[]{:S(2)}) copy-start(bf16[3,3,256,256]{3,2,1,0:T(8,128)(2,1)} %param.18) | copy-start | bytes 3538948
  60.0 6.7 %collective-permute-start.6 = (bf16[208,256]{1,0:T(8,128)(2,1)S(1)}, bf16[208,256]{1,0:T(8,128)(2,1)S(1)}, u32[]{:S(2)}, u32[]{:S(2)}) collective-permute-start(bf16[208,256]{1,0:T(8,128)(2,1)S(1)} %get-tuple-element.27), channel_id=1, source_target_pairs={{96,0},{0,32},{32,64},{64,96},{97,1},{1,33},{33,65},{65,97},{98,2}... | collective-permute-start | bytes 319496 | tf_op jit(solution)/shard_map/ppermute | solution.py:605
  60.2 6.5 %collective-permute-start.7 = (bf16[208,256]{1,0:T(8,128)(2,1)S(1)}, bf16[208,256]{1,0:T(8,128)(2,1)S(1)}, u32[]{:S(2)}, u32[]{:S(2)}) collective-permute-start(bf16[208,256]{1,0:T(8,128)(2,1)S(1)} %get-tuple-element.28), channel_id=1, source_target_pairs={{64,0},{96,32},{0,64},{32,96},{65,1},{97,33},{1,65},{33,97},{66,2}... | collective-permute-start | bytes 319496 | tf_op jit(solution)/shard_map/ppermute | solution.py:605
  62.0 5.1 %collective-permute-start.8 = (bf16[208,256]{1,0:T(8,128)(2,1)S(1)}, bf16[208,256]{1,0:T(8,128)(2,1)S(1)}, u32[]{:S(2)}, u32[]{:S(2)}) collective-permute-start(bf16[208,256]{1,0:T(8,128)(2,1)S(1)} %get-tuple-element.29), channel_id=1, source_target_pairs={{32,0},{64,32},{96,64},{0,96},{33,1},{65,33},{97,65},{1,97},{34,2}... | collective-permute-start | bytes 319496 | tf_op jit(solution)/shard_map/ppermute | solution.py:605
  70.4 16.4 %copy-start.13 = (f32[256]{0:T(256)S(1)}, f32[256]{0:T(256)}, u32[]{:S(2)}) copy-start(f32[256]{0:T(256)} %param.16) | copy-start | bytes 3076
  70.4 16.4 %copy-start.14 = (f32[256]{0:T(256)S(1)}, f32[256]{0:T(256)}, u32[]{:S(2)}) copy-start(f32[256]{0:T(256)} %param.17) | copy-start | bytes 3076
  70.4 16.3 %copy-start.9 = (s32[5]{0:T(128)S(1)}, s32[5]{0:T(128)}, u32[]{:S(2)}) copy-start(s32[5]{0:T(128)} %copy-done.8) | copy-start | bytes 64
  70.5 16.3 %all-to-all-start.1 = ((f32[128,1,128]{2,1,0:T(1,128)}), f32[128,1,128]{2,1,0:T(1,128)S(1)}, u32[]{:S(2)}, u32[]{:S(2)}) async-start(f32[128,1,128]{2,1,0:T(1,128)} %bitcast.18), calls=%async_computation.1 | async-start | bytes 131072 | tf_op jit(solution)/shard_map/all_to_all | solution.py:654
  78.4 14.7 %copy-start.3 = (f32[512,256]{1,0:T(8,128)}, f32[512,256]{1,0:T(8,128)S(1)}, u32[]{:S(2)}) copy-start(f32[512,256]{1,0:T(8,128)S(1)} %shard_map.143.grad_hidden) | copy-start | bytes 1572868
  86.8 11.2 %copy-start.12 = (f32[256]{0:T(256)S(1)}, f32[256]{0:T(256)}, u32[]{:S(2)}) copy-start(f32[256]{0:T(256)} %param.19) | copy-start | bytes 3076
  89.3 2.6 %collective-permute-start.9 = (bf16[2320,128]{1,0:T(8,128)(2,1)S(1)}, bf16[2320,128]{1,0:T(8,128)(2,1)S(1)}, u32[]{:S(2)}, u32[]{:S(2)}) collective-permute-start(bf16[2320,128]{1,0:T(8,128)(2,1)S(1)} %get-tuple-element.34), channel_id=1, source_target_pairs={{1,0},{0,1},{3,2},{2,3},{5,4},{4,5},{7,6},{6,7},{9,8},{8,9},{11,10... | collective-permute-start | bytes 1781768 | tf_op jit(solution)/shard_map/ppermute | solution.py:605
  93.1 20.1 %all-to-all-start.2 = ((bf16[64,48,128]{2,1,0:T(8,128)(2,1)}), bf16[64,48,128]{2,1,0:T(8,128)(2,1)S(1)}, u32[]{:S(2)}, u32[]{:S(2)}) async-start(bf16[64,48,128]{2,1,0:T(8,128)(2,1)} %shard_map.145), calls=%async_computation.2 | async-start | bytes 1572864 | tf_op jit(solution)/shard_map/all_to_all | solution.py:663
  98.0 20.9 %copy-start.4 = (f32[512,256]{1,0:T(8,128)S(1)}, f32[512,256]{1,0:T(8,128)}, u32[]{:S(2)}) copy-start(f32[512,256]{1,0:T(8,128)} %copy-done.3) | copy-start | bytes 1572868
  98.0 1.2 copy-start.5
  114.2 17.5 %all-to-all-start.3 = ((bf16[64,40,128]{2,1,0:T(8,128)(2,1)}), bf16[64,40,128]{2,1,0:T(8,128)(2,1)S(1)}, u32[]{:S(2)}, u32[]{:S(2)}) async-start(bf16[64,40,128]{2,1,0:T(8,128)(2,1)} %get-tuple-element.38), calls=%async_computation.3 | async-start | bytes 1310720 | tf_op jit(solution)/shard_map/all_to_all | solution.py:668
  131.7 4.6 %collective-permute-start.10 = (bf16[64,40,128]{2,1,0:T(8,128)(2,1)S(1)}, bf16[64,40,128]{2,1,0:T(8,128)(2,1)S(1)}, u32[]{:S(2)}, u32[]{:S(2)}) collective-permute-start(bf16[64,40,128]{2,1,0:T(8,128)(2,1)S(1)} %all-to-all-done.3.mine), channel_id=1, source_target_pairs={{1,0},{0,1},{3,2},{2,3},{5,4},{4,5},{7,6},{6,7},{9,8},{8,9},{11,10... | collective-permute-start | bytes 1966088 | tf_op jit(solution)/shard_map/ppermute | solution.py:605

commit v6 on v5

--- a/solution.py
+++ b/solution.py
@@ -74,6 +74,10 @@
 
 def iota(shape, dim):
     return lax.broadcasted_iota(jnp.int32, shape, dim)
+
+
+def flag(flags, index, shape):
+    return jnp.broadcast_to(flags[index : index + 1, : shape[1]], shape) == 1
 
 
 def split3(value):
@@ -314,10 +318,10 @@
     cell = iota((CELLS_IN, C), 0)
     col = lax.rem(cell, 10)
     outside = (
-        ((cell < 10) & (flags[0] == 1))
-        | ((cell >= 170) & (flags[1] == 1))
-        | ((col == 0) & (flags[2] == 1))
-        | ((col == 9) & (flags[3] == 1))
+        ((cell < 10) & flag(flags, 0, cell.shape))
+        | ((cell >= 170) & flag(flags, 1, cell.shape))
+        | ((col == 0) & flag(flags, 2, cell.shape))
+        | ((col == 9) & flag(flags, 3, cell.shape))
         | (cell >= 180)
     )
     merged = jnp.where(outside, 0.0, merged).astype(BF16)
@@ -335,7 +339,7 @@
             jax.ShapeDtypeStruct((CELLS_IN, C), BF16),
             jax.ShapeDtypeStruct((128, 128), F32),
         ),
-        in_specs=[pl.BlockSpec(memory_space=pltpu.SMEM), vmem, vmem, vmem, HBM, HBM, vmem],
+        in_specs=[pl.BlockSpec(memory_space=pltpu.VMEM), vmem, vmem, vmem, HBM, HBM, vmem],
         out_specs=(vmem, vmem),
         scratch_shapes=[
             pltpu.VMEM((PART + CELLS_IN, C), BF16),
@@ -391,11 +395,13 @@
         xhat = (field - mean) * inverse
         shifted = xhat * gain[...] + bias[...]
         sig = 0.5 * jnp.tanh(0.5 * shifted) + 0.5
-        outside = ((row < 16) & (flags[0] == 1)) | ((row >= 528) & (flags[1] == 1))
+        outside = ((row < 16) & flag(flags, 0, row.shape)) | (
+            (row >= 528) & flag(flags, 1, row.shape)
+        )
         if b == 0:
-            outside = outside | ((col == 0) & (flags[2] == 1))
+            outside = outside | ((col == 0) & flag(flags, 2, row.shape))
         if b == 2:
-            outside = outside | ((col == 15) & (flags[3] == 1))
+            outside = outside | ((col == 15) & flag(flags, 3, row.shape))
         hidden[b] = jnp.where(outside, 0.0, shifted * sig).astype(BF16)
         if b == 1:
             inner = slice(16, 528)
@@ -413,14 +419,14 @@
             given[2304:, :] = tail
     keep = pltpu.make_async_copy(hidden, hidden_far, sem)
     keep.start()
-    first = flags[4] == 0
+    second = flag(flags, 4, (C, 128))
     for a in range(3):
         for b in range(3):
             rows = slice((3 * a + b) * C, (3 * a + b + 1) * C)
             product = dot(hidden[b, 16 * a : 16 * a + 512, :], cot[...], ((0,), (0,)))
-            left, right = product[:, :128].astype(BF16), product[:, 128:].astype(BF16)
-            kept[rows, :] = jnp.where(first, left, right)
-            given[rows, :] = jnp.where(first, right, left)
+            left, right = product[:, :128], product[:, 128:]
+            kept[rows, :] = jnp.where(second, right, left).astype(BF16)
+            given[rows, :] = jnp.where(second, left, right).astype(BF16)
     keep.wait()
 
 
@@ -433,7 +439,7 @@
             jax.ShapeDtypeStruct((2320, 128), BF16),
             pltpu.HBM((3, WIN, C), BF16),
         ),
-        in_specs=[pl.BlockSpec(memory_space=pltpu.SMEM)] + [vmem] * 7,
+        in_specs=[pl.BlockSpec(memory_space=pltpu.VMEM)] + [vmem] * 7,
         out_specs=(vmem, vmem, HBM),
         scratch_shapes=[pltpu.VMEM((3, WIN, C), BF16), pltpu.SemaphoreType.DMA],
         compiler_params=params(),
@@ -459,16 +465,17 @@
     )(hidden, weight, conv_bias)
 
 
-def pair_kernel(kept, got, out_far, total, out, sems):
+def pair_kernel(flags, kept, got, out_far, total, out, sems):
     total[...] = kept[...].astype(F32) + got[...].astype(F32)
     tails = [r[2304:, :].astype(F32) for r in (kept, got)]
     sums = sum(t[0:4] + t[4:8] + t[8:12] for t in tails)
-    parts = [p.astype(F32) for p in split3(sums)]
+    sums = jnp.where(flag(flags, 4, (2, 128)), sums[2:4], sums[0:2])
+    parts = [p.astype(F32) for p in split3(sums)[:2]]
     tail = jnp.concatenate([jnp.zeros((36, 128), F32)] + parts, axis=0)
-    own = iota((48, 128), 0) < 36
+    own = iota((40, 128), 0) < 36
     copies = []
     for i in range(64):
-        out[i] = jnp.where(own, total[36 * i : 36 * i + 48, :], tail).astype(BF16)
+        out[i] = jnp.where(own, total[36 * i : 36 * i + 40, :], tail).astype(BF16)
         if i % 16 == 15:
             part = pl.ds(i - 15, 16)
             copies.append(pltpu.make_async_copy(out.at[part], out_far.at[part], sems.at[i // 16]))
@@ -477,23 +484,28 @@
         copy.wait()
 
 
-def pair_sum(kept, got):
+def pair_sum(flags, kept, got):
     return pl.pallas_call(
         pair_kernel,
-        out_shape=pltpu.HBM((64, 48, 128), BF16),
+        out_shape=pltpu.HBM((64, 40, 128), BF16),
+        in_specs=[
+            pl.BlockSpec(memory_space=pltpu.VMEM),
+            pl.BlockSpec(memory_space=pltpu.VMEM),
+            pl.BlockSpec(memory_space=pltpu.VMEM),
+        ],
         out_specs=HBM,
         scratch_shapes=[
             pltpu.VMEM((2320, 128), F32),
-            pltpu.VMEM((64, 48, 128), BF16),
+            pltpu.VMEM((64, 40, 128), BF16),
             pltpu.SemaphoreType.DMA((4,)),
         ],
         compiler_params=params(),
-    )(kept, got)
+    )(flags, kept, got)
 
 
 def share_kernel(got, out_far, sums, chunk, sems):
     total = jnp.sum(got[...].astype(F32), axis=0)
-    chunk[...] = jnp.broadcast_to((total[:40] * (1.0 / 256.0)).astype(BF16)[None], chunk.shape)
+    chunk[...] = jnp.broadcast_to((total * (1.0 / 256.0)).astype(BF16)[None], chunk.shape)
     size = chunk.shape[0]
     copies = [
         pltpu.make_async_copy(chunk, out_far.at[pl.ds(size * i, size)], sems.at[i])
@@ -501,10 +513,9 @@
     ]
     for copy in copies:
         copy.start()
-    quarters = total[36:40] + total[40:44] + total[44:48]
-    weight = jnp.concatenate([quarters[0:1], quarters[1:2]], axis=1)
-    shift_sum = jnp.concatenate([quarters[2:3], quarters[3:4]], axis=1)
-    sums[...] = jnp.concatenate([weight, shift_sum, jnp.zeros((6, C), F32)], axis=0)
+    halves = total[36:38] + total[38:40]
+    row = jnp.concatenate([halves[0:1], halves[1:2]], axis=1)
+    sums[...] = jnp.broadcast_to(row, sums.shape)
     for copy in copies:
         copy.wait()
 
@@ -521,7 +532,13 @@
     )(got)
 
 
-def field_kernel(merged, up, stats, gain, bias, grad_hidden, sums, field_out, norm_out):
+def field_kernel(
+    flags, merged, up, stats, gain, bias, grad_hidden, mine, other, field_out, norm_out
+):
+    second = flag(flags, 4, (8, C))
+    weight = jnp.where(second, other[...], mine[...])
+    plain = jnp.where(second, mine[...], other[...])
+    sums = jnp.where(iota((8, C), 0) == 0, weight, plain)
     mean, inverse = combine_groups(stats[...])
     value = dot(up[WIN + 16 : WIN + 528, :], merged[...])
     xhat = (value - mean) * inverse
@@ -529,28 +546,30 @@
     sig = 0.5 * jnp.tanh(0.5 * shifted) + 0.5
     grad_shift = grad_hidden[...] * sig * (1.0 + shifted * (1.0 - sig))
     same = jnp.where((iota((C, C), 0) >> 3) == (iota((C, C), 1) >> 3), 1.0, 0.0)
-    means = dot_exact(sums[...] * gain[...], same) * (1.0 / (65536 * SHARE))
+    means = dot_exact(sums * gain[...], same) * (1.0 / (65536 * SHARE))
     field = inverse * (grad_shift * gain[...] - means[1:2] - xhat * means[0:1])
     field_out[...] = field.astype(BF16)
     norm_out[...] = sums[:2] * (1.0 / 256.0)
 
 
-def field_gradient(merged, up, stats, gain, bias, grad_hidden, sums):
+def field_gradient(flags, merged, up, stats, gain, bias, grad_hidden, mine, other):
+    vmem = pl.BlockSpec(memory_space=pltpu.VMEM)
     return pl.pallas_call(
         field_kernel,
         out_shape=(
             jax.ShapeDtypeStruct((512, C), BF16),
             jax.ShapeDtypeStruct((2, C), F32),
         ),
+        in_specs=[pl.BlockSpec(memory_space=pltpu.VMEM)] + [vmem] * 8,
         compiler_params=params(),
         cost_estimate=pl.CostEstimate(
             flops=10**9, bytes_accessed=2 * 10**6, transcendentals=2 * 10**5
         ),
-    )(merged, up, stats, gain, bias, grad_hidden, sums)
+    )(flags, merged, up, stats, gain, bias, grad_hidden, mine, other)
 
 
 def layout_kernel(flags, mine, other, out_far, out, sems):
-    first = flags[4] == 0
+    second = flag(flags, 4, (72, 128))
     copies = []
     for i in range(0, 64, 2):
         halves = []
@@ -558,8 +577,8 @@
             pair = [ref[i + k].astype(F32)[:36] for k in range(2)]
             halves.append(jnp.concatenate(pair, axis=0))
         rows = slice(36 * i, 36 * i + 72)
-        out[rows, :128] = jnp.where(first, halves[0], halves[1])
-        out[rows, 128:] = jnp.where(first, halves[1], halves[0])
+        out[rows, :128] = jnp.where(second, halves[1], halves[0])
+        out[rows, 128:] = jnp.where(second, halves[0], halves[1])
         if i % 8 == 6:
             part = pl.ds(36 * (i - 6), 288)
             copies.append(pltpu.make_async_copy(out.at[part], out_far.at[part], sems.at[i // 8]))
@@ -573,14 +592,17 @@
     return pl.pallas_call(
         layout_kernel,
         out_shape=pltpu.HBM((2304, C), F32),
-        in_specs=[pl.BlockSpec(memory_space=pltpu.SMEM), vmem, vmem],
+        in_specs=[pl.BlockSpec(memory_space=pltpu.VMEM), vmem, vmem],
         out_specs=HBM,
         scratch_shapes=[pltpu.VMEM((2304, C), F32), pltpu.SemaphoreType.DMA((8,))],
         compiler_params=params(),
     )(flags, mine, other)
 
 
-def copies_kernel(cells, out_far, sems):
+def copies_kernel(cells_far, out_far, cells, sem, sems):
+    load = pltpu.make_async_copy(cells_far, cells, sem)
+    load.start()
+    load.wait()
     copies = [
         pltpu.make_async_copy(cells, out_far.at[i], sems.at[i]) for i in range(out_far.shape[0])
     ]
@@ -594,11 +616,15 @@
     return pl.pallas_call(
         copies_kernel,
         out_shape=pltpu.HBM((16, 128, C), BF16),
-        in_specs=[pl.BlockSpec(memory_space=pltpu.VMEM)],
+        in_specs=[HBM],
         out_specs=HBM,
-        scratch_shapes=[pltpu.SemaphoreType.DMA((16,))],
-        compiler_params=params(),
-    )(cells)
+        scratch_shapes=[
+            pltpu.VMEM((128, C), BF16),
+            pltpu.SemaphoreType.DMA,
+            pltpu.SemaphoreType.DMA((16,)),
+        ],
+        compiler_params=params(),
+    )(in_hbm(cells))
 
 
 def shift(value, axis, count, step):
@@ -619,7 +645,8 @@
 ):
     y, c = lax.axis_index("y"), lax.axis_index("c")
     block = lax.axis_index(ZXC)
-    flags = jnp.stack([y == 0, y == 3, block == 0, block == 31, c == 1]).astype(jnp.int32)
+    marks = [y == 0, y == 3, block == 0, block == 31, c == 1, c == 1, c == 1, c == 1]
+    flags = jnp.broadcast_to(jnp.stack(marks).astype(jnp.int32)[:, None], (8, C))
     up = jnp.asarray(UPSAMPLE, BF16)
     taps = conv_weight.reshape(9, C, C)
 
@@ -659,14 +686,16 @@
         flags, merged, up, stats2, gain2, bias2, cotangent.reshape(512, C), grad_hidden
     )
 
-    sent = pair_sum(kept, shift(given, "c", 2, 1))
+    sent = pair_sum(flags, kept, shift(given, "c", 2, 1))
     got = lax.all_to_all(sent, ("y", "z", "x"), 0, 0, tiled=True)
     fine = conv(hidden, taps, conv_bias[None])
     got, fine = lax.optimization_barrier((got, fine))
 
     chunk, sums = share_sum(got)
     spread = lax.all_to_all(chunk, ("y", "z", "x"), 0, 0, tiled=True)
-    field, grad_norm = field_gradient(merged, up, stats2, gain2, bias2, grad_hidden, sums)
+    field, grad_norm = field_gradient(
+        flags, merged, up, stats2, gain2, bias2, grad_hidden, sums, shift(sums, "c", 2, 1)
+    )
     spread, field = lax.optimization_barrier((spread, field))
     grad_conv = lay_out(flags, spread, shift(spread, "c", 2, 1)).reshape(3, 3, C, C)
     return (

time: 139 us -> 137 us (0.986)
  waiting for transfers between devices: 53.3 us -> 50.1 us
  starting transfers between devices: 45 us -> 46.9 us
    all_to_all x1, waiting for transfers between devices: 11.5 us -> 8.74 us  [per_device(): spread = lax.all_to_all(chunk, ('y', 'z', 'x'), 0, 0, tiled=True)]
    ppermute x9 -> x10, starting transfers between devices: 13.8 us -> 15.7 us  [shift(): lax.ppermute(value, axis, [((i + step) % count, i) for i in range(count)])]
    ppermute x9 -> x10, waiting for transfers between devices: 11.4 us -> 12.3 us  [shift(): lax.ppermute(value, axis, [((i + step) % count, i) for i in range(count)])]
  transfers between devices with their start and end apart: 15 -> 16, of which waited for: 10 -> 11; matrix products, arithmetic and copies ran while one was open for 2% -> 2% of each run, Pallas kernels for 3% -> 3%
where the time goes in v6:
time: 137 us; the launch traced here: 136 us
  waiting for transfers between devices  50.1 us (37%)
  starting transfers between devices  46.9 us (34%)
  Pallas kernels  34.5 us (25%)
  local copies, waits for them, and re-layouts  2.41 us (2%)
    pallas_call x1, Pallas kernels, partial_attention(): pl.pallas_call(attention_kernel, out_shape=(jax.ShapeDtypeStruct((PART, C...  17.6 us
    ppermute x10, starting transfers between devices, shift(): lax.ppermute(value, axis, [((i + step) % count, i) for i in range(count)])  15.7 us
    ppermute x10, waiting for transfers between devices, shift(): lax.ppermute(value, axis, [((i + step) % count, i) for i in range(count)])  12.3 us
    all_to_all x1, waiting for transfers between devices, per_device(): got = lax.all_to_all(sent, ('y', 'z', 'x'), 0, 0, tiled=True)  11.2 us
    all_to_all x1, waiting for transfers between devices, per_device(): lax.all_to_all(copies_of(own), ('z', 'x'), 0, 0, tiled=True)  9.44 us
    all_to_all x1, waiting for transfers between devices, per_device(): spread = lax.all_to_all(chunk, ('y', 'z', 'x'), 0, 0, tiled=True)  8.74 us
    all_to_all x1, starting transfers between devices, per_device(): lax.all_to_all(copies_of(own), ('z', 'x'), 0, 0, tiled=True)  8.44 us
    all_to_all x1, waiting for transfers between devices, per_device(): stats2 = lax.all_to_all(stats2.reshape(128, 1, 128), ALL, 0, 0, tiled=True)  8.42 us
  transfers between devices with their start and end apart: 16, of which 11 were waited for; matrix products, arithmetic and copies ran while one was open for 2% of the time, Pallas kernels for 3%

profile of v6, /device:TPU:1, one launch (start us, length us, event | category | flops | bytes accessed | tf_op | source)
XLA Modules:
  0.0 136.2 jit_solution(13469332012694167239)
XLA Ops:
  0.7 2.0 %shard_map.138 = bf16[16,128,256]{2,1,0:T(8,128)(2,1)} custom-call(bf16[128,256]{1,0:T(8,128)(2,1)} %bitcast.67), custom_call_target="tpu_custom_call" | custom-call | tf_op jit(solution)/shard_map/pallas_call | solution.py:616
  2.6 8.4 %all-to-all-start = ((bf16[16,128,256]{2,1,0:T(8,128)(2,1)}), bf16[16,128,256]{2,1,0:T(8,128)(2,1)S(1)}, u32[]{:S(2)}, u32[]{:S(2)}) async-start(bf16[16,128,256]{2,1,0:T(8,128)(2,1)} %shard_map.138), calls=%async_computation | async-start | bytes 2097152 | tf_op jit(solution)/shard_map/all_to_all | solution.py:654
  11.2 0.1 fusion.14
  11.3 2.9 %collective-permute-start.2 = (bf16[48,256]{1,0:T(8,128)(2,1)S(1)}, bf16[48,256]{1,0:T(8,128)(2,1)S(1)}, u32[]{:S(2)}, u32[]{:S(2)}) collective-permute-start(bf16[48,256]{1,0:T(8,128)(2,1)S(1)} %pad_maximum_fusion.3), channel_id=1, source_target_pairs={{1,0},{2,1},{3,2},{4,3},{5,4},{6,5},{7,6},{8,7},{9,8},{10,9},{11,1... | collective-permute-start | bytes 73736 | tf_op jit(solution)/shard_map/ppermute | solution.py:660
  14.2 3.4 %collective-permute-start.1 = (bf16[48,256]{1,0:T(8,128)(2,1)S(1)}, bf16[48,256]{1,0:T(8,128)(2,1)S(1)}, u32[]{:S(2)}, u32[]{:S(2)}) collective-permute-start(bf16[48,256]{1,0:T(8,128)(2,1)S(1)} %pad_maximum_fusion.2), channel_id=1, source_target_pairs={{0,1},{1,2},{2,3},{3,4},{4,5},{5,6},{6,7},{7,8},{8,9},{9,10},{10,1... | collective-permute-start | bytes 73736 | tf_op jit(solution)/shard_map/ppermute | solution.py:659
  17.6 9.4 %all-to-all-done = bf16[16,128,256]{2,1,0:T(8,128)(2,1)S(1)} async-done(((bf16[16,128,256]{2,1,0:T(8,128)(2,1)}), bf16[16,128,256]{2,1,0:T(8,128)(2,1)S(1)}, u32[]{:S(2)}, u32[]{:S(2)}) %all-to-all-start) | async-done | bytes 1048608 | tf_op jit(solution)/shard_map/all_to_all | solution.py:654
  27.1 2.6 %collective-permute-start = (bf16[2048,256]{1,0:T(8,128)(2,1)S(1)}, bf16[2048,256]{1,0:T(8,128)(2,1)S(1)}, u32[]{:S(2)}, u32[]{:S(2)}) collective-permute-start(bf16[2048,256]{1,0:T(8,128)(2,1)S(1)} %bitcast.48), channel_id=1, source_target_pairs={{1,0},{0,1},{3,2},{2,3},{5,4},{4,5},{7,6},{6,7},{9,8},{8,9},{11,10... | collective-permute-start | bytes 3145736 | tf_op jit(solution)/shard_map/ppermute | solution.py:631
  29.9 0.1 pad_maximum_fusion.1
  30.0 0.9 shard_map.139.first
  30.9 0.0 copy-start.1
  30.9 1.1 collective-permute-done.other
  32.0 1.6 %shard_map.140 = (bf16[208,256]{1,0:T(8,128)(2,1)S(1)}, bf16[208,256]{1,0:T(8,128)(2,1)}, bf16[176,256]{1,0:T(8,128)(2,1)}) custom-call(f32[8,256]{1,0:T(8,128)S(1)} %shard_map.139.first, bf16[2048,256]{1,0:T(8,128)(2,1)S(1)} %collective-permute-done.other, bf16[160,256]{1,0:T(8,128)(2,1)S(1)} %reshape.118.wide, bf16[2,32,256]{2,1,0:T(8,128)(2,1)S(1)} %pad.4.edges), custom_call_target="tpu_custom_call" | custom-call | tf_op jit(solution)/shard_map/pallas_call | solution.py:153
  33.6 1.3 collective-permute-start.5
  34.8 1.4 %collective-permute-start.4 = (bf16[208,256]{1,0:T(8,128)(2,1)S(1)}, bf16[208,256]{1,0:T(8,128)(2,1)S(1)}, u32[]{:S(2)}, u32[]{:S(2)}) collective-permute-start(bf16[208,256]{1,0:T(8,128)(2,1)S(1)} %get-tuple-element.24.near), channel_id=1, source_target_pairs={{32,0},{64,32},{96,64},{0,96},{33,1},{65,33},{97,65},{1,97},{34,2}... | collective-permute-start | bytes 319496 | tf_op jit(solution)/shard_map/ppermute | solution.py:631
  36.3 1.6 %collective-permute-start.3 = (bf16[176,256]{1,0:T(8,128)(2,1)}, bf16[176,256]{1,0:T(8,128)(2,1)}, u32[]{:S(2)}, u32[]{:S(2)}) collective-permute-start(bf16[176,256]{1,0:T(8,128)(2,1)} %get-tuple-element.25), channel_id=1, source_target_pairs={{64,0},{96,32},{0,64},{32,96},{65,1},{97,33},{1,65},{33,97},{66,2}... | collective-permute-start | bytes 270344 | tf_op jit(solution)/shard_map/ppermute | solution.py:631
  37.9 0.7 stack.29
  38.6 0.7 convert_element_type.12
  39.3 3.1 %collective-permute-done.3.far = bf16[176,256]{1,0:T(8,128)(2,1)} collective-permute-done((bf16[176,256]{1,0:T(8,128)(2,1)}, bf16[176,256]{1,0:T(8,128)(2,1)}, u32[]{:S(2)}, u32[]{:S(2)}) %collective-permute-start.3) | collective-permute-done | bytes 90144 | tf_op jit(solution)/shard_map/ppermute | solution.py:631
  42.4 17.6 %shard_map.141 = (bf16[208,256]{1,0:T(8,128)(2,1)S(1)}, bf16[208,256]{1,0:T(8,128)(2,1)S(1)}, bf16[208,256]{1,0:T(8,128)(2,1)S(1)}, bf16[400,256]{1,0:T(8,128)(2,1)}) custom-call(bf16[2048,256]{1,0:T(8,128)(2,1)S(1)} %bitcast.50, bf16[2048,256]{1,0:T(8,128)(2,1)S(1)} %collective-permute-done.other, bf16[208,256]{1,0:T(8,128)(2,1)S(1)} %get-tuple-element.24.near, ...), custom_call_target="tpu_custom_call" | custom-call | tf_op jit(solution)/shard_map/pallas_call | solution.py:270
  60.0 0.2 collective-permute-start.6
  60.2 1.8 %collective-permute-start.7 = (bf16[208,256]{1,0:T(8,128)(2,1)S(1)}, bf16[208,256]{1,0:T(8,128)(2,1)S(1)}, u32[]{:S(2)}, u32[]{:S(2)}) collective-permute-start(bf16[208,256]{1,0:T(8,128)(2,1)S(1)} %get-tuple-element.28), channel_id=1, source_target_pairs={{64,0},{96,32},{0,64},{32,96},{65,1},{97,33},{1,65},{33,97},{66,2}... | collective-permute-start | bytes 319496 | tf_op jit(solution)/shard_map/ppermute | solution.py:631
  62.1 0.9 collective-permute-start.8
  63.0 0.2 pad_maximum_fusion
  63.2 3.5 %collective-permute-done.6.p1 = bf16[208,256]{1,0:T(8,128)(2,1)S(1)} collective-permute-done((bf16[208,256]{1,0:T(8,128)(2,1)S(1)}, bf16[208,256]{1,0:T(8,128)(2,1)S(1)}, u32[]{:S(2)}, u32[]{:S(2)}) %collective-permute-start.6) | collective-permute-done | bytes 106528 | tf_op jit(solution)/shard_map/ppermute | solution.py:631
  66.8 0.4 collective-permute-done.8.p3
  67.2 0.1 broadcast_in_dim.34.flags
  67.2 2.8 %shard_map.142 = (bf16[192,256]{1,0:T(8,128)(2,1)S(1)}, f32[128,128]{1,0:T(8,128)}) custom-call(s32[8,256]{1,0:T(8,128)S(1)} %broadcast_in_dim.34.flags, bf16[208,256]{1,0:T(8,128)(2,1)S(1)} %collective-permute-done.6.p1, bf16[208,256]{1,0:T(8,128)(2,1)S(1)} %collective-permute-done.7.p2, bf16[208,256]{1,0:T(8,128)(2,1)S(1)} %collective-permute-done.8.p3, ...), custom_call_target="tpu_custom_call" | custom-call | tf_op jit(solution)/shard_map/pallas_call | solution.py:336
  70.0 6.9 %all-to-all-start.1 = ((f32[128,1,128]{2,1,0:T(1,128)}), f32[128,1,128]{2,1,0:T(1,128)S(1)}, u32[]{:S(2)}, u32[]{:S(2)}) async-start(f32[128,1,128]{2,1,0:T(1,128)} %bitcast.18), calls=%async_computation.1 | async-start | bytes 131072 | tf_op jit(solution)/shard_map/all_to_all | solution.py:681
  77.0 0.2 fusion.13
  77.1 0.8 shard_map.143.grad_hidden
  78.0 8.4 %all-to-all-done.1 = f32[128,1,128]{2,1,0:T(1,128)S(1)} async-done(((f32[128,1,128]{2,1,0:T(1,128)}), f32[128,1,128]{2,1,0:T(1,128)S(1)}, u32[]{:S(2)}, u32[]{:S(2)}) %all-to-all-start.1) | async-done | bytes 65568 | tf_op jit(solution)/shard_map/all_to_all | solution.py:681
  86.4 2.4 %shard_map.144 = (bf16[2320,128]{1,0:T(8,128)(2,1)S(1)}, bf16[2320,128]{1,0:T(8,128)(2,1)S(1)}, bf16[3,544,256]{2,1,0:T(8,128)(2,1)}) custom-call(s32[8,256]{1,0:T(8,128)S(1)} %broadcast_in_dim.34.flags, bf16[192,256]{1,0:T(8,128)(2,1)S(1)} %get-tuple-element.31.merged, bf16[1632,192]{1,0:T(8,128)(2,1)S(1)} %copy-done.1, f32[128,128]{1,0:T(8,128)S(1)} %bitcast.57, ...), custom_call_target="tpu_custom_call" | custom-call | tf_op jit(solution)/shard_map/pallas_call | solution.py:435
  88.8 0.9 collective-permute-start.9
  89.8 1.6 %collective-permute-done.9.got = bf16[2320,128]{1,0:T(8,128)(2,1)S(1)} collective-permute-done((bf16[2320,128]{1,0:T(8,128)(2,1)S(1)}, bf16[2320,128]{1,0:T(8,128)(2,1)S(1)}, u32[]{:S(2)}, u32[]{:S(2)}) %collective-permute-start.9) | collective-permute-done | bytes 593952 | tf_op jit(solution)/shard_map/ppermute | solution.py:631
  91.4 1.1 shard_map.145
  92.5 4.9 %all-to-all-start.2 = ((bf16[64,40,128]{2,1,0:T(8,128)(2,1)}), bf16[64,40,128]{2,1,0:T(8,128)(2,1)S(1)}, u32[]{:S(2)}, u32[]{:S(2)}) async-start(bf16[64,40,128]{2,1,0:T(8,128)(2,1)} %shard_map.145), calls=%async_computation.2 | async-start | bytes 1310720 | tf_op jit(solution)/shard_map/all_to_all | solution.py:690
  97.5 1.2 copy-done.5
  98.6 1.5 %shard_map.146 = bf16[512,256]{1,0:T(8,128)(2,1)} custom-call(bf16[3,544,256]{2,1,0:T(8,128)(2,1)S(1)} %copy-done.5, bf16[9,256,256]{2,1,0:T(8,128)(2,1)S(1)} %bitcast.52, f32[1,256]{1,0:T(1,128)S(1)} %bitcast.61), custom_call_target="tpu_custom_call" | custom-call | flops 603979776 | bytes 3000000 | tf_op jit(solution)/shard_map/pallas_call | solution.py:458
  100.1 11.2 %all-to-all-done.2.got = bf16[64,40,128]{2,1,0:T(8,128)(2,1)S(1)} async-done(((bf16[64,40,128]{2,1,0:T(8,128)(2,1)}), bf16[64,40,128]{2,1,0:T(8,128)(2,1)S(1)}, u32[]{:S(2)}, u32[]{:S(2)}) %all-to-all-start.2) | async-done | bytes 655392 | tf_op jit(solution)/shard_map/all_to_all | solution.py:690
  111.3 1.0 shard_map.147
  112.3 4.7 %all-to-all-start.3 = ((bf16[64,40,128]{2,1,0:T(8,128)(2,1)}), bf16[64,40,128]{2,1,0:T(8,128)(2,1)S(1)}, u32[]{:S(2)}, u32[]{:S(2)}) async-start(bf16[64,40,128]{2,1,0:T(8,128)(2,1)} %get-tuple-element.38), calls=%async_computation.3 | async-start | bytes 1310720 | tf_op jit(solution)/shard_map/all_to_all | solution.py:695
  117.0 1.9 %collective-permute-start.10 = (f32[8,256]{1,0:T(8,128)S(1)}, f32[8,256]{1,0:T(8,128)S(1)}, u32[]{:S(2)}, u32[]{:S(2)}) collective-permute-start(f32[8,256]{1,0:T(8,128)S(1)} %get-tuple-element.39.mine), channel_id=1, source_target_pairs={{1,0},{0,1},{3,2},{2,3},{5,4},{4,5},{7,6},{6,7},{9,8},{8,9},{11,10... | collective-permute-start | bytes 24584 | tf_op jit(solution)/shard_map/ppermute | solution.py:631
  118.9 0.8 collective-permute-done.10.other
  119.7 1.4 %shard_map.148 = (bf16[512,256]{1,0:T(8,128)(2,1)}, f32[2,256]{1,0:T(2,128)}) custom-call(s32[8,256]{1,0:T(8,128)S(1)} %broadcast_in_dim.34.flags, bf16[192,256]{1,0:T(8,128)(2,1)S(1)} %get-tuple-element.31.merged, bf16[1632,192]{1,0:T(8,128)(2,1)S(1)} %copy-done.1, f32[128,128]{1,0:T(8,128)S(1)} %bitcast.58, f32[1,256]{1,0:T(1,128)S(1)} %bitcast.63, ...), custom_call_target="tpu_custom_call" | custom-call | flops 1000000000 | bytes 2000000 | tf_op jit(solution)/shard_map/pallas_call | solution.py:557
  121.1 8.7 %all-to-all-done.3.mine = bf16[64,40,128]{2,1,0:T(8,128)(2,1)S(1)} async-done(((bf16[64,40,128]{2,1,0:T(8,128)(2,1)}), bf16[64,40,128]{2,1,0:T(8,128)(2,1)S(1)}, u32[]{:S(2)}, u32[]{:S(2)}) %all-to-all-start.3) | async-done | bytes 655392 | tf_op jit(solution)/shard_map/all_to_all | solution.py:695
  129.9 2.9 %collective-permute-start.11 = (bf16[64,40,128]{2,1,0:T(8,128)(2,1)S(1)}, bf16[64,40,128]{2,1,0:T(8,128)(2,1)S(1)}, u32[]{:S(2)}, u32[]{:S(2)}) collective-permute-start(bf16[64,40,128]{2,1,0:T(8,128)(2,1)S(1)} %all-to-all-done.3.mine), channel_id=1, source_target_pairs={{1,0},{0,1},{3,2},{2,3},{5,4},{4,5},{7,6},{6,7},{9,8},{8,9},{11,10... | collective-permute-start | bytes 1966088 | tf_op jit(solution)/shard_map/ppermute | solution.py:631
  132.8 1.7 %collective-permute-done.11.other = bf16[64,40,128]{2,1,0:T(8,128)(2,1)S(1)} collective-permute-done((bf16[64,40,128]{2,1,0:T(8,128)(2,1)S(1)}, bf16[64,40,128]{2,1,0:T(8,128)(2,1)S(1)}, u32[]{:S(2)}, u32[]{:S(2)}) %collective-permute-start.11) | collective-permute-done | bytes 655392 | tf_op jit(solution)/shard_map/ppermute | solution.py:631
  134.5 1.5 %shard_map.149 = f32[2304,256]{1,0:T(8,128)} custom-call(s32[8,256]{1,0:T(8,128)S(1)} %broadcast_in_dim.34.flags, bf16[64,40,128]{2,1,0:T(8,128)(2,1)S(1)} %all-to-all-done.3.mine, bf16[64,40,128]{2,1,0:T(8,128)(2,1)S(1)} %collective-permute-done.11.other), custom_call_target="tpu_custom_call" | custom-call | tf_op jit(solution)/shard_map/pallas_call | solution.py:592
  (51 shorter events, 0.3 us)
Async XLA Ops:
  0.6 10.5 %copy-start.11 = (bf16[16,8,256]{2,1,0:T(8,128)(2,1)S(1)}, bf16[16,8,256]{2,1,0:T(8,128)(2,1)}, u32[]{:S(2)}) copy-start(bf16[16,8,256]{2,1,0:T(8,128)(2,1)} %param.11) | copy-start | bytes 196612
  0.6 10.5 %copy-start.2 = (bf16[32,16,256]{2,1,0:T(8,128)(2,1)S(1)}, bf16[32,16,256]{2,1,0:T(8,128)(2,1)}, u32[]{:S(2)}) copy-start(bf16[32,16,256]{2,1,0:T(8,128)(2,1)} %param.20) | copy-start | bytes 786436
  2.6 24.4 %all-to-all-start = ((bf16[16,128,256]{2,1,0:T(8,128)(2,1)}), bf16[16,128,256]{2,1,0:T(8,128)(2,1)S(1)}, u32[]{:S(2)}, u32[]{:S(2)}) async-start(bf16[16,128,256]{2,1,0:T(8,128)(2,1)} %shard_map.138), calls=%async_computation | async-start | bytes 2097152 | tf_op jit(solution)/shard_map/all_to_all | solution.py:654
  11.1 31.3 %copy-start.6 = (f32[256]{0:T(256)S(1)}, f32[256]{0:T(256)}, u32[]{:S(2)}) copy-start(f32[256]{0:T(256)} %param.12) | copy-start | bytes 3076
  11.1 31.3 %copy-start.7 = (f32[256]{0:T(256)S(1)}, f32[256]{0:T(256)}, u32[]{:S(2)}) copy-start(f32[256]{0:T(256)} %param.13) | copy-start | bytes 3076
  11.3 18.4 %collective-permute-start.2 = (bf16[48,256]{1,0:T(8,128)(2,1)S(1)}, bf16[48,256]{1,0:T(8,128)(2,1)S(1)}, u32[]{:S(2)}, u32[]{:S(2)}) collective-permute-start(bf16[48,256]{1,0:T(8,128)(2,1)S(1)} %pad_maximum_fusion.3), channel_id=1, source_target_pairs={{1,0},{2,1},{3,2},{4,3},{5,4},{6,5},{7,6},{8,7},{9,8},{10,9},{11,1... | collective-permute-start | bytes 73736 | tf_op jit(solution)/shard_map/ppermute | solution.py:660
  14.2 15.6 %collective-permute-start.1 = (bf16[48,256]{1,0:T(8,128)(2,1)S(1)}, bf16[48,256]{1,0:T(8,128)(2,1)S(1)}, u32[]{:S(2)}, u32[]{:S(2)}) collective-permute-start(bf16[48,256]{1,0:T(8,128)(2,1)S(1)} %pad_maximum_fusion.2), channel_id=1, source_target_pairs={{0,1},{1,2},{2,3},{3,4},{4,5},{5,6},{6,7},{7,8},{8,9},{9,10},{10,1... | collective-permute-start | bytes 73736 | tf_op jit(solution)/shard_map/ppermute | solution.py:659
  27.1 4.9 %collective-permute-start = (bf16[2048,256]{1,0:T(8,128)(2,1)S(1)}, bf16[2048,256]{1,0:T(8,128)(2,1)S(1)}, u32[]{:S(2)}, u32[]{:S(2)}) collective-permute-start(bf16[2048,256]{1,0:T(8,128)(2,1)S(1)} %bitcast.48), channel_id=1, source_target_pairs={{1,0},{0,1},{3,2},{2,3},{5,4},{4,5},{7,6},{6,7},{9,8},{8,9},{11,10... | collective-permute-start | bytes 3145736 | tf_op jit(solution)/shard_map/ppermute | solution.py:631
  29.8 1.1 copy-start.12
  30.9 36.3 %copy-start.1 = (bf16[1632,192]{1,0:T(8,128)(2,1)S(1)}, bf16[1632,192]{1,0:T(8,128)(2,1)}, u32[]{:S(2)}) copy-start(bf16[1632,192]{1,0:T(8,128)(2,1)} %constant.31.clone.up) | copy-start | bytes 1880068
  33.6 8.8 %collective-permute-start.5 = (bf16[208,256]{1,0:T(8,128)(2,1)}, bf16[208,256]{1,0:T(8,128)(2,1)S(1)}, u32[]{:S(2)}, u32[]{:S(2)}) collective-permute-start(bf16[208,256]{1,0:T(8,128)(2,1)} %get-tuple-element.26), channel_id=1, source_target_pairs={{96,0},{0,32},{32,64},{64,96},{97,1},{1,33},{33,65},{65,97},{98,2}... | collective-permute-start | bytes 319496 | tf_op jit(solution)/shard_map/ppermute | solution.py:631
  34.8 7.5 %collective-permute-start.4 = (bf16[208,256]{1,0:T(8,128)(2,1)S(1)}, bf16[208,256]{1,0:T(8,128)(2,1)S(1)}, u32[]{:S(2)}, u32[]{:S(2)}) collective-permute-start(bf16[208,256]{1,0:T(8,128)(2,1)S(1)} %get-tuple-element.24.near), channel_id=1, source_target_pairs={{32,0},{64,32},{96,64},{0,96},{33,1},{65,33},{97,65},{1,97},{34,2}... | collective-permute-start | bytes 319496 | tf_op jit(solution)/shard_map/ppermute | solution.py:631
  36.3 6.1 %collective-permute-start.3 = (bf16[176,256]{1,0:T(8,128)(2,1)}, bf16[176,256]{1,0:T(8,128)(2,1)}, u32[]{:S(2)}, u32[]{:S(2)}) collective-permute-start(bf16[176,256]{1,0:T(8,128)(2,1)} %get-tuple-element.25), channel_id=1, source_target_pairs={{64,0},{96,32},{0,64},{32,96},{65,1},{97,33},{1,65},{33,97},{66,2}... | collective-permute-start | bytes 270344 | tf_op jit(solution)/shard_map/ppermute | solution.py:631
  38.6 24.4 %copy-start.13 = (bf16[32,1,256]{2,1,0:T(2,128)(2,1)S(1)}, bf16[32,1,256]{2,1,0:T(2,128)(2,1)}, u32[]{:S(2)}) copy-start(bf16[32,1,256]{2,1,0:T(2,128)(2,1)} %copy-done.12) | copy-start | bytes 49156
  60.0 17.1 %copy-start = (bf16[3,3,256,256]{3,2,1,0:T(8,128)(2,1)S(1)}, bf16[3,3,256,256]{3,2,1,0:T(8,128)(2,1)}, u32[]{:S(2)}) copy-start(bf16[3,3,256,256]{3,2,1,0:T(8,128)(2,1)} %param.18) | copy-start | bytes 3538948
  60.0 6.7 %collective-permute-start.6 = (bf16[208,256]{1,0:T(8,128)(2,1)S(1)}, bf16[208,256]{1,0:T(8,128)(2,1)S(1)}, u32[]{:S(2)}, u32[]{:S(2)}) collective-permute-start(bf16[208,256]{1,0:T(8,128)(2,1)S(1)} %get-tuple-element.27), channel_id=1, source_target_pairs={{96,0},{0,32},{32,64},{64,96},{97,1},{1,33},{33,65},{65,97},{98,2}... | collective-permute-start | bytes 319496 | tf_op jit(solution)/shard_map/ppermute | solution.py:631
  60.2 6.5 %collective-permute-start.7 = (bf16[208,256]{1,0:T(8,128)(2,1)S(1)}, bf16[208,256]{1,0:T(8,128)(2,1)S(1)}, u32[]{:S(2)}, u32[]{:S(2)}) collective-permute-start(bf16[208,256]{1,0:T(8,128)(2,1)S(1)} %get-tuple-element.28), channel_id=1, source_target_pairs={{64,0},{96,32},{0,64},{32,96},{65,1},{97,33},{1,65},{33,97},{66,2}... | collective-permute-start | bytes 319496 | tf_op jit(solution)/shard_map/ppermute | solution.py:631
  62.1 5.1 %collective-permute-start.8 = (bf16[208,256]{1,0:T(8,128)(2,1)S(1)}, bf16[208,256]{1,0:T(8,128)(2,1)S(1)}, u32[]{:S(2)}, u32[]{:S(2)}) collective-permute-start(bf16[208,256]{1,0:T(8,128)(2,1)S(1)} %get-tuple-element.29), channel_id=1, source_target_pairs={{32,0},{64,32},{96,64},{0,96},{33,1},{65,33},{97,65},{1,97},{34,2}... | collective-permute-start | bytes 319496 | tf_op jit(solution)/shard_map/ppermute | solution.py:631
  70.0 16.4 %copy-start.9 = (f32[256]{0:T(256)S(1)}, f32[256]{0:T(256)}, u32[]{:S(2)}) copy-start(f32[256]{0:T(256)} %param.16) | copy-start | bytes 3076
  70.0 16.4 %copy-start.10 = (f32[256]{0:T(256)S(1)}, f32[256]{0:T(256)}, u32[]{:S(2)}) copy-start(f32[256]{0:T(256)} %param.17) | copy-start | bytes 3076
  70.0 16.3 %all-to-all-start.1 = ((f32[128,1,128]{2,1,0:T(1,128)}), f32[128,1,128]{2,1,0:T(1,128)S(1)}, u32[]{:S(2)}, u32[]{:S(2)}) async-start(f32[128,1,128]{2,1,0:T(1,128)} %bitcast.18), calls=%async_computation.1 | async-start | bytes 131072 | tf_op jit(solution)/shard_map/all_to_all | solution.py:681
  77.9 14.6 %copy-start.3 = (f32[512,256]{1,0:T(8,128)}, f32[512,256]{1,0:T(8,128)S(1)}, u32[]{:S(2)}) copy-start(f32[512,256]{1,0:T(8,128)S(1)} %shard_map.143.grad_hidden) | copy-start | bytes 1572868
  86.4 11.0 %copy-start.8 = (f32[256]{0:T(256)S(1)}, f32[256]{0:T(256)}, u32[]{:S(2)}) copy-start(f32[256]{0:T(256)} %param.19) | copy-start | bytes 3076
  88.8 2.6 %collective-permute-start.9 = (bf16[2320,128]{1,0:T(8,128)(2,1)S(1)}, bf16[2320,128]{1,0:T(8,128)(2,1)S(1)}, u32[]{:S(2)}, u32[]{:S(2)}) collective-permute-start(bf16[2320,128]{1,0:T(8,128)(2,1)S(1)} %get-tuple-element.34), channel_id=1, source_target_pairs={{1,0},{0,1},{3,2},{2,3},{5,4},{4,5},{7,6},{6,7},{9,8},{8,9},{11,10... | collective-permute-start | bytes 1781768 | tf_op jit(solution)/shard_map/ppermute | solution.py:631
  92.5 18.8 %all-to-all-start.2 = ((bf16[64,40,128]{2,1,0:T(8,128)(2,1)}), bf16[64,40,128]{2,1,0:T(8,128)(2,1)S(1)}, u32[]{:S(2)}, u32[]{:S(2)}) async-start(bf16[64,40,128]{2,1,0:T(8,128)(2,1)} %shard_map.145), calls=%async_computation.2 | async-start | bytes 1310720 | tf_op jit(solution)/shard_map/all_to_all | solution.py:690
  97.4 22.3 %copy-start.4 = (f32[512,256]{1,0:T(8,128)S(1)}, f32[512,256]{1,0:T(8,128)}, u32[]{:S(2)}) copy-start(f32[512,256]{1,0:T(8,128)} %copy-done.3) | copy-start | bytes 1572868
  97.4 1.2 copy-start.5
  112.3 17.5 %all-to-all-start.3 = ((bf16[64,40,128]{2,1,0:T(8,128)(2,1)}), bf16[64,40,128]{2,1,0:T(8,128)(2,1)S(1)}, u32[]{:S(2)}, u32[]{:S(2)}) async-start(bf16[64,40,128]{2,1,0:T(8,128)(2,1)} %get-tuple-element.38), calls=%async_computation.3 | async-start | bytes 1310720 | tf_op jit(solution)/shard_map/all_to_all | solution.py:695
  117.0 2.8 %collective-permute-start.10 = (f32[8,256]{1,0:T(8,128)S(1)}, f32[8,256]{1,0:T(8,128)S(1)}, u32[]{:S(2)}, u32[]{:S(2)}) collective-permute-start(f32[8,256]{1,0:T(8,128)S(1)} %get-tuple-element.39.mine), channel_id=1, source_target_pairs={{1,0},{0,1},{3,2},{2,3},{5,4},{4,5},{7,6},{6,7},{9,8},{8,9},{11,10... | collective-permute-start | bytes 24584 | tf_op jit(solution)/shard_map/ppermute | solution.py:631
  129.9 4.6 %collective-permute-start.11 = (bf16[64,40,128]{2,1,0:T(8,128)(2,1)S(1)}, bf16[64,40,128]{2,1,0:T(8,128)(2,1)S(1)}, u32[]{:S(2)}, u32[]{:S(2)}) collective-permute-start(bf16[64,40,128]{2,1,0:T(8,128)(2,1)S(1)} %all-to-all-done.3.mine), channel_id=1, source_target_pairs={{1,0},{0,1},{3,2},{2,3},{5,4},{4,5},{7,6},{6,7},{9,8},{8,9},{11,10... | collective-permute-start | bytes 1966088 | tf_op jit(solution)/shard_map/ppermute | solution.py:631

commit v7 on v6

--- a/solution.py
+++ b/solution.py
@@ -140,7 +140,7 @@
 
 
 def rows_kernel(first, other, wide, edges, next_out, last_out, far_out):
-    rows = [first[0:2, :]] + stats_rows(other) + [jnp.zeros((12, C), F32)]
+    rows = [first[0:2, :], other[0:2, :], jnp.zeros((12, C), F32)]
     packed = jnp.concatenate(rows, axis=0).astype(BF16)
     for out in (next_out, last_out, far_out):
         out[:16, :] = packed
@@ -663,7 +663,8 @@
     edges = jnp.pad(jnp.stack([grad[0], grad[-1]]), ((0, 0), (0, 14), (0, 0)))
     other = shift(cells, "c", 2, 1)
 
-    near, last, far = stats_and_rows(local_stats(cells), other, wide, edges)
+    stats = local_stats(cells)
+    near, last, far = stats_and_rows(stats, shift(stats, "c", 2, 1), wide, edges)
     below, above, far = (
         shift(near, "y", 4, 1),
         shift(last, "y", 4, 3),

time: 137 us -> 136 us (level)
  Pallas kernels: 34.5 us -> 32.1 us
    ppermute x1, waiting for transfers between devices: 0.01 us -> 7.84 us  [per_device(): after = lax.ppermute(first, ZXC, [(i + 1, i) for i in range(31)])[:, None]]
    all_to_all x1, waiting for transfers between devices: 9.44 us -> 1.62 us  [per_device(): lax.all_to_all(copies_of(own), ('z', 'x'), 0, 0, tiled=True)]
    ppermute x10 -> x11, starting transfers between devices: 15.7 us -> 17.7 us  [shift(): lax.ppermute(value, axis, [((i + step) % count, i) for i in range(count)])]
    pallas_call x1, Pallas kernels: 1.57 us -> 0.02 us  [stats_and_rows(): pl.pallas_call(rows_kernel, out_shape=(pltpu.VMEM((208, C), BF16), pltpu....]
    ppermute x10 -> x11, waiting for transfers between devices: 12.3 us -> 12.4 us  [shift(): lax.ppermute(value, axis, [((i + step) % count, i) for i in range(count)])]
  transfers between devices with their start and end apart: 16 -> 17, of which waited for: 11 -> 14; matrix products, arithmetic and copies ran while one was open for 2% -> 2% of each run, Pallas kernels for 3% -> 3%
where the time goes in v7:
time: 136 us; the launch traced here: 135 us
  waiting for transfers between devices  50.3 us (37%)
  starting transfers between devices  47.8 us (35%)
  Pallas kernels  32.1 us (24%)
  local copies, waits for them, and re-layouts  2.77 us (2%)
    ppermute x11, starting transfers between devices, shift(): lax.ppermute(value, axis, [((i + step) % count, i) for i in range(count)])  17.7 us
    pallas_call x1, Pallas kernels, partial_attention(): pl.pallas_call(attention_kernel, out_shape=(jax.ShapeDtypeStruct((PART, C...  16.8 us
    ppermute x11, waiting for transfers between devices, shift(): lax.ppermute(value, axis, [((i + step) % count, i) for i in range(count)])  12.4 us
    all_to_all x1, waiting for transfers between devices, per_device(): got = lax.all_to_all(sent, ('y', 'z', 'x'), 0, 0, tiled=True)  11.3 us
    all_to_all x1, waiting for transfers between devices, per_device(): spread = lax.all_to_all(chunk, ('y', 'z', 'x'), 0, 0, tiled=True)  8.74 us
    all_to_all x1, starting transfers between devices, per_device(): lax.all_to_all(copies_of(own), ('z', 'x'), 0, 0, tiled=True)  8.44 us
    all_to_all x1, waiting for transfers between devices, per_device(): stats2 = lax.all_to_all(stats2.reshape(128, 1, 128), ALL, 0, 0, tiled=True)  8.43 us
    ppermute x1, waiting for transfers between devices, per_device(): after = lax.ppermute(first, ZXC, [(i + 1, i) for i in range(31)])[:, None]  7.84 us
  transfers between devices with their start and end apart: 17, of which 14 were waited for; matrix products, arithmetic and copies ran while one was open for 2% of the time, Pallas kernels for 3%

profile of v7, /device:TPU:1, one launch (start us, length us, event | category | flops | bytes accessed | tf_op | source)
XLA Modules:
  0.0 135.2 jit_solution(4041433987214839131)
XLA Ops:
  0.7 2.0 %shard_map.138 = bf16[16,128,256]{2,1,0:T(8,128)(2,1)} custom-call(bf16[128,256]{1,0:T(8,128)(2,1)} %bitcast.67), custom_call_target="tpu_custom_call" | custom-call | tf_op jit(solution)/shard_map/pallas_call | solution.py:616
  2.7 8.4 %all-to-all-start = ((bf16[16,128,256]{2,1,0:T(8,128)(2,1)}), bf16[16,128,256]{2,1,0:T(8,128)(2,1)S(1)}, u32[]{:S(2)}, u32[]{:S(2)}) async-start(bf16[16,128,256]{2,1,0:T(8,128)(2,1)} %shard_map.138), calls=%async_computation | async-start | bytes 2097152 | tf_op jit(solution)/shard_map/all_to_all | solution.py:654
  11.3 2.9 %collective-permute-start.3 = (bf16[48,256]{1,0:T(8,128)(2,1)S(1)}, bf16[48,256]{1,0:T(8,128)(2,1)S(1)}, u32[]{:S(2)}, u32[]{:S(2)}) collective-permute-start(bf16[48,256]{1,0:T(8,128)(2,1)S(1)} %pad_maximum_fusion.3), channel_id=1, source_target_pairs={{1,0},{2,1},{3,2},{4,3},{5,4},{6,5},{7,6},{8,7},{9,8},{10,9},{11,1... | collective-permute-start | bytes 73736 | tf_op jit(solution)/shard_map/ppermute | solution.py:660
  14.2 3.4 %collective-permute-start.2 = (bf16[48,256]{1,0:T(8,128)(2,1)S(1)}, bf16[48,256]{1,0:T(8,128)(2,1)S(1)}, u32[]{:S(2)}, u32[]{:S(2)}) collective-permute-start(bf16[48,256]{1,0:T(8,128)(2,1)S(1)} %pad_maximum_fusion.2), channel_id=1, source_target_pairs={{0,1},{1,2},{2,3},{3,4},{4,5},{5,6},{6,7},{7,8},{8,9},{9,10},{10,1... | collective-permute-start | bytes 73736 | tf_op jit(solution)/shard_map/ppermute | solution.py:659
  17.6 7.8 %collective-permute-done.3 = bf16[48,256]{1,0:T(8,128)(2,1)S(1)} collective-permute-done((bf16[48,256]{1,0:T(8,128)(2,1)S(1)}, bf16[48,256]{1,0:T(8,128)(2,1)S(1)}, u32[]{:S(2)}, u32[]{:S(2)}) %collective-permute-start.3) | collective-permute-done | bytes 24608 | tf_op jit(solution)/shard_map/ppermute | solution.py:660
  25.5 1.6 %all-to-all-done = bf16[16,128,256]{2,1,0:T(8,128)(2,1)S(1)} async-done(((bf16[16,128,256]{2,1,0:T(8,128)(2,1)}), bf16[16,128,256]{2,1,0:T(8,128)(2,1)S(1)}, u32[]{:S(2)}, u32[]{:S(2)}) %all-to-all-start) | async-done | bytes 1048608 | tf_op jit(solution)/shard_map/all_to_all | solution.py:654
  27.1 2.6 %collective-permute-start = (bf16[2048,256]{1,0:T(8,128)(2,1)S(1)}, bf16[2048,256]{1,0:T(8,128)(2,1)S(1)}, u32[]{:S(2)}, u32[]{:S(2)}) collective-permute-start(bf16[2048,256]{1,0:T(8,128)(2,1)S(1)} %bitcast.48), channel_id=1, source_target_pairs={{1,0},{0,1},{3,2},{2,3},{5,4},{4,5},{7,6},{6,7},{9,8},{8,9},{11,10... | collective-permute-start | bytes 3145736 | tf_op jit(solution)/shard_map/ppermute | solution.py:631
  29.9 0.7 pad_maximum_fusion.1
  30.6 0.9 shard_map.139.first
  31.5 0.1 collective-permute-start.1
  31.6 1.0 reshape.118.wide
  32.6 0.1 collective-permute-done.1.other
  32.8 1.4 %collective-permute-start.6 = (bf16[208,256]{1,0:T(8,128)(2,1)S(1)}, bf16[208,256]{1,0:T(8,128)(2,1)S(1)}, u32[]{:S(2)}, u32[]{:S(2)}) collective-permute-start(bf16[208,256]{1,0:T(8,128)(2,1)S(1)} %get-tuple-element.26), channel_id=1, source_target_pairs={{96,0},{0,32},{32,64},{64,96},{97,1},{1,33},{33,65},{65,97},{98,2}... | collective-permute-start | bytes 319496 | tf_op jit(solution)/shard_map/ppermute | solution.py:631
  34.1 0.1 stack.29
  34.3 2.7 %collective-permute-start.4 = (bf16[176,256]{1,0:T(8,128)(2,1)}, bf16[176,256]{1,0:T(8,128)(2,1)S(1)}, u32[]{:S(2)}, u32[]{:S(2)}) collective-permute-start(bf16[176,256]{1,0:T(8,128)(2,1)} %copy-done.9), channel_id=1, source_target_pairs={{64,0},{96,32},{0,64},{32,96},{65,1},{97,33},{1,65},{33,97},{66,2}... | collective-permute-start | bytes 270344 | tf_op jit(solution)/shard_map/ppermute | solution.py:631
  37.0 1.1 collective-permute-start.5
  38.0 0.4 collective-permute-done.6.up
  38.4 3.4 %collective-permute-done.5.down = bf16[208,256]{1,0:T(8,128)(2,1)S(1)} collective-permute-done((bf16[208,256]{1,0:T(8,128)(2,1)S(1)}, bf16[208,256]{1,0:T(8,128)(2,1)S(1)}, u32[]{:S(2)}, u32[]{:S(2)}) %collective-permute-start.5) | collective-permute-done | bytes 106528 | tf_op jit(solution)/shard_map/ppermute | solution.py:631
  41.8 16.8 %shard_map.141 = (bf16[208,256]{1,0:T(8,128)(2,1)S(1)}, bf16[208,256]{1,0:T(8,128)(2,1)S(1)}, bf16[208,256]{1,0:T(8,128)(2,1)S(1)}, bf16[400,256]{1,0:T(8,128)(2,1)}) custom-call(bf16[2048,256]{1,0:T(8,128)(2,1)S(1)} %bitcast.50, bf16[2048,256]{1,0:T(8,128)(2,1)S(1)} %collective-permute-done.other, bf16[208,256]{1,0:T(8,128)(2,1)S(1)} %get-tuple-element.24.near, ...), custom_call_target="tpu_custom_call" | custom-call | tf_op jit(solution)/shard_map/pallas_call | solution.py:270
  58.6 1.6 %collective-permute-start.7 = (bf16[208,256]{1,0:T(8,128)(2,1)S(1)}, bf16[208,256]{1,0:T(8,128)(2,1)S(1)}, u32[]{:S(2)}, u32[]{:S(2)}) collective-permute-start(bf16[208,256]{1,0:T(8,128)(2,1)S(1)} %get-tuple-element.27), channel_id=1, source_target_pairs={{96,0},{0,32},{32,64},{64,96},{97,1},{1,33},{33,65},{65,97},{98,2}... | collective-permute-start | bytes 319496 | tf_op jit(solution)/shard_map/ppermute | solution.py:631
  60.2 2.2 %collective-permute-start.8 = (bf16[208,256]{1,0:T(8,128)(2,1)S(1)}, bf16[208,256]{1,0:T(8,128)(2,1)S(1)}, u32[]{:S(2)}, u32[]{:S(2)}) collective-permute-start(bf16[208,256]{1,0:T(8,128)(2,1)S(1)} %get-tuple-element.28), channel_id=1, source_target_pairs={{64,0},{96,32},{0,64},{32,96},{65,1},{97,33},{1,65},{33,97},{66,2}... | collective-permute-start | bytes 319496 | tf_op jit(solution)/shard_map/ppermute | solution.py:631
  62.4 0.4 collective-permute-start.9
  62.8 0.2 pad_maximum_fusion
  63.0 0.5 collective-permute-done.7.p1
  63.5 2.8 %collective-permute-done.8.p2 = bf16[208,256]{1,0:T(8,128)(2,1)S(1)} collective-permute-done((bf16[208,256]{1,0:T(8,128)(2,1)S(1)}, bf16[208,256]{1,0:T(8,128)(2,1)S(1)}, u32[]{:S(2)}, u32[]{:S(2)}) %collective-permute-start.8) | collective-permute-done | bytes 106528 | tf_op jit(solution)/shard_map/ppermute | solution.py:631
  66.3 1.0 collective-permute-done.9.p3
  67.4 2.8 %shard_map.142 = (bf16[192,256]{1,0:T(8,128)(2,1)S(1)}, f32[128,128]{1,0:T(8,128)}) custom-call(s32[8,256]{1,0:T(8,128)S(1)} %broadcast_in_dim.34.flags, bf16[208,256]{1,0:T(8,128)(2,1)S(1)} %collective-permute-done.7.p1, bf16[208,256]{1,0:T(8,128)(2,1)S(1)} %collective-permute-done.8.p2, bf16[208,256]{1,0:T(8,128)(2,1)S(1)} %collective-permute-done.9.p3, ...), custom_call_target="tpu_custom_call" | custom-call | tf_op jit(solution)/shard_map/pallas_call | solution.py:336
  70.2 5.7 %all-to-all-start.1 = ((f32[128,1,128]{2,1,0:T(1,128)}), f32[128,1,128]{2,1,0:T(1,128)S(1)}, u32[]{:S(2)}, u32[]{:S(2)}) async-start(f32[128,1,128]{2,1,0:T(1,128)} %bitcast.18), calls=%async_computation.1 | async-start | bytes 131072 | tf_op jit(solution)/shard_map/all_to_all | solution.py:682
  76.0 0.2 fusion.13
  76.2 0.8 shard_map.143.grad_hidden
  77.0 8.4 %all-to-all-done.1 = f32[128,1,128]{2,1,0:T(1,128)S(1)} async-done(((f32[128,1,128]{2,1,0:T(1,128)}), f32[128,1,128]{2,1,0:T(1,128)S(1)}, u32[]{:S(2)}, u32[]{:S(2)}) %all-to-all-start.1) | async-done | bytes 65568 | tf_op jit(solution)/shard_map/all_to_all | solution.py:682
  85.4 2.4 %shard_map.144 = (bf16[2320,128]{1,0:T(8,128)(2,1)S(1)}, bf16[2320,128]{1,0:T(8,128)(2,1)S(1)}, bf16[3,544,256]{2,1,0:T(8,128)(2,1)}) custom-call(s32[8,256]{1,0:T(8,128)S(1)} %broadcast_in_dim.34.flags, bf16[192,256]{1,0:T(8,128)(2,1)S(1)} %get-tuple-element.31.merged, bf16[1632,192]{1,0:T(8,128)(2,1)S(1)} %copy-done.1, f32[128,128]{1,0:T(8,128)S(1)} %bitcast.57, ...), custom_call_target="tpu_custom_call" | custom-call | tf_op jit(solution)/shard_map/pallas_call | solution.py:435
  87.8 0.9 collective-permute-start.10
  88.8 1.6 %collective-permute-done.10.got = bf16[2320,128]{1,0:T(8,128)(2,1)S(1)} collective-permute-done((bf16[2320,128]{1,0:T(8,128)(2,1)S(1)}, bf16[2320,128]{1,0:T(8,128)(2,1)S(1)}, u32[]{:S(2)}, u32[]{:S(2)}) %collective-permute-start.10) | collective-permute-done | bytes 593952 | tf_op jit(solution)/shard_map/ppermute | solution.py:631
  90.4 1.1 shard_map.145
  91.5 4.9 %all-to-all-start.2 = ((bf16[64,40,128]{2,1,0:T(8,128)(2,1)}), bf16[64,40,128]{2,1,0:T(8,128)(2,1)S(1)}, u32[]{:S(2)}, u32[]{:S(2)}) async-start(bf16[64,40,128]{2,1,0:T(8,128)(2,1)} %shard_map.145), calls=%async_computation.2 | async-start | bytes 1310720 | tf_op jit(solution)/shard_map/all_to_all | solution.py:691
  96.4 1.1 copy-done.3
  97.6 1.5 %shard_map.146 = bf16[512,256]{1,0:T(8,128)(2,1)} custom-call(bf16[3,544,256]{2,1,0:T(8,128)(2,1)S(1)} %copy-done.3, bf16[9,256,256]{2,1,0:T(8,128)(2,1)S(1)} %bitcast.52, f32[1,256]{1,0:T(1,128)S(1)} %bitcast.61), custom_call_target="tpu_custom_call" | custom-call | flops 603979776 | bytes 3000000 | tf_op jit(solution)/shard_map/pallas_call | solution.py:458
  99.1 11.3 %all-to-all-done.2.got = bf16[64,40,128]{2,1,0:T(8,128)(2,1)S(1)} async-done(((bf16[64,40,128]{2,1,0:T(8,128)(2,1)}), bf16[64,40,128]{2,1,0:T(8,128)(2,1)S(1)}, u32[]{:S(2)}, u32[]{:S(2)}) %all-to-all-start.2) | async-done | bytes 655392 | tf_op jit(solution)/shard_map/all_to_all | solution.py:691
  110.3 1.0 shard_map.147
  111.3 4.7 %all-to-all-start.3 = ((bf16[64,40,128]{2,1,0:T(8,128)(2,1)}), bf16[64,40,128]{2,1,0:T(8,128)(2,1)S(1)}, u32[]{:S(2)}, u32[]{:S(2)}) async-start(bf16[64,40,128]{2,1,0:T(8,128)(2,1)} %get-tuple-element.38), calls=%async_computation.3 | async-start | bytes 1310720 | tf_op jit(solution)/shard_map/all_to_all | solution.py:696
  116.0 1.9 %collective-permute-start.11 = (f32[8,256]{1,0:T(8,128)S(1)}, f32[8,256]{1,0:T(8,128)S(1)}, u32[]{:S(2)}, u32[]{:S(2)}) collective-permute-start(f32[8,256]{1,0:T(8,128)S(1)} %get-tuple-element.39.mine), channel_id=1, source_target_pairs={{1,0},{0,1},{3,2},{2,3},{5,4},{4,5},{7,6},{6,7},{9,8},{8,9},{11,10... | collective-permute-start | bytes 24584 | tf_op jit(solution)/shard_map/ppermute | solution.py:631
  117.9 0.8 collective-permute-done.11.other
  118.7 1.4 %shard_map.148 = (bf16[512,256]{1,0:T(8,128)(2,1)}, f32[2,256]{1,0:T(2,128)}) custom-call(s32[8,256]{1,0:T(8,128)S(1)} %broadcast_in_dim.34.flags, bf16[192,256]{1,0:T(8,128)(2,1)S(1)} %get-tuple-element.31.merged, bf16[1632,192]{1,0:T(8,128)(2,1)S(1)} %copy-done.1, f32[128,128]{1,0:T(8,128)S(1)} %bitcast.58, f32[1,256]{1,0:T(1,128)S(1)} %bitcast.63, ...), custom_call_target="tpu_custom_call" | custom-call | flops 1000000000 | bytes 2000000 | tf_op jit(solution)/shard_map/pallas_call | solution.py:557
  120.1 8.7 %all-to-all-done.3.mine = bf16[64,40,128]{2,1,0:T(8,128)(2,1)S(1)} async-done(((bf16[64,40,128]{2,1,0:T(8,128)(2,1)}), bf16[64,40,128]{2,1,0:T(8,128)(2,1)S(1)}, u32[]{:S(2)}, u32[]{:S(2)}) %all-to-all-start.3) | async-done | bytes 655392 | tf_op jit(solution)/shard_map/all_to_all | solution.py:696
  128.9 2.9 %collective-permute-start.12 = (bf16[64,40,128]{2,1,0:T(8,128)(2,1)S(1)}, bf16[64,40,128]{2,1,0:T(8,128)(2,1)S(1)}, u32[]{:S(2)}, u32[]{:S(2)}) collective-permute-start(bf16[64,40,128]{2,1,0:T(8,128)(2,1)S(1)} %all-to-all-done.3.mine), channel_id=1, source_target_pairs={{1,0},{0,1},{3,2},{2,3},{5,4},{4,5},{7,6},{6,7},{9,8},{8,9},{11,10... | collective-permute-start | bytes 1966088 | tf_op jit(solution)/shard_map/ppermute | solution.py:631
  131.8 1.7 %collective-permute-done.12.other = bf16[64,40,128]{2,1,0:T(8,128)(2,1)S(1)} collective-permute-done((bf16[64,40,128]{2,1,0:T(8,128)(2,1)S(1)}, bf16[64,40,128]{2,1,0:T(8,128)(2,1)S(1)}, u32[]{:S(2)}, u32[]{:S(2)}) %collective-permute-start.12) | collective-permute-done | bytes 655392 | tf_op jit(solution)/shard_map/ppermute | solution.py:631
  133.5 1.5 %shard_map.149 = f32[2304,256]{1,0:T(8,128)} custom-call(s32[8,256]{1,0:T(8,128)S(1)} %broadcast_in_dim.34.flags, bf16[64,40,128]{2,1,0:T(8,128)(2,1)S(1)} %all-to-all-done.3.mine, bf16[64,40,128]{2,1,0:T(8,128)(2,1)S(1)} %collective-permute-done.12.other), custom_call_target="tpu_custom_call" | custom-call | tf_op jit(solution)/shard_map/pallas_call | solution.py:592
  (55 shorter events, 0.4 us)
Async XLA Ops:
  0.6 10.5 %copy-start.10 = (bf16[16,8,256]{2,1,0:T(8,128)(2,1)S(1)}, bf16[16,8,256]{2,1,0:T(8,128)(2,1)}, u32[]{:S(2)}) copy-start(bf16[16,8,256]{2,1,0:T(8,128)(2,1)} %param.11) | copy-start | bytes 196612
  0.6 10.5 %copy-start.2 = (bf16[32,16,256]{2,1,0:T(8,128)(2,1)S(1)}, bf16[32,16,256]{2,1,0:T(8,128)(2,1)}, u32[]{:S(2)}) copy-start(bf16[32,16,256]{2,1,0:T(8,128)(2,1)} %param.20) | copy-start | bytes 786436
  2.6 39.2 %copy-start.4 = (f32[256]{0:T(256)S(1)}, f32[256]{0:T(256)}, u32[]{:S(2)}) copy-start(f32[256]{0:T(256)} %param.12) | copy-start | bytes 3076
  2.7 39.2 %copy-start.5 = (f32[256]{0:T(256)S(1)}, f32[256]{0:T(256)}, u32[]{:S(2)}) copy-start(f32[256]{0:T(256)} %param.13) | copy-start | bytes 3076
  2.7 24.4 %all-to-all-start = ((bf16[16,128,256]{2,1,0:T(8,128)(2,1)}), bf16[16,128,256]{2,1,0:T(8,128)(2,1)S(1)}, u32[]{:S(2)}, u32[]{:S(2)}) async-start(bf16[16,128,256]{2,1,0:T(8,128)(2,1)} %shard_map.138), calls=%async_computation | async-start | bytes 2097152 | tf_op jit(solution)/shard_map/all_to_all | solution.py:654
  11.3 14.2 %collective-permute-start.3 = (bf16[48,256]{1,0:T(8,128)(2,1)S(1)}, bf16[48,256]{1,0:T(8,128)(2,1)S(1)}, u32[]{:S(2)}, u32[]{:S(2)}) collective-permute-start(bf16[48,256]{1,0:T(8,128)(2,1)S(1)} %pad_maximum_fusion.3), channel_id=1, source_target_pairs={{1,0},{2,1},{3,2},{4,3},{5,4},{6,5},{7,6},{8,7},{9,8},{10,9},{11,1... | collective-permute-start | bytes 73736 | tf_op jit(solution)/shard_map/ppermute | solution.py:660
  14.2 15.5 %collective-permute-start.2 = (bf16[48,256]{1,0:T(8,128)(2,1)S(1)}, bf16[48,256]{1,0:T(8,128)(2,1)S(1)}, u32[]{:S(2)}, u32[]{:S(2)}) collective-permute-start(bf16[48,256]{1,0:T(8,128)(2,1)S(1)} %pad_maximum_fusion.2), channel_id=1, source_target_pairs={{0,1},{1,2},{2,3},{3,4},{4,5},{5,6},{6,7},{7,8},{8,9},{9,10},{10,1... | collective-permute-start | bytes 73736 | tf_op jit(solution)/shard_map/ppermute | solution.py:659
  27.1 14.7 %collective-permute-start = (bf16[2048,256]{1,0:T(8,128)(2,1)S(1)}, bf16[2048,256]{1,0:T(8,128)(2,1)S(1)}, u32[]{:S(2)}, u32[]{:S(2)}) collective-permute-start(bf16[2048,256]{1,0:T(8,128)(2,1)S(1)} %bitcast.48), channel_id=1, source_target_pairs={{1,0},{0,1},{3,2},{2,3},{5,4},{4,5},{7,6},{6,7},{9,8},{8,9},{11,10... | collective-permute-start | bytes 3145736 | tf_op jit(solution)/shard_map/ppermute | solution.py:631
  29.8 2.9 %copy-start.11 = (bf16[32,1,256]{2,1,0:T(2,128)(2,1)}, bf16[32,1,256]{2,1,0:T(2,128)(2,1)S(1)}, u32[]{:S(2)}) copy-start(bf16[32,1,256]{2,1,0:T(2,128)(2,1)S(1)} %copy.36) | copy-start | bytes 49156
  29.9 1.7 %copy-start.13 = (bf16[32,1,256]{2,1,0:T(2,128)(2,1)}, bf16[32,1,256]{2,1,0:T(2,128)(2,1)S(1)}, u32[]{:S(2)}) copy-start(bf16[32,1,256]{2,1,0:T(2,128)(2,1)S(1)} %copy.35) | copy-start | bytes 49156
  31.5 35.9 %copy-start.1 = (bf16[1632,192]{1,0:T(8,128)(2,1)S(1)}, bf16[1632,192]{1,0:T(8,128)(2,1)}, u32[]{:S(2)}) copy-start(bf16[1632,192]{1,0:T(8,128)(2,1)} %constant.31.clone.up) | copy-start | bytes 1880068
  31.5 1.3 collective-permute-start.1
  32.8 1.4 %copy-start.9 = (bf16[176,256]{1,0:T(8,128)(2,1)}, bf16[176,256]{1,0:T(8,128)(2,1)S(1)}, u32[]{:S(2)}) copy-start(bf16[176,256]{1,0:T(8,128)(2,1)S(1)} %get-tuple-element.25) | copy-start | bytes 270340
  32.8 5.6 %collective-permute-start.6 = (bf16[208,256]{1,0:T(8,128)(2,1)S(1)}, bf16[208,256]{1,0:T(8,128)(2,1)S(1)}, u32[]{:S(2)}, u32[]{:S(2)}) collective-permute-start(bf16[208,256]{1,0:T(8,128)(2,1)S(1)} %get-tuple-element.26), channel_id=1, source_target_pairs={{96,0},{0,32},{32,64},{64,96},{97,1},{1,33},{33,65},{65,97},{98,2}... | collective-permute-start | bytes 319496 | tf_op jit(solution)/shard_map/ppermute | solution.py:631
  34.2 28.5 %copy-start.12 = (bf16[32,1,256]{2,1,0:T(2,128)(2,1)S(1)}, bf16[32,1,256]{2,1,0:T(2,128)(2,1)}, u32[]{:S(2)}) copy-start(bf16[32,1,256]{2,1,0:T(2,128)(2,1)} %copy-done.11) | copy-start | bytes 49156
  34.2 28.5 %copy-start.14 = (bf16[32,1,256]{2,1,0:T(2,128)(2,1)S(1)}, bf16[32,1,256]{2,1,0:T(2,128)(2,1)}, u32[]{:S(2)}) copy-start(bf16[32,1,256]{2,1,0:T(2,128)(2,1)} %copy-done.13) | copy-start | bytes 49156
  34.3 7.5 %collective-permute-start.4 = (bf16[176,256]{1,0:T(8,128)(2,1)}, bf16[176,256]{1,0:T(8,128)(2,1)S(1)}, u32[]{:S(2)}, u32[]{:S(2)}) collective-permute-start(bf16[176,256]{1,0:T(8,128)(2,1)} %copy-done.9), channel_id=1, source_target_pairs={{64,0},{96,32},{0,64},{32,96},{65,1},{97,33},{1,65},{33,97},{66,2}... | collective-permute-start | bytes 270344 | tf_op jit(solution)/shard_map/ppermute | solution.py:631
  37.0 4.8 %collective-permute-start.5 = (bf16[208,256]{1,0:T(8,128)(2,1)S(1)}, bf16[208,256]{1,0:T(8,128)(2,1)S(1)}, u32[]{:S(2)}, u32[]{:S(2)}) collective-permute-start(bf16[208,256]{1,0:T(8,128)(2,1)S(1)} %get-tuple-element.24.near), channel_id=1, source_target_pairs={{32,0},{64,32},{96,64},{0,96},{33,1},{65,33},{97,65},{1,97},{34,2}... | collective-permute-start | bytes 319496 | tf_op jit(solution)/shard_map/ppermute | solution.py:631
  58.6 17.5 %copy-start = (bf16[3,3,256,256]{3,2,1,0:T(8,128)(2,1)S(1)}, bf16[3,3,256,256]{3,2,1,0:T(8,128)(2,1)}, u32[]{:S(2)}) copy-start(bf16[3,3,256,256]{3,2,1,0:T(8,128)(2,1)} %param.18) | copy-start | bytes 3538948
  58.6 4.8 %collective-permute-start.7 = (bf16[208,256]{1,0:T(8,128)(2,1)S(1)}, bf16[208,256]{1,0:T(8,128)(2,1)S(1)}, u32[]{:S(2)}, u32[]{:S(2)}) collective-permute-start(bf16[208,256]{1,0:T(8,128)(2,1)S(1)} %get-tuple-element.27), channel_id=1, source_target_pairs={{96,0},{0,32},{32,64},{64,96},{97,1},{1,33},{33,65},{65,97},{98,2}... | collective-permute-start | bytes 319496 | tf_op jit(solution)/shard_map/ppermute | solution.py:631
  60.2 6.1 %collective-permute-start.8 = (bf16[208,256]{1,0:T(8,128)(2,1)S(1)}, bf16[208,256]{1,0:T(8,128)(2,1)S(1)}, u32[]{:S(2)}, u32[]{:S(2)}) collective-permute-start(bf16[208,256]{1,0:T(8,128)(2,1)S(1)} %get-tuple-element.28), channel_id=1, source_target_pairs={{64,0},{96,32},{0,64},{32,96},{65,1},{97,33},{1,65},{33,97},{66,2}... | collective-permute-start | bytes 319496 | tf_op jit(solution)/shard_map/ppermute | solution.py:631
  62.4 5.0 %collective-permute-start.9 = (bf16[208,256]{1,0:T(8,128)(2,1)S(1)}, bf16[208,256]{1,0:T(8,128)(2,1)S(1)}, u32[]{:S(2)}, u32[]{:S(2)}) collective-permute-start(bf16[208,256]{1,0:T(8,128)(2,1)S(1)} %get-tuple-element.29), channel_id=1, source_target_pairs={{32,0},{64,32},{96,64},{0,96},{33,1},{65,33},{97,65},{1,97},{34,2}... | collective-permute-start | bytes 319496 | tf_op jit(solution)/shard_map/ppermute | solution.py:631
  70.2 15.2 %copy-start.7 = (f32[256]{0:T(256)S(1)}, f32[256]{0:T(256)}, u32[]{:S(2)}) copy-start(f32[256]{0:T(256)} %param.16) | copy-start | bytes 3076
  70.2 15.2 %copy-start.8 = (f32[256]{0:T(256)S(1)}, f32[256]{0:T(256)}, u32[]{:S(2)}) copy-start(f32[256]{0:T(256)} %param.17) | copy-start | bytes 3076
  70.2 15.2 %all-to-all-start.1 = ((f32[128,1,128]{2,1,0:T(1,128)}), f32[128,1,128]{2,1,0:T(1,128)S(1)}, u32[]{:S(2)}, u32[]{:S(2)}) async-start(f32[128,1,128]{2,1,0:T(1,128)} %bitcast.18), calls=%async_computation.1 | async-start | bytes 131072 | tf_op jit(solution)/shard_map/all_to_all | solution.py:682
  85.4 11.0 %copy-start.6 = (f32[256]{0:T(256)S(1)}, f32[256]{0:T(256)}, u32[]{:S(2)}) copy-start(f32[256]{0:T(256)} %param.19) | copy-start | bytes 3076
  87.8 2.6 %collective-permute-start.10 = (bf16[2320,128]{1,0:T(8,128)(2,1)S(1)}, bf16[2320,128]{1,0:T(8,128)(2,1)S(1)}, u32[]{:S(2)}, u32[]{:S(2)}) collective-permute-start(bf16[2320,128]{1,0:T(8,128)(2,1)S(1)} %get-tuple-element.34), channel_id=1, source_target_pairs={{1,0},{0,1},{3,2},{2,3},{5,4},{4,5},{7,6},{6,7},{9,8},{8,9},{11,10... | collective-permute-start | bytes 1781768 | tf_op jit(solution)/shard_map/ppermute | solution.py:631
  91.5 18.8 %all-to-all-start.2 = ((bf16[64,40,128]{2,1,0:T(8,128)(2,1)}), bf16[64,40,128]{2,1,0:T(8,128)(2,1)S(1)}, u32[]{:S(2)}, u32[]{:S(2)}) async-start(bf16[64,40,128]{2,1,0:T(8,128)(2,1)} %shard_map.145), calls=%async_computation.2 | async-start | bytes 1310720 | tf_op jit(solution)/shard_map/all_to_all | solution.py:691
  96.4 1.2 copy-start.3
  111.3 17.5 %all-to-all-start.3 = ((bf16[64,40,128]{2,1,0:T(8,128)(2,1)}), bf16[64,40,128]{2,1,0:T(8,128)(2,1)S(1)}, u32[]{:S(2)}, u32[]{:S(2)}) async-start(bf16[64,40,128]{2,1,0:T(8,128)(2,1)} %get-tuple-element.38), calls=%async_computation.3 | async-start | bytes 1310720 | tf_op jit(solution)/shard_map/all_to_all | solution.py:696
  116.0 2.8 %collective-permute-start.11 = (f32[8,256]{1,0:T(8,128)S(1)}, f32[8,256]{1,0:T(8,128)S(1)}, u32[]{:S(2)}, u32[]{:S(2)}) collective-permute-start(f32[8,256]{1,0:T(8,128)S(1)} %get-tuple-element.39.mine), channel_id=1, source_target_pairs={{1,0},{0,1},{3,2},{2,3},{5,4},{4,5},{7,6},{6,7},{9,8},{8,9},{11,10... | collective-permute-start | bytes 24584 | tf_op jit(solution)/shard_map/ppermute | solution.py:631
  128.9 4.6 %collective-permute-start.12 = (bf16[64,40,128]{2,1,0:T(8,128)(2,1)S(1)}, bf16[64,40,128]{2,1,0:T(8,128)(2,1)S(1)}, u32[]{:S(2)}, u32[]{:S(2)}) collective-permute-start(bf16[64,40,128]{2,1,0:T(8,128)(2,1)S(1)} %all-to-all-done.3.mine), channel_id=1, source_target_pairs={{1,0},{0,1},{3,2},{2,3},{5,4},{4,5},{7,6},{6,7},{9,8},{8,9},{11,10... | collective-permute-start | bytes 1966088 | tf_op jit(solution)/shard_map/ppermute | solution.py:631

commit v8 on v7

--- a/solution.py
+++ b/solution.py
@@ -316,7 +316,7 @@
     loads[1].wait()
     merged = kept[PART:, :].astype(F32) + dot(attended.astype(BF16), w_proj[...])
     cell = iota((CELLS_IN, C), 0)
-    col = lax.rem(cell, 10)
+    col = cell - 10 * ((cell * 6554) >> 16)
     outside = (
         ((cell < 10) & flag(flags, 0, cell.shape))
         | ((cell >= 170) & flag(flags, 1, cell.shape))

time: 136 us -> 136 us (level)
  no operation moved by 1% of the time
where the time goes in v8:
time: 136 us; the launch traced here: 135 us
  waiting for transfers between devices  50.3 us (37%)
  starting transfers between devices  47.8 us (35%)
  Pallas kernels  32.1 us (24%)
  local copies, waits for them, and re-layouts  2.77 us (2%)
    ppermute x11, starting transfers between devices, shift(): lax.ppermute(value, axis, [((i + step) % count, i) for i in range(count)])  17.7 us
    pallas_call x1, Pallas kernels, partial_attention(): pl.pallas_call(attention_kernel, out_shape=(jax.ShapeDtypeStruct((PART, C...  16.8 us
    ppermute x11, waiting for transfers between devices, shift(): lax.ppermute(value, axis, [((i + step) % count, i) for i in range(count)])  12.4 us
    all_to_all x1, waiting for transfers between devices, per_device(): got = lax.all_to_all(sent, ('y', 'z', 'x'), 0, 0, tiled=True)  11.3 us
    all_to_all x1, waiting for transfers between devices, per_device(): spread = lax.all_to_all(chunk, ('y', 'z', 'x'), 0, 0, tiled=True)  8.74 us
    all_to_all x1, starting transfers between devices, per_device(): lax.all_to_all(copies_of(own), ('z', 'x'), 0, 0, tiled=True)  8.44 us
    all_to_all x1, waiting for transfers between devices, per_device(): stats2 = lax.all_to_all(stats2.reshape(128, 1, 128), ALL, 0, 0, tiled=True)  8.43 us
    ppermute x1, waiting for transfers between devices, per_device(): after = lax.ppermute(first, ZXC, [(i + 1, i) for i in range(31)])[:, None]  7.84 us
  transfers between devices with their start and end apart: 17, of which 14 were waited for; matrix products, arithmetic and copies ran while one was open for 2% of the time, Pallas kernels for 3%

profile of v8, /device:TPU:1, one launch (start us, length us, event | category | flops | bytes accessed | tf_op | source)
XLA Modules:
  0.0 135.2 jit_solution(13449661667867381836)
XLA Ops:
  0.7 2.0 %shard_map.138 = bf16[16,128,256]{2,1,0:T(8,128)(2,1)} custom-call(bf16[128,256]{1,0:T(8,128)(2,1)} %bitcast.67), custom_call_target="tpu_custom_call" | custom-call | tf_op jit(solution)/shard_map/pallas_call | solution.py:616
  2.7 8.4 %all-to-all-start = ((bf16[16,128,256]{2,1,0:T(8,128)(2,1)}), bf16[16,128,256]{2,1,0:T(8,128)(2,1)S(1)}, u32[]{:S(2)}, u32[]{:S(2)}) async-start(bf16[16,128,256]{2,1,0:T(8,128)(2,1)} %shard_map.138), calls=%async_computation | async-start | bytes 2097152 | tf_op jit(solution)/shard_map/all_to_all | solution.py:654
  11.3 2.9 %collective-permute-start.3 = (bf16[48,256]{1,0:T(8,128)(2,1)S(1)}, bf16[48,256]{1,0:T(8,128)(2,1)S(1)}, u32[]{:S(2)}, u32[]{:S(2)}) collective-permute-start(bf16[48,256]{1,0:T(8,128)(2,1)S(1)} %pad_maximum_fusion.3), channel_id=1, source_target_pairs={{1,0},{2,1},{3,2},{4,3},{5,4},{6,5},{7,6},{8,7},{9,8},{10,9},{11,1... | collective-permute-start | bytes 73736 | tf_op jit(solution)/shard_map/ppermute | solution.py:660
  14.2 3.4 %collective-permute-start.2 = (bf16[48,256]{1,0:T(8,128)(2,1)S(1)}, bf16[48,256]{1,0:T(8,128)(2,1)S(1)}, u32[]{:S(2)}, u32[]{:S(2)}) collective-permute-start(bf16[48,256]{1,0:T(8,128)(2,1)S(1)} %pad_maximum_fusion.2), channel_id=1, source_target_pairs={{0,1},{1,2},{2,3},{3,4},{4,5},{5,6},{6,7},{7,8},{8,9},{9,10},{10,1... | collective-permute-start | bytes 73736 | tf_op jit(solution)/shard_map/ppermute | solution.py:659
  17.6 7.8 %collective-permute-done.3 = bf16[48,256]{1,0:T(8,128)(2,1)S(1)} collective-permute-done((bf16[48,256]{1,0:T(8,128)(2,1)S(1)}, bf16[48,256]{1,0:T(8,128)(2,1)S(1)}, u32[]{:S(2)}, u32[]{:S(2)}) %collective-permute-start.3) | collective-permute-done | bytes 24608 | tf_op jit(solution)/shard_map/ppermute | solution.py:660
  25.5 1.6 %all-to-all-done = bf16[16,128,256]{2,1,0:T(8,128)(2,1)S(1)} async-done(((bf16[16,128,256]{2,1,0:T(8,128)(2,1)}), bf16[16,128,256]{2,1,0:T(8,128)(2,1)S(1)}, u32[]{:S(2)}, u32[]{:S(2)}) %all-to-all-start) | async-done | bytes 1048608 | tf_op jit(solution)/shard_map/all_to_all | solution.py:654
  27.1 2.6 %collective-permute-start = (bf16[2048,256]{1,0:T(8,128)(2,1)S(1)}, bf16[2048,256]{1,0:T(8,128)(2,1)S(1)}, u32[]{:S(2)}, u32[]{:S(2)}) collective-permute-start(bf16[2048,256]{1,0:T(8,128)(2,1)S(1)} %bitcast.48), channel_id=1, source_target_pairs={{1,0},{0,1},{3,2},{2,3},{5,4},{4,5},{7,6},{6,7},{9,8},{8,9},{11,10... | collective-permute-start | bytes 3145736 | tf_op jit(solution)/shard_map/ppermute | solution.py:631
  29.9 0.7 pad_maximum_fusion.1
  30.6 0.9 shard_map.139.first
  31.5 0.1 collective-permute-start.1
  31.6 1.0 reshape.118.wide
  32.6 0.1 collective-permute-done.1.other
  32.8 1.4 %collective-permute-start.6 = (bf16[208,256]{1,0:T(8,128)(2,1)S(1)}, bf16[208,256]{1,0:T(8,128)(2,1)S(1)}, u32[]{:S(2)}, u32[]{:S(2)}) collective-permute-start(bf16[208,256]{1,0:T(8,128)(2,1)S(1)} %get-tuple-element.26), channel_id=1, source_target_pairs={{96,0},{0,32},{32,64},{64,96},{97,1},{1,33},{33,65},{65,97},{98,2}... | collective-permute-start | bytes 319496 | tf_op jit(solution)/shard_map/ppermute | solution.py:631
  34.1 0.1 stack.29
  34.3 2.7 %collective-permute-start.4 = (bf16[176,256]{1,0:T(8,128)(2,1)}, bf16[176,256]{1,0:T(8,128)(2,1)S(1)}, u32[]{:S(2)}, u32[]{:S(2)}) collective-permute-start(bf16[176,256]{1,0:T(8,128)(2,1)} %copy-done.9), channel_id=1, source_target_pairs={{64,0},{96,32},{0,64},{32,96},{65,1},{97,33},{1,65},{33,97},{66,2}... | collective-permute-start | bytes 270344 | tf_op jit(solution)/shard_map/ppermute | solution.py:631
  37.0 1.1 collective-permute-start.5
  38.0 0.4 collective-permute-done.6.up
  38.4 3.4 %collective-permute-done.5.down = bf16[208,256]{1,0:T(8,128)(2,1)S(1)} collective-permute-done((bf16[208,256]{1,0:T(8,128)(2,1)S(1)}, bf16[208,256]{1,0:T(8,128)(2,1)S(1)}, u32[]{:S(2)}, u32[]{:S(2)}) %collective-permute-start.5) | collective-permute-done | bytes 106528 | tf_op jit(solution)/shard_map/ppermute | solution.py:631
  41.8 16.8 %shard_map.141 = (bf16[208,256]{1,0:T(8,128)(2,1)S(1)}, bf16[208,256]{1,0:T(8,128)(2,1)S(1)}, bf16[208,256]{1,0:T(8,128)(2,1)S(1)}, bf16[400,256]{1,0:T(8,128)(2,1)}) custom-call(bf16[2048,256]{1,0:T(8,128)(2,1)S(1)} %bitcast.50, bf16[2048,256]{1,0:T(8,128)(2,1)S(1)} %collective-permute-done.other, bf16[208,256]{1,0:T(8,128)(2,1)S(1)} %get-tuple-element.24.near, ...), custom_call_target="tpu_custom_call" | custom-call | tf_op jit(solution)/shard_map/pallas_call | solution.py:270
  58.6 1.6 %collective-permute-start.7 = (bf16[208,256]{1,0:T(8,128)(2,1)S(1)}, bf16[208,256]{1,0:T(8,128)(2,1)S(1)}, u32[]{:S(2)}, u32[]{:S(2)}) collective-permute-start(bf16[208,256]{1,0:T(8,128)(2,1)S(1)} %get-tuple-element.27), channel_id=1, source_target_pairs={{96,0},{0,32},{32,64},{64,96},{97,1},{1,33},{33,65},{65,97},{98,2}... | collective-permute-start | bytes 319496 | tf_op jit(solution)/shard_map/ppermute | solution.py:631
  60.2 2.2 %collective-permute-start.8 = (bf16[208,256]{1,0:T(8,128)(2,1)S(1)}, bf16[208,256]{1,0:T(8,128)(2,1)S(1)}, u32[]{:S(2)}, u32[]{:S(2)}) collective-permute-start(bf16[208,256]{1,0:T(8,128)(2,1)S(1)} %get-tuple-element.28), channel_id=1, source_target_pairs={{64,0},{96,32},{0,64},{32,96},{65,1},{97,33},{1,65},{33,97},{66,2}... | collective-permute-start | bytes 319496 | tf_op jit(solution)/shard_map/ppermute | solution.py:631
  62.4 0.4 collective-permute-start.9
  62.8 0.2 pad_maximum_fusion
  63.0 0.5 collective-permute-done.7.p1
  63.5 2.8 %collective-permute-done.8.p2 = bf16[208,256]{1,0:T(8,128)(2,1)S(1)} collective-permute-done((bf16[208,256]{1,0:T(8,128)(2,1)S(1)}, bf16[208,256]{1,0:T(8,128)(2,1)S(1)}, u32[]{:S(2)}, u32[]{:S(2)}) %collective-permute-start.8) | collective-permute-done | bytes 106528 | tf_op jit(solution)/shard_map/ppermute | solution.py:631
  66.3 1.0 collective-permute-done.9.p3
  67.4 2.8 %shard_map.142 = (bf16[192,256]{1,0:T(8,128)(2,1)S(1)}, f32[128,128]{1,0:T(8,128)}) custom-call(s32[8,256]{1,0:T(8,128)S(1)} %broadcast_in_dim.34.flags, bf16[208,256]{1,0:T(8,128)(2,1)S(1)} %collective-permute-done.7.p1, bf16[208,256]{1,0:T(8,128)(2,1)S(1)} %collective-permute-done.8.p2, bf16[208,256]{1,0:T(8,128)(2,1)S(1)} %collective-permute-done.9.p3, ...), custom_call_target="tpu_custom_call" | custom-call | tf_op jit(solution)/shard_map/pallas_call | solution.py:336
  70.2 5.7 %all-to-all-start.1 = ((f32[128,1,128]{2,1,0:T(1,128)}), f32[128,1,128]{2,1,0:T(1,128)S(1)}, u32[]{:S(2)}, u32[]{:S(2)}) async-start(f32[128,1,128]{2,1,0:T(1,128)} %bitcast.18), calls=%async_computation.1 | async-start | bytes 131072 | tf_op jit(solution)/shard_map/all_to_all | solution.py:682
  76.0 0.2 fusion.13
  76.2 0.8 shard_map.143.grad_hidden
  77.0 8.4 %all-to-all-done.1 = f32[128,1,128]{2,1,0:T(1,128)S(1)} async-done(((f32[128,1,128]{2,1,0:T(1,128)}), f32[128,1,128]{2,1,0:T(1,128)S(1)}, u32[]{:S(2)}, u32[]{:S(2)}) %all-to-all-start.1) | async-done | bytes 65568 | tf_op jit(solution)/shard_map/all_to_all | solution.py:682
  85.4 2.4 %shard_map.144 = (bf16[2320,128]{1,0:T(8,128)(2,1)S(1)}, bf16[2320,128]{1,0:T(8,128)(2,1)S(1)}, bf16[3,544,256]{2,1,0:T(8,128)(2,1)}) custom-call(s32[8,256]{1,0:T(8,128)S(1)} %broadcast_in_dim.34.flags, bf16[192,256]{1,0:T(8,128)(2,1)S(1)} %get-tuple-element.31.merged, bf16[1632,192]{1,0:T(8,128)(2,1)S(1)} %copy-done.1, f32[128,128]{1,0:T(8,128)S(1)} %bitcast.57, ...), custom_call_target="tpu_custom_call" | custom-call | tf_op jit(solution)/shard_map/pallas_call | solution.py:435
  87.8 0.9 collective-permute-start.10
  88.8 1.6 %collective-permute-done.10.got = bf16[2320,128]{1,0:T(8,128)(2,1)S(1)} collective-permute-done((bf16[2320,128]{1,0:T(8,128)(2,1)S(1)}, bf16[2320,128]{1,0:T(8,128)(2,1)S(1)}, u32[]{:S(2)}, u32[]{:S(2)}) %collective-permute-start.10) | collective-permute-done | bytes 593952 | tf_op jit(solution)/shard_map/ppermute | solution.py:631
  90.4 1.1 shard_map.145
  91.5 4.9 %all-to-all-start.2 = ((bf16[64,40,128]{2,1,0:T(8,128)(2,1)}), bf16[64,40,128]{2,1,0:T(8,128)(2,1)S(1)}, u32[]{:S(2)}, u32[]{:S(2)}) async-start(bf16[64,40,128]{2,1,0:T(8,128)(2,1)} %shard_map.145), calls=%async_computation.2 | async-start | bytes 1310720 | tf_op jit(solution)/shard_map/all_to_all | solution.py:691
  96.4 1.1 copy-done.3
  97.6 1.5 %shard_map.146 = bf16[512,256]{1,0:T(8,128)(2,1)} custom-call(bf16[3,544,256]{2,1,0:T(8,128)(2,1)S(1)} %copy-done.3, bf16[9,256,256]{2,1,0:T(8,128)(2,1)S(1)} %bitcast.52, f32[1,256]{1,0:T(1,128)S(1)} %bitcast.61), custom_call_target="tpu_custom_call" | custom-call | flops 603979776 | bytes 3000000 | tf_op jit(solution)/shard_map/pallas_call | solution.py:458
  99.1 11.3 %all-to-all-done.2.got = bf16[64,40,128]{2,1,0:T(8,128)(2,1)S(1)} async-done(((bf16[64,40,128]{2,1,0:T(8,128)(2,1)}), bf16[64,40,128]{2,1,0:T(8,128)(2,1)S(1)}, u32[]{:S(2)}, u32[]{:S(2)}) %all-to-all-start.2) | async-done | bytes 655392 | tf_op jit(solution)/shard_map/all_to_all | solution.py:691
  110.3 1.0 shard_map.147
  111.3 4.7 %all-to-all-start.3 = ((bf16[64,40,128]{2,1,0:T(8,128)(2,1)}), bf16[64,40,128]{2,1,0:T(8,128)(2,1)S(1)}, u32[]{:S(2)}, u32[]{:S(2)}) async-start(bf16[64,40,128]{2,1,0:T(8,128)(2,1)} %get-tuple-element.38), calls=%async_computation.3 | async-start | bytes 1310720 | tf_op jit(solution)/shard_map/all_to_all | solution.py:696
  116.0 1.9 %collective-permute-start.11 = (f32[8,256]{1,0:T(8,128)S(1)}, f32[8,256]{1,0:T(8,128)S(1)}, u32[]{:S(2)}, u32[]{:S(2)}) collective-permute-start(f32[8,256]{1,0:T(8,128)S(1)} %get-tuple-element.39.mine), channel_id=1, source_target_pairs={{1,0},{0,1},{3,2},{2,3},{5,4},{4,5},{7,6},{6,7},{9,8},{8,9},{11,10... | collective-permute-start | bytes 24584 | tf_op jit(solution)/shard_map/ppermute | solution.py:631
  117.9 0.8 collective-permute-done.11.other
  118.7 1.4 %shard_map.148 = (bf16[512,256]{1,0:T(8,128)(2,1)}, f32[2,256]{1,0:T(2,128)}) custom-call(s32[8,256]{1,0:T(8,128)S(1)} %broadcast_in_dim.34.flags, bf16[192,256]{1,0:T(8,128)(2,1)S(1)} %get-tuple-element.31.merged, bf16[1632,192]{1,0:T(8,128)(2,1)S(1)} %copy-done.1, f32[128,128]{1,0:T(8,128)S(1)} %bitcast.58, f32[1,256]{1,0:T(1,128)S(1)} %bitcast.63, ...), custom_call_target="tpu_custom_call" | custom-call | flops 1000000000 | bytes 2000000 | tf_op jit(solution)/shard_map/pallas_call | solution.py:557
  120.1 8.7 %all-to-all-done.3.mine = bf16[64,40,128]{2,1,0:T(8,128)(2,1)S(1)} async-done(((bf16[64,40,128]{2,1,0:T(8,128)(2,1)}), bf16[64,40,128]{2,1,0:T(8,128)(2,1)S(1)}, u32[]{:S(2)}, u32[]{:S(2)}) %all-to-all-start.3) | async-done | bytes 655392 | tf_op jit(solution)/shard_map/all_to_all | solution.py:696
  128.9 2.9 %collective-permute-start.12 = (bf16[64,40,128]{2,1,0:T(8,128)(2,1)S(1)}, bf16[64,40,128]{2,1,0:T(8,128)(2,1)S(1)}, u32[]{:S(2)}, u32[]{:S(2)}) collective-permute-start(bf16[64,40,128]{2,1,0:T(8,128)(2,1)S(1)} %all-to-all-done.3.mine), channel_id=1, source_target_pairs={{1,0},{0,1},{3,2},{2,3},{5,4},{4,5},{7,6},{6,7},{9,8},{8,9},{11,10... | collective-permute-start | bytes 1966088 | tf_op jit(solution)/shard_map/ppermute | solution.py:631
  131.8 1.7 %collective-permute-done.12.other = bf16[64,40,128]{2,1,0:T(8,128)(2,1)S(1)} collective-permute-done((bf16[64,40,128]{2,1,0:T(8,128)(2,1)S(1)}, bf16[64,40,128]{2,1,0:T(8,128)(2,1)S(1)}, u32[]{:S(2)}, u32[]{:S(2)}) %collective-permute-start.12) | collective-permute-done | bytes 655392 | tf_op jit(solution)/shard_map/ppermute | solution.py:631
  133.5 1.5 %shard_map.149 = f32[2304,256]{1,0:T(8,128)} custom-call(s32[8,256]{1,0:T(8,128)S(1)} %broadcast_in_dim.34.flags, bf16[64,40,128]{2,1,0:T(8,128)(2,1)S(1)} %all-to-all-done.3.mine, bf16[64,40,128]{2,1,0:T(8,128)(2,1)S(1)} %collective-permute-done.12.other), custom_call_target="tpu_custom_call" | custom-call | tf_op jit(solution)/shard_map/pallas_call | solution.py:592
  (55 shorter events, 0.4 us)
Async XLA Ops:
  0.6 10.5 %copy-start.10 = (bf16[16,8,256]{2,1,0:T(8,128)(2,1)S(1)}, bf16[16,8,256]{2,1,0:T(8,128)(2,1)}, u32[]{:S(2)}) copy-start(bf16[16,8,256]{2,1,0:T(8,128)(2,1)} %param.11) | copy-start | bytes 196612
  0.6 10.5 %copy-start.2 = (bf16[32,16,256]{2,1,0:T(8,128)(2,1)S(1)}, bf16[32,16,256]{2,1,0:T(8,128)(2,1)}, u32[]{:S(2)}) copy-start(bf16[32,16,256]{2,1,0:T(8,128)(2,1)} %param.20) | copy-start | bytes 786436
  2.6 39.2 %copy-start.4 = (f32[256]{0:T(256)S(1)}, f32[256]{0:T(256)}, u32[]{:S(2)}) copy-start(f32[256]{0:T(256)} %param.12) | copy-start | bytes 3076
  2.7 39.2 %copy-start.5 = (f32[256]{0:T(256)S(1)}, f32[256]{0:T(256)}, u32[]{:S(2)}) copy-start(f32[256]{0:T(256)} %param.13) | copy-start | bytes 3076
  2.7 24.4 %all-to-all-start = ((bf16[16,128,256]{2,1,0:T(8,128)(2,1)}), bf16[16,128,256]{2,1,0:T(8,128)(2,1)S(1)}, u32[]{:S(2)}, u32[]{:S(2)}) async-start(bf16[16,128,256]{2,1,0:T(8,128)(2,1)} %shard_map.138), calls=%async_computation | async-start | bytes 2097152 | tf_op jit(solution)/shard_map/all_to_all | solution.py:654
  11.3 14.2 %collective-permute-start.3 = (bf16[48,256]{1,0:T(8,128)(2,1)S(1)}, bf16[48,256]{1,0:T(8,128)(2,1)S(1)}, u32[]{:S(2)}, u32[]{:S(2)}) collective-permute-start(bf16[48,256]{1,0:T(8,128)(2,1)S(1)} %pad_maximum_fusion.3), channel_id=1, source_target_pairs={{1,0},{2,1},{3,2},{4,3},{5,4},{6,5},{7,6},{8,7},{9,8},{10,9},{11,1... | collective-permute-start | bytes 73736 | tf_op jit(solution)/shard_map/ppermute | solution.py:660
  14.2 15.5 %collective-permute-start.2 = (bf16[48,256]{1,0:T(8,128)(2,1)S(1)}, bf16[48,256]{1,0:T(8,128)(2,1)S(1)}, u32[]{:S(2)}, u32[]{:S(2)}) collective-permute-start(bf16[48,256]{1,0:T(8,128)(2,1)S(1)} %pad_maximum_fusion.2), channel_id=1, source_target_pairs={{0,1},{1,2},{2,3},{3,4},{4,5},{5,6},{6,7},{7,8},{8,9},{9,10},{10,1... | collective-permute-start | bytes 73736 | tf_op jit(solution)/shard_map/ppermute | solution.py:659
  27.1 14.7 %collective-permute-start = (bf16[2048,256]{1,0:T(8,128)(2,1)S(1)}, bf16[2048,256]{1,0:T(8,128)(2,1)S(1)}, u32[]{:S(2)}, u32[]{:S(2)}) collective-permute-start(bf16[2048,256]{1,0:T(8,128)(2,1)S(1)} %bitcast.48), channel_id=1, source_target_pairs={{1,0},{0,1},{3,2},{2,3},{5,4},{4,5},{7,6},{6,7},{9,8},{8,9},{11,10... | collective-permute-start | bytes 3145736 | tf_op jit(solution)/shard_map/ppermute | solution.py:631
  29.8 2.9 %copy-start.11 = (bf16[32,1,256]{2,1,0:T(2,128)(2,1)}, bf16[32,1,256]{2,1,0:T(2,128)(2,1)S(1)}, u32[]{:S(2)}) copy-start(bf16[32,1,256]{2,1,0:T(2,128)(2,1)S(1)} %copy.36) | copy-start | bytes 49156
  29.9 1.7 %copy-start.13 = (bf16[32,1,256]{2,1,0:T(2,128)(2,1)}, bf16[32,1,256]{2,1,0:T(2,128)(2,1)S(1)}, u32[]{:S(2)}) copy-start(bf16[32,1,256]{2,1,0:T(2,128)(2,1)S(1)} %copy.35) | copy-start | bytes 49156
  31.5 35.9 %copy-start.1 = (bf16[1632,192]{1,0:T(8,128)(2,1)S(1)}, bf16[1632,192]{1,0:T(8,128)(2,1)}, u32[]{:S(2)}) copy-start(bf16[1632,192]{1,0:T(8,128)(2,1)} %constant.31.clone.up) | copy-start | bytes 1880068
  31.5 1.3 collective-permute-start.1
  32.8 1.4 %copy-start.9 = (bf16[176,256]{1,0:T(8,128)(2,1)}, bf16[176,256]{1,0:T(8,128)(2,1)S(1)}, u32[]{:S(2)}) copy-start(bf16[176,256]{1,0:T(8,128)(2,1)S(1)} %get-tuple-element.25) | copy-start | bytes 270340
  32.8 5.6 %collective-permute-start.6 = (bf16[208,256]{1,0:T(8,128)(2,1)S(1)}, bf16[208,256]{1,0:T(8,128)(2,1)S(1)}, u32[]{:S(2)}, u32[]{:S(2)}) collective-permute-start(bf16[208,256]{1,0:T(8,128)(2,1)S(1)} %get-tuple-element.26), channel_id=1, source_target_pairs={{96,0},{0,32},{32,64},{64,96},{97,1},{1,33},{33,65},{65,97},{98,2}... | collective-permute-start | bytes 319496 | tf_op jit(solution)/shard_map/ppermute | solution.py:631
  34.2 28.5 %copy-start.12 = (bf16[32,1,256]{2,1,0:T(2,128)(2,1)S(1)}, bf16[32,1,256]{2,1,0:T(2,128)(2,1)}, u32[]{:S(2)}) copy-start(bf16[32,1,256]{2,1,0:T(2,128)(2,1)} %copy-done.11) | copy-start | bytes 49156
  34.2 28.5 %copy-start.14 = (bf16[32,1,256]{2,1,0:T(2,128)(2,1)S(1)}, bf16[32,1,256]{2,1,0:T(2,128)(2,1)}, u32[]{:S(2)}) copy-start(bf16[32,1,256]{2,1,0:T(2,128)(2,1)} %copy-done.13) | copy-start | bytes 49156
  34.3 7.5 %collective-permute-start.4 = (bf16[176,256]{1,0:T(8,128)(2,1)}, bf16[176,256]{1,0:T(8,128)(2,1)S(1)}, u32[]{:S(2)}, u32[]{:S(2)}) collective-permute-start(bf16[176,256]{1,0:T(8,128)(2,1)} %copy-done.9), channel_id=1, source_target_pairs={{64,0},{96,32},{0,64},{32,96},{65,1},{97,33},{1,65},{33,97},{66,2}... | collective-permute-start | bytes 270344 | tf_op jit(solution)/shard_map/ppermute | solution.py:631
  37.0 4.8 %collective-permute-start.5 = (bf16[208,256]{1,0:T(8,128)(2,1)S(1)}, bf16[208,256]{1,0:T(8,128)(2,1)S(1)}, u32[]{:S(2)}, u32[]{:S(2)}) collective-permute-start(bf16[208,256]{1,0:T(8,128)(2,1)S(1)} %get-tuple-element.24.near), channel_id=1, source_target_pairs={{32,0},{64,32},{96,64},{0,96},{33,1},{65,33},{97,65},{1,97},{34,2}... | collective-permute-start | bytes 319496 | tf_op jit(solution)/shard_map/ppermute | solution.py:631
  58.6 17.5 %copy-start = (bf16[3,3,256,256]{3,2,1,0:T(8,128)(2,1)S(1)}, bf16[3,3,256,256]{3,2,1,0:T(8,128)(2,1)}, u32[]{:S(2)}) copy-start(bf16[3,3,256,256]{3,2,1,0:T(8,128)(2,1)} %param.18) | copy-start | bytes 3538948
  58.6 4.8 %collective-permute-start.7 = (bf16[208,256]{1,0:T(8,128)(2,1)S(1)}, bf16[208,256]{1,0:T(8,128)(2,1)S(1)}, u32[]{:S(2)}, u32[]{:S(2)}) collective-permute-start(bf16[208,256]{1,0:T(8,128)(2,1)S(1)} %get-tuple-element.27), channel_id=1, source_target_pairs={{96,0},{0,32},{32,64},{64,96},{97,1},{1,33},{33,65},{65,97},{98,2}... | collective-permute-start | bytes 319496 | tf_op jit(solution)/shard_map/ppermute | solution.py:631
  60.2 6.1 %collective-permute-start.8 = (bf16[208,256]{1,0:T(8,128)(2,1)S(1)}, bf16[208,256]{1,0:T(8,128)(2,1)S(1)}, u32[]{:S(2)}, u32[]{:S(2)}) collective-permute-start(bf16[208,256]{1,0:T(8,128)(2,1)S(1)} %get-tuple-element.28), channel_id=1, source_target_pairs={{64,0},{96,32},{0,64},{32,96},{65,1},{97,33},{1,65},{33,97},{66,2}... | collective-permute-start | bytes 319496 | tf_op jit(solution)/shard_map/ppermute | solution.py:631
  62.4 5.0 %collective-permute-start.9 = (bf16[208,256]{1,0:T(8,128)(2,1)S(1)}, bf16[208,256]{1,0:T(8,128)(2,1)S(1)}, u32[]{:S(2)}, u32[]{:S(2)}) collective-permute-start(bf16[208,256]{1,0:T(8,128)(2,1)S(1)} %get-tuple-element.29), channel_id=1, source_target_pairs={{32,0},{64,32},{96,64},{0,96},{33,1},{65,33},{97,65},{1,97},{34,2}... | collective-permute-start | bytes 319496 | tf_op jit(solution)/shard_map/ppermute | solution.py:631
  70.2 15.2 %copy-start.7 = (f32[256]{0:T(256)S(1)}, f32[256]{0:T(256)}, u32[]{:S(2)}) copy-start(f32[256]{0:T(256)} %param.16) | copy-start | bytes 3076
  70.2 15.2 %copy-start.8 = (f32[256]{0:T(256)S(1)}, f32[256]{0:T(256)}, u32[]{:S(2)}) copy-start(f32[256]{0:T(256)} %param.17) | copy-start | bytes 3076
  70.2 15.2 %all-to-all-start.1 = ((f32[128,1,128]{2,1,0:T(1,128)}), f32[128,1,128]{2,1,0:T(1,128)S(1)}, u32[]{:S(2)}, u32[]{:S(2)}) async-start(f32[128,1,128]{2,1,0:T(1,128)} %bitcast.18), calls=%async_computation.1 | async-start | bytes 131072 | tf_op jit(solution)/shard_map/all_to_all | solution.py:682
  85.4 11.0 %copy-start.6 = (f32[256]{0:T(256)S(1)}, f32[256]{0:T(256)}, u32[]{:S(2)}) copy-start(f32[256]{0:T(256)} %param.19) | copy-start | bytes 3076
  87.8 2.6 %collective-permute-start.10 = (bf16[2320,128]{1,0:T(8,128)(2,1)S(1)}, bf16[2320,128]{1,0:T(8,128)(2,1)S(1)}, u32[]{:S(2)}, u32[]{:S(2)}) collective-permute-start(bf16[2320,128]{1,0:T(8,128)(2,1)S(1)} %get-tuple-element.34), channel_id=1, source_target_pairs={{1,0},{0,1},{3,2},{2,3},{5,4},{4,5},{7,6},{6,7},{9,8},{8,9},{11,10... | collective-permute-start | bytes 1781768 | tf_op jit(solution)/shard_map/ppermute | solution.py:631
  91.5 18.8 %all-to-all-start.2 = ((bf16[64,40,128]{2,1,0:T(8,128)(2,1)}), bf16[64,40,128]{2,1,0:T(8,128)(2,1)S(1)}, u32[]{:S(2)}, u32[]{:S(2)}) async-start(bf16[64,40,128]{2,1,0:T(8,128)(2,1)} %shard_map.145), calls=%async_computation.2 | async-start | bytes 1310720 | tf_op jit(solution)/shard_map/all_to_all | solution.py:691
  96.4 1.2 copy-start.3
  111.3 17.5 %all-to-all-start.3 = ((bf16[64,40,128]{2,1,0:T(8,128)(2,1)}), bf16[64,40,128]{2,1,0:T(8,128)(2,1)S(1)}, u32[]{:S(2)}, u32[]{:S(2)}) async-start(bf16[64,40,128]{2,1,0:T(8,128)(2,1)} %get-tuple-element.38), calls=%async_computation.3 | async-start | bytes 1310720 | tf_op jit(solution)/shard_map/all_to_all | solution.py:696
  116.0 2.8 %collective-permute-start.11 = (f32[8,256]{1,0:T(8,128)S(1)}, f32[8,256]{1,0:T(8,128)S(1)}, u32[]{:S(2)}, u32[]{:S(2)}) collective-permute-start(f32[8,256]{1,0:T(8,128)S(1)} %get-tuple-element.39.mine), channel_id=1, source_target_pairs={{1,0},{0,1},{3,2},{2,3},{5,4},{4,5},{7,6},{6,7},{9,8},{8,9},{11,10... | collective-permute-start | bytes 24584 | tf_op jit(solution)/shard_map/ppermute | solution.py:631
  128.9 4.6 %collective-permute-start.12 = (bf16[64,40,128]{2,1,0:T(8,128)(2,1)S(1)}, bf16[64,40,128]{2,1,0:T(8,128)(2,1)S(1)}, u32[]{:S(2)}, u32[]{:S(2)}) collective-permute-start(bf16[64,40,128]{2,1,0:T(8,128)(2,1)S(1)} %all-to-all-done.3.mine), channel_id=1, source_target_pairs={{1,0},{0,1},{3,2},{2,3},{5,4},{4,5},{7,6},{6,7},{9,8},{8,9},{11,10... | collective-permute-start | bytes 1966088 | tf_op jit(solution)/shard_map/ppermute | solution.py:631
